TPU v7x, 512 devices: a whole 4x8x8 slice. The times are simulated.
512 devices in a mesh: lon: 32 (over y, z_hi, core), lat: 16 (over x, z_lo).
Axes of the slice: x: 4, y: 8, z: 8 (z_hi: 2, z_lo: 4; z = z_hi * 4 + z_lo), core: 2. Of those that a mesh axis runs over, the one named last changes fastest.
Arguments:
- temp: float32 [8, 384, 4096], P(None, 'lat', 'lon'), may hold values from -6 to 6
- kmt: int32 [384, 4096], P('lat', 'lon'), may hold values from 0 to 8
- kappa: float32 [384, 4096], P('lat', 'lon'), may hold values from 0.05 to 0.5
- helm: float32 [384, 4096], P('lat', 'lon'), may hold values from 0.02 to 0.2
- forcing: float32 [384, 4096], P('lat', 'lon'), may hold values from -6 to 6
- cutoff: int32 [384], P('lat'), may hold values from 256 to 2049, as said below
- conv_in: bfloat16 [9, 64, 8], replicated, may hold values from -0.75 to 0.75
- conv_mid: bfloat16 [9, 64, 64], replicated, may hold values from -0.25 to 0.25
- conv_late: bfloat16 [9, 64, 64], replicated, may hold values from -0.25 to 0.25
- conv_out: bfloat16 [9, 8, 64], replicated, may hold values from -0.25 to 0.25
Outputs:
- temp_new: float32 [8, 384, 4096], P(None, 'lat', 'lon')
- surface: float32 [384, 4096], P('lat', 'lon')
- residual: float32 [384, 4096], P('lat', 'lon')
Inputs may be any that keep to these rules, and one draw needn't show every extreme that they name: `cutoff`: rows outside the 48 rows nearest each pole keep every wavenumber; the first row keeps 4096 // 16.
All inputs are finite; a program needn't handle non-finite values.
Results may differ from a plain program's by a relative error of at most 0.0003.
Values may be sent and summed in bfloat16 or wider, within the bound.
No kernel may reach another device: no remote copies, remote signals or barrier semaphores. Data moves between devices by JAX's collectives and lax.ppermute only.
A program may use at most 64 MiB of HBM per device.

v0:
```python
import math

import jax
import jax.numpy as jnp
from jax import lax
from jax.sharding import PartitionSpec as P

ITERS = 4


step_size = 0.25
highest = lax.Precision.HIGHEST


def with_halo(block, sides, width, periodic):
    for axis, dim in sides:
        count = lax.axis_size(axis)
        forward = [(i, i + 1) for i in range(count - 1)]
        if periodic:
            forward.append((count - 1, 0))
        backward = [(target, source) for source, target in forward]
        low = lax.ppermute(
            lax.slice_in_dim(block, block.shape[dim] - width, None, axis=dim), axis, forward
        )
        high = lax.ppermute(lax.slice_in_dim(block, 0, width, axis=dim), axis, backward)
        block = jnp.concatenate([low, block, high], axis=dim)
    return block


def extend_float(field):
    wide = with_halo(field, (("lon", 2),), 1, True)
    return with_halo(wide, (("lat", 1),), 1, False)


def extend_closure(field):
    wide = with_halo(field, (("lon", 2),), 1, True)
    return with_halo(wide, (("lat", 1),), 1, False)


def neighbours(padded):
    return [padded[:, 2:, 1:-1], padded[:, :-2, 1:-1], padded[:, 1:-1, 2:], padded[:, 1:-1, :-2]]


def centre(padded):
    return padded[:, 1:-1, 1:-1]


def diffuse(padded, levels):
    tracer = padded[:levels]
    wetness = padded[levels : 2 * levels]
    diffusive = padded[2 * levels :]
    total = jnp.zeros(centre(tracer).shape, jnp.float32)
    for near_t, near_w, near_k in zip(
        neighbours(tracer), neighbours(wetness), neighbours(diffusive)
    ):
        total = total + near_w * 0.5 * (centre(diffusive) + near_k) * (near_t - centre(tracer))
    return centre(wetness) * total


def convolve(padded, weight):
    rows = padded.shape[1] - 2
    cols = padded.shape[2] - 2
    total = jnp.zeros((weight.shape[1], rows, cols), jnp.float32)
    for tap in range(9):
        shift_a = tap // 3
        shift_b = tap % 3
        piece = padded[:, shift_a : shift_a + rows, shift_b : shift_b + cols]
        total = total + jnp.einsum(
            "oc,chw->ohw", weight[tap], piece, preferred_element_type=jnp.float32
        )
    return total


def angle_table(first, second, modulus):
    left = jnp.arange(first, dtype=jnp.int32)[:, None]
    right = jnp.arange(second, dtype=jnp.int32)[None, :]
    phase = (left * right % modulus).astype(jnp.float32) * (2.0 * math.pi / modulus)
    return (jnp.cos(phase), -jnp.sin(phase))


def filter_rows(lines, kept_count, blocks):
    count = lines.shape[0]
    length = lines.shape[1]
    width = length // blocks
    shaped = lines.reshape(count, blocks, width)
    outer_re, outer_im = angle_table(blocks, blocks, blocks)
    twist_re, twist_im = angle_table(blocks, width, length)
    inner_re, inner_im = angle_table(width, width, width)
    first_re = jnp.einsum("kp,rpm->rkm", outer_re, shaped, precision=highest)
    first_im = jnp.einsum("kp,rpm->rkm", outer_im, shaped, precision=highest)
    turned_re = first_re * twist_re - first_im * twist_im
    turned_im = first_re * twist_im + first_im * twist_re
    spec_re = jnp.einsum("rkm,mq->rkq", turned_re, inner_re, precision=highest) - jnp.einsum(
        "rkm,mq->rkq", turned_im, inner_im, precision=highest
    )
    spec_im = jnp.einsum("rkm,mq->rkq", turned_re, inner_im, precision=highest) + jnp.einsum(
        "rkm,mq->rkq", turned_im, inner_re, precision=highest
    )
    wave = (
        jnp.arange(blocks, dtype=jnp.int32)[:, None]
        + blocks * jnp.arange(width, dtype=jnp.int32)[None, :]
    )
    folded = jnp.minimum(wave, length - wave)
    keep = (folded[None] < kept_count[:, None, None]).astype(jnp.float32)
    spec_re = spec_re * keep
    spec_im = spec_im * keep
    back_re = jnp.einsum("rkq,mq->rkm", spec_re, inner_re, precision=highest) + jnp.einsum(
        "rkq,mq->rkm", spec_im, inner_im, precision=highest
    )
    back_im = jnp.einsum("rkq,mq->rkm", spec_im, inner_re, precision=highest) - jnp.einsum(
        "rkq,mq->rkm", spec_re, inner_im, precision=highest
    )
    unturn_re = back_re * twist_re + back_im * twist_im
    unturn_im = back_im * twist_re - back_re * twist_im
    result = jnp.einsum("kp,rkm->rpm", outer_re, unturn_re, precision=highest) + jnp.einsum(
        "kp,rkm->rpm", outer_im, unturn_im, precision=highest
    )
    return result.reshape(count, length) / length


def operate(field, sea_pad, helm):
    padded = extend_float(field)
    result = helm[None] * field
    for near_v, near_s in zip(neighbours(padded), neighbours(sea_pad)):
        result = result + centre(sea_pad) * near_s * (field - near_v)
    return result


def squares(residual):
    return lax.psum(jnp.sum(residual * residual), ("lon", "lat"))


def body(temp, kmt, kappa, helm, forcing, cutoff, conv_in, conv_mid, conv_late, conv_out):
    levels = temp.shape[0]
    lat_rows = temp.shape[1]
    lon_cols = temp.shape[2]
    depth_index = jnp.arange(levels, dtype=jnp.int32)[:, None, None]
    wet = (depth_index < kmt[None]).astype(jnp.float32)
    sea = wet[0]
    stack = jnp.concatenate([wet * temp, wet, kappa[None]], axis=0)
    padded = extend_float(stack)
    diff = diffuse(padded, levels)
    sea_pad = padded[levels : levels + 1]
    start_input = (wet * temp).astype(jnp.bfloat16)
    hidden = start_input
    for weight in [conv_in, conv_mid, conv_late]:
        hidden = (sea[None] * jax.nn.silu(convolve(extend_closure(hidden), weight))).astype(
            jnp.bfloat16
        )
    closure = convolve(extend_closure(hidden), conv_out)
    eddy = wet * closure
    advanced = wet * (temp + step_size * (diff + eddy))
    lines = advanced.reshape(levels * lat_rows, lon_cols)
    whole_rows = lax.all_to_all(lines, "lon", split_axis=0, concat_axis=1, tiled=True)
    row_count = whole_rows.shape[0]
    all_cuts = jnp.tile(cutoff, levels)
    first_row = lax.axis_index("lon") * row_count
    own_cuts = lax.dynamic_slice_in_dim(all_cuts, first_row, row_count, 0)
    filtered = filter_rows(whole_rows, own_cuts, lax.axis_size("lon"))
    returned = lax.all_to_all(filtered, "lon", split_axis=1, concat_axis=0, tiled=True)
    temp_new = returned.reshape(levels, lat_rows, lon_cols)
    rhs = sea * (jnp.sum(wet * temp_new, axis=0) / levels + forcing)
    surface = jnp.zeros((1, lat_rows, lon_cols), jnp.float32)
    residual = rhs[None]
    direction = residual
    norm_now = squares(residual)
    for step in range(ITERS):
        image = operate(direction, sea_pad, helm)
        alpha = norm_now / lax.psum(jnp.sum(direction * image), ("lon", "lat"))
        surface = surface + alpha * direction
        residual = residual - alpha * image
        norm_next = squares(residual)
        direction = residual + norm_next / norm_now * direction
        norm_now = norm_next
    return (temp_new, surface[0], residual[0])


def solution(mesh):
    return jax.shard_map(
        body,
        mesh=mesh,
        in_specs=(
            P(None, "lat", "lon"),
            P("lat", "lon"),
            P("lat", "lon"),
            P("lat", "lon"),
            P("lat", "lon"),
            P("lat"),
            P(),
            P(),
            P(),
            P(),
        ),
        out_specs=(P(None, "lat", "lon"), P("lat", "lon"), P("lat", "lon")),
        check_vma=False,
    )
```

profile of v0, /device:TPU:1, one launch (start us, length us, event | category | flops | bytes accessed | tf_op | source)
XLA Modules:
  0.0 1006.5 jit_solution(15976349495908596831)
XLA Ops:
  1.6 12.0 %collective-permute-start.4 = (bf16[8,24,1]{2,1,0:T(8,128)(2,1)S(1)}, bf16[8,24,1]{2,1,0:T(8,128)(2,1)S(1)}, u32[]{:S(2)}, u32[]{:S(2)}) collective-permute-start(bf16[8,24,1]{2,1,0:T(8,128)(2,1)S(1)} %get-tuple-element.66), channel_id=1, source_target_pairs={{0,16},{16,32},{32,48},{48,64},{64,80},{80,96},{96,112},{112,128},... | collective-permute-start | bytes 1160 | tf_op jit(solution)/shard_map/ppermute | solution.py:22
  17.2 6.4 collective-permute-start.1
  33.4 4.6 collective-permute-start.3
  41.6 7.9 collective-permute-start.8
  54.2 21.1 %collective-permute-done.9 = bf16[64,24,1]{2,0,1:T(8,128)(2,1)S(1)} collective-permute-done((bf16[64,24,1]{2,0,1:T(8,128)(2,1)S(1)}, bf16[64,24,1]{2,0,1:T(8,128)(2,1)S(1)}, u32[]{:S(2)}, u32[]{:S(2)}) %collective-permute-start.9) | collective-permute-done | bytes 3104 | tf_op jit(solution)/shard_map/ppermute | solution.py:25
  84.8 4.9 collective-permute-start.12
  92.0 9.2 collective-permute-done.12
  101.2 10.1 %collective-permute-done.13 = bf16[64,24,1]{2,0,1:T(8,128)(2,1)S(1)} collective-permute-done((bf16[64,24,1]{2,0,1:T(8,128)(2,1)S(1)}, bf16[64,24,1]{2,0,1:T(8,128)(2,1)S(1)}, u32[]{:S(2)}, u32[]{:S(2)}) %collective-permute-start.13) | collective-permute-done | bytes 3104 | tf_op jit(solution)/shard_map/ppermute | solution.py:25
  120.9 4.0 collective-permute-start.16
  127.0 11.0 %collective-permute-done.16 = bf16[64,24,1]{2,0,1:T(8,128)(2,1)S(1)} collective-permute-done((bf16[64,24,1]{2,0,1:T(8,128)(2,1)S(1)}, bf16[64,24,1]{2,0,1:T(8,128)(2,1)S(1)}, u32[]{:S(2)}, u32[]{:S(2)}) %collective-permute-start.16) | collective-permute-done | bytes 3104 | tf_op jit(solution)/shard_map/ppermute | solution.py:22
  138.0 4.3 collective-permute-done.17
  142.4 5.2 collective-permute-start.18
  157.0 14.7 %all-to-all-start = ((f32[32,6,128]{2,1,0:T(8,128)}), f32[32,6,128]{2,1,0:T(8,128)S(1)}, u32[]{:S(2)}, u32[]{:S(2)}) async-start(f32[32,6,128]{2,1,0:T(8,128)} %all_to_all.22), calls=%async_computation | async-start | bytes 262144 | tf_op jit(solution)/shard_map/all_to_all | solution.py:154
  171.7 13.2 %all-to-all-done = f32[32,6,128]{2,1,0:T(8,128)S(1)} async-done(((f32[32,6,128]{2,1,0:T(8,128)}), f32[32,6,128]{2,1,0:T(8,128)S(1)}, u32[]{:S(2)}, u32[]{:S(2)}) %all-to-all-start) | async-done | bytes 98336 | tf_op jit(solution)/shard_map/all_to_all | solution.py:154
  190.5 16.5 %all_to_all.29 = f32[6,32,128]{2,0,1:T(8,128)S(1)} all-to-all(f32[6,32,128]{2,0,1:T(8,128)S(1)} %copy.142), channel_id=1, replica_groups=mesh['lon'=32,'lat'=16] {'lon'}, dimensions={1} | all-to-all | bytes 196608 | tf_op jit(solution)/shard_map/all_to_all | solution.py:160
  213.1 7.0 collective-permute-done.21
  221.5 8.0 collective-permute-start.23
  230.9 104.9 %all-reduce = (f32[]{:T(128)}, f32[]{:T(128)}) all-reduce(f32[]{:T(128)} %get-tuple-element.24, f32[]{:T(128)} %get-tuple-element.18), channel_id=1, replica_groups=mesh['lon'=32,'lat'=16] {'lon','lat'}, use_global_device_ids=true, to_apply=%region_2.3 | all-reduce | flops 2 | bytes 16 | tf_op jit(solution)/shard_map/psum | solution.py:130
  337.7 94.3 %psum.58 = f32[]{:T(128)} all-reduce(f32[]{:T(128)} %multiply_reduce_fusion.5), channel_id=1, replica_groups=mesh['lon'=32,'lat'=16] {'lon','lat'}, use_global_device_ids=true, to_apply=%region_6.7 | all-reduce | flops 1 | bytes 8 | tf_op jit(solution)/shard_map/psum | solution.py:130
  433.5 6.3 collective-permute-start.24
  441.7 7.0 collective-permute-done.25
  450.1 4.0 collective-permute-start.27
  455.5 102.2 %psum.59 = f32[]{:T(128)} all-reduce(f32[]{:T(128)} %get-tuple-element.16), channel_id=1, replica_groups=mesh['lon'=32,'lat'=16] {'lon','lat'}, use_global_device_ids=true, to_apply=%region_8.9 | all-reduce | flops 1 | bytes 8 | tf_op jit(solution)/shard_map/psum | solution.py:169
  559.7 94.7 %psum.60 = f32[]{:T(128)} all-reduce(f32[]{:T(128)} %get-tuple-element.14), channel_id=1, replica_groups=mesh['lon'=32,'lat'=16] {'lon','lat'}, use_global_device_ids=true, to_apply=%region_10.11 | all-reduce | flops 1 | bytes 8 | tf_op jit(solution)/shard_map/psum | solution.py:130
  655.7 6.8 collective-permute-start.28
  664.5 7.0 collective-permute-done.29
  678.2 102.0 %psum.61 = f32[]{:T(128)} all-reduce(f32[]{:T(128)} %get-tuple-element.12), channel_id=1, replica_groups=mesh['lon'=32,'lat'=16] {'lon','lat'}, use_global_device_ids=true, to_apply=%region_12.13 | all-reduce | flops 1 | bytes 8 | tf_op jit(solution)/shard_map/psum | solution.py:169
  782.2 95.7 %psum.62 = f32[]{:T(128)} all-reduce(f32[]{:T(128)} %get-tuple-element.10), channel_id=1, replica_groups=mesh['lon'=32,'lat'=16] {'lon','lat'}, use_global_device_ids=true, to_apply=%region_14.15 | all-reduce | flops 1 | bytes 8 | tf_op jit(solution)/shard_map/psum | solution.py:130
  879.3 6.3 collective-permute-start.32
  887.6 7.0 collective-permute-done.33
  895.9 4.1 collective-permute-start.35
  901.5 102.5 %psum.63 = f32[]{:T(128)} all-reduce(f32[]{:T(128)} %get-tuple-element.8), channel_id=1, replica_groups=mesh['lon'=32,'lat'=16] {'lon','lat'}, use_global_device_ids=true, to_apply=%region_16.17 | all-reduce | flops 1 | bytes 8 | tf_op jit(solution)/shard_map/psum | solution.py:169
  (174 shorter events, 90.6 us)
Async XLA Ops:
  1.6 25.6 %collective-permute-start.4 = (bf16[8,24,1]{2,1,0:T(8,128)(2,1)S(1)}, bf16[8,24,1]{2,1,0:T(8,128)(2,1)S(1)}, u32[]{:S(2)}, u32[]{:S(2)}) collective-permute-start(bf16[8,24,1]{2,1,0:T(8,128)(2,1)S(1)} %get-tuple-element.66), channel_id=1, source_target_pairs={{0,16},{16,32},{32,48},{48,64},{64,80},{80,96},{96,112},{112,128},... | collective-permute-start | bytes 1160 | tf_op jit(solution)/shard_map/ppermute | solution.py:22
  13.7 13.6 %collective-permute-start.5 = (bf16[8,24,1]{2,1,0:T(8,128)(2,1)S(1)}, bf16[8,24,1]{2,1,0:T(8,128)(2,1)S(1)}, u32[]{:S(2)}, u32[]{:S(2)}) collective-permute-start(bf16[8,24,1]{2,1,0:T(8,128)(2,1)S(1)} %get-tuple-element.67), channel_id=1, source_target_pairs={{16,0},{32,16},{48,32},{64,48},{80,64},{96,80},{112,96},{128,112},... | collective-permute-start | bytes 1160 | tf_op jit(solution)/shard_map/ppermute | solution.py:25
  17.2 14.7 %collective-permute-start.1 = (f32[17,24,1]{2,1,0:T(8,128)S(1)}, f32[17,24,1]{2,1,0:T(8,128)S(1)}, u32[]{:S(2)}, u32[]{:S(2)}) collective-permute-start(f32[17,24,1]{2,1,0:T(8,128)S(1)} %get-tuple-element.51), channel_id=1, source_target_pairs={{16,0},{32,16},{48,32},{64,48},{80,64},{96,80},{112,96},{128,112},... | collective-permute-start | bytes 4904 | tf_op jit(solution)/shard_map/ppermute | solution.py:25
  23.6 8.3 collective-permute-start
  27.4 10.7 %collective-permute-start.6 = (bf16[8,1,130]{2,1,0:T(2,128)(2,1)S(1)}, bf16[8,1,130]{2,1,0:T(2,128)(2,1)S(1)}, u32[]{:S(2)}, u32[]{:S(2)}) collective-permute-start(bf16[8,1,130]{2,1,0:T(2,128)(2,1)S(1)} %get-tuple-element.55), channel_id=1, source_target_pairs={{0,1},{1,2},{2,3},{3,4},{4,5},{5,6},{6,7},{7,8},{8,9},{9,10},{10,1... | collective-permute-start | bytes 6248 | tf_op jit(solution)/shard_map/ppermute | solution.py:22
  30.5 7.6 collective-permute-start.7
  32.1 8.7 collective-permute-start.2
  33.4 7.4 collective-permute-start.3
  41.6 12.6 %collective-permute-start.8 = (bf16[64,24,1]{2,0,1:T(8,128)(2,1)S(1)}, bf16[64,24,1]{2,0,1:T(8,128)(2,1)S(1)}, u32[]{:S(2)}, u32[]{:S(2)}) collective-permute-start(bf16[64,24,1]{2,0,1:T(8,128)(2,1)S(1)} %get-tuple-element.49), channel_id=1, source_target_pairs={{0,16},{16,32},{32,48},{48,64},{64,80},{80,96},{96,112},{112,128},... | collective-permute-start | bytes 9224 | tf_op jit(solution)/shard_map/ppermute | solution.py:22
  49.5 25.8 %collective-permute-start.9 = (bf16[64,24,1]{2,0,1:T(8,128)(2,1)S(1)}, bf16[64,24,1]{2,0,1:T(8,128)(2,1)S(1)}, u32[]{:S(2)}, u32[]{:S(2)}) collective-permute-start(bf16[64,24,1]{2,0,1:T(8,128)(2,1)S(1)} %get-tuple-element.50), channel_id=1, source_target_pairs={{16,0},{32,16},{48,32},{64,48},{80,64},{96,80},{112,96},{128,112},... | collective-permute-start | bytes 9224 | tf_op jit(solution)/shard_map/ppermute | solution.py:25
  84.8 16.3 %collective-permute-start.12 = (bf16[64,24,1]{2,0,1:T(8,128)(2,1)S(1)}, bf16[64,24,1]{2,0,1:T(8,128)(2,1)S(1)}, u32[]{:S(2)}, u32[]{:S(2)}) collective-permute-start(bf16[64,24,1]{2,0,1:T(8,128)(2,1)S(1)} %get-tuple-element.47), channel_id=1, source_target_pairs={{0,16},{16,32},{32,48},{48,64},{64,80},{80,96},{96,112},{112,128},... | collective-permute-start | bytes 9224 | tf_op jit(solution)/shard_map/ppermute | solution.py:22
  89.8 21.5 %collective-permute-start.13 = (bf16[64,24,1]{2,0,1:T(8,128)(2,1)S(1)}, bf16[64,24,1]{2,0,1:T(8,128)(2,1)S(1)}, u32[]{:S(2)}, u32[]{:S(2)}) collective-permute-start(bf16[64,24,1]{2,0,1:T(8,128)(2,1)S(1)} %get-tuple-element.48), channel_id=1, source_target_pairs={{16,0},{32,16},{48,32},{64,48},{80,64},{96,80},{112,96},{128,112},... | collective-permute-start | bytes 9224 | tf_op jit(solution)/shard_map/ppermute | solution.py:25
  120.9 17.2 %collective-permute-start.16 = (bf16[64,24,1]{2,0,1:T(8,128)(2,1)S(1)}, bf16[64,24,1]{2,0,1:T(8,128)(2,1)S(1)}, u32[]{:S(2)}, u32[]{:S(2)}) collective-permute-start(bf16[64,24,1]{2,0,1:T(8,128)(2,1)S(1)} %get-tuple-element.45), channel_id=1, source_target_pairs={{0,16},{16,32},{32,48},{48,64},{64,80},{80,96},{96,112},{112,128},... | collective-permute-start | bytes 9224 | tf_op jit(solution)/shard_map/ppermute | solution.py:22
  124.9 17.4 %collective-permute-start.17 = (bf16[64,24,1]{2,0,1:T(8,128)(2,1)S(1)}, bf16[64,24,1]{2,0,1:T(8,128)(2,1)S(1)}, u32[]{:S(2)}, u32[]{:S(2)}) collective-permute-start(bf16[64,24,1]{2,0,1:T(8,128)(2,1)S(1)} %get-tuple-element.46), channel_id=1, source_target_pairs={{16,0},{32,16},{48,32},{64,48},{80,64},{96,80},{112,96},{128,112},... | collective-permute-start | bytes 9224 | tf_op jit(solution)/shard_map/ppermute | solution.py:25
  142.4 7.2 collective-permute-start.18
  147.6 5.8 collective-permute-start.19
  157.0 28.0 %all-to-all-start = ((f32[32,6,128]{2,1,0:T(8,128)}), f32[32,6,128]{2,1,0:T(8,128)S(1)}, u32[]{:S(2)}, u32[]{:S(2)}) async-start(f32[32,6,128]{2,1,0:T(8,128)} %all_to_all.22), calls=%async_computation | async-start | bytes 262144 | tf_op jit(solution)/shard_map/all_to_all | solution.py:154
  207.7 5.5 collective-permute-start.20
  211.2 8.9 collective-permute-start.21
  220.2 9.3 collective-permute-start.22
  221.5 8.7 collective-permute-start.23
  433.5 8.2 collective-permute-start.24
  439.8 8.9 collective-permute-start.25
  448.8 5.3 collective-permute-start.26
  450.1 4.7 collective-permute-start.27
  655.7 8.8 collective-permute-start.28
  662.6 8.9 collective-permute-start.29
  671.6 5.3 collective-permute-start.30
  879.3 8.3 collective-permute-start.32
  885.6 8.9 collective-permute-start.33
  894.6 5.4 collective-permute-start.34
  895.9 4.8 collective-permute-start.35
  (16 other events, 624.1 us)
where the time goes:
time: 1010 us
  blocking collectives  713 us (71%)
  starting transfers between devices  139 us (14%)
  waiting for transfers between devices  112 us (11%)
  matrix products  16.9 us (2%)
  other arithmetic  12.9 us (1%)
  between operations  11 us (1%)
    psum x4, blocking collectives, squares(): return lax.psum(jnp.sum(residual * residual), ('lon', 'lat'))  390 us
    psum x3, blocking collectives, body(): alpha = norm_now / lax.psum(jnp.sum(direction * image), ('lon', 'lat'))  307 us
    ppermute x18, starting transfers between devices, with_halo(): lax.ppermute(lax.slice_in_dim(block, block.shape[dim] - width, None, axis...  90.4 us
    ppermute x18, waiting for transfers between devices, with_halo(): lax.ppermute(lax.slice_in_dim(block, 0, width, axis=dim), axis, backward)  73.2 us
    ppermute x18, starting transfers between devices, with_halo(): lax.ppermute(lax.slice_in_dim(block, 0, width, axis=dim), axis, backward)  33.4 us
    ppermute x18, waiting for transfers between devices, with_halo(): lax.ppermute(lax.slice_in_dim(block, block.shape[dim] - width, None, axis...  25.5 us
  transfers between devices with their start and end apart: 37, of which 18 were waited for; matrix products, arithmetic and copies ran while one was open for 1% of the time, Pallas kernels for 0%

commit v1 on v0

v1 whole, which is shorter than its diff:
```python
import functools
import math

import jax
import jax.numpy as jnp
import numpy as np
from jax import lax
from jax.experimental import pallas as pl
from jax.experimental.pallas import tpu as pltpu
from jax.sharding import PartitionSpec as P

ITERS = 4
STEP = 0.25
LEV = 8
FIELDS = 16
KMT, KAPPA, HELM, FORCING, CUT = 8, 9, 10, 11, 12
HALO = 4
DEEP = 8
ROWS = 24
COLS = 128
TALL = ROWS + 2 * DEEP
WIDE = COLS + 2 * HALO
MID = ROWS + 2 * HALO
SLOTS = 20
VMEM_LIMIT = 48 * 1024 * 1024
highest = lax.Precision.HIGHEST


def call(kernel, outs, scratch=(), ins=None):
    spec = pl.BlockSpec(memory_space=pltpu.VMEM)
    return pl.pallas_call(
        kernel,
        out_shape=outs,
        out_specs=jax.tree.map(lambda _: spec, outs),
        scratch_shapes=scratch,
        compiler_params=pltpu.CompilerParams(vmem_limit_bytes=VMEM_LIMIT),
    )


def lane_index(shape):
    return lax.broadcasted_iota(jnp.int32, shape, len(shape) - 1)


def pack_kernel(own_ref, north_ref, south_ref, west_ref, east_ref):
    lane = lane_index((FIELDS, COLS))
    for part in range(TALL // SLOTS):
        first = jnp.zeros((FIELDS, COLS), jnp.float32)
        last = jnp.zeros((FIELDS, COLS), jnp.float32)
        for slot in range(SLOTS):
            row = part * SLOTS + slot
            if row < DEEP:
                here = north_ref[row]
            elif row < DEEP + ROWS:
                here = own_ref[row - DEEP]
            else:
                here = south_ref[row - DEEP - ROWS]
            inside = (lane >= HALO * slot) & (lane < HALO * (slot + 1))
            first = jnp.where(inside, pltpu.roll(here, HALO * slot, 1) if slot else here, first)
            last = jnp.where(inside, pltpu.roll(here, HALO * (slot + 1), 1), last)
        west_ref[part] = first
        east_ref[part] = last


def closure_kernel(
    own_ref,
    north_ref,
    south_ref,
    from_west_ref,
    from_east_ref,
    w_in_ref,
    w_mid_ref,
    w_late_ref,
    w_out_ref,
    out_ref,
    planes_ref,
    line_ref,
    ext,
    start,
    mask_odd,
    mask_even,
    act_a,
    act_b,
):
    lane = lane_index((FIELDS, COLS))
    depth = lax.broadcasted_iota(jnp.int32, (LEV, 2 * COLS), 0).astype(jnp.float32)
    for row in range(TALL):
        if row < DEEP:
            here = north_ref[row]
        elif row < DEEP + ROWS:
            here = own_ref[row - DEEP]
        else:
            here = south_ref[row - DEEP - ROWS]
        part, slot = row // SLOTS, row % SLOTS
        west = from_west_ref[part]
        if slot:
            west = pltpu.roll(west, COLS - HALO * slot, 1)
        east = from_east_ref[part]
        shift = (HALO - HALO * slot) % COLS
        if shift:
            east = pltpu.roll(east, shift, 1)
        moved = pltpu.roll(here, HALO, 1)
        ext[row, :, 0:COLS] = jnp.where(lane < HALO, west, moved)
        ext[row, :, COLS:] = jnp.where(
            lane < HALO, moved, jnp.where(lane < 2 * HALO, east, 0.0)
        )
    for row in range(TALL):
        wet = (depth < ext[row, KMT : KMT + 1, :]).astype(jnp.float32)
        start[row * FIELDS : row * FIELDS + LEV] = (wet * ext[row, 0:LEV, :]).astype(jnp.bfloat16)
        start[row * FIELDS + LEV : (row + 1) * FIELDS] = jnp.where(depth == 0, wet, 0.0).astype(
            jnp.bfloat16
        )

    def finish(total, mask):
        v = (
            pltpu.roll(total[:, 0:128], 1, 0)
            + total[:, 128:256]
            + pltpu.roll(total[:, 256:384], WIDE - 1, 0)
        )
        return (mask * (v / (1.0 + jnp.exp(-v)))).astype(jnp.bfloat16)

    for pair in range(19):
        window = start[2 * FIELDS * pair : 2 * FIELDS * (pair + 2), 0:WIDE]
        total = lax.dot_general(
            window, w_in_ref[...], (((0,), (0,)), ((), ())), preferred_element_type=jnp.float32
        )
        mask_odd[pair] = total[:, 384:512]
        mask_even[pair] = total[:, 512:640]
        act_a[pair] = finish(total, total[:, 384:512])
    for pair in range(18):
        both = jnp.concatenate([act_a[pair], act_a[pair + 1]], axis=1)
        total = jnp.dot(both, w_mid_ref[...], preferred_element_type=jnp.float32)
        act_b[pair] = finish(total, mask_even[pair])
    for pair in range(17):
        both = jnp.concatenate([act_b[pair], act_b[pair + 1]], axis=1)
        total = jnp.dot(both, w_late_ref[...], preferred_element_type=jnp.float32)
        act_a[pair] = finish(total, mask_odd[pair + 1])

    def cut(block, by):
        return pltpu.roll(block, 2 * COLS - by, 1)[:, 0:COLS]

    def wetness(row):
        return (depth < ext[row, KMT : KMT + 1, :]).astype(jnp.float32)

    for pair in range(16):
        both = jnp.concatenate([act_a[pair], act_a[pair + 1]], axis=1)
        total = lax.dot_general(
            w_out_ref[...], both, (((1,), (1,)), ((), ())), preferred_element_type=jnp.float32
        )
        total = jnp.concatenate(
            [total, jnp.zeros((48, 2 * COLS - WIDE), jnp.float32)], axis=1
        )
        closure = cut(total[0:16], HALO - 1) + cut(total[16:32], HALO) + cut(total[32:48], HALO + 1)
        for parity in range(2):
            row = DEEP - HALO + 2 * pair + parity
            wet_wide = wetness(row)
            tracer_wide = wet_wide * ext[row, 0:LEV, :]
            kappa_wide = ext[row, KAPPA : KAPPA + 1, :]
            wet = cut(wet_wide, HALO)
            tracer = cut(tracer_wide, HALO)
            kappa = cut(jnp.broadcast_to(kappa_wide, (LEV, 2 * COLS)), HALO)
            diff = jnp.zeros((LEV, COLS), jnp.float32)
            for near in (row + 1, row - 1):
                near_w = wetness(near)
                near_t = near_w * ext[near, 0:LEV, :]
                near_k = jnp.broadcast_to(ext[near, KAPPA : KAPPA + 1, :], (LEV, 2 * COLS))
                diff = diff + cut(near_w, HALO) * 0.5 * (kappa + cut(near_k, HALO)) * (
                    cut(near_t, HALO) - tracer
                )
            for by in (HALO + 1, HALO - 1):
                diff = diff + cut(wet_wide, by) * 0.5 * (
                    kappa + cut(jnp.broadcast_to(kappa_wide, (LEV, 2 * COLS)), by)
                ) * (cut(tracer_wide, by) - tracer)
            diff = wet * diff
            eddy = wet * closure[LEV * parity : LEV * (parity + 1)]
            temp = cut(ext[row, 0:LEV, :], HALO)
            out_ref[2 * pair + parity] = wet * (temp + STEP * (diff + eddy))
    first = DEEP - HALO
    for index, field in enumerate((KMT, HELM, FORCING)):
        planes_ref[index] = jnp.concatenate(
            [ext[row, field : field + 1, :] for row in range(first, first + MID)], axis=0
        )
    own_line = lax.axis_index("lon") + first
    line_ref[...] = ext[own_line, LEV:FIELDS, HALO : HALO + 1] + jnp.zeros((LEV, COLS), jnp.float32)


def filter_tables(blocks, width):
    length = blocks * width
    half = LEV // 2
    k = np.arange(blocks)
    outer = np.exp(-2j * np.pi * ((k[:, None] * k[None, :]) % blocks) / blocks)
    spread = np.zeros((blocks, 2, half, blocks, 2, half))
    for line in range(half):
        spread[:, 0, line, :, 0, line] = outer.real
        spread[:, 0, line, :, 1, line] = -outer.imag
        spread[:, 1, line, :, 0, line] = outer.imag
        spread[:, 1, line, :, 1, line] = outer.real
    spread = spread.reshape(blocks * LEV, blocks * LEV)
    m = np.arange(width)
    twist = np.exp(-2j * np.pi * (k[:, None] * m[None, :]) / length)
    sign = np.where(np.arange(LEV) < half, -1.0, 1.0)[None, :, None]
    twist_re = np.broadcast_to(twist.real[:, None, :], (blocks, LEV, width))
    twist_im = twist.imag[:, None, :] * sign
    inner = np.exp(-2j * np.pi * ((m[:, None] * m[None, :]) % width) / width)
    inner = np.concatenate([inner.real, inner.imag], axis=1)
    return [
        np.asarray(t, np.float32)
        for t in (spread, spread.T / length, twist_re, twist_im, inner)
    ]


def filter_kernel(
    x_ref, line_ref, spread_ref, back_ref, twist_re_ref, twist_im_ref, inner_ref, out_ref
):
    blocks, lev, width = x_ref.shape
    shape = (blocks, lev, width)
    length = blocks * width

    def partner(block):
        return pltpu.roll(block, lev // 2, 1)

    sign = jnp.where(lax.broadcasted_iota(jnp.int32, shape, 1) < lev // 2, -1.0, 1.0)
    x = x_ref[...].reshape(blocks * lev, width)
    y = jnp.dot(spread_ref[...], x, precision=highest, preferred_element_type=jnp.float32)
    y = y.reshape(shape)
    y = y * twist_re_ref[...] + partner(y) * twist_im_ref[...]
    s = jnp.dot(
        y.reshape(blocks * lev, width),
        inner_ref[...],
        precision=highest,
        preferred_element_type=jnp.float32,
    )
    s = s[:, 0:width].reshape(shape) + partner(s[:, width:].reshape(shape)) * sign
    wave = lax.broadcasted_iota(jnp.int32, shape, 0) + blocks * lane_index(shape)
    folded = jnp.minimum(wave, length - wave).astype(jnp.float32)
    s = jnp.where(folded < line_ref[CUT - LEV : CUT - LEV + 1, :][None], s, 0.0)
    y = jnp.dot(
        s.reshape(blocks * lev, width),
        inner_ref[...],
        precision=highest,
        preferred_element_type=jnp.float32,
    )
    y = y[:, 0:width].reshape(shape) - partner(y[:, width:].reshape(shape)) * sign
    y = y * twist_re_ref[...] - partner(y) * twist_im_ref[...]
    x = jnp.dot(
        back_ref[...],
        y.reshape(blocks * lev, width),
        precision=highest,
        preferred_element_type=jnp.float32,
    ).reshape(shape)
    out_ref[:, 0:lev, :] = x
    lane = lane_index((lev, width))
    for block in range(blocks):
        west = pltpu.roll(x[(block - 1) % blocks], HALO, 1)
        east = pltpu.roll(x[(block + 1) % blocks], HALO, 1)
        out_ref[block, lev : 2 * lev, :] = jnp.where(lane < HALO, west, east)


def two_sum(a, b):
    s = a + b
    t = s - a
    return s, (a - (s - t)) + (b - t)


def quick_sum(a, b):
    s = a + b
    return s, b - (s - a)


def split(a):
    c = a * 4097.0
    high = c - (c - a)
    return high, a - high


def two_product(a, b):
    p = a * b
    ah, al = split(a)
    bh, bl = split(b)
    return p, ((ah * bh - p) + ah * bl + al * bh) + al * bl


def pair_add(a, b):
    s, e = two_sum(a[0], b[0])
    return quick_sum(s, e + (a[1] + b[1]))


def pair_neg(a):
    return -a[0], -a[1]


def pair_mul(a, b):
    p, e = two_product(a[0], b[0])
    return quick_sum(p, e + (a[0] * b[1] + a[1] * b[0]))


def pair_div(a, b):
    q = a[0] / b[0]
    rest = pair_add(a, pair_neg(pair_mul((q, jnp.zeros_like(q)), b)))
    r = rest[0] / b[0]
    rest = pair_add(rest, pair_neg(pair_mul((r, jnp.zeros_like(r)), b)))
    return quick_sum(*quick_sum(q, r + rest[0] / b[0]))


def powers_kernel(x_ref, planes_ref, temp_ref, powers_ref, parts_ref, mean):
    depth = lax.broadcasted_iota(jnp.int32, (LEV, 2 * COLS), 0).astype(jnp.float32)
    lane = lane_index((LEV, COLS))
    for level in range(LEV):
        temp_ref[level] = x_ref[HALO : HALO + ROWS, level, :]
    for row in range(MID):
        moved = pltpu.roll(x_ref[row, 0:LEV, :], HALO, 1)
        edge = x_ref[row, LEV:, :]
        left = jnp.where(lane < HALO, edge, moved)
        right = jnp.where(lane < HALO, moved, jnp.where(lane < 2 * HALO, edge, 0.0))
        wide = jnp.concatenate([left, right], axis=1)
        wet = depth < planes_ref[0, row : row + 1, :]
        mean[row : row + 1, :] = jnp.sum(jnp.where(wet, wide, 0.0), axis=0, keepdims=True)
    sea = (planes_ref[0] > 0.0).astype(jnp.float32)

    def around(v):
        return (
            pltpu.roll(v, 1, 0)
            + pltpu.roll(v, MID - 1, 0)
            + pltpu.roll(v, 1, 1)
            + pltpu.roll(v, 2 * COLS - 1, 1)
        )

    diagonal = planes_ref[1] + sea * around(sea)
    powers = [sea * (mean[...] * (1.0 / LEV) + planes_ref[2])]
    for _ in range(ITERS):
        v = powers[-1]
        powers.append((diagonal * v - sea * around(v)) * 0.125)
    for index, v in enumerate(powers):
        powers_ref[index] = v
    row = lax.broadcasted_iota(jnp.int32, (MID, 2 * COLS), 0)
    column = lane_index((MID, 2 * COLS))
    own = (
        (row >= HALO) & (row < HALO + ROWS) & (column >= HALO) & (column < HALO + COLS)
    )
    owned = [jnp.where(own, v, 0.0) for v in powers]
    high_rows, low_rows = [], []
    for order in range(2 * ITERS):
        p, e = two_product(owned[order // 2], owned[order - order // 2])
        tiles = [
            (p[8 * i : 8 * i + 8, 128 * j : 128 * j + 128], e[8 * i : 8 * i + 8, 128 * j : 128 * j + 128])
            for i in range(MID // 8)
            for j in range(2)
        ]
        while len(tiles) > 1:
            tiles = [pair_add(a, b) for a, b in zip(tiles[::2], tiles[1::2])]
        total = tiles[0]
        for by in (4, 2, 1):
            total = pair_add(total, tuple(pltpu.roll(t, by, 0) for t in total))
        high_rows.append(total[0])
        low_rows.append(total[1])
    where = lax.broadcasted_iota(jnp.int32, (8, COLS), 0)
    high, low = high_rows[0], low_rows[0]
    for order in range(1, 2 * ITERS):
        high = jnp.where(where == order, high_rows[order], high)
        low = jnp.where(where == order, low_rows[order], low)
    total = (high, low)
    for by in (64, 32, 16, 8, 4, 2, 1):
        total = pair_add(total, tuple(pltpu.roll(t, by, 1) for t in total))
    spot = lax.broadcasted_iota(jnp.int32, (8, COLS), 0)
    message = jnp.where(lane == spot, total[0], 0.0) + jnp.where(lane == spot + 64, total[1], 0.0)
    message = jnp.sum(message, axis=0, keepdims=True)
    parts_ref[...] = jnp.broadcast_to(message, parts_ref.shape)


def combine_kernel(parts_ref, powers_ref, surface_ref, residual_ref, wide):
    count = parts_ref.shape[0] // 8
    tiles = [(parts_ref[8 * i : 8 * i + 8, :], None) for i in range(count)]
    merged = []
    for a, b in zip(tiles[::2], tiles[1::2]):
        merged.append(two_sum(a[0], b[0]))
    tiles = merged
    while len(tiles) > 1:
        tiles = [pair_add(a, b) for a, b in zip(tiles[::2], tiles[1::2])]
    total = tiles[0]
    for by in (4, 2, 1):
        total = pair_add(total, tuple(pltpu.roll(t, by, 0) for t in total))
    other = tuple(pltpu.roll(t, 64, 1) for t in total)
    total = pair_add(total, other)
    moments = [
        tuple(jnp.broadcast_to(t[:, order : order + 1], (8, COLS)) for t in total)
        for order in range(2 * ITERS)
    ]
    rho = list(moments)
    delta = list(moments)
    one = jnp.ones((8, COLS), jnp.float32)
    zero = jnp.zeros((8, COLS), jnp.float32)
    res = [one] + [zero] * ITERS
    way = [one] + [zero] * ITERS
    sol = [zero] * ITERS
    for step in range(ITERS):
        alpha = pair_div(rho[step], delta[step + 1])
        sol = [s + alpha[0] * w for s, w in zip(sol, way)]
        res = [res[0]] + [r - alpha[0] * w for r, w in zip(res[1:], way)]
        if step == ITERS - 1:
            break
        before = rho[step]
        last = 2 * ITERS - 1 - step
        rho = [
            None if order <= step or order >= last
            else pair_add(rho[order], pair_neg(pair_mul(alpha, delta[order + 1])))
            for order in range(2 * ITERS)
        ]
        beta = pair_neg(pair_mul(alpha, pair_div(rho[step + 1], before)))
        delta = [
            None if order <= step or order >= last
            else pair_add(rho[order], pair_mul(beta, delta[order]))
            for order in range(2 * ITERS)
        ]
        way = [r + beta[0] * w for r, w in zip(res, way)]
    for weights, target, factor in ((sol, surface_ref, 0.125), (res, residual_ref, 1.0)):
        for i in range(MID // 8):
            for j in range(2):
                spot = (slice(8 * i, 8 * i + 8), slice(128 * j, 128 * j + 128))
                value = weights[0] * powers_ref[(0,) + spot]
                for index in range(1, len(weights)):
                    value = value + weights[index] * powers_ref[(index,) + spot]
                wide[spot] = value * factor
        target[...] = wide[HALO : HALO + ROWS, HALO : HALO + COLS]


def paired(weight):
    _, outs, ins = weight.shape
    taps = jnp.transpose(weight.reshape(3, 3, outs, ins), (0, 3, 1, 2))
    upper = jnp.pad(taps, ((0, 1), (0, 0), (0, 0), (0, 0)))
    lower = jnp.pad(taps, ((1, 0), (0, 0), (0, 0), (0, 0)))
    return jnp.stack([upper, lower], axis=3)


def first_weight(weight):
    _, outs, _ = weight.shape
    taps = paired(weight).reshape(4, LEV, 6 * outs)
    taps = jnp.pad(taps, ((0, 0), (0, FIELDS - LEV), (0, 0)))
    masks = np.zeros((4, FIELDS, 4, outs), np.float32)
    for at, row in enumerate((1, 2, 2, 3)):
        masks[row, LEV, at] = 1.0
    masks = jnp.asarray(masks.reshape(4, FIELDS, 4 * outs), jnp.bfloat16)
    return jnp.concatenate([taps, masks], axis=2).reshape(4 * FIELDS, 10 * outs)


def forward(axis, periodic):
    count = lax.axis_size(axis)
    pairs = [(i, i + 1) for i in range(count - 1)]
    return pairs + [(count - 1, 0)] if periodic else pairs


def backward(axis, periodic):
    return [(target, source) for source, target in forward(axis, periodic)]


def body(temp, kmt, kappa, helm, forcing, cutoff, conv_in, conv_mid, conv_late, conv_out):
    f32 = jnp.float32
    shape = jax.ShapeDtypeStruct
    blocks = lax.axis_size("lon")
    cuts = jnp.broadcast_to(cutoff.astype(f32)[:, None], (ROWS, COLS))
    rest = jnp.zeros((FIELDS - CUT - 1, ROWS, COLS), f32)
    flat = jnp.stack([kmt.astype(f32), kappa, helm, forcing, cuts])
    own = jnp.transpose(jnp.concatenate([temp, flat, rest]), (1, 0, 2))
    north = lax.ppermute(own[ROWS - DEEP :], "lat", forward("lat", False))
    south = lax.ppermute(own[:DEEP], "lat", backward("lat", False))
    slab = shape((TALL // SLOTS, FIELDS, COLS), f32)
    first, last = call(pack_kernel, (slab, slab))(own, north, south)
    from_west = lax.ppermute(last, "lon", forward("lon", True))
    from_east = lax.ppermute(first, "lon", backward("lon", True))
    w_in = first_weight(conv_in)
    w_mid = paired(conv_mid).reshape(256, 384)
    w_late = paired(conv_late).reshape(256, 384)
    w_out = jnp.transpose(paired(conv_out).reshape(256, 48))
    lines, planes, line = call(
        closure_kernel,
        (
            shape((MID, LEV, COLS), f32),
            shape((3, MID, 2 * COLS), f32),
            shape((LEV, COLS), f32),
        ),
        (
            pltpu.VMEM((TALL, FIELDS, 2 * COLS), f32),
            pltpu.VMEM((TALL * FIELDS, 2 * COLS), jnp.bfloat16),
            pltpu.VMEM((19, WIDE, 128), f32),
            pltpu.VMEM((19, WIDE, 128), f32),
            pltpu.VMEM((19, WIDE, 128), jnp.bfloat16),
            pltpu.VMEM((19, WIDE, 128), jnp.bfloat16),
        ),
    )(own, north, south, from_west, from_east, w_in, w_mid, w_late, w_out)
    whole = lax.all_to_all(lines, "lon", split_axis=0, concat_axis=0, tiled=True)
    filtered = call(filter_kernel, shape((blocks, 2 * LEV, COLS), f32))(
        whole, line, *(jnp.asarray(t) for t in filter_tables(blocks, COLS))
    )
    back = lax.all_to_all(filtered, "lon", split_axis=0, concat_axis=0, tiled=True)
    everyone = blocks * lax.axis_size("lat")
    temp_new, powers, parts = call(
        powers_kernel,
        (
            shape((LEV, ROWS, COLS), f32),
            shape((ITERS + 1, MID, 2 * COLS), f32),
            shape((everyone, COLS), f32),
        ),
        (pltpu.VMEM((MID, 2 * COLS), f32),),
    )(back, planes)
    gathered = lax.all_to_all(parts, ("lon", "lat"), split_axis=0, concat_axis=0, tiled=True)
    surface, residual = call(
        combine_kernel,
        (shape((ROWS, COLS), f32), shape((ROWS, COLS), f32)),
        (pltpu.VMEM((MID, 2 * COLS), f32),),
    )(gathered, powers)
    return temp_new, surface, residual


def solution(mesh):
    return jax.shard_map(
        body,
        mesh=mesh,
        in_specs=(
            P(None, "lat", "lon"),
            P("lat", "lon"),
            P("lat", "lon"),
            P("lat", "lon"),
            P("lat", "lon"),
            P("lat"),
            P(),
            P(),
            P(),
            P(),
        ),
        out_specs=(P(None, "lat", "lon"), P("lat", "lon"), P("lat", "lon")),
        check_vma=False,
    )
```

time: 1010 us -> 113 us (0.11)
  blocking collectives: 713 us -> 69.8 us
  starting transfers between devices: 139 us -> 18.6 us
  waiting for transfers between devices: 112 us -> 7.17 us
  matrix products: 16.9 us -> 0 us
  other arithmetic: 12.9 us -> 0.24 us
    psum x7 -> x0, blocking collectives: 696 us -> none  [the longest x4 390 us: squares(): return lax.psum(jnp.sum(residual * residual), ('lon', 'lat'))]
    ppermute x36 -> x4, starting transfers between devices: 124 us -> 18.6 us  [the longest x1 10.4 us: body(): from_west = lax.ppermute(last, 'lon', forward('lon', True))]
    ppermute x36 -> x4, waiting for transfers between devices: 98.7 us -> 7.17 us  [the longest x1 5.49 us: body(): from_east = lax.ppermute(first, 'lon', backward('lon', True))]
    all_to_all x1 -> x3, blocking collectives: 16.5 us -> 69.8 us  [the longest x1 30.7 us: body(): lax.all_to_all(parts, ('lon', 'lat'), split_axis=0, concat_axis=0, tiled=...]
    dot_general x48 -> x0, matrix products: 16.9 us -> none  [the longest x36 11.5 us: convolve(): jnp.einsum('oc,chw->ohw', weight[tap], piece, preferred_element_type=jnp....]
    all_to_all x1 -> x0, starting transfers between devices: 14.7 us -> none  [body(): lax.all_to_all(lines, 'lon', split_axis=0, concat_axis=1, tiled=True)]
    all_to_all x1 -> x0, waiting for transfers between devices: 13.2 us -> none  [body(): lax.all_to_all(lines, 'lon', split_axis=0, concat_axis=1, tiled=True)]
  transfers between devices with their start and end apart: 37 -> 4, of which waited for: 18 -> 2; matrix products, arithmetic and copies ran while one was open for 1% -> 2% of each run, Pallas kernels for 0% -> 0%
where the time goes in v1:
time: 113 us; the launch traced here: 112 us
  blocking collectives  69.8 us (62%)
  starting transfers between devices  18.6 us (16%)
  Pallas kernels  8.89 us (8%)
  waiting for transfers between devices  7.17 us (6%)
  local copies, waits for them, and re-layouts  6.73 us (6%)
    all_to_all x1, blocking collectives, body(): lax.all_to_all(parts, ('lon', 'lat'), split_axis=0, concat_axis=0, tiled=...  30.7 us
    all_to_all x1, blocking collectives, body(): lax.all_to_all(lines, 'lon', split_axis=0, concat_axis=0, tiled=True)  20.5 us
    all_to_all x1, blocking collectives, body(): lax.all_to_all(filtered, 'lon', split_axis=0, concat_axis=0, tiled=True)  18.6 us
    ppermute x1, starting transfers between devices, body(): from_west = lax.ppermute(last, 'lon', forward('lon', True))  10.4 us
    ppermute x1, waiting for transfers between devices, body(): from_east = lax.ppermute(first, 'lon', backward('lon', True))  5.49 us
    ppermute x1, starting transfers between devices, body(): north = lax.ppermute(own[ROWS - DEEP:], 'lat', forward('lat', False))  4.96 us
    unnamed x33, local copies, waits for them, and re-layouts  4.73 us
    pallas_call x1, Pallas kernels, body(): call(closure_kernel, (shape((MID, LEV, COLS), f32), shape((3, MID, 2 * CO...  3.4 us
  transfers between devices with their start and end apart: 4, of which 2 were waited for; matrix products, arithmetic and copies ran while one was open for 2% of the time, Pallas kernels for 0%

profile of v1, /device:TPU:1, one launch (start us, length us, event | category | flops | bytes accessed | tf_op | source)
XLA Modules:
  0.0 112.4 jit_solution(6271011673391533824)
XLA Ops:
  0.7 0.9 copy.35
  1.6 0.1 stack_broadcast_in_dim.2
  1.8 0.7 copy-done.10
  2.5 0.1 concatenate.6
  2.6 5.0 %collective-permute-start = (f32[8,16,128]{2,1,0:T(8,128)S(1)}, f32[8,16,128]{2,1,0:T(8,128)S(1)}, u32[]{:S(2)}, u32[]{:S(2)}) collective-permute-start(f32[8,16,128]{2,1,0:T(8,128)S(1)} %get-tuple-element.24), channel_id=1, source_target_pairs={{0,1},{1,2},{2,3},{3,4},{4,5},{5,6},{6,7},{7,8},{8,9},{9,10},{10,1... | collective-permute-start | bytes 196616 | tf_op jit(solution)/shard_map/ppermute | solution.py:462
  7.6 1.3 %collective-permute-start.1 = (f32[8,16,128]{2,1,0:T(8,128)S(1)}, f32[8,16,128]{2,1,0:T(8,128)S(1)}, u32[]{:S(2)}, u32[]{:S(2)}) collective-permute-start(f32[8,16,128]{2,1,0:T(8,128)S(1)} %get-tuple-element.23), channel_id=1, source_target_pairs={{1,0},{2,1},{3,2},{4,3},{5,4},{6,5},{7,6},{8,7},{9,8},{10,9},{11,1... | collective-permute-start | bytes 196616 | tf_op jit(solution)/shard_map/ppermute | solution.py:463
  8.9 0.1 copy.37
  9.1 0.8 copy-done.6
  10.0 0.1 copy.39
  10.2 0.6 copy-done.8
  10.9 0.1 reshape.36
  11.0 0.6 copy-done.9
  11.7 0.1 pad_maximum_fusion
  11.8 0.1 pad_maximum_fusion.1
  11.8 0.7 copy-done.7
  12.6 1.7 %collective-permute-done.1.south_ref = f32[8,16,128]{2,1,0:T(8,128)S(1)} collective-permute-done((f32[8,16,128]{2,1,0:T(8,128)S(1)}, f32[8,16,128]{2,1,0:T(8,128)S(1)}, u32[]{:S(2)}, u32[]{:S(2)}) %collective-permute-start.1) | collective-permute-done | bytes 65568 | tf_op jit(solution)/shard_map/ppermute | solution.py:463
  14.2 0.2 shard_map.175
  14.5 10.4 %collective-permute-start.2 = (f32[2,16,128]{2,1,0:T(8,128)S(1)}, f32[2,16,128]{2,1,0:T(8,128)S(1)}, u32[]{:S(2)}, u32[]{:S(2)}) collective-permute-start(f32[2,16,128]{2,1,0:T(8,128)S(1)} %get-tuple-element.13), channel_id=1, source_target_pairs={{0,16},{16,32},{32,48},{48,64},{64,80},{80,96},{96,112},{112,128},... | collective-permute-start | bytes 49160 | tf_op jit(solution)/shard_map/ppermute | solution.py:466
  24.9 1.9 %collective-permute-start.3 = (f32[2,16,128]{2,1,0:T(8,128)S(1)}, f32[2,16,128]{2,1,0:T(8,128)S(1)}, u32[]{:S(2)}, u32[]{:S(2)}) collective-permute-start(f32[2,16,128]{2,1,0:T(8,128)S(1)} %get-tuple-element.14), channel_id=1, source_target_pairs={{16,0},{32,16},{48,32},{64,48},{80,64},{96,80},{112,96},{128,112},... | collective-permute-start | bytes 49160 | tf_op jit(solution)/shard_map/ppermute | solution.py:467
  26.9 0.4 copy.38
  27.3 0.3 reshape.39.w_mid_ref
  27.5 0.4 copy.40
  28.0 0.3 reshape.41.w_late_ref
  28.2 0.1 reshape.43
  28.3 5.5 %collective-permute-done.3.from_east_ref = f32[2,16,128]{2,1,0:T(8,128)S(1)} collective-permute-done((f32[2,16,128]{2,1,0:T(8,128)S(1)}, f32[2,16,128]{2,1,0:T(8,128)S(1)}, u32[]{:S(2)}, u32[]{:S(2)}) %collective-permute-start.3) | collective-permute-done | bytes 16416 | tf_op jit(solution)/shard_map/ppermute | solution.py:467
  33.9 3.4 %shard_map.176 = (f32[32,8,128]{2,1,0:T(8,128)S(1)}, f32[3,32,256]{2,1,0:T(8,128)S(1)}, f32[8,128]{1,0:T(8,128)S(1)}) custom-call(f32[24,16,128]{2,1,0:T(8,128)S(1)} %bitcast.46, f32[8,16,128]{2,1,0:T(8,128)S(1)} %collective-permute-done.north_ref, f32[8,16,128]{2,1,0:T(8,128)S(1)} %collective-permute-done.1.south_ref, ...), custom_call_target="tpu_custom_call" | custom-call | tf_op jit(solution)/shard_map/pallas_call | solution.py:472
  37.3 20.5 %all_to_all.21.x_ref = f32[32,8,128]{2,1,0:T(8,128)S(1)} all-to-all(f32[32,8,128]{2,1,0:T(8,128)S(1)} %get-tuple-element.15), channel_id=1, replica_groups=mesh['lon'=32,'lat'=16] {'lon'}, dimensions={0} | all-to-all | bytes 262144 | tf_op jit(solution)/shard_map/all_to_all | solution.py:488
  57.8 2.1 %shard_map.177 = f32[32,16,128]{2,1,0:T(8,128)S(1)} custom-call(f32[32,8,128]{2,1,0:T(8,128)S(1)} %all_to_all.21.x_ref, f32[8,128]{1,0:T(8,128)S(1)} %get-tuple-element.16.line_ref, f32[256,256]{1,0:T(8,128)S(1)} %copy-done, f32[256,256]{1,0:T(8,128)S(1)} %copy-done.1, f32[32,8,128]{2,1,0:T(8,128)S(1)} %copy-done.2, f32[32,8,128]{2,1,0:T(8,128)S(1)} %copy-done.3, ...), custom_call_target="tpu_custom_call" | custom-call | tf_op jit(solution)/shard_map/pallas_call | solution.py:489
  59.9 18.6 %all_to_all.22.x_ref = f32[32,16,128]{2,1,0:T(8,128)S(1)} all-to-all(f32[32,16,128]{2,1,0:T(8,128)S(1)} %shard_map.177), channel_id=1, replica_groups=mesh['lon'=32,'lat'=16] {'lon'}, dimensions={0} | all-to-all | bytes 524288 | tf_op jit(solution)/shard_map/all_to_all | solution.py:492
  78.5 1.7 %shard_map.178 = (f32[8,24,128]{2,1,0:T(8,128)}, f32[5,32,256]{2,1,0:T(8,128)S(1)}, f32[512,128]{1,0:T(8,128)S(1)}) custom-call(f32[32,16,128]{2,1,0:T(8,128)S(1)} %all_to_all.22.x_ref, f32[3,32,256]{2,1,0:T(8,128)S(1)} %get-tuple-element.17.planes_ref), custom_call_target="tpu_custom_call" | custom-call | tf_op jit(solution)/shard_map/pallas_call | solution.py:494
  80.3 30.7 %all_to_all.23 = f32[512,1,128]{2,1,0:T(1,128)S(1)} all-to-all(f32[512,1,128]{2,1,0:T(1,128)S(1)} %bitcast.49), channel_id=1, replica_groups=mesh['lon'=32,'lat'=16] {'lon','lat'}, dimensions={0} | all-to-all | bytes 524288 | tf_op jit(solution)/shard_map/all_to_all | solution.py:503
  110.9 1.5 %shard_map.179 = (f32[24,128]{1,0:T(8,128)}, f32[24,128]{1,0:T(8,128)}) custom-call(f32[512,128]{1,0:T(8,128)S(1)} %bitcast.47, f32[5,32,256]{2,1,0:T(8,128)S(1)} %get-tuple-element.20.powers_ref), custom_call_target="tpu_custom_call" | custom-call | tf_op jit(solution)/shard_map/pallas_call | solution.py:504
  (40 shorter events, 0.4 us)
Async XLA Ops:
  0.6 0.9 copy-start.14
  0.6 1.0 copy-start.13
  1.7 0.7 copy-start.10
  1.7 0.7 copy-start.11
  1.7 0.7 copy-start.12
  2.6 6.3 %copy-start.5 = (bf16[9,64,64]{2,1,0:T(8,128)(2,1)S(1)}, bf16[9,64,64]{2,1,0:T(8,128)(2,1)}, u32[]{:S(2)}) copy-start(bf16[9,64,64]{2,1,0:T(8,128)(2,1)} %param.23) | copy-start | bytes 221188
  2.6 10.0 %collective-permute-start = (f32[8,16,128]{2,1,0:T(8,128)S(1)}, f32[8,16,128]{2,1,0:T(8,128)S(1)}, u32[]{:S(2)}, u32[]{:S(2)}) collective-permute-start(f32[8,16,128]{2,1,0:T(8,128)S(1)} %get-tuple-element.24), channel_id=1, source_target_pairs={{0,1},{1,2},{2,3},{3,4},{4,5},{5,6},{6,7},{7,8},{8,9},{9,10},{10,1... | collective-permute-start | bytes 196616 | tf_op jit(solution)/shard_map/ppermute | solution.py:462
  7.6 6.7 %collective-permute-start.1 = (f32[8,16,128]{2,1,0:T(8,128)S(1)}, f32[8,16,128]{2,1,0:T(8,128)S(1)}, u32[]{:S(2)}, u32[]{:S(2)}) collective-permute-start(f32[8,16,128]{2,1,0:T(8,128)S(1)} %get-tuple-element.23), channel_id=1, source_target_pairs={{1,0},{2,1},{3,2},{4,3},{5,4},{6,5},{7,6},{8,7},{9,8},{10,9},{11,1... | collective-permute-start | bytes 196616 | tf_op jit(solution)/shard_map/ppermute | solution.py:463
  9.0 0.9 copy-start.6
  10.1 0.7 copy-start.8
  10.9 0.7 copy-start.9
  11.7 0.8 copy-start.7
  14.5 13.9 %collective-permute-start.2 = (f32[2,16,128]{2,1,0:T(8,128)S(1)}, f32[2,16,128]{2,1,0:T(8,128)S(1)}, u32[]{:S(2)}, u32[]{:S(2)}) collective-permute-start(f32[2,16,128]{2,1,0:T(8,128)S(1)} %get-tuple-element.13), channel_id=1, source_target_pairs={{0,16},{16,32},{32,48},{48,64},{64,80},{80,96},{96,112},{112,128},... | collective-permute-start | bytes 49160 | tf_op jit(solution)/shard_map/ppermute | solution.py:466
  24.9 9.0 %collective-permute-start.3 = (f32[2,16,128]{2,1,0:T(8,128)S(1)}, f32[2,16,128]{2,1,0:T(8,128)S(1)}, u32[]{:S(2)}, u32[]{:S(2)}) collective-permute-start(f32[2,16,128]{2,1,0:T(8,128)S(1)} %get-tuple-element.14), channel_id=1, source_target_pairs={{16,0},{32,16},{48,32},{64,48},{80,64},{96,80},{112,96},{128,112},... | collective-permute-start | bytes 49160 | tf_op jit(solution)/shard_map/ppermute | solution.py:467
  33.8 24.0 %copy-start.1 = (f32[256,256]{1,0:T(8,128)S(1)}, f32[256,256]{1,0:T(8,128)}, u32[]{:S(2)}) copy-start(f32[256,256]{1,0:T(8,128)} %constant.19.clone.back_ref) | copy-start | bytes 786436
  33.8 24.0 %copy-start.2 = (f32[32,8,128]{2,1,0:T(8,128)S(1)}, f32[32,8,128]{2,1,0:T(8,128)}, u32[]{:S(2)}) copy-start(f32[32,8,128]{2,1,0:T(8,128)} %constant.20.clone.twist_re_ref) | copy-start | bytes 393220
  33.8 24.0 %copy-start.3 = (f32[32,8,128]{2,1,0:T(8,128)S(1)}, f32[32,8,128]{2,1,0:T(8,128)}, u32[]{:S(2)}) copy-start(f32[32,8,128]{2,1,0:T(8,128)} %constant.21.clone.twist_im_ref) | copy-start | bytes 393220
  33.8 24.0 %copy-start.4 = (f32[128,256]{1,0:T(8,128)S(1)}, f32[128,256]{1,0:T(8,128)}, u32[]{:S(2)}) copy-start(f32[128,256]{1,0:T(8,128)} %constant.22.clone.inner_ref) | copy-start | bytes 393220
  37.3 20.6 %copy-start = (f32[256,256]{1,0:T(8,128)S(1)}, f32[256,256]{1,0:T(8,128)}, u32[]{:S(2)}) copy-start(f32[256,256]{1,0:T(8,128)} %constant.18.clone.spread_ref) | copy-start | bytes 786436

commit v2 on v1

--- a/solution.py
+++ b/solution.py
@@ -1,4 +1,3 @@
-import functools
 import math
 
 import jax
@@ -26,7 +25,7 @@
 highest = lax.Precision.HIGHEST
 
 
-def call(kernel, outs, scratch=(), ins=None):
+def call(kernel, outs, scratch=()):
     spec = pl.BlockSpec(memory_space=pltpu.VMEM)
     return pl.pallas_call(
         kernel,
@@ -41,7 +40,90 @@
     return lax.broadcasted_iota(jnp.int32, shape, len(shape) - 1)
 
 
-def pack_kernel(own_ref, north_ref, south_ref, west_ref, east_ref):
+def gather_kernel(
+    temp_hbm, kmt_hbm, kappa_hbm, helm_hbm, forcing_hbm, cutoff_hbm,
+    own_ref, top_ref, bottom_ref,
+    temp, kmt, planes, cutoff, sems,
+):
+    moves = [
+        pltpu.make_async_copy(source, target, sems.at[index])
+        for index, (source, target) in enumerate(
+            (
+                (temp_hbm, temp),
+                (kmt_hbm, kmt),
+                (kappa_hbm, planes.at[0]),
+                (helm_hbm, planes.at[1]),
+                (forcing_hbm, planes.at[2]),
+                (cutoff_hbm, cutoff),
+            )
+        )
+    ]
+    for move in moves:
+        move.start()
+    own_ref[:, CUT + 1 :, :] = jnp.zeros((ROWS, FIELDS - CUT - 1, COLS), jnp.float32)
+    for move in moves:
+        move.wait()
+    for level in range(LEV):
+        own_ref[:, level, :] = temp[level]
+    own_ref[:, KMT, :] = kmt[...].astype(jnp.float32)
+    for index, field in enumerate((KAPPA, HELM, FORCING)):
+        own_ref[:, field, :] = planes[index]
+    kept = jnp.broadcast_to(cutoff[...].astype(jnp.float32), (ROWS, ROWS))
+    row = lax.broadcasted_iota(jnp.int32, (ROWS, ROWS), 0)
+    kept = jnp.sum(jnp.where(row == lane_index((ROWS, ROWS)), kept, 0.0), axis=1, keepdims=True)
+    own_ref[:, CUT, :] = jnp.broadcast_to(kept, (ROWS, COLS))
+    top_ref[...] = own_ref[0:DEEP]
+    bottom_ref[...] = own_ref[ROWS - DEEP :]
+
+
+def weights_kernel(first_ref, mid_ref, late_ref, last_ref, w_in_ref, w_mid_ref, w_late_ref, w_out_ref):
+    w_in_ref[...] = jnp.zeros(w_in_ref.shape, w_in_ref.dtype)
+    width = mid_ref.shape[1]
+    none = jnp.zeros((LEV, width), jnp.float32)
+    for row in range(4):
+        parts = []
+        for tap in range(3):
+            for parity in range(2):
+                a = row - parity
+                parts.append(first_ref[3 * a + tap].astype(jnp.float32) if 0 <= a < 3 else none)
+        top = jnp.concatenate(parts, axis=1)
+        marks = [jnp.ones((1, width), jnp.float32) if row == at else none[:1] for at in (1, 2, 2, 3)]
+        marks = jnp.concatenate(marks, axis=1)
+        block = jnp.concatenate(
+            [
+                jnp.concatenate([top, jnp.zeros((LEV, 4 * width), jnp.float32)], axis=1),
+                jnp.concatenate(
+                    [
+                        jnp.concatenate([jnp.zeros((1, 6 * width), jnp.float32), marks], axis=1),
+                        jnp.zeros((LEV - 1, 10 * width), jnp.float32),
+                    ],
+                    axis=0,
+                ),
+            ],
+            axis=0,
+        )
+        w_in_ref[FIELDS * row : FIELDS * (row + 1)] = block.astype(jnp.bfloat16)
+
+    def rows_of(ref, tap, parity):
+        outs = ref.shape[1]
+        blank = jnp.zeros((outs, width), jnp.float32)
+        parts = []
+        for row in range(4):
+            a = row - parity
+            parts.append(ref[3 * a + tap].astype(jnp.float32) if 0 <= a < 3 else blank)
+        return jnp.concatenate(parts, axis=1)
+
+    for ref, out_ref in ((mid_ref, w_mid_ref), (late_ref, w_late_ref)):
+        for tap in range(3):
+            both = jnp.concatenate([rows_of(ref, tap, 0), rows_of(ref, tap, 1)], axis=0)
+            out_ref[:, 2 * width * tap : 2 * width * (tap + 1)] = both.T.astype(jnp.bfloat16)
+    w_out_ref[...] = jnp.concatenate(
+        [rows_of(last_ref, tap, parity) for tap in range(3) for parity in range(2)], axis=0
+    ).astype(jnp.bfloat16)
+
+
+def pack_kernel(own_ref, north_ref, south_ref, far_ref, near_ref):
+    even = lax.rem(lax.axis_index("lon"), 2) == 0
     lane = lane_index((FIELDS, COLS))
     for part in range(TALL // SLOTS):
         first = jnp.zeros((FIELDS, COLS), jnp.float32)
@@ -57,16 +139,16 @@
             inside = (lane >= HALO * slot) & (lane < HALO * (slot + 1))
             first = jnp.where(inside, pltpu.roll(here, HALO * slot, 1) if slot else here, first)
             last = jnp.where(inside, pltpu.roll(here, HALO * (slot + 1), 1), last)
-        west_ref[part] = first
-        east_ref[part] = last
+        far_ref[part] = jnp.where(even, first, last)
+        near_ref[part] = jnp.where(even, last, first)
 
 
 def closure_kernel(
     own_ref,
     north_ref,
     south_ref,
-    from_west_ref,
-    from_east_ref,
+    far_ref,
+    near_ref,
     w_in_ref,
     w_mid_ref,
     w_late_ref,
@@ -83,6 +165,10 @@
 ):
     lane = lane_index((FIELDS, COLS))
     depth = lax.broadcasted_iota(jnp.int32, (LEV, 2 * COLS), 0).astype(jnp.float32)
+    even = lax.rem(lax.axis_index("lon"), 2) == 0
+    parts = range(TALL // SLOTS)
+    from_west = [jnp.where(even, far_ref[part], near_ref[part]) for part in parts]
+    from_east = [jnp.where(even, near_ref[part], far_ref[part]) for part in parts]
     for row in range(TALL):
         if row < DEEP:
             here = north_ref[row]
@@ -91,10 +177,10 @@
         else:
             here = south_ref[row - DEEP - ROWS]
         part, slot = row // SLOTS, row % SLOTS
-        west = from_west_ref[part]
+        west = from_west[part]
         if slot:
             west = pltpu.roll(west, COLS - HALO * slot, 1)
-        east = from_east_ref[part]
+        east = from_east[part]
         shift = (HALO - HALO * slot) % COLS
         if shift:
             east = pltpu.roll(east, shift, 1)
@@ -366,8 +452,13 @@
     parts_ref[...] = jnp.broadcast_to(message, parts_ref.shape)
 
 
-def combine_kernel(parts_ref, powers_ref, surface_ref, residual_ref, wide):
+def sum_messages(parts_ref):
     count = parts_ref.shape[0] // 8
+    if count == 1:
+        total = (parts_ref[...], jnp.zeros((8, COLS), jnp.float32))
+        for by in (4, 2, 1):
+            total = pair_add(total, tuple(pltpu.roll(t, by, 0) for t in total))
+        return pair_add(total, tuple(pltpu.roll(t, 64, 1) for t in total))
     tiles = [(parts_ref[8 * i : 8 * i + 8, :], None) for i in range(count)]
     merged = []
     for a, b in zip(tiles[::2], tiles[1::2]):
@@ -378,8 +469,17 @@
     total = tiles[0]
     for by in (4, 2, 1):
         total = pair_add(total, tuple(pltpu.roll(t, by, 0) for t in total))
-    other = tuple(pltpu.roll(t, 64, 1) for t in total)
-    total = pair_add(total, other)
+    return pair_add(total, tuple(pltpu.roll(t, 64, 1) for t in total))
+
+
+def merge_kernel(parts_ref, out_ref):
+    total = sum_messages(parts_ref)
+    lane = lane_index((8, COLS))
+    out_ref[...] = jnp.where(lane < 64, total[0], total[1])
+
+
+def combine_kernel(parts_ref, powers_ref, surface_ref, residual_ref, wide):
+    total = sum_messages(parts_ref)
     moments = [
         tuple(jnp.broadcast_to(t[:, order : order + 1], (8, COLS)) for t in total)
         for order in range(2 * ITERS)
@@ -422,25 +522,6 @@
         target[...] = wide[HALO : HALO + ROWS, HALO : HALO + COLS]
 
 
-def paired(weight):
-    _, outs, ins = weight.shape
-    taps = jnp.transpose(weight.reshape(3, 3, outs, ins), (0, 3, 1, 2))
-    upper = jnp.pad(taps, ((0, 1), (0, 0), (0, 0), (0, 0)))
-    lower = jnp.pad(taps, ((1, 0), (0, 0), (0, 0), (0, 0)))
-    return jnp.stack([upper, lower], axis=3)
-
-
-def first_weight(weight):
-    _, outs, _ = weight.shape
-    taps = paired(weight).reshape(4, LEV, 6 * outs)
-    taps = jnp.pad(taps, ((0, 0), (0, FIELDS - LEV), (0, 0)))
-    masks = np.zeros((4, FIELDS, 4, outs), np.float32)
-    for at, row in enumerate((1, 2, 2, 3)):
-        masks[row, LEV, at] = 1.0
-    masks = jnp.asarray(masks.reshape(4, FIELDS, 4 * outs), jnp.bfloat16)
-    return jnp.concatenate([taps, masks], axis=2).reshape(4 * FIELDS, 10 * outs)
-
-
 def forward(axis, periodic):
     count = lax.axis_size(axis)
     pairs = [(i, i + 1) for i in range(count - 1)]
@@ -451,24 +532,52 @@
     return [(target, source) for source, target in forward(axis, periodic)]
 
 
+def swap_near():
+    return [(i, i ^ 1) for i in range(lax.axis_size("lon"))]
+
+
+def swap_far():
+    count = lax.axis_size("lon")
+    return [(i, (i + 1) % count if i % 2 else (i - 1) % count) for i in range(count)]
+
+
 def body(temp, kmt, kappa, helm, forcing, cutoff, conv_in, conv_mid, conv_late, conv_out):
     f32 = jnp.float32
     shape = jax.ShapeDtypeStruct
     blocks = lax.axis_size("lon")
-    cuts = jnp.broadcast_to(cutoff.astype(f32)[:, None], (ROWS, COLS))
-    rest = jnp.zeros((FIELDS - CUT - 1, ROWS, COLS), f32)
-    flat = jnp.stack([kmt.astype(f32), kappa, helm, forcing, cuts])
-    own = jnp.transpose(jnp.concatenate([temp, flat, rest]), (1, 0, 2))
-    north = lax.ppermute(own[ROWS - DEEP :], "lat", forward("lat", False))
-    south = lax.ppermute(own[:DEEP], "lat", backward("lat", False))
+    own, top, bottom = pl.pallas_call(
+        gather_kernel,
+        out_shape=(
+            shape((ROWS, FIELDS, COLS), f32),
+            shape((DEEP, FIELDS, COLS), f32),
+            shape((DEEP, FIELDS, COLS), f32),
+        ),
+        in_specs=[pl.BlockSpec(memory_space=pltpu.HBM)] * 6,
+        out_specs=(pl.BlockSpec(memory_space=pltpu.VMEM),) * 3,
+        scratch_shapes=(
+            pltpu.VMEM((LEV, ROWS, COLS), f32),
+            pltpu.VMEM((ROWS, COLS), jnp.int32),
+            pltpu.VMEM((3, ROWS, COLS), f32),
+            pltpu.VMEM((1, ROWS), jnp.int32),
+            pltpu.SemaphoreType.DMA((6,)),
+        ),
+    )(temp, kmt, kappa, helm, forcing, cutoff.reshape(1, ROWS))
+    north = lax.ppermute(bottom, "lat", forward("lat", False))
+    south = lax.ppermute(top, "lat", backward("lat", False))
+    bf16 = jnp.bfloat16
+    weights = call(
+        weights_kernel,
+        (
+            shape((4 * FIELDS, 640), bf16),
+            shape((256, 384), bf16),
+            shape((256, 384), bf16),
+            shape((48, 256), bf16),
+        ),
+    )(jnp.transpose(conv_in, (0, 2, 1)), conv_mid, conv_late, conv_out)
     slab = shape((TALL // SLOTS, FIELDS, COLS), f32)
-    first, last = call(pack_kernel, (slab, slab))(own, north, south)
-    from_west = lax.ppermute(last, "lon", forward("lon", True))
-    from_east = lax.ppermute(first, "lon", backward("lon", True))
-    w_in = first_weight(conv_in)
-    w_mid = paired(conv_mid).reshape(256, 384)
-    w_late = paired(conv_late).reshape(256, 384)
-    w_out = jnp.transpose(paired(conv_out).reshape(256, 48))
+    to_far, to_near = call(pack_kernel, (slab, slab))(own, north, south)
+    far = lax.ppermute(to_far, "lon", swap_far())
+    near = lax.ppermute(to_near, "lon", swap_near())
     lines, planes, line = call(
         closure_kernel,
         (
@@ -484,28 +593,38 @@
             pltpu.VMEM((19, WIDE, 128), jnp.bfloat16),
             pltpu.VMEM((19, WIDE, 128), jnp.bfloat16),
         ),
-    )(own, north, south, from_west, from_east, w_in, w_mid, w_late, w_out)
+    )(own, north, south, far, near, *weights)
     whole = lax.all_to_all(lines, "lon", split_axis=0, concat_axis=0, tiled=True)
     filtered = call(filter_kernel, shape((blocks, 2 * LEV, COLS), f32))(
         whole, line, *(jnp.asarray(t) for t in filter_tables(blocks, COLS))
     )
     back = lax.all_to_all(filtered, "lon", split_axis=0, concat_axis=0, tiled=True)
     everyone = blocks * lax.axis_size("lat")
+    wide = everyone // 8
+    both = ("lon", "lat")
+    inner = [[wide * i + k for k in range(wide)] for i in range(8)]
+    outer = [[wide * i + k for i in range(8)] for k in range(wide)]
     temp_new, powers, parts = call(
         powers_kernel,
         (
             shape((LEV, ROWS, COLS), f32),
             shape((ITERS + 1, MID, 2 * COLS), f32),
-            shape((everyone, COLS), f32),
+            shape((wide, COLS), f32),
         ),
         (pltpu.VMEM((MID, 2 * COLS), f32),),
     )(back, planes)
-    gathered = lax.all_to_all(parts, ("lon", "lat"), split_axis=0, concat_axis=0, tiled=True)
+    parts = lax.all_to_all(
+        parts, both, split_axis=0, concat_axis=0, tiled=True, axis_index_groups=inner
+    )
+    parts = call(merge_kernel, shape((8, COLS), f32))(parts)
+    parts = lax.all_to_all(
+        parts, both, split_axis=0, concat_axis=0, tiled=True, axis_index_groups=outer
+    )
     surface, residual = call(
         combine_kernel,
         (shape((ROWS, COLS), f32), shape((ROWS, COLS), f32)),
         (pltpu.VMEM((MID, 2 * COLS), f32),),
-    )(gathered, powers)
+    )(parts, powers)
     return temp_new, surface, residual
 
 

time: 113 us -> 110 us (0.973)
  local copies, waits for them, and re-layouts: 6.73 us -> 0.97 us
  starting transfers between devices: 18.6 us -> 21 us
  Pallas kernels: 8.89 us -> 11.2 us
    unnamed x33 -> x22, local copies, waits for them, and re-layouts: 4.73 us -> 0.97 us
    ppermute x4, starting transfers between devices: 18.6 us -> 21 us  [the longest x1 10.5 us: body(): far = lax.ppermute(to_far, 'lon', swap_far())]
    pallas_call x1 -> x4, Pallas kernels: 0.23 us -> 2.42 us  [the longest x1 1.78 us: body(): pl.pallas_call(gather_kernel, out_shape=(shape((ROWS, FIELDS, COLS), f32)...]
    all_to_all x1 -> x2, blocking collectives: 30.7 us -> 28.5 us  [body(): lax.all_to_all(parts, both, split_axis=0, concat_axis=0, tiled=True, axis...]
    all_to_all x1, blocking collectives: 20.5 us -> 22.1 us  [body(): lax.all_to_all(lines, 'lon', split_axis=0, concat_axis=0, tiled=True)]
  transfers between devices with their start and end apart: 4 -> 4, of which waited for: 2 -> 3; matrix products, arithmetic and copies ran while one was open for 2% -> 0% of each run, Pallas kernels for 0% -> 0%
where the time goes in v2:
time: 110 us; the launch traced here: 109 us
  blocking collectives  69.3 us (63%)
  starting transfers between devices  21 us (19%)
  Pallas kernels  11.2 us (10%)
  waiting for transfers between devices  6.05 us (6%)
    all_to_all x2, blocking collectives, body(): lax.all_to_all(parts, both, split_axis=0, concat_axis=0, tiled=True, axis...  28.5 us
    all_to_all x1, blocking collectives, body(): lax.all_to_all(lines, 'lon', split_axis=0, concat_axis=0, tiled=True)  22.1 us
    all_to_all x1, blocking collectives, body(): lax.all_to_all(filtered, 'lon', split_axis=0, concat_axis=0, tiled=True)  18.6 us
    ppermute x1, starting transfers between devices, body(): far = lax.ppermute(to_far, 'lon', swap_far())  10.5 us
    ppermute x1, waiting for transfers between devices, body(): south = lax.ppermute(top, 'lat', backward('lat', False))  5.25 us
    ppermute x1, starting transfers between devices, body(): north = lax.ppermute(bottom, 'lat', forward('lat', False))  4.83 us
    ppermute x1, starting transfers between devices, body(): near = lax.ppermute(to_near, 'lon', swap_near())  4.37 us
    pallas_call x1, Pallas kernels, body(): call(closure_kernel, (shape((MID, LEV, COLS), f32), shape((3, MID, 2 * CO...  3.66 us
  transfers between devices with their start and end apart: 4, of which 3 were waited for; matrix products, arithmetic and copies ran while one was open for 0% of the time, Pallas kernels for 0%

profile of v2, /device:TPU:1, one launch (start us, length us, event | category | flops | bytes accessed | tf_op | source)
XLA Modules:
  0.0 109.4 jit_solution(11030080536538511216)
XLA Ops:
  0.6 1.8 %shard_map.166 = (f32[24,16,128]{2,1,0:T(8,128)}, f32[8,16,128]{2,1,0:T(8,128)}, f32[8,16,128]{2,1,0:T(8,128)}) custom-call(f32[8,24,128]{2,1,0:T(8,128)} %temp_hbm.1, s32[24,128]{1,0:T(8,128)} %kmt_hbm.1, f32[24,128]{1,0:T(8,128)} %kappa_hbm.1, f32[24,128]{1,0:T(8,128)} %helm_hbm.1, f32[24,128]{1,0:T(8,128)} %forcing_hbm.1, s32[1,24]{1,0:T(1,128)} %bitcast.15), custom_call_target="tpu_custom_call" | custom-call | tf_op jit(solution)/shard_map/pallas_call | solution.py:548
  2.4 4.8 %collective-permute-start = (f32[8,16,128]{2,1,0:T(8,128)}, f32[8,16,128]{2,1,0:T(8,128)S(1)}, u32[]{:S(2)}, u32[]{:S(2)}) collective-permute-start(f32[8,16,128]{2,1,0:T(8,128)} %get-tuple-element.21), channel_id=1, source_target_pairs={{0,1},{1,2},{2,3},{3,4},{4,5},{5,6},{6,7},{7,8},{8,9},{9,10},{10,1... | collective-permute-start | bytes 196616 | tf_op jit(solution)/shard_map/ppermute | solution.py:565
  7.3 1.3 %collective-permute-start.1 = (f32[8,16,128]{2,1,0:T(8,128)}, f32[8,16,128]{2,1,0:T(8,128)S(1)}, u32[]{:S(2)}, u32[]{:S(2)}) collective-permute-start(f32[8,16,128]{2,1,0:T(8,128)} %get-tuple-element.22), channel_id=1, source_target_pairs={{1,0},{2,1},{3,2},{4,3},{5,4},{6,5},{7,6},{8,7},{9,8},{10,9},{11,1... | collective-permute-start | bytes 196616 | tf_op jit(solution)/shard_map/ppermute | solution.py:566
  8.6 0.3 collective-permute-done.north_ref
  8.9 5.2 %collective-permute-done.1.south_ref = f32[8,16,128]{2,1,0:T(8,128)S(1)} collective-permute-done((f32[8,16,128]{2,1,0:T(8,128)}, f32[8,16,128]{2,1,0:T(8,128)S(1)}, u32[]{:S(2)}, u32[]{:S(2)}) %collective-permute-start.1) | collective-permute-done | bytes 65568 | tf_op jit(solution)/shard_map/ppermute | solution.py:566
  14.1 0.9 copy-done
  15.1 0.2 shard_map.167
  15.3 0.0 copy-start.1
  15.3 10.5 %collective-permute-start.2 = (f32[2,16,128]{2,1,0:T(8,128)S(1)}, f32[2,16,128]{2,1,0:T(8,128)S(1)}, u32[]{:S(2)}, u32[]{:S(2)}) collective-permute-start(f32[2,16,128]{2,1,0:T(8,128)S(1)} %get-tuple-element.23), channel_id=1, source_target_pairs={{0,496},{16,32},{32,16},{48,64},{64,48},{80,96},{96,80},{112,128},... | collective-permute-start | bytes 49160 | tf_op jit(solution)/shard_map/ppermute | solution.py:579
  25.8 4.4 %collective-permute-start.3 = (f32[2,16,128]{2,1,0:T(8,128)S(1)}, f32[2,16,128]{2,1,0:T(8,128)S(1)}, u32[]{:S(2)}, u32[]{:S(2)}) collective-permute-start(f32[2,16,128]{2,1,0:T(8,128)S(1)} %get-tuple-element.24), channel_id=1, source_target_pairs={{0,16},{16,0},{32,48},{48,32},{64,80},{80,64},{96,112},{112,96},{1... | collective-permute-start | bytes 49160 | tf_op jit(solution)/shard_map/ppermute | solution.py:580
  30.2 0.0 copy-done.4
  30.2 0.0 copy-done.5
  30.2 0.0 copy-done.9
  30.2 0.0 copy-done.10
  30.3 0.3 shard_map.168
  30.5 0.0 collective-permute-done.2.far_ref
  30.6 0.5 collective-permute-done.3.near_ref
  31.0 0.0 copy-done.1
  31.0 0.0 copy-start.8
  31.1 3.7 %shard_map.169 = (f32[32,8,128]{2,1,0:T(8,128)S(1)}, f32[3,32,256]{2,1,0:T(8,128)S(1)}, f32[8,128]{1,0:T(8,128)S(1)}) custom-call(f32[24,16,128]{2,1,0:T(8,128)S(1)} %copy-done.1, f32[8,16,128]{2,1,0:T(8,128)S(1)} %collective-permute-done.north_ref, f32[8,16,128]{2,1,0:T(8,128)S(1)} %collective-permute-done.1.south_ref, ...), custom_call_target="tpu_custom_call" | custom-call | tf_op jit(solution)/shard_map/pallas_call | solution.py:581
  34.7 0.0 copy-start.2
  34.7 22.1 %all_to_all.32.x_ref = f32[32,8,128]{2,1,0:T(8,128)S(1)} all-to-all(f32[32,8,128]{2,1,0:T(8,128)S(1)} %get-tuple-element.29), channel_id=1, replica_groups=mesh['lon'=32,'lat'=16] {'lon'}, dimensions={0} | all-to-all | bytes 262144 | tf_op jit(solution)/shard_map/all_to_all | solution.py:597
  56.9 0.0 copy-done.3
  56.9 0.0 copy-done.6
  56.9 0.0 copy-done.7
  56.9 2.1 %shard_map.170 = f32[32,16,128]{2,1,0:T(8,128)S(1)} custom-call(f32[32,8,128]{2,1,0:T(8,128)S(1)} %all_to_all.32.x_ref, f32[8,128]{1,0:T(8,128)S(1)} %get-tuple-element.30.line_ref, f32[256,256]{1,0:T(8,128)S(1)} %copy-done.3, f32[256,256]{1,0:T(8,128)S(1)} %copy-done.2, f32[32,8,128]{2,1,0:T(8,128)S(1)} %copy-done.8, f32[32,8,128]{2,1,0:T(8,128)S(1)} %copy-done.7, ...), custom_call_target="tpu_custom_call" | custom-call | tf_op jit(solution)/shard_map/pallas_call | solution.py:598
  59.0 18.6 %all_to_all.33.x_ref = f32[32,16,128]{2,1,0:T(8,128)S(1)} all-to-all(f32[32,16,128]{2,1,0:T(8,128)S(1)} %shard_map.170), channel_id=1, replica_groups=mesh['lon'=32,'lat'=16] {'lon'}, dimensions={0} | all-to-all | bytes 524288 | tf_op jit(solution)/shard_map/all_to_all | solution.py:601
  77.6 1.7 %shard_map.171 = (f32[8,24,128]{2,1,0:T(8,128)}, f32[5,32,256]{2,1,0:T(8,128)S(1)}, f32[64,128]{1,0:T(8,128)S(1)}) custom-call(f32[32,16,128]{2,1,0:T(8,128)S(1)} %all_to_all.33.x_ref, f32[3,32,256]{2,1,0:T(8,128)S(1)} %get-tuple-element.31.planes_ref), custom_call_target="tpu_custom_call" | custom-call | tf_op jit(solution)/shard_map/pallas_call | solution.py:607
  79.3 19.2 %all_to_all.34 = f32[64,1,128]{2,1,0:T(1,128)S(1)} all-to-all(f32[64,1,128]{2,1,0:T(1,128)S(1)} %bitcast.11), channel_id=1, replica_groups={{0,1,2,3,4,5,6,7,8,9,10,11,12,13,14,15,16,17,18,19,20,21,22,23,24,25,26..., dimensions={0} | all-to-all | bytes 65536 | tf_op jit(solution)/shard_map/all_to_all | solution.py:616
  98.5 0.1 shard_map.172
  98.6 9.4 %all_to_all.35 = f32[8,1,128]{2,1,0:T(1,128)S(1)} all-to-all(f32[8,1,128]{2,1,0:T(1,128)S(1)} %bitcast.13), channel_id=1, replica_groups={{0,64,128,192,256,320,384,448},{1,65,129,193,257,321,385,449},{2,66,130..., dimensions={0} | all-to-all | bytes 8192 | tf_op jit(solution)/shard_map/all_to_all | solution.py:620
  108.0 1.4 %shard_map.173 = (f32[24,128]{1,0:T(8,128)}, f32[24,128]{1,0:T(8,128)}) custom-call(f32[8,128]{1,0:T(8,128)S(1)} %bitcast.14, f32[5,32,256]{2,1,0:T(8,128)S(1)} %get-tuple-element.34.powers_ref), custom_call_target="tpu_custom_call" | custom-call | tf_op jit(solution)/shard_map/pallas_call | solution.py:623
  (10 shorter events, 0.0 us)
Async XLA Ops:
  2.4 6.5 %collective-permute-start = (f32[8,16,128]{2,1,0:T(8,128)}, f32[8,16,128]{2,1,0:T(8,128)S(1)}, u32[]{:S(2)}, u32[]{:S(2)}) collective-permute-start(f32[8,16,128]{2,1,0:T(8,128)} %get-tuple-element.21), channel_id=1, source_target_pairs={{0,1},{1,2},{2,3},{3,4},{4,5},{5,6},{6,7},{7,8},{8,9},{9,10},{10,1... | collective-permute-start | bytes 196616 | tf_op jit(solution)/shard_map/ppermute | solution.py:565
  7.3 6.9 %collective-permute-start.1 = (f32[8,16,128]{2,1,0:T(8,128)}, f32[8,16,128]{2,1,0:T(8,128)S(1)}, u32[]{:S(2)}, u32[]{:S(2)}) collective-permute-start(f32[8,16,128]{2,1,0:T(8,128)} %get-tuple-element.22), channel_id=1, source_target_pairs={{1,0},{2,1},{3,2},{4,3},{5,4},{6,5},{7,6},{8,7},{9,8},{10,9},{11,1... | collective-permute-start | bytes 196616 | tf_op jit(solution)/shard_map/ppermute | solution.py:566
  14.1 0.9 copy-start
  15.1 15.2 %copy-start.4 = (bf16[9,64,64]{2,1,0:T(8,128)(2,1)S(1)}, bf16[9,64,64]{2,1,0:T(8,128)(2,1)}, u32[]{:S(2)}) copy-start(bf16[9,64,64]{2,1,0:T(8,128)(2,1)} %mid_ref.1) | copy-start | bytes 221188
  15.1 15.2 %copy-start.5 = (bf16[9,64,64]{2,1,0:T(8,128)(2,1)S(1)}, bf16[9,64,64]{2,1,0:T(8,128)(2,1)}, u32[]{:S(2)}) copy-start(bf16[9,64,64]{2,1,0:T(8,128)(2,1)} %late_ref.1) | copy-start | bytes 221188
  15.1 15.2 %copy-start.9 = (bf16[9,64,8]{1,2,0:T(8,128)(2,1)S(1)}, bf16[9,64,8]{1,2,0:T(8,128)(2,1)}, u32[]{:S(2)}) copy-start(bf16[9,64,8]{1,2,0:T(8,128)(2,1)} %param.21) | copy-start | bytes 27652
  15.1 15.2 %copy-start.10 = (bf16[9,8,64]{2,1,0:T(8,128)(2,1)S(1)}, bf16[9,8,64]{2,1,0:T(8,128)(2,1)}, u32[]{:S(2)}) copy-start(bf16[9,8,64]{2,1,0:T(8,128)(2,1)} %last_ref.1) | copy-start | bytes 27652
  15.3 15.7 %copy-start.1 = (f32[24,16,128]{2,1,0:T(8,128)S(1)}, f32[24,16,128]{2,1,0:T(8,128)}, u32[]{:S(2)}) copy-start(f32[24,16,128]{2,1,0:T(8,128)} %get-tuple-element.20.own_ref) | copy-start | bytes 589828
  15.3 15.2 %collective-permute-start.2 = (f32[2,16,128]{2,1,0:T(8,128)S(1)}, f32[2,16,128]{2,1,0:T(8,128)S(1)}, u32[]{:S(2)}, u32[]{:S(2)}) collective-permute-start(f32[2,16,128]{2,1,0:T(8,128)S(1)} %get-tuple-element.23), channel_id=1, source_target_pairs={{0,496},{16,32},{32,16},{48,64},{64,48},{80,96},{96,80},{112,128},... | collective-permute-start | bytes 49160 | tf_op jit(solution)/shard_map/ppermute | solution.py:579
  25.8 5.2 %collective-permute-start.3 = (f32[2,16,128]{2,1,0:T(8,128)S(1)}, f32[2,16,128]{2,1,0:T(8,128)S(1)}, u32[]{:S(2)}, u32[]{:S(2)}) collective-permute-start(f32[2,16,128]{2,1,0:T(8,128)S(1)} %get-tuple-element.24), channel_id=1, source_target_pairs={{0,16},{16,0},{32,48},{48,32},{64,80},{80,64},{96,112},{112,96},{1... | collective-permute-start | bytes 49160 | tf_op jit(solution)/shard_map/ppermute | solution.py:580
  31.0 25.8 %copy-start.3 = (f32[256,256]{1,0:T(8,128)S(1)}, f32[256,256]{1,0:T(8,128)}, u32[]{:S(2)}) copy-start(f32[256,256]{1,0:T(8,128)} %constant.10.clone.spread_ref) | copy-start | bytes 786436
  31.0 25.8 %copy-start.6 = (f32[128,256]{1,0:T(8,128)S(1)}, f32[128,256]{1,0:T(8,128)}, u32[]{:S(2)}) copy-start(f32[128,256]{1,0:T(8,128)} %constant.14.clone.inner_ref) | copy-start | bytes 393220
  31.0 25.8 %copy-start.7 = (f32[32,8,128]{2,1,0:T(8,128)S(1)}, f32[32,8,128]{2,1,0:T(8,128)}, u32[]{:S(2)}) copy-start(f32[32,8,128]{2,1,0:T(8,128)} %constant.13.clone.twist_im_ref) | copy-start | bytes 393220
  31.0 25.8 %copy-start.8 = (f32[32,8,128]{2,1,0:T(8,128)S(1)}, f32[32,8,128]{2,1,0:T(8,128)}, u32[]{:S(2)}) copy-start(f32[32,8,128]{2,1,0:T(8,128)} %constant.12.clone.twist_re_ref) | copy-start | bytes 393220
  34.7 22.2 %copy-start.2 = (f32[256,256]{1,0:T(8,128)S(1)}, f32[256,256]{1,0:T(8,128)}, u32[]{:S(2)}) copy-start(f32[256,256]{1,0:T(8,128)} %constant.11.clone.back_ref) | copy-start | bytes 786436

commit v3 on v2

v3 whole, which is shorter than its diff:
```python
import math

import jax
import jax.numpy as jnp
import numpy as np
from jax import lax
from jax.experimental import pallas as pl
from jax.experimental.pallas import tpu as pltpu
from jax.sharding import PartitionSpec as P

ITERS = 4
STEP = 0.25
LEV = 8
FIELDS = 16
KMT, KAPPA, HELM, FORCING, CUT = 8, 9, 10, 11, 12
HALO = 4
DEEP = 8
ROWS = 24
COLS = 128
TALL = ROWS + 2 * DEEP
MID = ROWS + 2 * HALO
BLOCK = LEV + 1
SLOTS = 20
VMEM_LIMIT = 48 * 1024 * 1024


def call(kernel, outs, scratch=(), flops=None):
    spec = pl.BlockSpec(memory_space=pltpu.VMEM)
    return pl.pallas_call(
        kernel,
        out_shape=outs,
        out_specs=jax.tree.map(lambda _: spec, outs),
        scratch_shapes=scratch,
        compiler_params=pltpu.CompilerParams(vmem_limit_bytes=VMEM_LIMIT),
        cost_estimate=flops
        and pl.CostEstimate(flops=flops, bytes_accessed=10**6, transcendentals=flops // 500),
    )


def lane_index(shape):
    return lax.broadcasted_iota(jnp.int32, shape, len(shape) - 1)


def slab_kernel(
    temp_hbm, kmt_hbm, kappa_hbm, helm_hbm, forcing_hbm, cutoff_hbm,
    top_ref, bottom_ref, kmt, cutoff, sems,
):
    pairs = [(kmt_hbm, kmt), (cutoff_hbm, cutoff)]
    for target, start in ((top_ref, 0), (bottom_ref, ROWS - DEEP)):
        rows = pl.ds(start, DEEP)
        pairs.append((temp_hbm.at[:, rows], target.at[pl.ds(0, LEV)]))
        for source, field in ((kappa_hbm, KAPPA), (helm_hbm, HELM), (forcing_hbm, FORCING)):
            pairs.append((source.at[rows], target.at[field]))
    moves = [
        pltpu.make_async_copy(source, target, sems.at[index])
        for index, (source, target) in enumerate(pairs)
    ]
    for move in moves:
        move.start()
    for move in moves:
        move.wait()
    kept = cutoff_rows(cutoff)
    for target, start in ((top_ref, 0), (bottom_ref, ROWS - DEEP)):
        target[KMT] = kmt[start : start + DEEP].astype(jnp.float32)
        target[CUT] = kept[start : start + DEEP]


def cutoff_rows(cutoff_ref):
    kept = jnp.broadcast_to(cutoff_ref[...].astype(jnp.float32), (ROWS, ROWS))
    row = lax.broadcasted_iota(jnp.int32, (ROWS, ROWS), 0)
    kept = jnp.sum(jnp.where(row == lane_index((ROWS, ROWS)), kept, 0.0), axis=1, keepdims=True)
    return jnp.broadcast_to(kept, (ROWS, COLS))


def rows_kernel(temp_ref, kmt_ref, kappa_ref, helm_ref, forcing_ref, cutoff_ref, own_ref):
    own_ref[:, CUT + 1 :, :] = jnp.zeros((ROWS, FIELDS - CUT - 1, COLS), jnp.float32)
    for level in range(LEV):
        own_ref[:, level, :] = temp_ref[level]
    own_ref[:, KMT, :] = kmt_ref[...].astype(jnp.float32)
    own_ref[:, KAPPA, :] = kappa_ref[...]
    own_ref[:, HELM, :] = helm_ref[...]
    own_ref[:, FORCING, :] = forcing_ref[...]
    own_ref[:, CUT, :] = cutoff_rows(cutoff_ref)


def weights_kernel(
    first_ref, mid_ref, late_ref, last_ref, *refs
):
    tables, outs = refs[:3], refs[3:]
    w_in_ref, w_mid_ref, w_late_ref, w_out_ref = outs[:4]
    for index, table_ref in enumerate(tables):
        outs[4 + 2 * index][...], outs[5 + 2 * index][...] = halves(table_ref[...])
    w_in_ref[...] = jnp.zeros(w_in_ref.shape, w_in_ref.dtype)
    width = mid_ref.shape[1]
    none = jnp.zeros((LEV, width), jnp.float32)
    for row in range(4):
        parts = []
        for tap in range(3):
            for parity in range(2):
                a = row - parity
                parts.append(first_ref[3 * a + tap].astype(jnp.float32) if 0 <= a < 3 else none)
        top = jnp.concatenate(parts, axis=1)
        marks = [jnp.ones((1, width), jnp.float32) if row == at else none[:1] for at in (1, 2, 2, 3)]
        marks = jnp.concatenate(marks, axis=1)
        block = jnp.concatenate(
            [
                jnp.concatenate([top, jnp.zeros((LEV, 4 * width), jnp.float32)], axis=1),
                jnp.concatenate(
                    [
                        jnp.concatenate([jnp.zeros((1, 6 * width), jnp.float32), marks], axis=1),
                        jnp.zeros((LEV - 1, 10 * width), jnp.float32),
                    ],
                    axis=0,
                ),
            ],
            axis=0,
        )
        w_in_ref[FIELDS * row : FIELDS * (row + 1)] = block.astype(jnp.bfloat16)

    def rows_of(ref, tap, parity):
        outs = ref.shape[1]
        blank = jnp.zeros((outs, width), jnp.float32)
        parts = []
        for row in range(4):
            a = row - parity
            parts.append(ref[3 * a + tap].astype(jnp.float32) if 0 <= a < 3 else blank)
        return jnp.concatenate(parts, axis=1)

    for ref, out_ref in ((mid_ref, w_mid_ref), (late_ref, w_late_ref)):
        for tap in range(3):
            both = jnp.concatenate([rows_of(ref, tap, 0), rows_of(ref, tap, 1)], axis=0)
            out_ref[:, 2 * width * tap : 2 * width * (tap + 1)] = both.T.astype(jnp.bfloat16)
    w_out_ref[...] = jnp.concatenate(
        [rows_of(last_ref, tap, parity) for tap in range(3) for parity in range(2)], axis=0
    ).astype(jnp.bfloat16)


def pack_kernel(own_ref, north_ref, south_ref, rows_ref, far_ref, near_ref):
    even = lax.rem(lax.axis_index("lon"), 2) == 0
    rows_ref[DEEP : DEEP + ROWS] = own_ref[...]
    for slab_ref, start in ((north_ref, 0), (south_ref, DEEP + ROWS)):
        rows = slice(start, start + DEEP)
        rows_ref[rows, CUT + 1 :, :] = jnp.zeros((DEEP, FIELDS - CUT - 1, COLS), jnp.float32)
        for field in range(CUT + 1):
            rows_ref[rows, field, :] = slab_ref[field]
    lane = lane_index((FIELDS, COLS))
    for part in range(TALL // SLOTS):
        first = jnp.zeros((FIELDS, COLS), jnp.float32)
        last = jnp.zeros((FIELDS, COLS), jnp.float32)
        for slot in range(SLOTS):
            here = rows_ref[part * SLOTS + slot]
            inside = (lane >= HALO * slot) & (lane < HALO * (slot + 1))
            first = jnp.where(inside, pltpu.roll(here, HALO * slot, 1) if slot else here, first)
            last = jnp.where(inside, pltpu.roll(here, HALO * (slot + 1), 1), last)
        far_ref[part] = jnp.where(even, first, last)
        near_ref[part] = jnp.where(even, last, first)


def closure_layers(window, pairs, stride, weights, acts, masks):
    w_in_ref, w_mid_ref, w_late_ref, w_out_ref = weights
    act_a, act_b = acts
    mask_odd, mask_even = masks

    def chunks(count):
        return range(-(-count * stride // COLS))

    def at(chunk, shift=0):
        return slice(COLS * chunk + shift, COLS * (chunk + 1) + shift)

    def both(act, chunk):
        return jnp.concatenate([act[at(chunk)], act[at(chunk, stride)]], axis=1)

    def finish(total, mask):
        v = (
            pltpu.roll(total[:, 0:128], 1, 0)
            + total[:, 128:256]
            + pltpu.roll(total[:, 256:384], COLS - 1, 0)
        )
        return (mask * (v / (1.0 + jnp.exp(-v)))).astype(jnp.bfloat16)

    for chunk in chunks(pairs):
        total = lax.dot_general(
            window(chunk),
            w_in_ref[...],
            (((0,), (0,)), ((), ())),
            preferred_element_type=jnp.float32,
        )
        mask_odd[at(chunk)] = total[:, 384:512]
        mask_even[at(chunk)] = total[:, 512:640]
        act_a[at(chunk)] = finish(total, total[:, 384:512])
    for chunk in chunks(pairs - 1):
        total = jnp.dot(both(act_a, chunk), w_mid_ref[...], preferred_element_type=jnp.float32)
        act_b[at(chunk)] = finish(total, mask_even[at(chunk)])
    for chunk in chunks(pairs - 2):
        total = jnp.dot(both(act_b, chunk), w_late_ref[...], preferred_element_type=jnp.float32)
        act_a[at(chunk)] = finish(total, mask_odd[at(chunk, stride)])
    results = []
    for chunk in chunks(pairs - 3):
        total = lax.dot_general(
            w_out_ref[...],
            both(act_a, chunk),
            (((1,), (1,)), ((), ())),
            preferred_element_type=jnp.float32,
        )
        results.append(
            pltpu.roll(total[0:16], 1, 1) + total[16:32] + pltpu.roll(total[32:48], COLS - 1, 1)
        )
    return results


def level_index():
    return lax.broadcasted_iota(jnp.int32, (LEV, COLS), 0).astype(jnp.float32)


def wetness(block):
    return (level_index() < block[KMT : KMT + 1]).astype(jnp.float32)


def first_input(block):
    wet = wetness(block)
    sea = jnp.where(level_index() == 0.0, wet, 0.0)
    return jnp.concatenate([wet * block[0:LEV], sea], axis=0).astype(jnp.bfloat16)


def advance(here, north, south, closure):
    wet = wetness(here)
    temp = here[0:LEV]
    tracer = wet * temp
    kappa = jnp.broadcast_to(here[KAPPA : KAPPA + 1], (LEV, COLS))
    diff = jnp.zeros((LEV, COLS), jnp.float32)
    for near in (south, north):
        near_w = wetness(near)
        diff = diff + near_w * 0.5 * (kappa + near[KAPPA : KAPPA + 1]) * (
            near_w * near[0:LEV] - tracer
        )
    for by in (COLS - 1, 1):
        diff = diff + pltpu.roll(wet, by, 1) * 0.5 * (kappa + pltpu.roll(kappa, by, 1)) * (
            pltpu.roll(tracer, by, 1) - tracer
        )
    diff = wet * diff
    eddy = wet * closure
    return wet * (temp + STEP * (diff + eddy))


FIRST = DEEP - HALO


def interior_kernel(
    rows_ref, w_in_ref, w_mid_ref, w_late_ref, w_out_ref, out_ref, line_ref,
    start, mask_odd, mask_even, act_a, act_b,
):
    for row in range(TALL):
        start[row * FIELDS : (row + 1) * FIELDS] = first_input(rows_ref[row])
    results = closure_layers(
        lambda chunk: start[2 * FIELDS * chunk : 2 * FIELDS * (chunk + 2)],
        TALL // 2 - 1,
        COLS,
        (w_in_ref, w_mid_ref, w_late_ref, w_out_ref),
        (act_a, act_b),
        (mask_odd, mask_even),
    )
    for pair, closure in enumerate(results):
        for parity in range(2):
            row = FIRST + 2 * pair + parity
            out_ref[2 * pair + parity] = advance(
                rows_ref[row],
                rows_ref[row - 1],
                rows_ref[row + 1],
                closure[LEV * parity : LEV * (parity + 1)],
            )
    own_line = lax.axis_index("lon") + FIRST
    line_ref[...] = rows_ref[own_line, LEV:FIELDS, :]


STRIP = 32
PER = COLS // STRIP


def edge_kernel(
    rows_ref, far_ref, near_ref, inside_ref, w_in_ref, w_mid_ref, w_late_ref, w_out_ref,
    out_ref, planes_ref, strips, mask_odd, mask_even, act_a, act_b,
):
    lane = lane_index((FIELDS, COLS))
    even = lax.rem(lax.axis_index("lon"), 2) == 0
    parts = range(TALL // SLOTS)
    from_west = [jnp.where(even, far_ref[part], near_ref[part]) for part in parts]
    from_east = [jnp.where(even, near_ref[part], far_ref[part]) for part in parts]
    for row in range(TALL):
        part, slot = row // SLOTS, row % SLOTS
        here = rows_ref[row]
        strip = jnp.where(lane < 24, pltpu.roll(from_east[part], (20 - HALO * slot) % COLS, 1) if slot != 5 else from_east[part], 0.0)
        strip = jnp.where(lane < 20, pltpu.roll(here, 20, 1), strip)
        strip = jnp.where(lane < 12, pltpu.roll(here, 4, 1), strip)
        west = pltpu.roll(from_west[part], COLS - HALO * slot, 1) if slot else from_west[part]
        strips[row] = jnp.where(lane < 4, west, strip)

    def side_by_side(parity, start):
        total = None
        for slot in range(PER):
            row = 2 * (start + slot) + parity
            if row >= TALL:
                continue
            piece = strips[row]
            piece = pltpu.roll(piece, STRIP * slot, 1) if slot else piece
            total = piece if total is None else total + piece
        return total

    def window(chunk):
        at = PER * chunk
        return jnp.concatenate(
            [
                first_input(block)
                for block in (
                    side_by_side(0, at),
                    side_by_side(1, at),
                    side_by_side(0, at + 1),
                    side_by_side(1, at + 1),
                )
            ],
            axis=0,
        )

    act_a[5 * COLS :] = jnp.zeros((COLS, COLS), jnp.bfloat16)
    act_b[5 * COLS :] = jnp.zeros((COLS, COLS), jnp.bfloat16)
    mask_odd[5 * COLS :] = jnp.zeros((COLS, COLS), jnp.float32)
    results = closure_layers(
        window,
        TALL // 2 - 1,
        STRIP,
        (w_in_ref, w_mid_ref, w_late_ref, w_out_ref),
        (act_a, act_b),
        (mask_odd, mask_even),
    )
    at_lane = lane_index((LEV, COLS))
    for chunk in range(4):
        at = PER * chunk + FIRST // 2
        closure = results[chunk]
        north = side_by_side(1, at - 1)
        upper = side_by_side(0, at)
        lower = side_by_side(1, at)
        south = side_by_side(0, at + 1)
        for parity, value in (
            (0, advance(upper, north, lower, closure[0:LEV])),
            (1, advance(lower, upper, south, closure[LEV : 2 * LEV])),
        ):
            for slot in range(PER):
                row = 2 * (PER * chunk + slot) + parity
                left = pltpu.roll(value, COLS - STRIP * slot - 4, 1)
                shift = (108 - STRIP * slot) % COLS
                right = pltpu.roll(value, shift, 1)
                out_ref[row] = jnp.where(
                    at_lane < HALO,
                    left,
                    jnp.where(at_lane >= COLS - HALO, right, inside_ref[row]),
                )
    plane_lane = lane_index((MID, COLS))
    for index, field in enumerate((KMT, HELM, FORCING)):
        moved = pltpu.roll(rows_ref[FIRST : FIRST + MID, field, :], HALO, 1)
        edge = strips[FIRST : FIRST + MID, field, :]
        planes_ref[index, :, 0:COLS] = jnp.where(plane_lane < HALO, edge, moved)
        planes_ref[index, :, COLS:] = jnp.where(
            plane_lane < HALO,
            moved,
            jnp.where(plane_lane < 2 * HALO, pltpu.roll(edge, COLS - 16, 1), 0.0),
        )


def filter_tables(blocks, width):
    length = blocks * width
    half = LEV // 2
    k = np.arange(blocks)
    outer = np.exp(-2j * np.pi * ((k[:, None] * k[None, :]) % blocks) / blocks)
    spread = np.zeros((blocks, 2, half, blocks, 2, half))
    for line in range(half):
        spread[:, 0, line, :, 0, line] = outer.real
        spread[:, 0, line, :, 1, line] = -outer.imag
        spread[:, 1, line, :, 0, line] = outer.imag
        spread[:, 1, line, :, 1, line] = outer.real
    spread = spread.reshape(blocks * LEV, blocks * LEV)
    m = np.arange(width)
    twist = np.exp(-2j * np.pi * (k[:, None] * m[None, :]) / length)
    sign = np.where(np.arange(LEV) < half, -1.0, 1.0)[None, :, None]
    twist_re = np.broadcast_to(twist.real[:, None, :], (blocks, LEV, width))
    twist_im = twist.imag[:, None, :] * sign
    inner = np.exp(-2j * np.pi * ((m[:, None] * m[None, :]) % width) / width)
    inner = np.concatenate([inner.real, inner.imag], axis=1)
    return [
        np.asarray(t, np.float32)
        for t in (spread, spread.T / length, inner, twist_re, twist_im)
    ]


def halves(x):
    high = x.astype(jnp.bfloat16)
    return high, (x - high.astype(jnp.float32)).astype(jnp.bfloat16)


def split_dot(a, b):
    def dot(x, y):
        return jnp.dot(x, y, preferred_element_type=jnp.float32)

    return dot(a[0], b[0]) + (dot(a[0], b[1]) + dot(a[1], b[0]))


def filter_kernel(
    x_ref, line_ref, spread_ref, spread_low, back_ref, back_low, inner_ref, inner_low,
    twist_re_ref, twist_im_ref, out_ref,
):
    blocks, lev, width = x_ref.shape
    shape = (blocks, lev, width)
    flat = (blocks * lev, width)
    length = blocks * width
    inner = (inner_ref[...], inner_low[...])

    def partner(block):
        return pltpu.roll(block, lev // 2, 1)

    sign = jnp.where(lax.broadcasted_iota(jnp.int32, shape, 1) < lev // 2, -1.0, 1.0)
    y = split_dot((spread_ref[...], spread_low[...]), halves(x_ref[...].reshape(flat)))
    y = y.reshape(shape)
    y = y * twist_re_ref[...] + partner(y) * twist_im_ref[...]
    s = split_dot(halves(y.reshape(flat)), inner)
    s = s[:, 0:width].reshape(shape) + partner(s[:, width:].reshape(shape)) * sign
    wave = lax.broadcasted_iota(jnp.int32, shape, 0) + blocks * lane_index(shape)
    folded = jnp.minimum(wave, length - wave).astype(jnp.float32)
    s = jnp.where(folded < line_ref[CUT - LEV : CUT - LEV + 1, :][None], s, 0.0)
    y = split_dot(halves(s.reshape(flat)), inner)
    y = y[:, 0:width].reshape(shape) - partner(y[:, width:].reshape(shape)) * sign
    y = y * twist_re_ref[...] - partner(y) * twist_im_ref[...]
    x = split_dot((back_ref[...], back_low[...]), halves(y.reshape(flat))).reshape(shape)
    lane = lane_index((lev, width))
    moved = [pltpu.roll(x[block], HALO, 1) for block in range(blocks)]
    for block in range(blocks):
        edge = jnp.where(lane < HALO, moved[block - 1], moved[(block + 1) % blocks])
        edge = jnp.where(lane < 2 * HALO, edge, 0.0)
        edge = pltpu.roll(edge, 0, 1, stride=2 * HALO, stride_axis=0)
        row = BLOCK * block
        out_ref[row : row + lev, :] = x[block]
        out_ref[row + lev : row + BLOCK, :] = jnp.sum(edge, axis=0, keepdims=True)


def two_sum(a, b):
    s = a + b
    t = s - a
    return s, (a - (s - t)) + (b - t)


def quick_sum(a, b):
    s = a + b
    return s, b - (s - a)


def split(a):
    c = a * 4097.0
    high = c - (c - a)
    return high, a - high


def two_product(a, b):
    p = a * b
    ah, al = split(a)
    bh, bl = split(b)
    return p, ((ah * bh - p) + ah * bl + al * bh) + al * bl


def pair_add(a, b):
    s, e = two_sum(a[0], b[0])
    return quick_sum(s, e + (a[1] + b[1]))


def pair_neg(a):
    return -a[0], -a[1]


def pair_mul(a, b):
    p, e = two_product(a[0], b[0])
    return quick_sum(p, e + (a[0] * b[1] + a[1] * b[0]))


def pair_div(a, b):
    q = a[0] / b[0]
    rest = pair_add(a, pair_neg(pair_mul((q, jnp.zeros_like(q)), b)))
    r = rest[0] / b[0]
    rest = pair_add(rest, pair_neg(pair_mul((r, jnp.zeros_like(r)), b)))
    return quick_sum(*quick_sum(q, r + rest[0] / b[0]))


def powers_kernel(x_ref, planes_ref, temp_ref, powers_ref, parts_ref):
    lane = lane_index((LEV, COLS))
    wide_lane = lane_index((MID, COLS))
    kmt_left = planes_ref[0, :, 0:COLS]
    kmt_right = planes_ref[0, :, COLS:]
    kmt = pltpu.roll(jnp.where(wide_lane < HALO, kmt_right, kmt_left), COLS - HALO, 1)
    mean = jnp.zeros((MID, COLS), jnp.float32)
    for level in range(LEV):
        temp_ref[level] = x_ref[pl.ds(HALO * BLOCK + level, ROWS, stride=BLOCK), :]
        here = x_ref[pl.ds(level, MID, stride=BLOCK), :]
        mean = mean + jnp.where(kmt > level, here, 0.0)
    edge = x_ref[pl.ds(LEV, MID, stride=BLOCK), :]
    edge_kmt = jnp.where(wide_lane < HALO, kmt_left, kmt_right)
    edge_kmt = jnp.where(wide_lane < 2 * HALO, edge_kmt, 0.0)
    for by in (8, 16, 32, 64):
        edge_kmt = edge_kmt + pltpu.roll(edge_kmt, by, 1)
    edge = jnp.where(edge_kmt > (wide_lane // (2 * HALO)).astype(jnp.float32), edge, 0.0)
    for by in (64, 32, 16, 8):
        edge = edge + pltpu.roll(edge, by, 1)
    moved = pltpu.roll(mean, HALO, 1)
    mean = jnp.concatenate(
        [
            jnp.where(wide_lane < HALO, edge, moved),
            jnp.where(wide_lane < HALO, moved, jnp.where(wide_lane < 2 * HALO, edge, 0.0)),
        ],
        axis=1,
    )
    sea = (planes_ref[0] > 0.0).astype(jnp.float32)

    def around(v):
        return (
            pltpu.roll(v, 1, 0)
            + pltpu.roll(v, MID - 1, 0)
            + pltpu.roll(v, 1, 1)
            + pltpu.roll(v, 2 * COLS - 1, 1)
        )

    diagonal = planes_ref[1] + sea * around(sea)
    powers = [sea * (mean * (1.0 / LEV) + planes_ref[2])]
    for _ in range(ITERS):
        v = powers[-1]
        powers.append((diagonal * v - sea * around(v)) * 0.125)
    for index, v in enumerate(powers):
        powers_ref[index] = v
    row = lax.broadcasted_iota(jnp.int32, (MID, 2 * COLS), 0)
    column = lane_index((MID, 2 * COLS))
    own = (
        (row >= HALO) & (row < HALO + ROWS) & (column >= HALO) & (column < HALO + COLS)
    )
    owned = [jnp.where(own, v, 0.0) for v in powers]
    high_rows, low_rows = [], []
    for order in range(2 * ITERS):
        p, e = two_product(owned[order // 2], owned[order - order // 2])
        tiles = [
            (p[8 * i : 8 * i + 8, 128 * j : 128 * j + 128], e[8 * i : 8 * i + 8, 128 * j : 128 * j + 128])
            for i in range(MID // 8)
            for j in range(2)
        ]
        while len(tiles) > 1:
            tiles = [pair_add(a, b) for a, b in zip(tiles[::2], tiles[1::2])]
        total = tiles[0]
        for by in (4, 2, 1):
            total = pair_add(total, tuple(pltpu.roll(t, by, 0) for t in total))
        high_rows.append(total[0])
        low_rows.append(total[1])
    where = lax.broadcasted_iota(jnp.int32, (8, COLS), 0)
    high, low = high_rows[0], low_rows[0]
    for order in range(1, 2 * ITERS):
        high = jnp.where(where == order, high_rows[order], high)
        low = jnp.where(where == order, low_rows[order], low)
    total = (high, low)
    for by in (64, 32, 16, 8, 4, 2, 1):
        total = pair_add(total, tuple(pltpu.roll(t, by, 1) for t in total))
    spot = lax.broadcasted_iota(jnp.int32, (8, COLS), 0)
    message = jnp.where(lane == spot, total[0], 0.0) + jnp.where(lane == spot + 64, total[1], 0.0)
    message = jnp.sum(message, axis=0, keepdims=True)
    parts_ref[...] = jnp.broadcast_to(message, parts_ref.shape)


def sum_messages(parts_ref):
    count = parts_ref.shape[0] // 8
    if count == 1:
        total = (parts_ref[...], jnp.zeros((8, COLS), jnp.float32))
        for by in (4, 2, 1):
            total = pair_add(total, tuple(pltpu.roll(t, by, 0) for t in total))
        return pair_add(total, tuple(pltpu.roll(t, 64, 1) for t in total))
    tiles = [(parts_ref[8 * i : 8 * i + 8, :], None) for i in range(count)]
    merged = []
    for a, b in zip(tiles[::2], tiles[1::2]):
        merged.append(two_sum(a[0], b[0]))
    tiles = merged
    while len(tiles) > 1:
        tiles = [pair_add(a, b) for a, b in zip(tiles[::2], tiles[1::2])]
    total = tiles[0]
    for by in (4, 2, 1):
        total = pair_add(total, tuple(pltpu.roll(t, by, 0) for t in total))
    return pair_add(total, tuple(pltpu.roll(t, 64, 1) for t in total))


def merge_kernel(parts_ref, out_ref):
    total = sum_messages(parts_ref)
    lane = lane_index((8, COLS))
    out_ref[...] = jnp.where(lane < 64, total[0], total[1])


def combine_kernel(parts_ref, powers_ref, surface_ref, residual_ref, wide):
    total = sum_messages(parts_ref)
    moments = [
        tuple(jnp.broadcast_to(t[:, order : order + 1], (8, COLS)) for t in total)
        for order in range(2 * ITERS)
    ]
    rho = list(moments)
    delta = list(moments)
    one = jnp.ones((8, COLS), jnp.float32)
    zero = jnp.zeros((8, COLS), jnp.float32)
    res = [one] + [zero] * ITERS
    way = [one] + [zero] * ITERS
    sol = [zero] * ITERS
    for step in range(ITERS):
        alpha = pair_div(rho[step], delta[step + 1])
        sol = [s + alpha[0] * w for s, w in zip(sol, way)]
        res = [res[0]] + [r - alpha[0] * w for r, w in zip(res[1:], way)]
        if step == ITERS - 1:
            break
        before = rho[step]
        last = 2 * ITERS - 1 - step
        rho = [
            None if order <= step or order >= last
            else pair_add(rho[order], pair_neg(pair_mul(alpha, delta[order + 1])))
            for order in range(2 * ITERS)
        ]
        beta = pair_neg(pair_mul(alpha, pair_div(rho[step + 1], before)))
        delta = [
            None if order <= step or order >= last
            else pair_add(rho[order], pair_mul(beta, delta[order]))
            for order in range(2 * ITERS)
        ]
        way = [r + beta[0] * w for r, w in zip(res, way)]
    for weights, target, factor in ((sol, surface_ref, 0.125), (res, residual_ref, 1.0)):
        for i in range(MID // 8):
            for j in range(2):
                spot = (slice(8 * i, 8 * i + 8), slice(128 * j, 128 * j + 128))
                value = weights[0] * powers_ref[(0,) + spot]
                for index in range(1, len(weights)):
                    value = value + weights[index] * powers_ref[(index,) + spot]
                wide[spot] = value * factor
        target[...] = wide[HALO : HALO + ROWS, HALO : HALO + COLS]


def forward(axis, periodic):
    count = lax.axis_size(axis)
    pairs = [(i, i + 1) for i in range(count - 1)]
    return pairs + [(count - 1, 0)] if periodic else pairs


def backward(axis, periodic):
    return [(target, source) for source, target in forward(axis, periodic)]


def swap_near():
    return [(i, i ^ 1) for i in range(lax.axis_size("lon"))]


def swap_far():
    count = lax.axis_size("lon")
    return [(i, (i + 1) % count if i % 2 else (i - 1) % count) for i in range(count)]


def body(temp, kmt, kappa, helm, forcing, cutoff, conv_in, conv_mid, conv_late, conv_out):
    f32 = jnp.float32
    shape = jax.ShapeDtypeStruct
    blocks = lax.axis_size("lon")
    bf16 = jnp.bfloat16
    vmem = pl.BlockSpec(memory_space=pltpu.VMEM)
    cutoff = cutoff.reshape(1, ROWS)
    fields = (temp, kmt, kappa, helm, forcing, cutoff)
    slab = shape((CUT + 1, DEEP, COLS), f32)
    top, bottom = pl.pallas_call(
        slab_kernel,
        out_shape=(slab, slab),
        in_specs=[pl.BlockSpec(memory_space=pltpu.HBM)] * 6,
        out_specs=(vmem, vmem),
        scratch_shapes=(
            pltpu.VMEM((ROWS, COLS), jnp.int32),
            pltpu.VMEM((1, ROWS), jnp.int32),
            pltpu.SemaphoreType.DMA((10,)),
        ),
        compiler_params=pltpu.CompilerParams(vmem_limit_bytes=VMEM_LIMIT),
    )(*(pltpu.with_memory_space_constraint(field, pltpu.HBM) for field in fields))
    north = lax.ppermute(bottom, "lat", forward("lat", False))
    south = lax.ppermute(top, "lat", backward("lat", False))
    own = call(rows_kernel, shape((ROWS, FIELDS, COLS), f32), (), 10**6)(*fields)
    tables = [jnp.asarray(table) for table in filter_tables(blocks, COLS)]
    weights = call(
        weights_kernel,
        (
            shape((4 * FIELDS, 640), bf16),
            shape((256, 384), bf16),
            shape((256, 384), bf16),
            shape((48, 256), bf16),
        )
        + tuple(shape(table.shape, bf16) for table in tables[:3] for _ in range(2)),
        (),
        10**6,
    )(jnp.transpose(conv_in, (0, 2, 1)), conv_mid, conv_late, conv_out, *tables[:3])
    weights, splits = weights[:4], weights[4:]
    ends = shape((TALL // SLOTS, FIELDS, COLS), f32)
    rows, to_far, to_near = call(
        pack_kernel, (shape((TALL, FIELDS, COLS), f32), ends, ends)
    )(own, north, south)
    far = lax.ppermute(to_far, "lon", swap_far())
    near = lax.ppermute(to_near, "lon", swap_near())

    def closure_scratch(chunks):
        cells = chunks * COLS
        return (
            pltpu.VMEM((cells, 128), f32),
            pltpu.VMEM((cells, 128), f32),
            pltpu.VMEM((cells, 128), bf16),
            pltpu.VMEM((cells, 128), bf16),
        )

    block = shape((MID, LEV, COLS), f32)
    inside, line = call(
        interior_kernel,
        (block, shape((LEV, COLS), f32)),
        (pltpu.VMEM((TALL * FIELDS, COLS), bf16),) + closure_scratch(19),
        10**9,
    )(rows, *weights)
    lines, planes = call(
        edge_kernel,
        (block, shape((3, MID, 2 * COLS), f32)),
        (pltpu.VMEM((TALL, FIELDS, COLS), f32),) + closure_scratch(6),
    )(rows, far, near, inside, *weights)
    whole = lax.all_to_all(lines, "lon", split_axis=0, concat_axis=0, tiled=True)
    filtered = call(filter_kernel, shape((BLOCK * blocks, COLS), f32))(
        whole, line, *splits, *tables[3:]
    )
    back = lax.all_to_all(
        filtered.reshape(BLOCK * blocks, 1, COLS), "lon", split_axis=0, concat_axis=0, tiled=True
    ).reshape(BLOCK * blocks, COLS)
    everyone = blocks * lax.axis_size("lat")
    wide = everyone // 8
    both = ("lon", "lat")
    inner = [[wide * i + k for k in range(wide)] for i in range(8)]
    outer = [[wide * i + k for i in range(8)] for k in range(wide)]
    temp_new, powers, parts = call(
        powers_kernel,
        (
            shape((LEV, ROWS, COLS), f32),
            shape((ITERS + 1, MID, 2 * COLS), f32),
            shape((wide, COLS), f32),
        ),
    )(back, planes)
    parts = lax.all_to_all(
        parts, both, split_axis=0, concat_axis=0, tiled=True, axis_index_groups=inner
    )
    parts = call(merge_kernel, shape((8, COLS), f32))(parts)
    parts = lax.all_to_all(
        parts, both, split_axis=0, concat_axis=0, tiled=True, axis_index_groups=outer
    )
    surface, residual = call(
        combine_kernel,
        (shape((ROWS, COLS), f32), shape((ROWS, COLS), f32)),
        (pltpu.VMEM((MID, 2 * COLS), f32),),
    )(parts, powers)
    return temp_new, surface, residual


def solution(mesh):
    return jax.shard_map(
        body,
        mesh=mesh,
        in_specs=(
            P(None, "lat", "lon"),
            P("lat", "lon"),
            P("lat", "lon"),
            P("lat", "lon"),
            P("lat", "lon"),
            P("lat"),
            P(),
            P(),
            P(),
            P(),
        ),
        out_specs=(P(None, "lat", "lon"), P("lat", "lon"), P("lat", "lon")),
        check_vma=False,
    )
```

time: 110 us -> 107 us (0.973)
  local copies, waits for them, and re-layouts: 0.97 us -> 7.72 us
  waiting for transfers between devices: 6.05 us -> 0.01 us
  blocking collectives: 69.3 us -> 65.3 us
    unnamed x22 -> x30, local copies, waits for them, and re-layouts: 0.97 us -> 7.72 us
    ppermute x1, waiting for transfers between devices: 5.25 us -> 0.01 us  [body(): south = lax.ppermute(top, 'lat', backward('lat', False))]
    all_to_all x1, blocking collectives: 18.6 us -> 16.7 us  [body(): lax.all_to_all(filtered.reshape(BLOCK * blocks, 1, COLS), 'lon', split_ax...]
    all_to_all x1, blocking collectives: 22.1 us -> 20.3 us  [body(): lax.all_to_all(lines, 'lon', split_axis=0, concat_axis=0, tiled=True)]
    pallas_call x4 -> x6, Pallas kernels: 7.73 us -> 7.22 us  [the longest x1 2.65 us: body(): call(interior_kernel, (block, shape((LEV, COLS), f32)), (pltpu.VMEM((TALL...]
  transfers between devices with their start and end apart: 4 -> 4, of which waited for: 3 -> 0; matrix products, arithmetic and copies ran while one was open for 0% -> 0% of each run, Pallas kernels for 0% -> 3%
where the time goes in v3:
time: 107 us; the launch traced here: 106 us
  blocking collectives  65.3 us (61%)
  starting transfers between devices  21.2 us (20%)
  Pallas kernels  11 us (10%)
  local copies, waits for them, and re-layouts  7.72 us (7%)
    all_to_all x2, blocking collectives, body(): lax.all_to_all(parts, both, split_axis=0, concat_axis=0, tiled=True, axis...  28.3 us
    all_to_all x1, blocking collectives, body(): lax.all_to_all(lines, 'lon', split_axis=0, concat_axis=0, tiled=True)  20.3 us
    all_to_all x1, blocking collectives, body(): lax.all_to_all(filtered.reshape(BLOCK * blocks, 1, COLS), 'lon', split_ax...  16.7 us
    ppermute x1, starting transfers between devices, body(): far = lax.ppermute(to_far, 'lon', swap_far())  10.6 us
    unnamed x30, local copies, waits for them, and re-layouts  7.72 us
    ppermute x1, starting transfers between devices, body(): north = lax.ppermute(bottom, 'lat', forward('lat', False))  4.83 us
    ppermute x1, starting transfers between devices, body(): near = lax.ppermute(to_near, 'lon', swap_near())  4.37 us
    pallas_call x1, Pallas kernels, body(): call(interior_kernel, (block, shape((LEV, COLS), f32)), (pltpu.VMEM((TALL...  2.65 us
  transfers between devices with their start and end apart: 4, of which 0 were waited for; matrix products, arithmetic and copies ran while one was open for 0% of the time, Pallas kernels for 3%

profile of v3, /device:TPU:1, one launch (start us, length us, event | category | flops | bytes accessed | tf_op | source)
XLA Modules:
  0.0 106.0 jit_solution(2067050408320208845)
XLA Ops:
  0.6 0.0 copy-start.1
  0.7 1.1 %shard_map.167 = (f32[13,8,128]{2,1,0:T(8,128)S(1)}, f32[13,8,128]{2,1,0:T(8,128)S(1)}) custom-call(f32[8,24,128]{2,1,0:T(8,128)} %temp_hbm.1, s32[24,128]{1,0:T(8,128)} %kmt_hbm.1, f32[24,128]{1,0:T(8,128)} %kappa_hbm.1, f32[24,128]{1,0:T(8,128)} %helm_hbm.1, f32[24,128]{1,0:T(8,128)} %forcing_hbm.1, s32[1,24]{1,0:T(1,128)} %bitcast.21), custom_call_target="tpu_custom_call" | custom-call | tf_op jit(solution)/shard_map/pallas_call | solution.py:665
  1.7 4.8 %collective-permute-start = (f32[13,8,128]{2,1,0:T(8,128)S(1)}, f32[13,8,128]{2,1,0:T(8,128)S(1)}, u32[]{:S(2)}, u32[]{:S(2)}) collective-permute-start(f32[13,8,128]{2,1,0:T(8,128)S(1)} %get-tuple-element.27), channel_id=1, source_target_pairs={{0,1},{1,2},{2,3},{3,4},{4,5},{5,6},{6,7},{7,8},{8,9},{9,10},{10,1... | collective-permute-start | bytes 159752 | tf_op jit(solution)/shard_map/ppermute | solution.py:677
  6.6 0.0 copy-start.7
  6.6 1.4 %collective-permute-start.1 = (f32[13,8,128]{2,1,0:T(8,128)S(1)}, f32[13,8,128]{2,1,0:T(8,128)S(1)}, u32[]{:S(2)}, u32[]{:S(2)}) collective-permute-start(f32[13,8,128]{2,1,0:T(8,128)S(1)} %get-tuple-element.28), channel_id=1, source_target_pairs={{1,0},{2,1},{3,2},{4,3},{5,4},{6,5},{7,6},{8,7},{9,8},{10,9},{11,1... | collective-permute-start | bytes 159752 | tf_op jit(solution)/shard_map/ppermute | solution.py:678
  8.0 0.7 copy-done.8
  8.7 0.7 copy-done.9
  9.4 0.7 copy-done.10
  10.2 0.7 copy-done.11
  10.9 0.7 copy-done.14
  11.5 0.1 shard_map.166.own_ref
  11.6 0.0 copy-start.2
  11.7 0.9 copy-done.2
  12.6 0.9 copy-done.3
  13.5 0.9 copy-done.4
  14.4 0.7 copy-done.12
  15.1 0.7 copy-done.13
  15.9 0.4 shard_map.169
  16.3 0.3 shard_map.168
  16.6 10.6 %collective-permute-start.2 = (f32[2,16,128]{2,1,0:T(8,128)S(1)}, f32[2,16,128]{2,1,0:T(8,128)S(1)}, u32[]{:S(2)}, u32[]{:S(2)}) collective-permute-start(f32[2,16,128]{2,1,0:T(8,128)S(1)} %get-tuple-element.30), channel_id=1, source_target_pairs={{0,496},{16,32},{32,16},{48,64},{64,48},{80,96},{96,80},{112,128},... | collective-permute-start | bytes 49160 | tf_op jit(solution)/shard_map/ppermute | solution.py:698
  27.1 4.4 %collective-permute-start.3 = (f32[2,16,128]{2,1,0:T(8,128)S(1)}, f32[2,16,128]{2,1,0:T(8,128)S(1)}, u32[]{:S(2)}, u32[]{:S(2)}) collective-permute-start(f32[2,16,128]{2,1,0:T(8,128)S(1)} %get-tuple-element.31), channel_id=1, source_target_pairs={{0,16},{16,0},{32,48},{48,32},{64,80},{80,64},{96,112},{112,96},{1... | collective-permute-start | bytes 49160 | tf_op jit(solution)/shard_map/ppermute | solution.py:699
  31.5 2.7 %shard_map.170 = (f32[32,8,128]{2,1,0:T(8,128)S(1)}, f32[8,128]{1,0:T(8,128)S(1)}) custom-call(f32[40,16,128]{2,1,0:T(8,128)S(1)} %get-tuple-element.29.rows_ref, bf16[64,640]{1,0:T(8,128)(2,1)S(1)} %get-tuple-element.32.w_in_ref, bf16[256,384]{1,0:T(8,128)(2,1)S(1)} %get-tuple-element.33.w_mid_ref, bf16[256,384]{1,0:T(8,128)(2,1)S(1)} %get-tuple-element.34.w_late_ref, ...), custom_call_target="tpu_custom_call" | custom-call | flops 1000000000 | bytes 1000000 | tf_op jit(solution)/shard_map/pallas_call | solution.py:711
  34.2 1.9 %shard_map.171 = (f32[32,8,128]{2,1,0:T(8,128)S(1)}, f32[3,32,256]{2,1,0:T(8,128)S(1)}) custom-call(f32[40,16,128]{2,1,0:T(8,128)S(1)} %get-tuple-element.29.rows_ref, f32[2,16,128]{2,1,0:T(8,128)S(1)} %collective-permute-done.2.far_ref, f32[2,16,128]{2,1,0:T(8,128)S(1)} %collective-permute-done.3.near_ref, f32[32,8,128]{2,1,0:T(8,128)S(1)} %get-tuple-element.36.inside_ref, ...), custom_call_target="tpu_custom_call" | custom-call | tf_op jit(solution)/shard_map/pallas_call | solution.py:717
  36.1 0.0 copy-start.5
  36.1 20.3 %all_to_all.32.x_ref = f32[32,8,128]{2,1,0:T(8,128)S(1)} all-to-all(f32[32,8,128]{2,1,0:T(8,128)S(1)} %get-tuple-element.37), channel_id=1, replica_groups=mesh['lon'=32,'lat'=16] {'lon'}, dimensions={0} | all-to-all | bytes 262144 | tf_op jit(solution)/shard_map/all_to_all | solution.py:722
  56.4 1.2 %shard_map.172 = f32[288,128]{1,0:T(8,128)S(1)} custom-call(f32[32,8,128]{2,1,0:T(8,128)S(1)} %all_to_all.32.x_ref, f32[8,128]{1,0:T(8,128)S(1)} %get-tuple-element.38.line_ref, bf16[256,256]{1,0:T(8,128)(2,1)S(1)} %get-tuple-element.39.spread_ref, bf16[256,256]{1,0:T(8,128)(2,1)S(1)} %get-tuple-element.40.spread_low, ...), custom_call_target="tpu_custom_call" | custom-call | tf_op jit(solution)/shard_map/pallas_call | solution.py:723
  57.6 16.7 %all_to_all.33 = f32[288,1,128]{2,1,0:T(1,128)S(1)} all-to-all(f32[288,1,128]{2,1,0:T(1,128)S(1)} %bitcast.14), channel_id=1, replica_groups=mesh['lon'=32,'lat'=16] {'lon'}, dimensions={0} | all-to-all | bytes 294912 | tf_op jit(solution)/shard_map/all_to_all | solution.py:726
  74.3 1.9 %shard_map.173 = (f32[8,24,128]{2,1,0:T(8,128)}, f32[5,32,256]{2,1,0:T(8,128)S(1)}, f32[64,128]{1,0:T(8,128)S(1)}) custom-call(f32[288,128]{1,0:T(8,128)S(1)} %bitcast.15, f32[3,32,256]{2,1,0:T(8,128)S(1)} %get-tuple-element.45.planes_ref), custom_call_target="tpu_custom_call" | custom-call | tf_op jit(solution)/shard_map/pallas_call | solution.py:734
  76.2 19.4 %all_to_all.34 = f32[64,1,128]{2,1,0:T(1,128)S(1)} all-to-all(f32[64,1,128]{2,1,0:T(1,128)S(1)} %bitcast.17), channel_id=1, replica_groups={{0,1,2,3,4,5,6,7,8,9,10,11,12,13,14,15,16,17,18,19,20,21,22,23,24,25,26..., dimensions={0} | all-to-all | bytes 65536 | tf_op jit(solution)/shard_map/all_to_all | solution.py:742
  95.6 0.1 shard_map.174
  95.8 8.9 %all_to_all.35 = f32[8,1,128]{2,1,0:T(1,128)S(1)} all-to-all(f32[8,1,128]{2,1,0:T(1,128)S(1)} %bitcast.19), channel_id=1, replica_groups={{0,64,128,192,256,320,384,448},{1,65,129,193,257,321,385,449},{2,66,130..., dimensions={0} | all-to-all | bytes 8192 | tf_op jit(solution)/shard_map/all_to_all | solution.py:746
  104.7 1.4 %shard_map.175 = (f32[24,128]{1,0:T(8,128)}, f32[24,128]{1,0:T(8,128)}) custom-call(f32[8,128]{1,0:T(8,128)S(1)} %bitcast.20, f32[5,32,256]{2,1,0:T(8,128)S(1)} %get-tuple-element.48.powers_ref), custom_call_target="tpu_custom_call" | custom-call | tf_op jit(solution)/shard_map/pallas_call | solution.py:749
  (20 shorter events, 0.0 us)
Async XLA Ops:
  0.6 7.4 %copy-start = (f32[8,24,128]{2,1,0:T(8,128)S(1)}, f32[8,24,128]{2,1,0:T(8,128)}, u32[]{:S(2)}) copy-start(f32[8,24,128]{2,1,0:T(8,128)} %temp_hbm.1) | copy-start | bytes 294916
  0.6 11.0 %copy-start.1 = (f32[256,256]{1,0:T(8,128)S(1)}, f32[256,256]{1,0:T(8,128)}, u32[]{:S(2)}) copy-start(f32[256,256]{1,0:T(8,128)} %constant.11.clone.refs_1_) | copy-start | bytes 786436
  1.7 14.5 %collective-permute-start = (f32[13,8,128]{2,1,0:T(8,128)S(1)}, f32[13,8,128]{2,1,0:T(8,128)S(1)}, u32[]{:S(2)}, u32[]{:S(2)}) collective-permute-start(f32[13,8,128]{2,1,0:T(8,128)S(1)} %get-tuple-element.27), channel_id=1, source_target_pairs={{0,1},{1,2},{2,3},{3,4},{4,5},{5,6},{6,7},{7,8},{8,9},{9,10},{10,1... | collective-permute-start | bytes 159752 | tf_op jit(solution)/shard_map/ppermute | solution.py:677
  6.6 5.1 %copy-start.7 = (f32[128,256]{1,0:T(8,128)S(1)}, f32[128,256]{1,0:T(8,128)}, u32[]{:S(2)}) copy-start(f32[128,256]{1,0:T(8,128)} %constant.12.clone.refs_2_) | copy-start | bytes 393220
  6.6 9.7 %collective-permute-start.1 = (f32[13,8,128]{2,1,0:T(8,128)S(1)}, f32[13,8,128]{2,1,0:T(8,128)S(1)}, u32[]{:S(2)}, u32[]{:S(2)}) collective-permute-start(f32[13,8,128]{2,1,0:T(8,128)S(1)} %get-tuple-element.28), channel_id=1, source_target_pairs={{1,0},{2,1},{3,2},{4,3},{5,4},{6,5},{7,6},{8,7},{9,8},{10,9},{11,1... | collective-permute-start | bytes 159752 | tf_op jit(solution)/shard_map/ppermute | solution.py:678
  8.0 0.7 copy-start.8
  8.7 0.7 copy-start.9
  9.4 0.7 copy-start.10
  10.2 0.7 copy-start.11
  10.9 0.7 copy-start.14
  11.6 1.0 copy-start.2
  12.6 0.9 copy-start.3
  13.5 0.9 copy-start.4
  14.4 0.7 copy-start.12
  15.1 0.7 copy-start.13
  16.6 17.6 %collective-permute-start.2 = (f32[2,16,128]{2,1,0:T(8,128)S(1)}, f32[2,16,128]{2,1,0:T(8,128)S(1)}, u32[]{:S(2)}, u32[]{:S(2)}) collective-permute-start(f32[2,16,128]{2,1,0:T(8,128)S(1)} %get-tuple-element.30), channel_id=1, source_target_pairs={{0,496},{16,32},{32,16},{48,64},{64,48},{80,96},{96,80},{112,128},... | collective-permute-start | bytes 49160 | tf_op jit(solution)/shard_map/ppermute | solution.py:698
  27.1 7.0 %collective-permute-start.3 = (f32[2,16,128]{2,1,0:T(8,128)S(1)}, f32[2,16,128]{2,1,0:T(8,128)S(1)}, u32[]{:S(2)}, u32[]{:S(2)}) collective-permute-start(f32[2,16,128]{2,1,0:T(8,128)S(1)} %get-tuple-element.31), channel_id=1, source_target_pairs={{0,16},{16,0},{32,48},{48,32},{64,80},{80,64},{96,112},{112,96},{1... | collective-permute-start | bytes 49160 | tf_op jit(solution)/shard_map/ppermute | solution.py:699
  36.1 20.3 %copy-start.5 = (f32[32,8,128]{2,1,0:T(8,128)S(1)}, f32[32,8,128]{2,1,0:T(8,128)}, u32[]{:S(2)}) copy-start(f32[32,8,128]{2,1,0:T(8,128)} %constant.14.clone.twist_im_ref) | copy-start | bytes 393220
  36.1 20.3 %copy-start.6 = (f32[32,8,128]{2,1,0:T(8,128)S(1)}, f32[32,8,128]{2,1,0:T(8,128)}, u32[]{:S(2)}) copy-start(f32[32,8,128]{2,1,0:T(8,128)} %constant.13.clone.twist_re_ref) | copy-start | bytes 393220

commit v4 on v3

--- a/solution.py
+++ b/solution.py
@@ -72,7 +72,25 @@
     return jnp.broadcast_to(kept, (ROWS, COLS))
 
 
-def rows_kernel(temp_ref, kmt_ref, kappa_ref, helm_ref, forcing_ref, cutoff_ref, own_ref):
+def prepare_kernel(*refs):
+    sources, refs = refs[:13], refs[13:]
+    outs, refs = refs[:11], refs[11:]
+    held, sems = refs[:13], refs[13]
+    moves = [
+        pltpu.make_async_copy(source, target, sems.at[index])
+        for index, (source, target) in enumerate(zip(sources, held))
+    ]
+    for move in moves:
+        move.start()
+    for move in moves:
+        move.wait()
+    fill_rows(*held[:6], outs[0])
+    fill_weights(*held[6:10], *outs[1:5])
+    for index, table in enumerate(held[10:]):
+        outs[5 + 2 * index][...], outs[6 + 2 * index][...] = halves(table[...])
+
+
+def fill_rows(temp_ref, kmt_ref, kappa_ref, helm_ref, forcing_ref, cutoff_ref, own_ref):
     own_ref[:, CUT + 1 :, :] = jnp.zeros((ROWS, FIELDS - CUT - 1, COLS), jnp.float32)
     for level in range(LEV):
         own_ref[:, level, :] = temp_ref[level]
@@ -83,13 +101,9 @@
     own_ref[:, CUT, :] = cutoff_rows(cutoff_ref)
 
 
-def weights_kernel(
-    first_ref, mid_ref, late_ref, last_ref, *refs
+def fill_weights(
+    first_ref, mid_ref, late_ref, last_ref, w_in_ref, w_mid_ref, w_late_ref, w_out_ref
 ):
-    tables, outs = refs[:3], refs[3:]
-    w_in_ref, w_mid_ref, w_late_ref, w_out_ref = outs[:4]
-    for index, table_ref in enumerate(tables):
-        outs[4 + 2 * index][...], outs[5 + 2 * index][...] = halves(table_ref[...])
     w_in_ref[...] = jnp.zeros(w_in_ref.shape, w_in_ref.dtype)
     width = mid_ref.shape[1]
     none = jnp.zeros((LEV, width), jnp.float32)
@@ -676,21 +690,27 @@
     )(*(pltpu.with_memory_space_constraint(field, pltpu.HBM) for field in fields))
     north = lax.ppermute(bottom, "lat", forward("lat", False))
     south = lax.ppermute(top, "lat", backward("lat", False))
-    own = call(rows_kernel, shape((ROWS, FIELDS, COLS), f32), (), 10**6)(*fields)
     tables = [jnp.asarray(table) for table in filter_tables(blocks, COLS)]
-    weights = call(
-        weights_kernel,
-        (
-            shape((4 * FIELDS, 640), bf16),
-            shape((256, 384), bf16),
-            shape((256, 384), bf16),
-            shape((48, 256), bf16),
-        )
-        + tuple(shape(table.shape, bf16) for table in tables[:3] for _ in range(2)),
-        (),
-        10**6,
-    )(jnp.transpose(conv_in, (0, 2, 1)), conv_mid, conv_late, conv_out, *tables[:3])
-    weights, splits = weights[:4], weights[4:]
+    sources = fields + (jnp.transpose(conv_in, (0, 2, 1)), conv_mid, conv_late, conv_out)
+    sources = sources + tuple(tables[:3])
+    outs = (
+        shape((ROWS, FIELDS, COLS), f32),
+        shape((4 * FIELDS, 640), bf16),
+        shape((256, 384), bf16),
+        shape((256, 384), bf16),
+        shape((48, 256), bf16),
+    ) + tuple(shape(table.shape, bf16) for table in tables[:3] for _ in range(2))
+    own, *prepared = pl.pallas_call(
+        prepare_kernel,
+        out_shape=outs,
+        in_specs=[pl.BlockSpec(memory_space=pltpu.HBM)] * len(sources),
+        out_specs=(vmem,) * len(outs),
+        scratch_shapes=tuple(pltpu.VMEM(source.shape, source.dtype) for source in sources)
+        + (pltpu.SemaphoreType.DMA((len(sources),)),),
+        compiler_params=pltpu.CompilerParams(vmem_limit_bytes=VMEM_LIMIT),
+        cost_estimate=pl.CostEstimate(flops=10**6, bytes_accessed=2 * 10**6, transcendentals=0),
+    )(*(pltpu.with_memory_space_constraint(source, pltpu.HBM) for source in sources))
+    weights, splits = prepared[:4], prepared[4:]
     ends = shape((TALL // SLOTS, FIELDS, COLS), f32)
     rows, to_far, to_near = call(
         pack_kernel, (shape((TALL, FIELDS, COLS), f32), ends, ends)

time: 107 us -> 103 us (0.963)
  local copies, waits for them, and re-layouts: 7.72 us -> 0.01 us
  waiting for transfers between devices: 0.01 us -> 2.95 us
  Pallas kernels: 11 us -> 12.6 us
  starting transfers between devices: 21.2 us -> 19.9 us
    unnamed x30 -> x4, local copies, waits for them, and re-layouts: 7.72 us -> 0.01 us
    ppermute x1, waiting for transfers between devices: 0.01 us -> 2.94 us  [body(): south = lax.ppermute(top, 'lat', backward('lat', False))]
    pallas_call x2 -> x1, Pallas kernels: 0.49 us -> 2.01 us  [body(): pl.pallas_call(prepare_kernel, out_shape=outs, in_specs=[pl.BlockSpec(mem...]
  transfers between devices with their start and end apart: 4 -> 4, of which waited for: 0 -> 1; matrix products, arithmetic and copies ran while one was open for 0% -> 0% of each run, Pallas kernels for 3% -> 5%
where the time goes in v4:
time: 103 us; the launch traced here: 102 us
  blocking collectives  66.2 us (64%)
  starting transfers between devices  19.9 us (19%)
  Pallas kernels  12.6 us (12%)
  waiting for transfers between devices  2.95 us (3%)
    all_to_all x2, blocking collectives, body(): lax.all_to_all(parts, both, split_axis=0, concat_axis=0, tiled=True, axis...  28.5 us
    all_to_all x1, blocking collectives, body(): lax.all_to_all(lines, 'lon', split_axis=0, concat_axis=0, tiled=True)  21 us
    all_to_all x1, blocking collectives, body(): lax.all_to_all(filtered.reshape(BLOCK * blocks, 1, COLS), 'lon', split_ax...  16.7 us
    ppermute x1, starting transfers between devices, body(): far = lax.ppermute(to_far, 'lon', swap_far())  10.3 us
    ppermute x1, starting transfers between devices, body(): north = lax.ppermute(bottom, 'lat', forward('lat', False))  4.83 us
    ppermute x1, starting transfers between devices, body(): near = lax.ppermute(to_near, 'lon', swap_near())  3.42 us
    ppermute x1, waiting for transfers between devices, body(): south = lax.ppermute(top, 'lat', backward('lat', False))  2.94 us
    pallas_call x1, Pallas kernels, body(): call(interior_kernel, (block, shape((LEV, COLS), f32)), (pltpu.VMEM((TALL...  2.77 us
  transfers between devices with their start and end apart: 4, of which 1 were waited for; matrix products, arithmetic and copies ran while one was open for 0% of the time, Pallas kernels for 5%

profile of v4, /device:TPU:1, one launch (start us, length us, event | category | flops | bytes accessed | tf_op | source)
XLA Modules:
  0.0 102.4 jit_solution(548280142863112581)
XLA Ops:
  0.6 1.0 %shard_map.167 = (f32[13,8,128]{2,1,0:T(8,128)S(1)}, f32[13,8,128]{2,1,0:T(8,128)S(1)}) custom-call(f32[8,24,128]{2,1,0:T(8,128)} %temp_hbm.1, s32[24,128]{1,0:T(8,128)} %kmt_hbm.1, f32[24,128]{1,0:T(8,128)} %kappa_hbm.1, f32[24,128]{1,0:T(8,128)} %helm_hbm.1, f32[24,128]{1,0:T(8,128)} %forcing_hbm.1, s32[1,24]{1,0:T(1,128)} %bitcast.21), custom_call_target="tpu_custom_call" | custom-call | tf_op jit(solution)/shard_map/pallas_call | solution.py:679
  1.7 4.8 %collective-permute-start = (f32[13,8,128]{2,1,0:T(8,128)S(1)}, f32[13,8,128]{2,1,0:T(8,128)S(1)}, u32[]{:S(2)}, u32[]{:S(2)}) collective-permute-start(f32[13,8,128]{2,1,0:T(8,128)S(1)} %get-tuple-element.29), channel_id=1, source_target_pairs={{0,1},{1,2},{2,3},{3,4},{4,5},{5,6},{6,7},{7,8},{8,9},{9,10},{10,1... | collective-permute-start | bytes 159752 | tf_op jit(solution)/shard_map/ppermute | solution.py:691
  6.5 1.3 %collective-permute-start.1 = (f32[13,8,128]{2,1,0:T(8,128)S(1)}, f32[13,8,128]{2,1,0:T(8,128)S(1)}, u32[]{:S(2)}, u32[]{:S(2)}) collective-permute-start(f32[13,8,128]{2,1,0:T(8,128)S(1)} %get-tuple-element.30), channel_id=1, source_target_pairs={{1,0},{2,1},{3,2},{4,3},{5,4},{6,5},{7,6},{8,7},{9,8},{10,9},{11,1... | collective-permute-start | bytes 159752 | tf_op jit(solution)/shard_map/ppermute | solution.py:692
  7.8 2.0 %shard_map.166 = (f32[24,16,128]{2,1,0:T(8,128)S(1)}, bf16[64,640]{1,0:T(8,128)(2,1)S(1)}, bf16[256,384]{1,0:T(8,128)(2,1)S(1)}, bf16[256,384]{1,0:T(8,128)(2,1)...) custom-call(f32[8,24,128]{2,1,0:T(8,128)} %temp_hbm.1, ...), custom_call_target="tpu_custom_call" | custom-call | flops 1000000 | bytes 2000000 | tf_op jit(solution)/shard_map/pallas_call | solution.py:703
  9.8 0.0 collective-permute-done.north_ref
  9.8 2.9 %collective-permute-done.1.south_ref = f32[13,8,128]{2,1,0:T(8,128)S(1)} collective-permute-done((f32[13,8,128]{2,1,0:T(8,128)S(1)}, f32[13,8,128]{2,1,0:T(8,128)S(1)}, u32[]{:S(2)}, u32[]{:S(2)}) %collective-permute-start.1) | collective-permute-done | bytes 53280 | tf_op jit(solution)/shard_map/ppermute | solution.py:692
  12.8 0.3 shard_map.168
  13.0 10.3 %collective-permute-start.2 = (f32[2,16,128]{2,1,0:T(8,128)S(1)}, f32[2,16,128]{2,1,0:T(8,128)S(1)}, u32[]{:S(2)}, u32[]{:S(2)}) collective-permute-start(f32[2,16,128]{2,1,0:T(8,128)S(1)} %get-tuple-element.32), channel_id=1, source_target_pairs={{0,496},{16,32},{32,16},{48,64},{64,48},{80,96},{96,80},{112,128},... | collective-permute-start | bytes 49160 | tf_op jit(solution)/shard_map/ppermute | solution.py:718
  23.4 3.4 %collective-permute-start.3 = (f32[2,16,128]{2,1,0:T(8,128)S(1)}, f32[2,16,128]{2,1,0:T(8,128)S(1)}, u32[]{:S(2)}, u32[]{:S(2)}) collective-permute-start(f32[2,16,128]{2,1,0:T(8,128)S(1)} %get-tuple-element.33), channel_id=1, source_target_pairs={{0,16},{16,0},{32,48},{48,32},{64,80},{80,64},{96,112},{112,96},{1... | collective-permute-start | bytes 49160 | tf_op jit(solution)/shard_map/ppermute | solution.py:719
  26.8 2.8 %shard_map.169 = (f32[32,8,128]{2,1,0:T(8,128)S(1)}, f32[8,128]{1,0:T(8,128)S(1)}) custom-call(f32[40,16,128]{2,1,0:T(8,128)S(1)} %get-tuple-element.31.rows_ref, bf16[64,640]{1,0:T(8,128)(2,1)S(1)} %get-tuple-element.34.w_in_ref, bf16[256,384]{1,0:T(8,128)(2,1)S(1)} %get-tuple-element.35.w_mid_ref, bf16[256,384]{1,0:T(8,128)(2,1)S(1)} %get-tuple-element.36.w_late_ref, ...), custom_call_target="tpu_custom_call" | custom-call | flops 1000000000 | bytes 1000000 | tf_op jit(solution)/shard_map/pallas_call | solution.py:731
  29.6 0.0 collective-permute-done.2.far_ref
  29.6 0.0 collective-permute-done.3.near_ref
  29.6 1.9 %shard_map.170 = (f32[32,8,128]{2,1,0:T(8,128)S(1)}, f32[3,32,256]{2,1,0:T(8,128)S(1)}) custom-call(f32[40,16,128]{2,1,0:T(8,128)S(1)} %get-tuple-element.31.rows_ref, f32[2,16,128]{2,1,0:T(8,128)S(1)} %collective-permute-done.2.far_ref, f32[2,16,128]{2,1,0:T(8,128)S(1)} %collective-permute-done.3.near_ref, f32[32,8,128]{2,1,0:T(8,128)S(1)} %get-tuple-element.38.inside_ref, ...), custom_call_target="tpu_custom_call" | custom-call | tf_op jit(solution)/shard_map/pallas_call | solution.py:737
  31.5 0.0 copy-start
  31.6 0.0 copy-start.1
  31.6 21.0 %all_to_all.32.x_ref = f32[32,8,128]{2,1,0:T(8,128)S(1)} all-to-all(f32[32,8,128]{2,1,0:T(8,128)S(1)} %get-tuple-element.39), channel_id=1, replica_groups=mesh['lon'=32,'lat'=16] {'lon'}, dimensions={0} | all-to-all | bytes 262144 | tf_op jit(solution)/shard_map/all_to_all | solution.py:742
  52.6 0.0 copy-done
  52.6 0.0 copy-done.1
  52.6 1.2 %shard_map.171 = f32[288,128]{1,0:T(8,128)S(1)} custom-call(f32[32,8,128]{2,1,0:T(8,128)S(1)} %all_to_all.32.x_ref, f32[8,128]{1,0:T(8,128)S(1)} %get-tuple-element.40.line_ref, bf16[256,256]{1,0:T(8,128)(2,1)S(1)} %get-tuple-element.41.spread_ref, bf16[256,256]{1,0:T(8,128)(2,1)S(1)} %get-tuple-element.42.spread_low, ...), custom_call_target="tpu_custom_call" | custom-call | tf_op jit(solution)/shard_map/pallas_call | solution.py:743
  53.8 16.7 %all_to_all.33 = f32[288,1,128]{2,1,0:T(1,128)S(1)} all-to-all(f32[288,1,128]{2,1,0:T(1,128)S(1)} %bitcast.14), channel_id=1, replica_groups=mesh['lon'=32,'lat'=16] {'lon'}, dimensions={0} | all-to-all | bytes 294912 | tf_op jit(solution)/shard_map/all_to_all | solution.py:746
  70.6 1.9 %shard_map.172 = (f32[8,24,128]{2,1,0:T(8,128)}, f32[5,32,256]{2,1,0:T(8,128)S(1)}, f32[64,128]{1,0:T(8,128)S(1)}) custom-call(f32[288,128]{1,0:T(8,128)S(1)} %bitcast.15, f32[3,32,256]{2,1,0:T(8,128)S(1)} %get-tuple-element.47.planes_ref), custom_call_target="tpu_custom_call" | custom-call | tf_op jit(solution)/shard_map/pallas_call | solution.py:754
  72.5 19.3 %all_to_all.34 = f32[64,1,128]{2,1,0:T(1,128)S(1)} all-to-all(f32[64,1,128]{2,1,0:T(1,128)S(1)} %bitcast.17), channel_id=1, replica_groups={{0,1,2,3,4,5,6,7,8,9,10,11,12,13,14,15,16,17,18,19,20,21,22,23,24,25,26..., dimensions={0} | all-to-all | bytes 65536 | tf_op jit(solution)/shard_map/all_to_all | solution.py:762
  91.8 0.1 shard_map.173
  91.9 9.1 %all_to_all.35 = f32[8,1,128]{2,1,0:T(1,128)S(1)} all-to-all(f32[8,1,128]{2,1,0:T(1,128)S(1)} %bitcast.18), channel_id=1, replica_groups={{0,64,128,192,256,320,384,448},{1,65,129,193,257,321,385,449},{2,66,130..., dimensions={0} | all-to-all | bytes 8192 | tf_op jit(solution)/shard_map/all_to_all | solution.py:766
  101.1 1.4 %shard_map.174 = (f32[24,128]{1,0:T(8,128)}, f32[24,128]{1,0:T(8,128)}) custom-call(f32[8,128]{1,0:T(8,128)S(1)} %bitcast.19, f32[5,32,256]{2,1,0:T(8,128)S(1)} %get-tuple-element.50.powers_ref), custom_call_target="tpu_custom_call" | custom-call | tf_op jit(solution)/shard_map/pallas_call | solution.py:769
Async XLA Ops:
  1.7 8.2 %collective-permute-start = (f32[13,8,128]{2,1,0:T(8,128)S(1)}, f32[13,8,128]{2,1,0:T(8,128)S(1)}, u32[]{:S(2)}, u32[]{:S(2)}) collective-permute-start(f32[13,8,128]{2,1,0:T(8,128)S(1)} %get-tuple-element.29), channel_id=1, source_target_pairs={{0,1},{1,2},{2,3},{3,4},{4,5},{5,6},{6,7},{7,8},{8,9},{9,10},{10,1... | collective-permute-start | bytes 159752 | tf_op jit(solution)/shard_map/ppermute | solution.py:691
  6.5 6.3 %collective-permute-start.1 = (f32[13,8,128]{2,1,0:T(8,128)S(1)}, f32[13,8,128]{2,1,0:T(8,128)S(1)}, u32[]{:S(2)}, u32[]{:S(2)}) collective-permute-start(f32[13,8,128]{2,1,0:T(8,128)S(1)} %get-tuple-element.30), channel_id=1, source_target_pairs={{1,0},{2,1},{3,2},{4,3},{5,4},{6,5},{7,6},{8,7},{9,8},{10,9},{11,1... | collective-permute-start | bytes 159752 | tf_op jit(solution)/shard_map/ppermute | solution.py:692
  13.0 16.5 %collective-permute-start.2 = (f32[2,16,128]{2,1,0:T(8,128)S(1)}, f32[2,16,128]{2,1,0:T(8,128)S(1)}, u32[]{:S(2)}, u32[]{:S(2)}) collective-permute-start(f32[2,16,128]{2,1,0:T(8,128)S(1)} %get-tuple-element.32), channel_id=1, source_target_pairs={{0,496},{16,32},{32,16},{48,64},{64,48},{80,96},{96,80},{112,128},... | collective-permute-start | bytes 49160 | tf_op jit(solution)/shard_map/ppermute | solution.py:718
  23.4 6.2 %collective-permute-start.3 = (f32[2,16,128]{2,1,0:T(8,128)S(1)}, f32[2,16,128]{2,1,0:T(8,128)S(1)}, u32[]{:S(2)}, u32[]{:S(2)}) collective-permute-start(f32[2,16,128]{2,1,0:T(8,128)S(1)} %get-tuple-element.33), channel_id=1, source_target_pairs={{0,16},{16,0},{32,48},{48,32},{64,80},{80,64},{96,112},{112,96},{1... | collective-permute-start | bytes 49160 | tf_op jit(solution)/shard_map/ppermute | solution.py:719
  31.5 21.1 %copy-start = (f32[32,8,128]{2,1,0:T(8,128)S(1)}, f32[32,8,128]{2,1,0:T(8,128)}, u32[]{:S(2)}) copy-start(f32[32,8,128]{2,1,0:T(8,128)} %constant.14.clone.twist_im_ref) | copy-start | bytes 393220
  31.6 21.1 %copy-start.1 = (f32[32,8,128]{2,1,0:T(8,128)S(1)}, f32[32,8,128]{2,1,0:T(8,128)}, u32[]{:S(2)}) copy-start(f32[32,8,128]{2,1,0:T(8,128)} %constant.13.clone.twist_re_ref) | copy-start | bytes 393220

commit v5 on v4

--- a/solution.py
+++ b/solution.py
@@ -13,6 +13,7 @@
 LEV = 8
 FIELDS = 16
 KMT, KAPPA, HELM, FORCING, CUT = 8, 9, 10, 11, 12
+BAND = 48
 HALO = 4
 DEEP = 8
 ROWS = 24
@@ -39,6 +40,21 @@
 
 def lane_index(shape):
     return lax.broadcasted_iota(jnp.int32, shape, len(shape) - 1)
+
+
+def fetching(kernel, outs, sources, held, before=()):
+    spec = pl.BlockSpec(memory_space=pltpu.VMEM)
+    return pl.pallas_call(
+        kernel,
+        out_shape=outs,
+        in_specs=[pl.BlockSpec(memory_space=pl.ANY)] * len(before)
+        + [pl.BlockSpec(memory_space=pltpu.HBM)] * len(sources),
+        out_specs=jax.tree.map(lambda _: spec, outs),
+        scratch_shapes=tuple(pltpu.VMEM(source.shape, source.dtype) for source in held)
+        + (pltpu.SemaphoreType.DMA((len(sources),)),),
+        compiler_params=pltpu.CompilerParams(vmem_limit_bytes=VMEM_LIMIT),
+        cost_estimate=pl.CostEstimate(flops=10**6, bytes_accessed=2 * 10**6, transcendentals=0),
+    )(*before, *(pltpu.with_memory_space_constraint(source, pltpu.HBM) for source in sources))
 
 
 def slab_kernel(
@@ -72,22 +88,30 @@
     return jnp.broadcast_to(kept, (ROWS, COLS))
 
 
-def prepare_kernel(*refs):
-    sources, refs = refs[:13], refs[13:]
-    outs, refs = refs[:11], refs[11:]
-    held, sems = refs[:13], refs[13]
+def fetch(sources, targets, sems):
     moves = [
         pltpu.make_async_copy(source, target, sems.at[index])
-        for index, (source, target) in enumerate(zip(sources, held))
+        for index, (source, target) in enumerate(zip(sources, targets))
     ]
     for move in moves:
         move.start()
     for move in moves:
         move.wait()
-    fill_rows(*held[:6], outs[0])
-    fill_weights(*held[6:10], *outs[1:5])
-    for index, table in enumerate(held[10:]):
-        outs[5 + 2 * index][...], outs[6 + 2 * index][...] = halves(table[...])
+
+
+def rows_kernel(*refs):
+    fetch(refs[:6], refs[7:13], refs[13])
+    fill_rows(*refs[7:13], refs[6])
+
+
+def weights_kernel(_, *refs):
+    sources, refs = refs[:9], refs[9:]
+    outs, refs = refs[:12], refs[12:]
+    held, sems = refs[:7], refs[7]
+    fetch(sources, tuple(held) + tuple(outs[10:]), sems)
+    fill_weights(*held[:4], *outs[:4])
+    for index, table in enumerate(held[4:]):
+        outs[4 + 2 * index][...], outs[5 + 2 * index][...] = halves(table[...])
 
 
 def fill_rows(temp_ref, kmt_ref, kappa_ref, helm_ref, forcing_ref, cutoff_ref, own_ref):
@@ -453,6 +477,29 @@
         out_ref[row + lev : row + BLOCK, :] = jnp.sum(edge, axis=0, keepdims=True)
 
 
+def ends_kernel(x_ref, far_ref, near_ref):
+    even = lax.rem(lax.axis_index("lon"), 2) == 0
+    lane = lane_index((LEV, COLS))
+    packed = []
+    for row in range(MID):
+        edge = jnp.where(lane < 2 * HALO, pltpu.roll(x_ref[row], HALO, 1), 0.0)
+        edge = pltpu.roll(edge, 0, 1, stride=2 * HALO, stride_axis=0)
+        packed.append(jnp.sum(edge, axis=0, keepdims=True))
+    packed = jnp.concatenate(packed, axis=0)
+    to_east = lax.rem(lane_index((MID, COLS)), 2 * HALO) < HALO
+    last = jnp.where(to_east, packed, 0.0)
+    first = jnp.where(to_east, 0.0, packed)
+    far_ref[...] = jnp.where(even, first, last)
+    near_ref[...] = jnp.where(even, last, first)
+
+
+def plain_kernel(x_ref, far_ref, near_ref, out_ref):
+    edge = far_ref[...] + near_ref[...]
+    for row in range(MID):
+        out_ref[BLOCK * row : BLOCK * row + LEV, :] = x_ref[row]
+        out_ref[BLOCK * row + LEV : BLOCK * (row + 1), :] = edge[row : row + 1]
+
+
 def two_sum(a, b):
     s = a + b
     t = s - a
@@ -499,7 +546,7 @@
     return quick_sum(*quick_sum(q, r + rest[0] / b[0]))
 
 
-def powers_kernel(x_ref, planes_ref, temp_ref, powers_ref, parts_ref):
+def powers_kernel(x_ref, planes_ref, powers_ref, parts_ref):
     lane = lane_index((LEV, COLS))
     wide_lane = lane_index((MID, COLS))
     kmt_left = planes_ref[0, :, 0:COLS]
@@ -507,7 +554,6 @@
     kmt = pltpu.roll(jnp.where(wide_lane < HALO, kmt_right, kmt_left), COLS - HALO, 1)
     mean = jnp.zeros((MID, COLS), jnp.float32)
     for level in range(LEV):
-        temp_ref[level] = x_ref[pl.ds(HALO * BLOCK + level, ROWS, stride=BLOCK), :]
         here = x_ref[pl.ds(level, MID, stride=BLOCK), :]
         mean = mean + jnp.where(kmt > level, here, 0.0)
     edge = x_ref[pl.ds(LEV, MID, stride=BLOCK), :]
@@ -604,7 +650,13 @@
     out_ref[...] = jnp.where(lane < 64, total[0], total[1])
 
 
-def combine_kernel(parts_ref, powers_ref, surface_ref, residual_ref, wide):
+def combine_kernel(
+    parts_ref, powers_ref, x_ref, temp_hbm, surface_ref, residual_ref, wide, temp, sem
+):
+    for level in range(LEV):
+        temp[level] = x_ref[pl.ds(HALO * BLOCK + level, ROWS, stride=BLOCK), :]
+    move = pltpu.make_async_copy(temp, temp_hbm, sem)
+    move.start()
     total = sum_messages(parts_ref)
     moments = [
         tuple(jnp.broadcast_to(t[:, order : order + 1], (8, COLS)) for t in total)
@@ -646,6 +698,7 @@
                     value = value + weights[index] * powers_ref[(index,) + spot]
                 wide[spot] = value * factor
         target[...] = wide[HALO : HALO + ROWS, HALO : HALO + COLS]
+    move.wait()
 
 
 def forward(axis, periodic):
@@ -690,33 +743,26 @@
     )(*(pltpu.with_memory_space_constraint(field, pltpu.HBM) for field in fields))
     north = lax.ppermute(bottom, "lat", forward("lat", False))
     south = lax.ppermute(top, "lat", backward("lat", False))
-    tables = [jnp.asarray(table) for table in filter_tables(blocks, COLS)]
-    sources = fields + (jnp.transpose(conv_in, (0, 2, 1)), conv_mid, conv_late, conv_out)
-    sources = sources + tuple(tables[:3])
-    outs = (
-        shape((ROWS, FIELDS, COLS), f32),
-        shape((4 * FIELDS, 640), bf16),
-        shape((256, 384), bf16),
-        shape((256, 384), bf16),
-        shape((48, 256), bf16),
-    ) + tuple(shape(table.shape, bf16) for table in tables[:3] for _ in range(2))
-    own, *prepared = pl.pallas_call(
-        prepare_kernel,
-        out_shape=outs,
-        in_specs=[pl.BlockSpec(memory_space=pltpu.HBM)] * len(sources),
-        out_specs=(vmem,) * len(outs),
-        scratch_shapes=tuple(pltpu.VMEM(source.shape, source.dtype) for source in sources)
-        + (pltpu.SemaphoreType.DMA((len(sources),)),),
-        compiler_params=pltpu.CompilerParams(vmem_limit_bytes=VMEM_LIMIT),
-        cost_estimate=pl.CostEstimate(flops=10**6, bytes_accessed=2 * 10**6, transcendentals=0),
-    )(*(pltpu.with_memory_space_constraint(source, pltpu.HBM) for source in sources))
-    weights, splits = prepared[:4], prepared[4:]
+    own = fetching(rows_kernel, shape((ROWS, FIELDS, COLS), f32), fields, fields)
     ends = shape((TALL // SLOTS, FIELDS, COLS), f32)
     rows, to_far, to_near = call(
         pack_kernel, (shape((TALL, FIELDS, COLS), f32), ends, ends)
     )(own, north, south)
     far = lax.ppermute(to_far, "lon", swap_far())
     near = lax.ppermute(to_near, "lon", swap_near())
+
+    tables = [jnp.asarray(table) for table in filter_tables(blocks, COLS)]
+    sources = (jnp.transpose(conv_in, (0, 2, 1)), conv_mid, conv_late, conv_out, *tables)
+    outs = (
+        shape((4 * FIELDS, 640), bf16),
+        shape((256, 384), bf16),
+        shape((256, 384), bf16),
+        shape((48, 256), bf16),
+    )
+    outs = outs + tuple(shape(table.shape, bf16) for table in tables[:3] for _ in range(2))
+    outs = outs + tuple(shape(table.shape, f32) for table in tables[3:])
+    prepared = fetching(weights_kernel, outs, sources, sources[:7], (to_near,))
+    weights, tables = prepared[:4], prepared[4:]
 
     def closure_scratch(chunks):
         cells = chunks * COLS
@@ -739,22 +785,32 @@
         (block, shape((3, MID, 2 * COLS), f32)),
         (pltpu.VMEM((TALL, FIELDS, COLS), f32),) + closure_scratch(6),
     )(rows, far, near, inside, *weights)
-    whole = lax.all_to_all(lines, "lon", split_axis=0, concat_axis=0, tiled=True)
-    filtered = call(filter_kernel, shape((BLOCK * blocks, COLS), f32))(
-        whole, line, *splits, *tables[3:]
-    )
-    back = lax.all_to_all(
-        filtered.reshape(BLOCK * blocks, 1, COLS), "lon", split_axis=0, concat_axis=0, tiled=True
-    ).reshape(BLOCK * blocks, COLS)
+
+    def filtered_block(lines, line, tables):
+        whole = lax.all_to_all(lines, "lon", split_axis=0, concat_axis=0, tiled=True)
+        result = call(filter_kernel, shape((BLOCK * blocks, COLS), f32))(whole, line, *tables)
+        result = result.reshape(BLOCK * blocks, 1, COLS)
+        result = lax.all_to_all(result, "lon", split_axis=0, concat_axis=0, tiled=True)
+        return result.reshape(BLOCK * blocks, COLS)
+
+    def plain_block(lines, line, tables):
+        ends = shape((MID, COLS), f32)
+        to_far, to_near = call(ends_kernel, (ends, ends))(lines)
+        far = lax.ppermute(to_far, "lon", swap_far())
+        near = lax.ppermute(to_near, "lon", swap_near())
+        return call(plain_kernel, shape((BLOCK * MID, COLS), f32))(lines, far, near)
+
+    top_row = lax.axis_index("lat") * ROWS - HALO
+    polar = (top_row < BAND) | (top_row + MID > ROWS * lax.axis_size("lat") - BAND)
+    back = lax.cond(polar, filtered_block, plain_block, lines, line, tables)
     everyone = blocks * lax.axis_size("lat")
     wide = everyone // 8
     both = ("lon", "lat")
     inner = [[wide * i + k for k in range(wide)] for i in range(8)]
     outer = [[wide * i + k for i in range(8)] for k in range(wide)]
-    temp_new, powers, parts = call(
+    powers, parts = call(
         powers_kernel,
         (
-            shape((LEV, ROWS, COLS), f32),
             shape((ITERS + 1, MID, 2 * COLS), f32),
             shape((wide, COLS), f32),
         ),
@@ -766,11 +822,22 @@
     parts = lax.all_to_all(
         parts, both, split_axis=0, concat_axis=0, tiled=True, axis_index_groups=outer
     )
-    surface, residual = call(
+    temp_new, surface, residual = pl.pallas_call(
         combine_kernel,
-        (shape((ROWS, COLS), f32), shape((ROWS, COLS), f32)),
-        (pltpu.VMEM((MID, 2 * COLS), f32),),
-    )(parts, powers)
+        out_shape=(
+            shape((LEV, ROWS, COLS), f32),
+            shape((ROWS, COLS), f32),
+            shape((ROWS, COLS), f32),
+        ),
+        in_specs=[vmem] * 3,
+        out_specs=(pl.BlockSpec(memory_space=pltpu.HBM), vmem, vmem),
+        scratch_shapes=(
+            pltpu.VMEM((MID, 2 * COLS), f32),
+            pltpu.VMEM((LEV, ROWS, COLS), f32),
+            pltpu.SemaphoreType.DMA,
+        ),
+        compiler_params=pltpu.CompilerParams(vmem_limit_bytes=VMEM_LIMIT),
+    )(parts, powers, back)
     return temp_new, surface, residual
 
 

time: 103 us -> 102 us (level)
  starting transfers between devices: 19.9 us -> 18.4 us
    all_to_all x2, blocking collectives: 28.5 us -> 24.8 us  [body(): lax.all_to_all(parts, both, split_axis=0, concat_axis=0, tiled=True, axis...]
    ppermute x1, starting transfers between devices: 10.3 us -> 7.25 us  [body(): far = lax.ppermute(to_far, 'lon', swap_far())]
    all_to_all x2, blocking collectives: 37.8 us -> 40.4 us  [the longest x1 23.7 us: filtered_block(): lax.all_to_all(lines, 'lon', split_axis=0, concat_axis=0, tiled=True)]
    ppermute x1, starting transfers between devices: 3.42 us -> 5.01 us  [body(): near = lax.ppermute(to_near, 'lon', swap_near())]
    pallas_call x4 -> x5, Pallas kernels: 6.51 us -> 7.57 us  [the longest x2 2.89 us: fetching(): pl.pallas_call(kernel, out_shape=outs, in_specs=[pl.BlockSpec(memory_spac...]
  transfers between devices with their start and end apart: 4 -> 4, of which waited for: 1 -> 1; matrix products, arithmetic and copies ran while one was open for 0% -> 0% of each run, Pallas kernels for 5% -> 6%
where the time goes in v5:
time: 102 us
  blocking collectives  65.2 us (64%)
  starting transfers between devices  18.4 us (18%)
  Pallas kernels  13.6 us (13%)
  waiting for transfers between devices  3.89 us (4%)
    all_to_all x2, blocking collectives, body(): lax.all_to_all(parts, both, split_axis=0, concat_axis=0, tiled=True, axis...  24.8 us
    all_to_all x1, blocking collectives, filtered_block(): lax.all_to_all(lines, 'lon', split_axis=0, concat_axis=0, tiled=True)  23.7 us
    all_to_all x1, blocking collectives, filtered_block(): lax.all_to_all(result, 'lon', split_axis=0, concat_axis=0, tiled=True)  16.7 us
    ppermute x1, starting transfers between devices, body(): far = lax.ppermute(to_far, 'lon', swap_far())  7.25 us
    ppermute x1, starting transfers between devices, body(): near = lax.ppermute(to_near, 'lon', swap_near())  5.01 us
    ppermute x1, starting transfers between devices, body(): north = lax.ppermute(bottom, 'lat', forward('lat', False))  4.83 us
    ppermute x1, waiting for transfers between devices, body(): south = lax.ppermute(top, 'lat', backward('lat', False))  3.88 us
    pallas_call x2, Pallas kernels, fetching(): pl.pallas_call(kernel, out_shape=outs, in_specs=[pl.BlockSpec(memory_spac...  2.89 us
  transfers between devices with their start and end apart: 4, of which 1 were waited for; matrix products, arithmetic and copies ran while one was open for 0% of the time, Pallas kernels for 6%

profile of v5, /device:TPU:1, one launch (start us, length us, event | category | flops | bytes accessed | tf_op | source)
XLA Modules:
  0.0 101.8 jit_solution(10602170497546593865)
XLA Ops:
  0.6 1.0 %shard_map.167 = (f32[13,8,128]{2,1,0:T(8,128)S(1)}, f32[13,8,128]{2,1,0:T(8,128)S(1)}) custom-call(f32[8,24,128]{2,1,0:T(8,128)} %temp_hbm.1, s32[24,128]{1,0:T(8,128)} %kmt_hbm.1, f32[24,128]{1,0:T(8,128)} %kappa_hbm.1, f32[24,128]{1,0:T(8,128)} %helm_hbm.1, f32[24,128]{1,0:T(8,128)} %forcing_hbm.1, s32[1,24]{1,0:T(1,128)} %bitcast.21), custom_call_target="tpu_custom_call" | custom-call | tf_op jit(solution)/shard_map/pallas_call | solution.py:732
  1.7 4.8 %collective-permute-start.2 = (f32[13,8,128]{2,1,0:T(8,128)S(1)}, f32[13,8,128]{2,1,0:T(8,128)S(1)}, u32[]{:S(2)}, u32[]{:S(2)}) collective-permute-start(f32[13,8,128]{2,1,0:T(8,128)S(1)} %get-tuple-element.62), channel_id=1, source_target_pairs={{0,1},{1,2},{2,3},{3,4},{4,5},{5,6},{6,7},{7,8},{8,9},{9,10},{10,1... | collective-permute-start | bytes 159752 | tf_op jit(solution)/shard_map/ppermute | solution.py:744
  6.5 1.3 %collective-permute-start.3 = (f32[13,8,128]{2,1,0:T(8,128)S(1)}, f32[13,8,128]{2,1,0:T(8,128)S(1)}, u32[]{:S(2)}, u32[]{:S(2)}) collective-permute-start(f32[13,8,128]{2,1,0:T(8,128)S(1)} %get-tuple-element.63), channel_id=1, source_target_pairs={{1,0},{2,1},{3,2},{4,3},{5,4},{6,5},{7,6},{8,7},{9,8},{10,9},{11,1... | collective-permute-start | bytes 159752 | tf_op jit(solution)/shard_map/ppermute | solution.py:745
  7.8 1.1 %shard_map.166.own_ref = f32[24,16,128]{2,1,0:T(8,128)S(1)} custom-call(f32[8,24,128]{2,1,0:T(8,128)} %temp_hbm.1, s32[24,128]{1,0:T(8,128)} %kmt_hbm.1, f32[24,128]{1,0:T(8,128)} %kappa_hbm.1, f32[24,128]{1,0:T(8,128)} %helm_hbm.1, f32[24,128]{1,0:T(8,128)} %forcing_hbm.1, s32[1,24]{1,0:T(1,128)} %bitcast.22), custom_call_target="tpu_custom_call" | custom-call | flops 1000000 | bytes 2000000 | tf_op jit(solution)/shard_map/pallas_call | solution.py:47
  8.9 0.0 collective-permute-done.2.north_ref
  8.9 3.9 %collective-permute-done.3.south_ref = f32[13,8,128]{2,1,0:T(8,128)S(1)} collective-permute-done((f32[13,8,128]{2,1,0:T(8,128)S(1)}, f32[13,8,128]{2,1,0:T(8,128)S(1)}, u32[]{:S(2)}, u32[]{:S(2)}) %collective-permute-start.3) | collective-permute-done | bytes 53280 | tf_op jit(solution)/shard_map/ppermute | solution.py:745
  12.8 0.3 shard_map.168
  13.0 5.0 %collective-permute-start.5 = (f32[2,16,128]{2,1,0:T(8,128)S(1)}, f32[2,16,128]{2,1,0:T(8,128)S(1)}, u32[]{:S(2)}, u32[]{:S(2)}) collective-permute-start(f32[2,16,128]{2,1,0:T(8,128)S(1)} %get-tuple-element.66._), channel_id=1, source_target_pairs={{0,16},{16,0},{32,48},{48,32},{64,80},{80,64},{96,112},{112,96},{1... | collective-permute-start | bytes 49160 | tf_op jit(solution)/shard_map/ppermute | solution.py:752
  18.1 7.2 %collective-permute-start.4 = (f32[2,16,128]{2,1,0:T(8,128)S(1)}, f32[2,16,128]{2,1,0:T(8,128)S(1)}, u32[]{:S(2)}, u32[]{:S(2)}) collective-permute-start(f32[2,16,128]{2,1,0:T(8,128)S(1)} %get-tuple-element.65), channel_id=1, source_target_pairs={{0,496},{16,32},{32,16},{48,64},{64,48},{80,96},{96,80},{112,128},... | collective-permute-start | bytes 49160 | tf_op jit(solution)/shard_map/ppermute | solution.py:751
  25.3 1.8 %shard_map.169 = (bf16[64,640]{1,0:T(8,128)(2,1)S(1)}, bf16[256,384]{1,0:T(8,128)(2,1)S(1)}, bf16[256,384]{1,0:T(8,128)(2,1)S(1)}, bf16[48,256]{1,0:T(8,128)(2,1...) custom-call(f32[2,16,128]{2,1,0:T(8,128)S(1)} %get-tuple-element.66., ...), custom_call_target="tpu_custom_call" | custom-call | flops 1000000 | bytes 2000000 | tf_op jit(solution)/shard_map/pallas_call | solution.py:47
  27.2 2.7 %shard_map.170 = (f32[32,8,128]{2,1,0:T(8,128)S(1)}, f32[8,128]{1,0:T(8,128)S(1)}) custom-call(f32[40,16,128]{2,1,0:T(8,128)S(1)} %get-tuple-element.64.rows_ref, bf16[64,640]{1,0:T(8,128)(2,1)S(1)} %get-tuple-element.67.w_in_ref, bf16[256,384]{1,0:T(8,128)(2,1)S(1)} %get-tuple-element.68.w_mid_ref, bf16[256,384]{1,0:T(8,128)(2,1)S(1)} %get-tuple-element.69.w_late_ref, ...), custom_call_target="tpu_custom_call" | custom-call | flops 1000000000 | bytes 1000000 | tf_op jit(solution)/shard_map/pallas_call | solution.py:777
  29.9 0.0 collective-permute-done.5.near_ref
  29.9 0.0 collective-permute-done.4.far_ref
  29.9 1.9 %shard_map.171 = (f32[32,8,128]{2,1,0:T(8,128)S(1)}, f32[3,32,256]{2,1,0:T(8,128)S(1)}) custom-call(f32[40,16,128]{2,1,0:T(8,128)S(1)} %get-tuple-element.64.rows_ref, f32[2,16,128]{2,1,0:T(8,128)S(1)} %collective-permute-done.4.far_ref, f32[2,16,128]{2,1,0:T(8,128)S(1)} %collective-permute-done.5.near_ref, f32[32,8,128]{2,1,0:T(8,128)S(1)} %get-tuple-element.71.inside_ref, ...), custom_call_target="tpu_custom_call" | custom-call | tf_op jit(solution)/shard_map/pallas_call | solution.py:783
  31.8 41.7 %conditional.1 = (f32[288,128]{1,0:T(8,128)S(1)}) conditional(s32[]{:T(128)} %convert_element_type.3, f32[32,8,128]{2,1,0:T(8,128)S(1)} %get-tuple-element.72, (f32[32,8,128]{2,1,0:T(8,128)S(1)}, f32[8,128]{1,0:T(8,128)S(1)}, bf16[256,256]{1,0:T(8,128)(2,1)S(1)}, bf16[256,256]{1,0:T(8,128)(2,1)S(1)}, bf16[256,256]{1,0:T(8,128)(2,1)S(1)}, ...), branch_computations={%region_0.0_spmd, %region_1.0_spmd} | conditional | bytes 557064 | solution.py:805
  31.8 23.7 %all_to_all.30.x_ref = f32[32,8,128]{2,1,0:T(8,128)S(1)} all-to-all(f32[32,8,128]{2,1,0:T(8,128)S(1)} %get-tuple-element.26), channel_id=1, replica_groups=mesh['lon'=32,'lat'=16] {'lon'}, dimensions={0} | all-to-all | bytes 262144 | tf_op jit(solution)/shard_map/cond/branch_1_fun/all_to_all | solution.py:790
  55.5 1.2 %branch_1_fun.1 = f32[288,128]{1,0:T(8,128)S(1)} custom-call(f32[32,8,128]{2,1,0:T(8,128)S(1)} %all_to_all.30.x_ref, f32[8,128]{1,0:T(8,128)S(1)} %get-tuple-element.27.line_ref, bf16[256,256]{1,0:T(8,128)(2,1)S(1)} %get-tuple-element.28.spread_ref, bf16[256,256]{1,0:T(8,128)(2,1)S(1)} %get-tuple-element.29.spread_low, ...), custom_call_target="tpu_custom_call" | custom-call | tf_op jit(solution)/shard_map/cond/branch_1_fun/pallas_call | solution.py:791
  56.8 16.7 %all_to_all.31 = f32[288,1,128]{2,1,0:T(1,128)S(1)} all-to-all(f32[288,1,128]{2,1,0:T(1,128)S(1)} %bitcast.14), channel_id=1, replica_groups=mesh['lon'=32,'lat'=16] {'lon'}, dimensions={0} | all-to-all | bytes 294912 | tf_op jit(solution)/shard_map/cond/branch_1_fun/all_to_all | solution.py:793
  73.5 1.5 %shard_map.172 = (f32[5,32,256]{2,1,0:T(8,128)S(1)}, f32[64,128]{1,0:T(8,128)S(1)}) custom-call(f32[288,128]{1,0:T(8,128)S(1)} %get-tuple-element.85.x_ref, f32[3,32,256]{2,1,0:T(8,128)S(1)} %get-tuple-element.82.planes_ref), custom_call_target="tpu_custom_call" | custom-call | tf_op jit(solution)/shard_map/pallas_call | solution.py:811
  75.0 15.6 %all_to_all.32 = f32[64,1,128]{2,1,0:T(1,128)S(1)} all-to-all(f32[64,1,128]{2,1,0:T(1,128)S(1)} %bitcast.16), channel_id=1, replica_groups={{0,1,2,3,4,5,6,7,8,9,10,11,12,13,14,15,16,17,18,19,20,21,22,23,24,25,26..., dimensions={0} | all-to-all | bytes 65536 | tf_op jit(solution)/shard_map/all_to_all | solution.py:818
  90.6 0.1 shard_map.173
  90.7 9.1 %all_to_all.33 = f32[8,1,128]{2,1,0:T(1,128)S(1)} all-to-all(f32[8,1,128]{2,1,0:T(1,128)S(1)} %bitcast.18), channel_id=1, replica_groups={{0,64,128,192,256,320,384,448},{1,65,129,193,257,321,385,449},{2,66,130..., dimensions={0} | all-to-all | bytes 8192 | tf_op jit(solution)/shard_map/all_to_all | solution.py:822
  99.9 1.9 %shard_map.174 = (f32[8,24,128]{2,1,0:T(8,128)}, f32[24,128]{1,0:T(8,128)}, f32[24,128]{1,0:T(8,128)}) custom-call(f32[8,128]{1,0:T(8,128)S(1)} %bitcast.17, f32[5,32,256]{2,1,0:T(8,128)S(1)} %get-tuple-element.84.powers_ref, f32[288,128]{1,0:T(8,128)S(1)} %get-tuple-element.85.x_ref), custom_call_target="tpu_custom_call" | custom-call | tf_op jit(solution)/shard_map/pallas_call | solution.py:825
Async XLA Ops:
  1.7 7.2 %collective-permute-start.2 = (f32[13,8,128]{2,1,0:T(8,128)S(1)}, f32[13,8,128]{2,1,0:T(8,128)S(1)}, u32[]{:S(2)}, u32[]{:S(2)}) collective-permute-start(f32[13,8,128]{2,1,0:T(8,128)S(1)} %get-tuple-element.62), channel_id=1, source_target_pairs={{0,1},{1,2},{2,3},{3,4},{4,5},{5,6},{6,7},{7,8},{8,9},{9,10},{10,1... | collective-permute-start | bytes 159752 | tf_op jit(solution)/shard_map/ppermute | solution.py:744
  6.5 6.3 %collective-permute-start.3 = (f32[13,8,128]{2,1,0:T(8,128)S(1)}, f32[13,8,128]{2,1,0:T(8,128)S(1)}, u32[]{:S(2)}, u32[]{:S(2)}) collective-permute-start(f32[13,8,128]{2,1,0:T(8,128)S(1)} %get-tuple-element.63), channel_id=1, source_target_pairs={{1,0},{2,1},{3,2},{4,3},{5,4},{6,5},{7,6},{8,7},{9,8},{10,9},{11,1... | collective-permute-start | bytes 159752 | tf_op jit(solution)/shard_map/ppermute | solution.py:745
  13.0 16.8 %collective-permute-start.5 = (f32[2,16,128]{2,1,0:T(8,128)S(1)}, f32[2,16,128]{2,1,0:T(8,128)S(1)}, u32[]{:S(2)}, u32[]{:S(2)}) collective-permute-start(f32[2,16,128]{2,1,0:T(8,128)S(1)} %get-tuple-element.66._), channel_id=1, source_target_pairs={{0,16},{16,0},{32,48},{48,32},{64,80},{80,64},{96,112},{112,96},{1... | collective-permute-start | bytes 49160 | tf_op jit(solution)/shard_map/ppermute | solution.py:752
  18.1 11.8 %collective-permute-start.4 = (f32[2,16,128]{2,1,0:T(8,128)S(1)}, f32[2,16,128]{2,1,0:T(8,128)S(1)}, u32[]{:S(2)}, u32[]{:S(2)}) collective-permute-start(f32[2,16,128]{2,1,0:T(8,128)S(1)} %get-tuple-element.65), channel_id=1, source_target_pairs={{0,496},{16,32},{32,16},{48,64},{64,48},{80,96},{96,80},{112,128},... | collective-permute-start | bytes 49160 | tf_op jit(solution)/shard_map/ppermute | solution.py:751

commit v6 on v5

--- a/solution.py
+++ b/solution.py
@@ -25,7 +25,7 @@
 VMEM_LIMIT = 48 * 1024 * 1024
 
 
-def call(kernel, outs, scratch=(), flops=None):
+def call(kernel, outs, scratch=()):
     spec = pl.BlockSpec(memory_space=pltpu.VMEM)
     return pl.pallas_call(
         kernel,
@@ -33,8 +33,6 @@
         out_specs=jax.tree.map(lambda _: spec, outs),
         scratch_shapes=scratch,
         compiler_params=pltpu.CompilerParams(vmem_limit_bytes=VMEM_LIMIT),
-        cost_estimate=flops
-        and pl.CostEstimate(flops=flops, bytes_accessed=10**6, transcendentals=flops // 500),
     )
 
 
@@ -42,19 +40,21 @@
     return lax.broadcasted_iota(jnp.int32, shape, len(shape) - 1)
 
 
-def fetching(kernel, outs, sources, held, before=()):
+def fetching(kernel, outs, sources, held, rest=(), scratch=(), flops=10**6):
     spec = pl.BlockSpec(memory_space=pltpu.VMEM)
     return pl.pallas_call(
         kernel,
         out_shape=outs,
-        in_specs=[pl.BlockSpec(memory_space=pl.ANY)] * len(before)
-        + [pl.BlockSpec(memory_space=pltpu.HBM)] * len(sources),
+        in_specs=[pl.BlockSpec(memory_space=pltpu.HBM)] * len(sources) + [spec] * len(rest),
         out_specs=jax.tree.map(lambda _: spec, outs),
         scratch_shapes=tuple(pltpu.VMEM(source.shape, source.dtype) for source in held)
-        + (pltpu.SemaphoreType.DMA((len(sources),)),),
+        + (pltpu.SemaphoreType.DMA((len(sources),)),)
+        + tuple(scratch),
         compiler_params=pltpu.CompilerParams(vmem_limit_bytes=VMEM_LIMIT),
-        cost_estimate=pl.CostEstimate(flops=10**6, bytes_accessed=2 * 10**6, transcendentals=0),
-    )(*before, *(pltpu.with_memory_space_constraint(source, pltpu.HBM) for source in sources))
+        cost_estimate=pl.CostEstimate(
+            flops=flops, bytes_accessed=2 * 10**6, transcendentals=flops // 500
+        ),
+    )(*(pltpu.with_memory_space_constraint(source, pltpu.HBM) for source in sources), *rest)
 
 
 def slab_kernel(
@@ -95,23 +95,13 @@
     ]
     for move in moves:
         move.start()
-    for move in moves:
+    return moves
+
+
+def rows_kernel(*refs):
+    for move in fetch(refs[:6], refs[7:13], refs[13]):
         move.wait()
-
-
-def rows_kernel(*refs):
-    fetch(refs[:6], refs[7:13], refs[13])
     fill_rows(*refs[7:13], refs[6])
-
-
-def weights_kernel(_, *refs):
-    sources, refs = refs[:9], refs[9:]
-    outs, refs = refs[:12], refs[12:]
-    held, sems = refs[:7], refs[7]
-    fetch(sources, tuple(held) + tuple(outs[10:]), sems)
-    fill_weights(*held[:4], *outs[:4])
-    for index, table in enumerate(held[4:]):
-        outs[4 + 2 * index][...], outs[5 + 2 * index][...] = halves(table[...])
 
 
 def fill_rows(temp_ref, kmt_ref, kappa_ref, helm_ref, forcing_ref, cutoff_ref, own_ref):
@@ -283,17 +273,24 @@
 FIRST = DEEP - HALO
 
 
-def interior_kernel(
-    rows_ref, w_in_ref, w_mid_ref, w_late_ref, w_out_ref, out_ref, line_ref,
-    start, mask_odd, mask_even, act_a, act_b,
-):
+def interior_kernel(*refs):
+    sources, rows_ref, refs = refs[:9], refs[9], refs[10:]
+    out_ref, line_ref, weights, tables, refs = refs[0], refs[1], refs[2:6], refs[6:14], refs[14:]
+    held, sems = refs[:7], refs[7]
+    start, mask_odd, mask_even, act_a, act_b = refs[8:]
+    moves = fetch(sources, tuple(held) + tuple(tables[6:]), sems)
     for row in range(TALL):
         start[row * FIELDS : (row + 1) * FIELDS] = first_input(rows_ref[row])
+    for move in moves:
+        move.wait()
+    fill_weights(*held[:4], *weights)
+    for index, table in enumerate(held[4:]):
+        tables[2 * index][...], tables[2 * index + 1][...] = halves(table[...])
     results = closure_layers(
         lambda chunk: start[2 * FIELDS * chunk : 2 * FIELDS * (chunk + 2)],
         TALL // 2 - 1,
         COLS,
-        (w_in_ref, w_mid_ref, w_late_ref, w_out_ref),
+        weights,
         (act_a, act_b),
         (mask_odd, mask_even),
     )
@@ -761,9 +758,6 @@
     )
     outs = outs + tuple(shape(table.shape, bf16) for table in tables[:3] for _ in range(2))
     outs = outs + tuple(shape(table.shape, f32) for table in tables[3:])
-    prepared = fetching(weights_kernel, outs, sources, sources[:7], (to_near,))
-    weights, tables = prepared[:4], prepared[4:]
-
     def closure_scratch(chunks):
         cells = chunks * COLS
         return (
@@ -774,12 +768,16 @@
         )
 
     block = shape((MID, LEV, COLS), f32)
-    inside, line = call(
+    inside, line, *prepared = fetching(
         interior_kernel,
-        (block, shape((LEV, COLS), f32)),
+        (block, shape((LEV, COLS), f32)) + outs,
+        sources,
+        sources[:7],
+        (rows,),
         (pltpu.VMEM((TALL * FIELDS, COLS), bf16),) + closure_scratch(19),
         10**9,
-    )(rows, *weights)
+    )
+    weights, tables = prepared[:4], prepared[4:]
     lines, planes = call(
         edge_kernel,
         (block, shape((3, MID, 2 * COLS), f32)),

time: 102 us -> 99.3 us (0.974)
  blocking collectives: 65.2 us -> 61 us
  starting transfers between devices: 18.4 us -> 19.9 us
    all_to_all x1, blocking collectives: 23.7 us -> 19.3 us  [filtered_block(): lax.all_to_all(lines, 'lon', split_axis=0, concat_axis=0, tiled=True)]
    ppermute x1, starting transfers between devices: 7.25 us -> 10.3 us  [body(): far = lax.ppermute(to_far, 'lon', swap_far())]
    pallas_call x1 -> x0, Pallas kernels: 2.72 us -> none  [body(): call(interior_kernel, (block, shape((LEV, COLS), f32)), (pltpu.VMEM((TALL...]
    pallas_call x2, Pallas kernels: 2.89 us -> 5.39 us  [fetching(): pl.pallas_call(kernel, out_shape=outs, in_specs=[pl.BlockSpec(memory_spac...]
    ppermute x1, starting transfers between devices: 5.01 us -> 3.42 us  [body(): near = lax.ppermute(to_near, 'lon', swap_near())]
  transfers between devices with their start and end apart: 4 -> 4, of which waited for: 1 -> 1; matrix products, arithmetic and copies ran while one was open for 0% -> 0% of each run, Pallas kernels for 6% -> 5%
where the time goes in v6:
time: 99.3 us; the launch traced here: 98.9 us
  blocking collectives  61 us (61%)
  starting transfers between devices  19.9 us (20%)
  Pallas kernels  13.4 us (13%)
  waiting for transfers between devices  3.89 us (4%)
    all_to_all x2, blocking collectives, body(): lax.all_to_all(parts, both, split_axis=0, concat_axis=0, tiled=True, axis...  24.9 us
    all_to_all x1, blocking collectives, filtered_block(): lax.all_to_all(lines, 'lon', split_axis=0, concat_axis=0, tiled=True)  19.3 us
    all_to_all x1, blocking collectives, filtered_block(): lax.all_to_all(result, 'lon', split_axis=0, concat_axis=0, tiled=True)  16.7 us
    ppermute x1, starting transfers between devices, body(): far = lax.ppermute(to_far, 'lon', swap_far())  10.3 us
    pallas_call x2, Pallas kernels, fetching(): pl.pallas_call(kernel, out_shape=outs, in_specs=[pl.BlockSpec(memory_spac...  5.39 us
    ppermute x1, starting transfers between devices, body(): north = lax.ppermute(bottom, 'lat', forward('lat', False))  4.83 us
    ppermute x1, waiting for transfers between devices, body(): south = lax.ppermute(top, 'lat', backward('lat', False))  3.88 us
    ppermute x1, starting transfers between devices, body(): near = lax.ppermute(to_near, 'lon', swap_near())  3.42 us
  transfers between devices with their start and end apart: 4, of which 1 were waited for; matrix products, arithmetic and copies ran while one was open for 0% of the time, Pallas kernels for 5%

profile of v6, /device:TPU:1, one launch (start us, length us, event | category | flops | bytes accessed | tf_op | source)
XLA Modules:
  0.0 98.9 jit_solution(10346380415600727836)
XLA Ops:
  0.6 1.0 %shard_map.167 = (f32[13,8,128]{2,1,0:T(8,128)S(1)}, f32[13,8,128]{2,1,0:T(8,128)S(1)}) custom-call(f32[8,24,128]{2,1,0:T(8,128)} %temp_hbm.1, s32[24,128]{1,0:T(8,128)} %kmt_hbm.1, f32[24,128]{1,0:T(8,128)} %kappa_hbm.1, f32[24,128]{1,0:T(8,128)} %helm_hbm.1, f32[24,128]{1,0:T(8,128)} %forcing_hbm.1, s32[1,24]{1,0:T(1,128)} %bitcast.20), custom_call_target="tpu_custom_call" | custom-call | tf_op jit(solution)/shard_map/pallas_call | solution.py:729
  1.7 4.8 %collective-permute-start.2 = (f32[13,8,128]{2,1,0:T(8,128)S(1)}, f32[13,8,128]{2,1,0:T(8,128)S(1)}, u32[]{:S(2)}, u32[]{:S(2)}) collective-permute-start(f32[13,8,128]{2,1,0:T(8,128)S(1)} %get-tuple-element.62), channel_id=1, source_target_pairs={{0,1},{1,2},{2,3},{3,4},{4,5},{5,6},{6,7},{7,8},{8,9},{9,10},{10,1... | collective-permute-start | bytes 159752 | tf_op jit(solution)/shard_map/ppermute | solution.py:741
  6.5 1.3 %collective-permute-start.3 = (f32[13,8,128]{2,1,0:T(8,128)S(1)}, f32[13,8,128]{2,1,0:T(8,128)S(1)}, u32[]{:S(2)}, u32[]{:S(2)}) collective-permute-start(f32[13,8,128]{2,1,0:T(8,128)S(1)} %get-tuple-element.63), channel_id=1, source_target_pairs={{1,0},{2,1},{3,2},{4,3},{5,4},{6,5},{7,6},{8,7},{9,8},{10,9},{11,1... | collective-permute-start | bytes 159752 | tf_op jit(solution)/shard_map/ppermute | solution.py:742
  7.8 1.1 %shard_map.166.own_ref = f32[24,16,128]{2,1,0:T(8,128)S(1)} custom-call(f32[8,24,128]{2,1,0:T(8,128)} %temp_hbm.1, s32[24,128]{1,0:T(8,128)} %kmt_hbm.1, f32[24,128]{1,0:T(8,128)} %kappa_hbm.1, f32[24,128]{1,0:T(8,128)} %helm_hbm.1, f32[24,128]{1,0:T(8,128)} %forcing_hbm.1, s32[1,24]{1,0:T(1,128)} %bitcast.21), custom_call_target="tpu_custom_call" | custom-call | flops 1000000 | bytes 2000000 | tf_op jit(solution)/shard_map/pallas_call | solution.py:45
  8.9 0.0 collective-permute-done.2.north_ref
  8.9 3.9 %collective-permute-done.3.south_ref = f32[13,8,128]{2,1,0:T(8,128)S(1)} collective-permute-done((f32[13,8,128]{2,1,0:T(8,128)S(1)}, f32[13,8,128]{2,1,0:T(8,128)S(1)}, u32[]{:S(2)}, u32[]{:S(2)}) %collective-permute-start.3) | collective-permute-done | bytes 53280 | tf_op jit(solution)/shard_map/ppermute | solution.py:742
  12.8 0.3 shard_map.168
  13.0 10.3 %collective-permute-start.4 = (f32[2,16,128]{2,1,0:T(8,128)S(1)}, f32[2,16,128]{2,1,0:T(8,128)S(1)}, u32[]{:S(2)}, u32[]{:S(2)}) collective-permute-start(f32[2,16,128]{2,1,0:T(8,128)S(1)} %get-tuple-element.65), channel_id=1, source_target_pairs={{0,496},{16,32},{32,16},{48,64},{64,48},{80,96},{96,80},{112,128},... | collective-permute-start | bytes 49160 | tf_op jit(solution)/shard_map/ppermute | solution.py:748
  23.4 3.4 %collective-permute-start.5 = (f32[2,16,128]{2,1,0:T(8,128)S(1)}, f32[2,16,128]{2,1,0:T(8,128)S(1)}, u32[]{:S(2)}, u32[]{:S(2)}) collective-permute-start(f32[2,16,128]{2,1,0:T(8,128)S(1)} %get-tuple-element.66), channel_id=1, source_target_pairs={{0,16},{16,0},{32,48},{48,32},{64,80},{80,64},{96,112},{112,96},{1... | collective-permute-start | bytes 49160 | tf_op jit(solution)/shard_map/ppermute | solution.py:749
  26.8 4.3 %shard_map.169 = (f32[32,8,128]{2,1,0:T(8,128)S(1)}, f32[8,128]{1,0:T(8,128)S(1)}, bf16[64,640]{1,0:T(8,128)(2,1)S(1)}, bf16[256,384]{1,0:T(8,128)(2,1)S(1)}, bf...) custom-call(bf16[9,8,64]{2,1,0:T(8,128)(2,1)} %bitcast.22, ...), custom_call_target="tpu_custom_call" | custom-call | flops 1000000000 | bytes 2000000 | tf_op jit(solution)/shard_map/pallas_call | solution.py:45
  31.1 0.0 collective-permute-done.4.far_ref
  31.2 0.0 collective-permute-done.5.near_ref
  31.2 1.9 %shard_map.170 = (f32[32,8,128]{2,1,0:T(8,128)S(1)}, f32[3,32,256]{2,1,0:T(8,128)S(1)}) custom-call(f32[40,16,128]{2,1,0:T(8,128)S(1)} %get-tuple-element.64.refs_9_.rows_ref, f32[2,16,128]{2,1,0:T(8,128)S(1)} %collective-permute-done.4.far_ref, f32[2,16,128]{2,1,0:T(8,128)S(1)} %collective-permute-done.5.near_ref, ...), custom_call_target="tpu_custom_call" | custom-call | tf_op jit(solution)/shard_map/pallas_call | solution.py:781
  33.1 37.3 %conditional.1 = (f32[288,128]{1,0:T(8,128)S(1)}) conditional(s32[]{:T(128)} %convert_element_type.3, f32[32,8,128]{2,1,0:T(8,128)S(1)} %get-tuple-element.72, (f32[32,8,128]{2,1,0:T(8,128)S(1)}, f32[8,128]{1,0:T(8,128)S(1)}, bf16[256,256]{1,0:T(8,128)(2,1)S(1)}, bf16[256,256]{1,0:T(8,128)(2,1)S(1)}, bf16[256,256]{1,0:T(8,128)(2,1)S(1)}, ...), branch_computations={%region_0.0_spmd, %region_1.0_spmd} | conditional | bytes 557064 | solution.py:803
  33.1 19.3 %all_to_all.30.x_ref = f32[32,8,128]{2,1,0:T(8,128)S(1)} all-to-all(f32[32,8,128]{2,1,0:T(8,128)S(1)} %get-tuple-element.26), channel_id=1, replica_groups=mesh['lon'=32,'lat'=16] {'lon'}, dimensions={0} | all-to-all | bytes 262144 | tf_op jit(solution)/shard_map/cond/branch_1_fun/all_to_all | solution.py:788
  52.4 1.2 %branch_1_fun.1 = f32[288,128]{1,0:T(8,128)S(1)} custom-call(f32[32,8,128]{2,1,0:T(8,128)S(1)} %all_to_all.30.x_ref, f32[8,128]{1,0:T(8,128)S(1)} %get-tuple-element.27.line_ref, bf16[256,256]{1,0:T(8,128)(2,1)S(1)} %get-tuple-element.28.spread_ref, bf16[256,256]{1,0:T(8,128)(2,1)S(1)} %get-tuple-element.29.spread_low, ...), custom_call_target="tpu_custom_call" | custom-call | tf_op jit(solution)/shard_map/cond/branch_1_fun/pallas_call | solution.py:789
  53.6 16.7 %all_to_all.31 = f32[288,1,128]{2,1,0:T(1,128)S(1)} all-to-all(f32[288,1,128]{2,1,0:T(1,128)S(1)} %bitcast.14), channel_id=1, replica_groups=mesh['lon'=32,'lat'=16] {'lon'}, dimensions={0} | all-to-all | bytes 294912 | tf_op jit(solution)/shard_map/cond/branch_1_fun/all_to_all | solution.py:791
  70.4 1.5 %shard_map.171 = (f32[5,32,256]{2,1,0:T(8,128)S(1)}, f32[64,128]{1,0:T(8,128)S(1)}) custom-call(f32[288,128]{1,0:T(8,128)S(1)} %get-tuple-element.85.x_ref, f32[3,32,256]{2,1,0:T(8,128)S(1)} %get-tuple-element.82.planes_ref), custom_call_target="tpu_custom_call" | custom-call | tf_op jit(solution)/shard_map/pallas_call | solution.py:809
  71.9 15.8 %all_to_all.32 = f32[64,1,128]{2,1,0:T(1,128)S(1)} all-to-all(f32[64,1,128]{2,1,0:T(1,128)S(1)} %bitcast.16), channel_id=1, replica_groups={{0,1,2,3,4,5,6,7,8,9,10,11,12,13,14,15,16,17,18,19,20,21,22,23,24,25,26..., dimensions={0} | all-to-all | bytes 65536 | tf_op jit(solution)/shard_map/all_to_all | solution.py:816
  87.7 0.1 shard_map.172
  87.8 9.1 %all_to_all.33 = f32[8,1,128]{2,1,0:T(1,128)S(1)} all-to-all(f32[8,1,128]{2,1,0:T(1,128)S(1)} %bitcast.18), channel_id=1, replica_groups={{0,64,128,192,256,320,384,448},{1,65,129,193,257,321,385,449},{2,66,130..., dimensions={0} | all-to-all | bytes 8192 | tf_op jit(solution)/shard_map/all_to_all | solution.py:820
  96.9 1.9 %shard_map.173 = (f32[8,24,128]{2,1,0:T(8,128)}, f32[24,128]{1,0:T(8,128)}, f32[24,128]{1,0:T(8,128)}) custom-call(f32[8,128]{1,0:T(8,128)S(1)} %bitcast.17, f32[5,32,256]{2,1,0:T(8,128)S(1)} %get-tuple-element.84.powers_ref, f32[288,128]{1,0:T(8,128)S(1)} %get-tuple-element.85.x_ref), custom_call_target="tpu_custom_call" | custom-call | tf_op jit(solution)/shard_map/pallas_call | solution.py:823
Async XLA Ops:
  1.7 7.2 %collective-permute-start.2 = (f32[13,8,128]{2,1,0:T(8,128)S(1)}, f32[13,8,128]{2,1,0:T(8,128)S(1)}, u32[]{:S(2)}, u32[]{:S(2)}) collective-permute-start(f32[13,8,128]{2,1,0:T(8,128)S(1)} %get-tuple-element.62), channel_id=1, source_target_pairs={{0,1},{1,2},{2,3},{3,4},{4,5},{5,6},{6,7},{7,8},{8,9},{9,10},{10,1... | collective-permute-start | bytes 159752 | tf_op jit(solution)/shard_map/ppermute | solution.py:741
  6.5 6.3 %collective-permute-start.3 = (f32[13,8,128]{2,1,0:T(8,128)S(1)}, f32[13,8,128]{2,1,0:T(8,128)S(1)}, u32[]{:S(2)}, u32[]{:S(2)}) collective-permute-start(f32[13,8,128]{2,1,0:T(8,128)S(1)} %get-tuple-element.63), channel_id=1, source_target_pairs={{1,0},{2,1},{3,2},{4,3},{5,4},{6,5},{7,6},{8,7},{9,8},{10,9},{11,1... | collective-permute-start | bytes 159752 | tf_op jit(solution)/shard_map/ppermute | solution.py:742
  13.0 18.1 %collective-permute-start.4 = (f32[2,16,128]{2,1,0:T(8,128)S(1)}, f32[2,16,128]{2,1,0:T(8,128)S(1)}, u32[]{:S(2)}, u32[]{:S(2)}) collective-permute-start(f32[2,16,128]{2,1,0:T(8,128)S(1)} %get-tuple-element.65), channel_id=1, source_target_pairs={{0,496},{16,32},{32,16},{48,64},{64,48},{80,96},{96,80},{112,128},... | collective-permute-start | bytes 49160 | tf_op jit(solution)/shard_map/ppermute | solution.py:748
  23.4 7.8 %collective-permute-start.5 = (f32[2,16,128]{2,1,0:T(8,128)S(1)}, f32[2,16,128]{2,1,0:T(8,128)S(1)}, u32[]{:S(2)}, u32[]{:S(2)}) collective-permute-start(f32[2,16,128]{2,1,0:T(8,128)S(1)} %get-tuple-element.66), channel_id=1, source_target_pairs={{0,16},{16,0},{32,48},{48,32},{64,80},{80,64},{96,112},{112,96},{1... | collective-permute-start | bytes 49160 | tf_op jit(solution)/shard_map/ppermute | solution.py:749

commit v7 on v6

--- a/solution.py
+++ b/solution.py
@@ -25,7 +25,7 @@
 VMEM_LIMIT = 48 * 1024 * 1024
 
 
-def call(kernel, outs, scratch=()):
+def call(kernel, outs, scratch=(), flops=None):
     spec = pl.BlockSpec(memory_space=pltpu.VMEM)
     return pl.pallas_call(
         kernel,
@@ -45,16 +45,13 @@
     return pl.pallas_call(
         kernel,
         out_shape=outs,
-        in_specs=[pl.BlockSpec(memory_space=pltpu.HBM)] * len(sources) + [spec] * len(rest),
+        in_specs=[pl.BlockSpec(memory_space=pltpu.HBM)] * len(sources),
         out_specs=jax.tree.map(lambda _: spec, outs),
         scratch_shapes=tuple(pltpu.VMEM(source.shape, source.dtype) for source in held)
-        + (pltpu.SemaphoreType.DMA((len(sources),)),)
-        + tuple(scratch),
+        + (pltpu.SemaphoreType.DMA((len(sources),)),),
         compiler_params=pltpu.CompilerParams(vmem_limit_bytes=VMEM_LIMIT),
-        cost_estimate=pl.CostEstimate(
-            flops=flops, bytes_accessed=2 * 10**6, transcendentals=flops // 500
-        ),
-    )(*(pltpu.with_memory_space_constraint(source, pltpu.HBM) for source in sources), *rest)
+        cost_estimate=pl.CostEstimate(flops=10**6, bytes_accessed=2 * 10**6, transcendentals=0),
+    )(*(pltpu.with_memory_space_constraint(source, pltpu.HBM) for source in sources))
 
 
 def slab_kernel(
@@ -75,17 +72,15 @@
         move.start()
     for move in moves:
         move.wait()
-    kept = cutoff_rows(cutoff)
     for target, start in ((top_ref, 0), (bottom_ref, ROWS - DEEP)):
         target[KMT] = kmt[start : start + DEEP].astype(jnp.float32)
-        target[CUT] = kept[start : start + DEEP]
-
-
-def cutoff_rows(cutoff_ref):
-    kept = jnp.broadcast_to(cutoff_ref[...].astype(jnp.float32), (ROWS, ROWS))
-    row = lax.broadcasted_iota(jnp.int32, (ROWS, ROWS), 0)
-    kept = jnp.sum(jnp.where(row == lane_index((ROWS, ROWS)), kept, 0.0), axis=1, keepdims=True)
-    return jnp.broadcast_to(kept, (ROWS, COLS))
+        target[CUT] = cutoff_lanes(cutoff)
+
+
+def cutoff_lanes(cutoff_ref):
+    line = cutoff_ref[...].astype(jnp.float32)
+    line = jnp.concatenate([line, jnp.zeros((1, COLS - ROWS), jnp.float32)], axis=1)
+    return jnp.broadcast_to(line, (DEEP, COLS))
 
 
 def fetch(sources, targets, sems):
@@ -99,9 +94,13 @@
 
 
 def rows_kernel(*refs):
-    for move in fetch(refs[:6], refs[7:13], refs[13]):
+    sources, own_ref, raw, held, sems = refs[:15], refs[15], refs[16:25], refs[25:31], refs[31]
+    moves = fetch(sources, tuple(held) + tuple(raw), sems)
+    for move in moves[: len(held)]:
         move.wait()
-    fill_rows(*refs[7:13], refs[6])
+    fill_rows(*held, own_ref)
+    for move in moves[len(held) :]:
+        move.wait()
 
 
 def fill_rows(temp_ref, kmt_ref, kappa_ref, helm_ref, forcing_ref, cutoff_ref, own_ref):
@@ -112,7 +111,7 @@
     own_ref[:, KAPPA, :] = kappa_ref[...]
     own_ref[:, HELM, :] = helm_ref[...]
     own_ref[:, FORCING, :] = forcing_ref[...]
-    own_ref[:, CUT, :] = cutoff_rows(cutoff_ref)
+    own_ref[:, CUT, :] = jnp.broadcast_to(cutoff_lanes(cutoff_ref)[:1], (ROWS, COLS))
 
 
 def fill_weights(
@@ -163,7 +162,7 @@
     ).astype(jnp.bfloat16)
 
 
-def pack_kernel(own_ref, north_ref, south_ref, rows_ref, far_ref, near_ref):
+def pack_kernel(own_ref, north_ref, south_ref, rows_ref, far_ref, near_ref, cut_ref):
     even = lax.rem(lax.axis_index("lon"), 2) == 0
     rows_ref[DEEP : DEEP + ROWS] = own_ref[...]
     for slab_ref, start in ((north_ref, 0), (south_ref, DEEP + ROWS)):
@@ -171,6 +170,11 @@
         rows_ref[rows, CUT + 1 :, :] = jnp.zeros((DEEP, FIELDS - CUT - 1, COLS), jnp.float32)
         for field in range(CUT + 1):
             rows_ref[rows, field, :] = slab_ref[field]
+    lane = lane_index((DEEP, COLS))
+    north = pltpu.roll(north_ref[CUT], COLS - (ROWS - DEEP), 1)
+    south = pltpu.roll(south_ref[CUT], DEEP + ROWS, 1)
+    own = pltpu.roll(jnp.broadcast_to(own_ref[0, CUT : CUT + 1, :], (DEEP, COLS)), DEEP, 1)
+    cut_ref[...] = jnp.where(lane < DEEP, north, jnp.where(lane < DEEP + ROWS, own, south))
     lane = lane_index((FIELDS, COLS))
     for part in range(TALL // SLOTS):
         first = jnp.zeros((FIELDS, COLS), jnp.float32)
@@ -274,18 +278,14 @@
 
 
 def interior_kernel(*refs):
-    sources, rows_ref, refs = refs[:9], refs[9], refs[10:]
-    out_ref, line_ref, weights, tables, refs = refs[0], refs[1], refs[2:6], refs[6:14], refs[14:]
-    held, sems = refs[:7], refs[7]
-    start, mask_odd, mask_even, act_a, act_b = refs[8:]
-    moves = fetch(sources, tuple(held) + tuple(tables[6:]), sems)
+    rows_ref, cut_ref, raw, refs = refs[0], refs[1], refs[2:9], refs[9:]
+    out_ref, line_ref, weights, tables, refs = refs[0], refs[1], refs[2:6], refs[6:12], refs[12:]
+    start, mask_odd, mask_even, act_a, act_b = refs
+    fill_weights(*raw[:4], *weights)
+    for index, table in enumerate(raw[4:]):
+        tables[2 * index][...], tables[2 * index + 1][...] = halves(table[...])
     for row in range(TALL):
         start[row * FIELDS : (row + 1) * FIELDS] = first_input(rows_ref[row])
-    for move in moves:
-        move.wait()
-    fill_weights(*held[:4], *weights)
-    for index, table in enumerate(held[4:]):
-        tables[2 * index][...], tables[2 * index + 1][...] = halves(table[...])
     results = closure_layers(
         lambda chunk: start[2 * FIELDS * chunk : 2 * FIELDS * (chunk + 2)],
         TALL // 2 - 1,
@@ -303,8 +303,9 @@
                 rows_ref[row + 1],
                 closure[LEV * parity : LEV * (parity + 1)],
             )
-    own_line = lax.axis_index("lon") + FIRST
-    line_ref[...] = rows_ref[own_line, LEV:FIELDS, :]
+    own_line = lane_index((LEV, COLS)) == lax.axis_index("lon") + FIRST
+    kept = jnp.sum(jnp.where(own_line, cut_ref[...], 0.0), axis=1, keepdims=True)
+    line_ref[...] = jnp.broadcast_to(kept, (LEV, COLS))
 
 
 STRIP = 32
@@ -458,7 +459,7 @@
     s = s[:, 0:width].reshape(shape) + partner(s[:, width:].reshape(shape)) * sign
     wave = lax.broadcasted_iota(jnp.int32, shape, 0) + blocks * lane_index(shape)
     folded = jnp.minimum(wave, length - wave).astype(jnp.float32)
-    s = jnp.where(folded < line_ref[CUT - LEV : CUT - LEV + 1, :][None], s, 0.0)
+    s = jnp.where(folded < line_ref[0:1, :][None], s, 0.0)
     y = split_dot(halves(s.reshape(flat)), inner)
     y = y[:, 0:width].reshape(shape) - partner(y[:, width:].reshape(shape)) * sign
     y = y * twist_re_ref[...] - partner(y) * twist_im_ref[...]
@@ -535,15 +536,17 @@
     return quick_sum(p, e + (a[0] * b[1] + a[1] * b[0]))
 
 
-def pair_div(a, b):
-    q = a[0] / b[0]
-    rest = pair_add(a, pair_neg(pair_mul((q, jnp.zeros_like(q)), b)))
-    r = rest[0] / b[0]
-    rest = pair_add(rest, pair_neg(pair_mul((r, jnp.zeros_like(r)), b)))
-    return quick_sum(*quick_sum(q, r + rest[0] / b[0]))
-
-
-def powers_kernel(x_ref, planes_ref, powers_ref, parts_ref):
+def pair_inverse(a):
+    x = 1.0 / a[0]
+    p, e = two_product(a[0], x)
+    return quick_sum(x, x * (((1.0 - p) - e) - a[1] * x))
+
+
+def powers_kernel(x_ref, planes_ref, temp_hbm, powers_ref, parts_ref, temp, sem):
+    for level in range(LEV):
+        temp[level] = x_ref[pl.ds(HALO * BLOCK + level, ROWS, stride=BLOCK), :]
+    move = pltpu.make_async_copy(temp, temp_hbm, sem)
+    move.start()
     lane = lane_index((LEV, COLS))
     wide_lane = lane_index((MID, COLS))
     kmt_left = planes_ref[0, :, 0:COLS]
@@ -619,6 +622,7 @@
     message = jnp.where(lane == spot, total[0], 0.0) + jnp.where(lane == spot + 64, total[1], 0.0)
     message = jnp.sum(message, axis=0, keepdims=True)
     parts_ref[...] = jnp.broadcast_to(message, parts_ref.shape)
+    move.wait()
 
 
 def sum_messages(parts_ref):
@@ -647,13 +651,7 @@
     out_ref[...] = jnp.where(lane < 64, total[0], total[1])
 
 
-def combine_kernel(
-    parts_ref, powers_ref, x_ref, temp_hbm, surface_ref, residual_ref, wide, temp, sem
-):
-    for level in range(LEV):
-        temp[level] = x_ref[pl.ds(HALO * BLOCK + level, ROWS, stride=BLOCK), :]
-    move = pltpu.make_async_copy(temp, temp_hbm, sem)
-    move.start()
+def combine_kernel(parts_ref, powers_ref, surface_ref, residual_ref, wide):
     total = sum_messages(parts_ref)
     moments = [
         tuple(jnp.broadcast_to(t[:, order : order + 1], (8, COLS)) for t in total)
@@ -667,19 +665,19 @@
     way = [one] + [zero] * ITERS
     sol = [zero] * ITERS
     for step in range(ITERS):
-        alpha = pair_div(rho[step], delta[step + 1])
+        inverse = pair_inverse(delta[step + 1])
+        alpha = pair_mul(rho[step], inverse)
         sol = [s + alpha[0] * w for s, w in zip(sol, way)]
         res = [res[0]] + [r - alpha[0] * w for r, w in zip(res[1:], way)]
         if step == ITERS - 1:
             break
-        before = rho[step]
         last = 2 * ITERS - 1 - step
         rho = [
             None if order <= step or order >= last
             else pair_add(rho[order], pair_neg(pair_mul(alpha, delta[order + 1])))
             for order in range(2 * ITERS)
         ]
-        beta = pair_neg(pair_mul(alpha, pair_div(rho[step + 1], before)))
+        beta = pair_neg(pair_mul(rho[step + 1], inverse))
         delta = [
             None if order <= step or order >= last
             else pair_add(rho[order], pair_mul(beta, delta[order]))
@@ -695,7 +693,6 @@
                     value = value + weights[index] * powers_ref[(index,) + spot]
                 wide[spot] = value * factor
         target[...] = wide[HALO : HALO + ROWS, HALO : HALO + COLS]
-    move.wait()
 
 
 def forward(axis, periodic):
@@ -740,16 +737,22 @@
     )(*(pltpu.with_memory_space_constraint(field, pltpu.HBM) for field in fields))
     north = lax.ppermute(bottom, "lat", forward("lat", False))
     south = lax.ppermute(top, "lat", backward("lat", False))
-    own = fetching(rows_kernel, shape((ROWS, FIELDS, COLS), f32), fields, fields)
+    tables = tuple(jnp.asarray(table) for table in filter_tables(blocks, COLS))
+    sources = (jnp.transpose(conv_in, (0, 2, 1)), conv_mid, conv_late, conv_out) + tables
+    own, *raw = fetching(
+        rows_kernel,
+        (shape((ROWS, FIELDS, COLS), f32),)
+        + tuple(shape(source.shape, source.dtype) for source in sources),
+        fields + sources,
+        fields,
+    )
     ends = shape((TALL // SLOTS, FIELDS, COLS), f32)
-    rows, to_far, to_near = call(
-        pack_kernel, (shape((TALL, FIELDS, COLS), f32), ends, ends)
+    rows, to_far, to_near, cuts = call(
+        pack_kernel, (shape((TALL, FIELDS, COLS), f32), ends, ends, shape((DEEP, COLS), f32))
     )(own, north, south)
     far = lax.ppermute(to_far, "lon", swap_far())
     near = lax.ppermute(to_near, "lon", swap_near())
 
-    tables = [jnp.asarray(table) for table in filter_tables(blocks, COLS)]
-    sources = (jnp.transpose(conv_in, (0, 2, 1)), conv_mid, conv_late, conv_out, *tables)
     outs = (
         shape((4 * FIELDS, 640), bf16),
         shape((256, 384), bf16),
@@ -757,7 +760,6 @@
         shape((48, 256), bf16),
     )
     outs = outs + tuple(shape(table.shape, bf16) for table in tables[:3] for _ in range(2))
-    outs = outs + tuple(shape(table.shape, f32) for table in tables[3:])
     def closure_scratch(chunks):
         cells = chunks * COLS
         return (
@@ -768,16 +770,13 @@
         )
 
     block = shape((MID, LEV, COLS), f32)
-    inside, line, *prepared = fetching(
+    inside, line, *prepared = call(
         interior_kernel,
         (block, shape((LEV, COLS), f32)) + outs,
-        sources,
-        sources[:7],
-        (rows,),
         (pltpu.VMEM((TALL * FIELDS, COLS), bf16),) + closure_scratch(19),
         10**9,
-    )
-    weights, tables = prepared[:4], prepared[4:]
+    )(rows, cuts, *raw[:7])
+    weights, tables = prepared[:4], prepared[4:] + raw[7:]
     lines, planes = call(
         edge_kernel,
         (block, shape((3, MID, 2 * COLS), f32)),
@@ -806,12 +805,17 @@
     both = ("lon", "lat")
     inner = [[wide * i + k for k in range(wide)] for i in range(8)]
     outer = [[wide * i + k for i in range(8)] for k in range(wide)]
-    powers, parts = call(
+    temp_new, powers, parts = pl.pallas_call(
         powers_kernel,
-        (
+        out_shape=(
+            shape((LEV, ROWS, COLS), f32),
             shape((ITERS + 1, MID, 2 * COLS), f32),
             shape((wide, COLS), f32),
         ),
+        in_specs=[vmem] * 2,
+        out_specs=(pl.BlockSpec(memory_space=pltpu.HBM), vmem, vmem),
+        scratch_shapes=(pltpu.VMEM((LEV, ROWS, COLS), f32), pltpu.SemaphoreType.DMA),
+        compiler_params=pltpu.CompilerParams(vmem_limit_bytes=VMEM_LIMIT),
     )(back, planes)
     parts = lax.all_to_all(
         parts, both, split_axis=0, concat_axis=0, tiled=True, axis_index_groups=inner
@@ -820,22 +824,11 @@
     parts = lax.all_to_all(
         parts, both, split_axis=0, concat_axis=0, tiled=True, axis_index_groups=outer
     )
-    temp_new, surface, residual = pl.pallas_call(
+    surface, residual = call(
         combine_kernel,
-        out_shape=(
-            shape((LEV, ROWS, COLS), f32),
-            shape((ROWS, COLS), f32),
-            shape((ROWS, COLS), f32),
-        ),
-        in_specs=[vmem] * 3,
-        out_specs=(pl.BlockSpec(memory_space=pltpu.HBM), vmem, vmem),
-        scratch_shapes=(
-            pltpu.VMEM((MID, 2 * COLS), f32),
-            pltpu.VMEM((LEV, ROWS, COLS), f32),
-            pltpu.SemaphoreType.DMA,
-        ),
-        compiler_params=pltpu.CompilerParams(vmem_limit_bytes=VMEM_LIMIT),
-    )(parts, powers, back)
+        (shape((ROWS, COLS), f32), shape((ROWS, COLS), f32)),
+        (pltpu.VMEM((MID, 2 * COLS), f32),),
+    )(parts, powers)
     return temp_new, surface, residual
 
 

time: 99.3 us -> 98.9 us (level)
  Pallas kernels: 13.4 us -> 12.1 us
  blocking collectives: 61 us -> 62.3 us
    pallas_call x2 -> x1, Pallas kernels: 5.39 us -> 1.59 us  [fetching(): pl.pallas_call(kernel, out_shape=outs, in_specs=[pl.BlockSpec(memory_spac...]
    pallas_call x3 -> x4, Pallas kernels: 3.72 us -> 6.3 us  [the longest x1 2.98 us: body(): call(interior_kernel, (block, shape((LEV, COLS), f32)) + outs, (pltpu.VME...]
    all_to_all x1, blocking collectives: 19.3 us -> 20.7 us  [filtered_block(): lax.all_to_all(lines, 'lon', split_axis=0, concat_axis=0, tiled=True)]
where the time goes in v7:
time: 98.9 us; the launch traced here: 98.5 us
  blocking collectives  62.3 us (63%)
  starting transfers between devices  19.9 us (20%)
  Pallas kernels  12.1 us (12%)
  waiting for transfers between devices  3.37 us (3%)
    all_to_all x2, blocking collectives, body(): lax.all_to_all(parts, both, split_axis=0, concat_axis=0, tiled=True, axis...  24.9 us
    all_to_all x1, blocking collectives, filtered_block(): lax.all_to_all(lines, 'lon', split_axis=0, concat_axis=0, tiled=True)  20.7 us
    all_to_all x1, blocking collectives, filtered_block(): lax.all_to_all(result, 'lon', split_axis=0, concat_axis=0, tiled=True)  16.7 us
    ppermute x1, starting transfers between devices, body(): far = lax.ppermute(to_far, 'lon', swap_far())  10.3 us
    ppermute x1, starting transfers between devices, body(): north = lax.ppermute(bottom, 'lat', forward('lat', False))  4.83 us
    ppermute x1, starting transfers between devices, body(): near = lax.ppermute(to_near, 'lon', swap_near())  3.42 us
    ppermute x1, waiting for transfers between devices, body(): south = lax.ppermute(top, 'lat', backward('lat', False))  3.36 us
    pallas_call x1, Pallas kernels, body(): call(interior_kernel, (block, shape((LEV, COLS), f32)) + outs, (pltpu.VME...  2.98 us
  transfers between devices with their start and end apart: 4, of which 1 were waited for; matrix products, arithmetic and copies ran while one was open for 0% of the time, Pallas kernels for 5%

profile of v7, /device:TPU:1, one launch (start us, length us, event | category | flops | bytes accessed | tf_op | source)
XLA Modules:
  0.0 98.5 jit_solution(10920050967061162409)
XLA Ops:
  0.6 1.0 shard_map.167
  1.6 4.8 %collective-permute-start.2 = (f32[13,8,128]{2,1,0:T(8,128)S(1)}, f32[13,8,128]{2,1,0:T(8,128)S(1)}, u32[]{:S(2)}, u32[]{:S(2)}) collective-permute-start(f32[13,8,128]{2,1,0:T(8,128)S(1)} %get-tuple-element.75), channel_id=1, source_target_pairs={{0,1},{1,2},{2,3},{3,4},{4,5},{5,6},{6,7},{7,8},{8,9},{9,10},{10,1... | collective-permute-start | bytes 159752 | tf_op jit(solution)/shard_map/ppermute | solution.py:738
  6.4 1.3 %collective-permute-start.3 = (f32[13,8,128]{2,1,0:T(8,128)S(1)}, f32[13,8,128]{2,1,0:T(8,128)S(1)}, u32[]{:S(2)}, u32[]{:S(2)}) collective-permute-start(f32[13,8,128]{2,1,0:T(8,128)S(1)} %get-tuple-element.76), channel_id=1, source_target_pairs={{1,0},{2,1},{3,2},{4,3},{5,4},{6,5},{7,6},{8,7},{9,8},{10,9},{11,1... | collective-permute-start | bytes 159752 | tf_op jit(solution)/shard_map/ppermute | solution.py:739
  7.7 1.6 %shard_map.166 = (f32[24,16,128]{2,1,0:T(8,128)S(1)}, bf16[9,8,64]{2,1,0:T(8,128)(2,1)S(1)}, bf16[9,64,64]{2,1,0:T(8,128)(2,1)S(1)}, bf16[9,64,64]{2,1,0:T(8,128...) custom-call(f32[8,24,128]{2,1,0:T(8,128)} %temp_hbm.1, ...), custom_call_target="tpu_custom_call" | custom-call | flops 1000000 | bytes 2000000 | tf_op jit(solution)/shard_map/pallas_call | solution.py:45
  9.3 0.0 collective-permute-done.2.north_ref
  9.3 3.4 %collective-permute-done.3.south_ref = f32[13,8,128]{2,1,0:T(8,128)S(1)} collective-permute-done((f32[13,8,128]{2,1,0:T(8,128)S(1)}, f32[13,8,128]{2,1,0:T(8,128)S(1)}, u32[]{:S(2)}, u32[]{:S(2)}) %collective-permute-start.3) | collective-permute-done | bytes 53280 | tf_op jit(solution)/shard_map/ppermute | solution.py:739
  12.7 0.3 shard_map.168
  13.0 10.3 %collective-permute-start.4 = (f32[2,16,128]{2,1,0:T(8,128)S(1)}, f32[2,16,128]{2,1,0:T(8,128)S(1)}, u32[]{:S(2)}, u32[]{:S(2)}) collective-permute-start(f32[2,16,128]{2,1,0:T(8,128)S(1)} %get-tuple-element.78), channel_id=1, source_target_pairs={{0,496},{16,32},{32,16},{48,64},{64,48},{80,96},{96,80},{112,128},... | collective-permute-start | bytes 49160 | tf_op jit(solution)/shard_map/ppermute | solution.py:753
  23.3 3.4 %collective-permute-start.5 = (f32[2,16,128]{2,1,0:T(8,128)S(1)}, f32[2,16,128]{2,1,0:T(8,128)S(1)}, u32[]{:S(2)}, u32[]{:S(2)}) collective-permute-start(f32[2,16,128]{2,1,0:T(8,128)S(1)} %get-tuple-element.79), channel_id=1, source_target_pairs={{0,16},{16,0},{32,48},{48,32},{64,80},{80,64},{96,112},{112,96},{1... | collective-permute-start | bytes 49160 | tf_op jit(solution)/shard_map/ppermute | solution.py:754
  26.7 3.0 %shard_map.169 = (f32[32,8,128]{2,1,0:T(8,128)S(1)}, f32[8,128]{1,0:T(8,128)S(1)}, bf16[64,640]{1,0:T(8,128)(2,1)S(1)}, bf16[256,384]{1,0:T(8,128)(2,1)S(1)}, bf...) custom-call(f32[40,16,128]{2,1,0:T(8,128)S(1)} %get-tuple-element.77, ...), custom_call_target="tpu_custom_call" | custom-call | tf_op jit(solution)/shard_map/pallas_call | solution.py:773
  29.7 0.0 collective-permute-done.4.far_ref
  29.7 0.0 collective-permute-done.5.near_ref
  29.7 1.9 %shard_map.170 = (f32[32,8,128]{2,1,0:T(8,128)S(1)}, f32[3,32,256]{2,1,0:T(8,128)S(1)}) custom-call(f32[40,16,128]{2,1,0:T(8,128)S(1)} %get-tuple-element.77.refs_0_.rows_ref, f32[2,16,128]{2,1,0:T(8,128)S(1)} %collective-permute-done.4.far_ref, f32[2,16,128]{2,1,0:T(8,128)S(1)} %collective-permute-done.5.near_ref, ...), custom_call_target="tpu_custom_call" | custom-call | tf_op jit(solution)/shard_map/pallas_call | solution.py:780
  31.7 38.7 %conditional.1 = (f32[288,128]{1,0:T(8,128)S(1)}) conditional(s32[]{:T(128)} %convert_element_type.3, f32[32,8,128]{2,1,0:T(8,128)S(1)} %get-tuple-element.93, (f32[32,8,128]{2,1,0:T(8,128)S(1)}, f32[8,128]{1,0:T(8,128)S(1)}, bf16[256,256]{1,0:T(8,128)(2,1)S(1)}, bf16[256,256]{1,0:T(8,128)(2,1)S(1)}, bf16[256,256]{1,0:T(8,128)(2,1)S(1)}, ...), branch_computations={%region_0.0_spmd, %region_1.0_spmd} | conditional | bytes 557064 | solution.py:802
  31.7 20.7 %all_to_all.30.x_ref = f32[32,8,128]{2,1,0:T(8,128)S(1)} all-to-all(f32[32,8,128]{2,1,0:T(8,128)S(1)} %get-tuple-element.26), channel_id=1, replica_groups=mesh['lon'=32,'lat'=16] {'lon'}, dimensions={0} | all-to-all | bytes 262144 | tf_op jit(solution)/shard_map/cond/branch_1_fun/all_to_all | solution.py:787
  52.4 1.2 %branch_1_fun.1 = f32[288,128]{1,0:T(8,128)S(1)} custom-call(f32[32,8,128]{2,1,0:T(8,128)S(1)} %all_to_all.30.x_ref, f32[8,128]{1,0:T(8,128)S(1)} %get-tuple-element.27.line_ref, bf16[256,256]{1,0:T(8,128)(2,1)S(1)} %get-tuple-element.28.spread_ref, bf16[256,256]{1,0:T(8,128)(2,1)S(1)} %get-tuple-element.29.spread_low, ...), custom_call_target="tpu_custom_call" | custom-call | tf_op jit(solution)/shard_map/cond/branch_1_fun/pallas_call | solution.py:788
  53.6 16.7 %all_to_all.31 = f32[288,1,128]{2,1,0:T(1,128)S(1)} all-to-all(f32[288,1,128]{2,1,0:T(1,128)S(1)} %bitcast.14), channel_id=1, replica_groups=mesh['lon'=32,'lat'=16] {'lon'}, dimensions={0} | all-to-all | bytes 294912 | tf_op jit(solution)/shard_map/cond/branch_1_fun/all_to_all | solution.py:790
  70.3 1.9 %shard_map.171 = (f32[8,24,128]{2,1,0:T(8,128)}, f32[5,32,256]{2,1,0:T(8,128)S(1)}, f32[64,128]{1,0:T(8,128)S(1)}) custom-call(f32[288,128]{1,0:T(8,128)S(1)} %get-tuple-element.109.x_ref, f32[3,32,256]{2,1,0:T(8,128)S(1)} %get-tuple-element.103.planes_ref), custom_call_target="tpu_custom_call" | custom-call | tf_op jit(solution)/shard_map/pallas_call | solution.py:808
  72.3 15.8 %all_to_all.32 = f32[64,1,128]{2,1,0:T(1,128)S(1)} all-to-all(f32[64,1,128]{2,1,0:T(1,128)S(1)} %bitcast.16), channel_id=1, replica_groups={{0,1,2,3,4,5,6,7,8,9,10,11,12,13,14,15,16,17,18,19,20,21,22,23,24,25,26..., dimensions={0} | all-to-all | bytes 65536 | tf_op jit(solution)/shard_map/all_to_all | solution.py:820
  88.0 0.1 shard_map.172
  88.2 9.1 %all_to_all.33 = f32[8,1,128]{2,1,0:T(1,128)S(1)} all-to-all(f32[8,1,128]{2,1,0:T(1,128)S(1)} %bitcast.17), channel_id=1, replica_groups={{0,64,128,192,256,320,384,448},{1,65,129,193,257,321,385,449},{2,66,130..., dimensions={0} | all-to-all | bytes 8192 | tf_op jit(solution)/shard_map/all_to_all | solution.py:824
  97.3 1.1 %shard_map.173 = (f32[24,128]{1,0:T(8,128)}, f32[24,128]{1,0:T(8,128)}) custom-call(f32[8,128]{1,0:T(8,128)S(1)} %bitcast.18, f32[5,32,256]{2,1,0:T(8,128)S(1)} %get-tuple-element.106.powers_ref), custom_call_target="tpu_custom_call" | custom-call | tf_op jit(solution)/shard_map/pallas_call | solution.py:827
Async XLA Ops:
  1.6 7.7 %collective-permute-start.2 = (f32[13,8,128]{2,1,0:T(8,128)S(1)}, f32[13,8,128]{2,1,0:T(8,128)S(1)}, u32[]{:S(2)}, u32[]{:S(2)}) collective-permute-start(f32[13,8,128]{2,1,0:T(8,128)S(1)} %get-tuple-element.75), channel_id=1, source_target_pairs={{0,1},{1,2},{2,3},{3,4},{4,5},{5,6},{6,7},{7,8},{8,9},{9,10},{10,1... | collective-permute-start | bytes 159752 | tf_op jit(solution)/shard_map/ppermute | solution.py:738
  6.4 6.3 %collective-permute-start.3 = (f32[13,8,128]{2,1,0:T(8,128)S(1)}, f32[13,8,128]{2,1,0:T(8,128)S(1)}, u32[]{:S(2)}, u32[]{:S(2)}) collective-permute-start(f32[13,8,128]{2,1,0:T(8,128)S(1)} %get-tuple-element.76), channel_id=1, source_target_pairs={{1,0},{2,1},{3,2},{4,3},{5,4},{6,5},{7,6},{8,7},{9,8},{10,9},{11,1... | collective-permute-start | bytes 159752 | tf_op jit(solution)/shard_map/ppermute | solution.py:739
  13.0 16.8 %collective-permute-start.4 = (f32[2,16,128]{2,1,0:T(8,128)S(1)}, f32[2,16,128]{2,1,0:T(8,128)S(1)}, u32[]{:S(2)}, u32[]{:S(2)}) collective-permute-start(f32[2,16,128]{2,1,0:T(8,128)S(1)} %get-tuple-element.78), channel_id=1, source_target_pairs={{0,496},{16,32},{32,16},{48,64},{64,48},{80,96},{96,80},{112,128},... | collective-permute-start | bytes 49160 | tf_op jit(solution)/shard_map/ppermute | solution.py:753
  23.3 6.4 %collective-permute-start.5 = (f32[2,16,128]{2,1,0:T(8,128)S(1)}, f32[2,16,128]{2,1,0:T(8,128)S(1)}, u32[]{:S(2)}, u32[]{:S(2)}) collective-permute-start(f32[2,16,128]{2,1,0:T(8,128)S(1)} %get-tuple-element.79), channel_id=1, source_target_pairs={{0,16},{16,0},{32,48},{48,32},{64,80},{80,64},{96,112},{112,96},{1... | collective-permute-start | bytes 49160 | tf_op jit(solution)/shard_map/ppermute | solution.py:754

commit v8 on v7

--- a/solution.py
+++ b/solution.py
@@ -542,11 +542,12 @@
     return quick_sum(x, x * (((1.0 - p) - e) - a[1] * x))
 
 
-def powers_kernel(x_ref, planes_ref, temp_hbm, powers_ref, parts_ref, temp, sem):
+def powers_kernel(x_ref, planes_ref, temp_hbm, powers_ref, parts_ref, temp, sems):
+    moves = []
     for level in range(LEV):
         temp[level] = x_ref[pl.ds(HALO * BLOCK + level, ROWS, stride=BLOCK), :]
-    move = pltpu.make_async_copy(temp, temp_hbm, sem)
-    move.start()
+        moves.append(pltpu.make_async_copy(temp.at[level], temp_hbm.at[level], sems.at[level]))
+        moves[-1].start()
     lane = lane_index((LEV, COLS))
     wide_lane = lane_index((MID, COLS))
     kmt_left = planes_ref[0, :, 0:COLS]
@@ -622,21 +623,14 @@
     message = jnp.where(lane == spot, total[0], 0.0) + jnp.where(lane == spot + 64, total[1], 0.0)
     message = jnp.sum(message, axis=0, keepdims=True)
     parts_ref[...] = jnp.broadcast_to(message, parts_ref.shape)
-    move.wait()
+    for move in moves:
+        move.wait()
 
 
 def sum_messages(parts_ref):
     count = parts_ref.shape[0] // 8
-    if count == 1:
-        total = (parts_ref[...], jnp.zeros((8, COLS), jnp.float32))
-        for by in (4, 2, 1):
-            total = pair_add(total, tuple(pltpu.roll(t, by, 0) for t in total))
-        return pair_add(total, tuple(pltpu.roll(t, 64, 1) for t in total))
-    tiles = [(parts_ref[8 * i : 8 * i + 8, :], None) for i in range(count)]
-    merged = []
-    for a, b in zip(tiles[::2], tiles[1::2]):
-        merged.append(two_sum(a[0], b[0]))
-    tiles = merged
+    tiles = [parts_ref[8 * i : 8 * i + 8, :] for i in range(count)]
+    tiles = [two_sum(a, b) for a, b in zip(tiles[::2], tiles[1::2])]
     while len(tiles) > 1:
         tiles = [pair_add(a, b) for a, b in zip(tiles[::2], tiles[1::2])]
     total = tiles[0]
@@ -648,7 +642,8 @@
 def merge_kernel(parts_ref, out_ref):
     total = sum_messages(parts_ref)
     lane = lane_index((8, COLS))
-    out_ref[...] = jnp.where(lane < 64, total[0], total[1])
+    merged = jnp.where(lane < 64, total[0], total[1])
+    out_ref[...] = jnp.broadcast_to(merged[:1], out_ref.shape)
 
 
 def combine_kernel(parts_ref, powers_ref, surface_ref, residual_ref, wide):
@@ -705,6 +700,15 @@
     return [(target, source) for source, target in forward(axis, periodic)]
 
 
+def reduction_groups(lon, lat):
+    inner, outer = {}, {}
+    for i in range(lon):
+        for j in range(lat):
+            inner.setdefault((i // 4, j // 4), []).append(i * lat + j)
+            outer.setdefault((i % 4, j % 4), []).append(i * lat + j)
+    return list(inner.values()), list(outer.values())
+
+
 def swap_near():
     return [(i, i ^ 1) for i in range(lax.axis_size("lon"))]
 
@@ -801,10 +805,9 @@
     polar = (top_row < BAND) | (top_row + MID > ROWS * lax.axis_size("lat") - BAND)
     back = lax.cond(polar, filtered_block, plain_block, lines, line, tables)
     everyone = blocks * lax.axis_size("lat")
-    wide = everyone // 8
     both = ("lon", "lat")
-    inner = [[wide * i + k for k in range(wide)] for i in range(8)]
-    outer = [[wide * i + k for i in range(8)] for k in range(wide)]
+    inner, outer = reduction_groups(blocks, lax.axis_size("lat"))
+    wide = len(inner[0])
     temp_new, powers, parts = pl.pallas_call(
         powers_kernel,
         out_shape=(
@@ -814,13 +817,13 @@
         ),
         in_specs=[vmem] * 2,
         out_specs=(pl.BlockSpec(memory_space=pltpu.HBM), vmem, vmem),
-        scratch_shapes=(pltpu.VMEM((LEV, ROWS, COLS), f32), pltpu.SemaphoreType.DMA),
+        scratch_shapes=(pltpu.VMEM((LEV, ROWS, COLS), f32), pltpu.SemaphoreType.DMA((LEV,))),
         compiler_params=pltpu.CompilerParams(vmem_limit_bytes=VMEM_LIMIT),
     )(back, planes)
     parts = lax.all_to_all(
         parts, both, split_axis=0, concat_axis=0, tiled=True, axis_index_groups=inner
     )
-    parts = call(merge_kernel, shape((8, COLS), f32))(parts)
+    parts = call(merge_kernel, shape((everyone // wide, COLS), f32))(parts)
     parts = lax.all_to_all(
         parts, both, split_axis=0, concat_axis=0, tiled=True, axis_index_groups=outer
     )

time: 98.9 us -> 98.6 us (level)
  no operation moved by 1% of the time
where the time goes in v8:
time: 98.6 us; the launch traced here: 98.2 us
  blocking collectives  61.8 us (63%)
  starting transfers between devices  19.9 us (20%)
  Pallas kernels  12.3 us (12%)
  waiting for transfers between devices  3.37 us (3%)
    all_to_all x2, blocking collectives, body(): lax.all_to_all(parts, both, split_axis=0, concat_axis=0, tiled=True, axis...  24.4 us
    all_to_all x1, blocking collectives, filtered_block(): lax.all_to_all(lines, 'lon', split_axis=0, concat_axis=0, tiled=True)  20.7 us
    all_to_all x1, blocking collectives, filtered_block(): lax.all_to_all(result, 'lon', split_axis=0, concat_axis=0, tiled=True)  16.7 us
    ppermute x1, starting transfers between devices, body(): far = lax.ppermute(to_far, 'lon', swap_far())  10.3 us
    ppermute x1, starting transfers between devices, body(): north = lax.ppermute(bottom, 'lat', forward('lat', False))  4.83 us
    ppermute x1, starting transfers between devices, body(): near = lax.ppermute(to_near, 'lon', swap_near())  3.42 us
    ppermute x1, waiting for transfers between devices, body(): south = lax.ppermute(top, 'lat', backward('lat', False))  3.36 us
    pallas_call x1, Pallas kernels, body(): call(interior_kernel, (block, shape((LEV, COLS), f32)) + outs, (pltpu.VME...  2.98 us
  transfers between devices with their start and end apart: 4, of which 1 were waited for; matrix products, arithmetic and copies ran while one was open for 0% of the time, Pallas kernels for 5%

profile of v8, /device:TPU:1, one launch (start us, length us, event | category | flops | bytes accessed | tf_op | source)
XLA Modules:
  0.0 98.2 jit_solution(8348897985556380862)
XLA Ops:
  0.6 1.0 shard_map.167
  1.6 4.8 %collective-permute-start.2 = (f32[13,8,128]{2,1,0:T(8,128)S(1)}, f32[13,8,128]{2,1,0:T(8,128)S(1)}, u32[]{:S(2)}, u32[]{:S(2)}) collective-permute-start(f32[13,8,128]{2,1,0:T(8,128)S(1)} %get-tuple-element.75), channel_id=1, source_target_pairs={{0,1},{1,2},{2,3},{3,4},{4,5},{5,6},{6,7},{7,8},{8,9},{9,10},{10,1... | collective-permute-start | bytes 159752 | tf_op jit(solution)/shard_map/ppermute | solution.py:742
  6.4 1.3 %collective-permute-start.3 = (f32[13,8,128]{2,1,0:T(8,128)S(1)}, f32[13,8,128]{2,1,0:T(8,128)S(1)}, u32[]{:S(2)}, u32[]{:S(2)}) collective-permute-start(f32[13,8,128]{2,1,0:T(8,128)S(1)} %get-tuple-element.76), channel_id=1, source_target_pairs={{1,0},{2,1},{3,2},{4,3},{5,4},{6,5},{7,6},{8,7},{9,8},{10,9},{11,1... | collective-permute-start | bytes 159752 | tf_op jit(solution)/shard_map/ppermute | solution.py:743
  7.7 1.6 %shard_map.166 = (f32[24,16,128]{2,1,0:T(8,128)S(1)}, bf16[9,8,64]{2,1,0:T(8,128)(2,1)S(1)}, bf16[9,64,64]{2,1,0:T(8,128)(2,1)S(1)}, bf16[9,64,64]{2,1,0:T(8,128...) custom-call(f32[8,24,128]{2,1,0:T(8,128)} %temp_hbm.1, ...), custom_call_target="tpu_custom_call" | custom-call | flops 1000000 | bytes 2000000 | tf_op jit(solution)/shard_map/pallas_call | solution.py:45
  9.3 0.0 collective-permute-done.2.north_ref
  9.3 3.4 %collective-permute-done.3.south_ref = f32[13,8,128]{2,1,0:T(8,128)S(1)} collective-permute-done((f32[13,8,128]{2,1,0:T(8,128)S(1)}, f32[13,8,128]{2,1,0:T(8,128)S(1)}, u32[]{:S(2)}, u32[]{:S(2)}) %collective-permute-start.3) | collective-permute-done | bytes 53280 | tf_op jit(solution)/shard_map/ppermute | solution.py:743
  12.7 0.3 shard_map.168
  13.0 10.3 %collective-permute-start.4 = (f32[2,16,128]{2,1,0:T(8,128)S(1)}, f32[2,16,128]{2,1,0:T(8,128)S(1)}, u32[]{:S(2)}, u32[]{:S(2)}) collective-permute-start(f32[2,16,128]{2,1,0:T(8,128)S(1)} %get-tuple-element.78), channel_id=1, source_target_pairs={{0,496},{16,32},{32,16},{48,64},{64,48},{80,96},{96,80},{112,128},... | collective-permute-start | bytes 49160 | tf_op jit(solution)/shard_map/ppermute | solution.py:757
  23.3 3.4 %collective-permute-start.5 = (f32[2,16,128]{2,1,0:T(8,128)S(1)}, f32[2,16,128]{2,1,0:T(8,128)S(1)}, u32[]{:S(2)}, u32[]{:S(2)}) collective-permute-start(f32[2,16,128]{2,1,0:T(8,128)S(1)} %get-tuple-element.79), channel_id=1, source_target_pairs={{0,16},{16,0},{32,48},{48,32},{64,80},{80,64},{96,112},{112,96},{1... | collective-permute-start | bytes 49160 | tf_op jit(solution)/shard_map/ppermute | solution.py:758
  26.7 3.0 %shard_map.169 = (f32[32,8,128]{2,1,0:T(8,128)S(1)}, f32[8,128]{1,0:T(8,128)S(1)}, bf16[64,640]{1,0:T(8,128)(2,1)S(1)}, bf16[256,384]{1,0:T(8,128)(2,1)S(1)}, bf...) custom-call(f32[40,16,128]{2,1,0:T(8,128)S(1)} %get-tuple-element.77, ...), custom_call_target="tpu_custom_call" | custom-call | tf_op jit(solution)/shard_map/pallas_call | solution.py:777
  29.7 0.0 collective-permute-done.4.far_ref
  29.7 0.0 collective-permute-done.5.near_ref
  29.7 1.9 %shard_map.170 = (f32[32,8,128]{2,1,0:T(8,128)S(1)}, f32[3,32,256]{2,1,0:T(8,128)S(1)}) custom-call(f32[40,16,128]{2,1,0:T(8,128)S(1)} %get-tuple-element.77.refs_0_.rows_ref, f32[2,16,128]{2,1,0:T(8,128)S(1)} %collective-permute-done.4.far_ref, f32[2,16,128]{2,1,0:T(8,128)S(1)} %collective-permute-done.5.near_ref, ...), custom_call_target="tpu_custom_call" | custom-call | tf_op jit(solution)/shard_map/pallas_call | solution.py:784
  31.7 38.7 %conditional.1 = (f32[288,128]{1,0:T(8,128)S(1)}) conditional(s32[]{:T(128)} %convert_element_type.3, f32[32,8,128]{2,1,0:T(8,128)S(1)} %get-tuple-element.93, (f32[32,8,128]{2,1,0:T(8,128)S(1)}, f32[8,128]{1,0:T(8,128)S(1)}, bf16[256,256]{1,0:T(8,128)(2,1)S(1)}, bf16[256,256]{1,0:T(8,128)(2,1)S(1)}, bf16[256,256]{1,0:T(8,128)(2,1)S(1)}, ...), branch_computations={%region_0.0_spmd, %region_1.0_spmd} | conditional | bytes 557064 | solution.py:806
  31.7 20.7 %all_to_all.30.x_ref = f32[32,8,128]{2,1,0:T(8,128)S(1)} all-to-all(f32[32,8,128]{2,1,0:T(8,128)S(1)} %get-tuple-element.26), channel_id=1, replica_groups=mesh['lon'=32,'lat'=16] {'lon'}, dimensions={0} | all-to-all | bytes 262144 | tf_op jit(solution)/shard_map/cond/branch_1_fun/all_to_all | solution.py:791
  52.4 1.2 %branch_1_fun.1 = f32[288,128]{1,0:T(8,128)S(1)} custom-call(f32[32,8,128]{2,1,0:T(8,128)S(1)} %all_to_all.30.x_ref, f32[8,128]{1,0:T(8,128)S(1)} %get-tuple-element.27.line_ref, bf16[256,256]{1,0:T(8,128)(2,1)S(1)} %get-tuple-element.28.spread_ref, bf16[256,256]{1,0:T(8,128)(2,1)S(1)} %get-tuple-element.29.spread_low, ...), custom_call_target="tpu_custom_call" | custom-call | tf_op jit(solution)/shard_map/cond/branch_1_fun/pallas_call | solution.py:792
  53.6 16.7 %all_to_all.31 = f32[288,1,128]{2,1,0:T(1,128)S(1)} all-to-all(f32[288,1,128]{2,1,0:T(1,128)S(1)} %bitcast.14), channel_id=1, replica_groups=mesh['lon'=32,'lat'=16] {'lon'}, dimensions={0} | all-to-all | bytes 294912 | tf_op jit(solution)/shard_map/cond/branch_1_fun/all_to_all | solution.py:794
  70.3 2.1 %shard_map.171 = (f32[8,24,128]{2,1,0:T(8,128)}, f32[5,32,256]{2,1,0:T(8,128)S(1)}, f32[16,128]{1,0:T(8,128)S(1)}) custom-call(f32[288,128]{1,0:T(8,128)S(1)} %get-tuple-element.109.x_ref, f32[3,32,256]{2,1,0:T(8,128)S(1)} %get-tuple-element.103.planes_ref), custom_call_target="tpu_custom_call" | custom-call | tf_op jit(solution)/shard_map/pallas_call | solution.py:811
  72.5 10.8 %all_to_all.32 = f32[16,1,128]{2,1,0:T(1,128)S(1)} all-to-all(f32[16,1,128]{2,1,0:T(1,128)S(1)} %bitcast.18), channel_id=1, replica_groups={{0,1,2,3,16,17,18,19,32,33,34,35,48,49,50,51},{4,5,6,7,20,21,22,23,36,3..., dimensions={0} | all-to-all | bytes 16384 | tf_op jit(solution)/shard_map/all_to_all | solution.py:823
  83.3 0.1 shard_map.172
  83.4 13.6 %all_to_all.33 = f32[32,1,128]{2,1,0:T(1,128)S(1)} all-to-all(f32[32,1,128]{2,1,0:T(1,128)S(1)} %bitcast.15), channel_id=1, replica_groups={{0,4,8,12,64,68,72,76,128,132,136,140,192,196,200,204,256,260,264,268,3..., dimensions={0} | all-to-all | bytes 32768 | tf_op jit(solution)/shard_map/all_to_all | solution.py:827
  97.0 1.1 %shard_map.173 = (f32[24,128]{1,0:T(8,128)}, f32[24,128]{1,0:T(8,128)}) custom-call(f32[32,128]{1,0:T(8,128)S(1)} %bitcast.16, f32[5,32,256]{2,1,0:T(8,128)S(1)} %get-tuple-element.106.powers_ref), custom_call_target="tpu_custom_call" | custom-call | tf_op jit(solution)/shard_map/pallas_call | solution.py:830
Async XLA Ops:
  1.6 7.7 %collective-permute-start.2 = (f32[13,8,128]{2,1,0:T(8,128)S(1)}, f32[13,8,128]{2,1,0:T(8,128)S(1)}, u32[]{:S(2)}, u32[]{:S(2)}) collective-permute-start(f32[13,8,128]{2,1,0:T(8,128)S(1)} %get-tuple-element.75), channel_id=1, source_target_pairs={{0,1},{1,2},{2,3},{3,4},{4,5},{5,6},{6,7},{7,8},{8,9},{9,10},{10,1... | collective-permute-start | bytes 159752 | tf_op jit(solution)/shard_map/ppermute | solution.py:742
  6.4 6.3 %collective-permute-start.3 = (f32[13,8,128]{2,1,0:T(8,128)S(1)}, f32[13,8,128]{2,1,0:T(8,128)S(1)}, u32[]{:S(2)}, u32[]{:S(2)}) collective-permute-start(f32[13,8,128]{2,1,0:T(8,128)S(1)} %get-tuple-element.76), channel_id=1, source_target_pairs={{1,0},{2,1},{3,2},{4,3},{5,4},{6,5},{7,6},{8,7},{9,8},{10,9},{11,1... | collective-permute-start | bytes 159752 | tf_op jit(solution)/shard_map/ppermute | solution.py:743
  13.0 16.8 %collective-permute-start.4 = (f32[2,16,128]{2,1,0:T(8,128)S(1)}, f32[2,16,128]{2,1,0:T(8,128)S(1)}, u32[]{:S(2)}, u32[]{:S(2)}) collective-permute-start(f32[2,16,128]{2,1,0:T(8,128)S(1)} %get-tuple-element.78), channel_id=1, source_target_pairs={{0,496},{16,32},{32,16},{48,64},{64,48},{80,96},{96,80},{112,128},... | collective-permute-start | bytes 49160 | tf_op jit(solution)/shard_map/ppermute | solution.py:757
  23.3 6.4 %collective-permute-start.5 = (f32[2,16,128]{2,1,0:T(8,128)S(1)}, f32[2,16,128]{2,1,0:T(8,128)S(1)}, u32[]{:S(2)}, u32[]{:S(2)}) collective-permute-start(f32[2,16,128]{2,1,0:T(8,128)S(1)} %get-tuple-element.79), channel_id=1, source_target_pairs={{0,16},{16,0},{32,48},{48,32},{64,80},{80,64},{96,112},{112,96},{1... | collective-permute-start | bytes 49160 | tf_op jit(solution)/shard_map/ppermute | solution.py:758

commit v9 on v8

--- a/solution.py
+++ b/solution.py
@@ -12,7 +12,7 @@
 STEP = 0.25
 LEV = 8
 FIELDS = 16
-KMT, KAPPA, HELM, FORCING, CUT = 8, 9, 10, 11, 12
+KMT, HELM, FORCING, KAPPA, CUT = 8, 9, 10, 11, 12
 BAND = 48
 HALO = 4
 DEEP = 8
@@ -20,8 +20,10 @@
 COLS = 128
 TALL = ROWS + 2 * DEEP
 MID = ROWS + 2 * HALO
-BLOCK = LEV + 1
+BLOCK = LEV + 3
+FIRST = DEEP - HALO
 SLOTS = 20
+ENDS = TALL // SLOTS * FIELDS
 VMEM_LIMIT = 48 * 1024 * 1024
 
 
@@ -185,7 +187,9 @@
             first = jnp.where(inside, pltpu.roll(here, HALO * slot, 1) if slot else here, first)
             last = jnp.where(inside, pltpu.roll(here, HALO * (slot + 1), 1), last)
         far_ref[part] = jnp.where(even, first, last)
-        near_ref[part] = jnp.where(even, last, first)
+        near_ref[FIELDS * part : FIELDS * (part + 1)] = jnp.where(even, last, first)
+    for at, field in ((ENDS, KMT), (ENDS + MID, HELM)):
+        near_ref[at : at + MID] = rows_ref[FIRST : FIRST + MID, field, :]
 
 
 def closure_layers(window, pairs, stride, weights, acts, masks):
@@ -274,12 +278,11 @@
     return wet * (temp + STEP * (diff + eddy))
 
 
-FIRST = DEEP - HALO
-
-
 def interior_kernel(*refs):
-    rows_ref, cut_ref, raw, refs = refs[0], refs[1], refs[2:9], refs[9:]
-    out_ref, line_ref, weights, tables, refs = refs[0], refs[1], refs[2:6], refs[6:12], refs[12:]
+    rows_ref, cut_ref, slab_ref, raw, refs = refs[0], refs[1], refs[2], refs[3:10], refs[10:]
+    out_ref, line_ref, near_ref, weights, tables = refs[0], refs[1], refs[2], refs[3:7], refs[7:13]
+    refs = refs[13:]
+    near_ref[...] = slab_ref[...]
     start, mask_odd, mask_even, act_a, act_b = refs
     fill_weights(*raw[:4], *weights)
     for index, table in enumerate(raw[4:]):
@@ -314,13 +317,14 @@
 
 def edge_kernel(
     rows_ref, far_ref, near_ref, inside_ref, w_in_ref, w_mid_ref, w_late_ref, w_out_ref,
-    out_ref, planes_ref, strips, mask_odd, mask_even, act_a, act_b,
+    out_ref, strips, mask_odd, mask_even, act_a, act_b,
 ):
     lane = lane_index((FIELDS, COLS))
     even = lax.rem(lax.axis_index("lon"), 2) == 0
     parts = range(TALL // SLOTS)
-    from_west = [jnp.where(even, far_ref[part], near_ref[part]) for part in parts]
-    from_east = [jnp.where(even, near_ref[part], far_ref[part]) for part in parts]
+    near = [near_ref[FIELDS * part : FIELDS * (part + 1)] for part in parts]
+    from_west = [jnp.where(even, far_ref[part], near[part]) for part in parts]
+    from_east = [jnp.where(even, near[part], far_ref[part]) for part in parts]
     for row in range(TALL):
         part, slot = row // SLOTS, row % SLOTS
         here = rows_ref[row]
@@ -384,21 +388,14 @@
                 left = pltpu.roll(value, COLS - STRIP * slot - 4, 1)
                 shift = (108 - STRIP * slot) % COLS
                 right = pltpu.roll(value, shift, 1)
-                out_ref[row] = jnp.where(
+                out_ref[BLOCK * row : BLOCK * row + LEV] = jnp.where(
                     at_lane < HALO,
                     left,
                     jnp.where(at_lane >= COLS - HALO, right, inside_ref[row]),
                 )
-    plane_lane = lane_index((MID, COLS))
-    for index, field in enumerate((KMT, HELM, FORCING)):
-        moved = pltpu.roll(rows_ref[FIRST : FIRST + MID, field, :], HALO, 1)
-        edge = strips[FIRST : FIRST + MID, field, :]
-        planes_ref[index, :, 0:COLS] = jnp.where(plane_lane < HALO, edge, moved)
-        planes_ref[index, :, COLS:] = jnp.where(
-            plane_lane < HALO,
-            moved,
-            jnp.where(plane_lane < 2 * HALO, pltpu.roll(edge, COLS - 16, 1), 0.0),
-        )
+                out_ref[BLOCK * row + LEV : BLOCK * (row + 1)] = rows_ref[
+                    FIRST + row, KMT : FORCING + 1, :
+                ]
 
 
 def filter_tables(blocks, width):
@@ -406,23 +403,20 @@
     half = LEV // 2
     k = np.arange(blocks)
     outer = np.exp(-2j * np.pi * ((k[:, None] * k[None, :]) % blocks) / blocks)
-    spread = np.zeros((blocks, 2, half, blocks, 2, half))
+    spread = np.zeros((2, half, blocks, 2, half, blocks))
     for line in range(half):
-        spread[:, 0, line, :, 0, line] = outer.real
-        spread[:, 0, line, :, 1, line] = -outer.imag
-        spread[:, 1, line, :, 0, line] = outer.imag
-        spread[:, 1, line, :, 1, line] = outer.real
+        spread[0, line, :, 0, line] = outer.real
+        spread[0, line, :, 1, line] = -outer.imag
+        spread[1, line, :, 0, line] = outer.imag
+        spread[1, line, :, 1, line] = outer.real
     spread = spread.reshape(blocks * LEV, blocks * LEV)
     m = np.arange(width)
     twist = np.exp(-2j * np.pi * (k[:, None] * m[None, :]) / length)
-    sign = np.where(np.arange(LEV) < half, -1.0, 1.0)[None, :, None]
-    twist_re = np.broadcast_to(twist.real[:, None, :], (blocks, LEV, width))
-    twist_im = twist.imag[:, None, :] * sign
     inner = np.exp(-2j * np.pi * ((m[:, None] * m[None, :]) % width) / width)
     inner = np.concatenate([inner.real, inner.imag], axis=1)
     return [
         np.asarray(t, np.float32)
-        for t in (spread, spread.T / length, inner, twist_re, twist_im)
+        for t in (spread, spread.T / length, inner, twist.real, twist.imag)
     ]
 
 
@@ -436,66 +430,91 @@
         return jnp.dot(x, y, preferred_element_type=jnp.float32)
 
     return dot(a[0], b[0]) + (dot(a[0], b[1]) + dot(a[1], b[0]))
+
+
+def every(ref, row):
+    return ref[pl.ds(row, ref.shape[0] // BLOCK, stride=BLOCK), :]
+
+
+def solver_rows(levels, kmt, helm, forcing):
+    mean = jnp.zeros(kmt.shape, jnp.float32)
+    for level, plane in enumerate(levels):
+        mean = mean + jnp.where(kmt > level, plane, 0.0)
+    rhs = jnp.where(kmt > 0.0, mean * (1.0 / LEV) + forcing, 0.0)
+    lane = lane_index(kmt.shape)
+    ends = jnp.where(lane < 24, pltpu.roll(helm, 20, 1), 0.0)
+    ends = jnp.where(lane < 16, pltpu.roll(kmt, 12, 1), ends)
+    return rhs, jnp.where(lane < 8, pltpu.roll(rhs, 4, 1), ends)
 
 
 def filter_kernel(
     x_ref, line_ref, spread_ref, spread_low, back_ref, back_low, inner_ref, inner_low,
     twist_re_ref, twist_im_ref, out_ref,
 ):
-    blocks, lev, width = x_ref.shape
-    shape = (blocks, lev, width)
-    flat = (blocks * lev, width)
-    length = blocks * width
+    blocks = x_ref.shape[0] // BLOCK
+    length = blocks * COLS
+    half = LEV // 2 * blocks
+    shape = (half, COLS)
     inner = (inner_ref[...], inner_low[...])
-
-    def partner(block):
-        return pltpu.roll(block, lev // 2, 1)
-
-    sign = jnp.where(lax.broadcasted_iota(jnp.int32, shape, 1) < lev // 2, -1.0, 1.0)
-    y = split_dot((spread_ref[...], spread_low[...]), halves(x_ref[...].reshape(flat)))
-    y = y.reshape(shape)
-    y = y * twist_re_ref[...] + partner(y) * twist_im_ref[...]
-    s = split_dot(halves(y.reshape(flat)), inner)
-    s = s[:, 0:width].reshape(shape) + partner(s[:, width:].reshape(shape)) * sign
-    wave = lax.broadcasted_iota(jnp.int32, shape, 0) + blocks * lane_index(shape)
+    turn_re = jnp.concatenate([twist_re_ref[...]] * (LEV // 2), axis=0)
+    turn_im = jnp.concatenate([twist_im_ref[...]] * (LEV // 2), axis=0)
+    x = jnp.concatenate([every(x_ref, level) for level in range(LEV)], axis=0)
+    y = split_dot((spread_ref[...], spread_low[...]), halves(x))
+    re, im = y[:half], y[half:]
+    re, im = re * turn_re - im * turn_im, im * turn_re + re * turn_im
+    s = split_dot(halves(jnp.concatenate([re, im], axis=0)), inner)
+    re, im = s[:half, :COLS] - s[half:, COLS:], s[half:, :COLS] + s[:half, COLS:]
+    wave = lax.rem(lax.broadcasted_iota(jnp.int32, shape, 0), blocks) + blocks * lane_index(shape)
     folded = jnp.minimum(wave, length - wave).astype(jnp.float32)
-    s = jnp.where(folded < line_ref[0:1, :][None], s, 0.0)
-    y = split_dot(halves(s.reshape(flat)), inner)
-    y = y[:, 0:width].reshape(shape) - partner(y[:, width:].reshape(shape)) * sign
-    y = y * twist_re_ref[...] - partner(y) * twist_im_ref[...]
-    x = split_dot((back_ref[...], back_low[...]), halves(y.reshape(flat))).reshape(shape)
-    lane = lane_index((lev, width))
-    moved = [pltpu.roll(x[block], HALO, 1) for block in range(blocks)]
-    for block in range(blocks):
-        edge = jnp.where(lane < HALO, moved[block - 1], moved[(block + 1) % blocks])
-        edge = jnp.where(lane < 2 * HALO, edge, 0.0)
-        edge = pltpu.roll(edge, 0, 1, stride=2 * HALO, stride_axis=0)
-        row = BLOCK * block
-        out_ref[row : row + lev, :] = x[block]
-        out_ref[row + lev : row + BLOCK, :] = jnp.sum(edge, axis=0, keepdims=True)
-
-
-def ends_kernel(x_ref, far_ref, near_ref):
+    keep = folded < line_ref[0:1, :]
+    re, im = jnp.where(keep, re, 0.0), jnp.where(keep, im, 0.0)
+    s = split_dot(halves(jnp.concatenate([re, im], axis=0)), inner)
+    re, im = s[:half, :COLS] + s[half:, COLS:], s[half:, :COLS] - s[:half, COLS:]
+    re, im = re * turn_re + im * turn_im, im * turn_re - re * turn_im
+    x = split_dot((back_ref[...], back_low[...]), halves(jnp.concatenate([re, im], axis=0)))
+    levels = [x[blocks * level : blocks * (level + 1)] for level in range(LEV)]
+    for level, plane in enumerate(levels):
+        out_ref[pl.ds(level, blocks, stride=BLOCK), :] = plane
+    rhs, ends = solver_rows(
+        levels, every(x_ref, LEV), every(x_ref, LEV + 1), every(x_ref, LEV + 2)
+    )
+    shape = (blocks, COLS)
+    even = lax.rem(lax.broadcasted_iota(jnp.int32, shape, 0), 2) == 0
+
+    def ahead(plane, by):
+        return pltpu.roll(plane, (blocks - by) % blocks, 0)
+
+    border = jnp.where(
+        lax.rem(lane_index(shape), 2 * HALO) < HALO,
+        jnp.where(even, ahead(ends, -1), ahead(ends, -2)),
+        jnp.where(even, ahead(ends, 2), ahead(ends, 1)),
+    )
+    out_ref[pl.ds(LEV, blocks, stride=BLOCK), :] = rhs
+    out_ref[pl.ds(LEV + 1, blocks, stride=BLOCK), :] = jnp.where(
+        even, ahead(rhs, 1), ahead(rhs, -1)
+    )
+    out_ref[pl.ds(LEV + 2, blocks, stride=BLOCK), :] = border
+
+
+def ends_kernel(x_ref, rhs_ref, ends_ref):
+    rhs_ref[...], ends_ref[...] = solver_rows(
+        [every(x_ref, level) for level in range(LEV)],
+        every(x_ref, LEV),
+        every(x_ref, LEV + 1),
+        every(x_ref, LEV + 2),
+    )
+
+
+def plain_kernel(x_ref, rhs_ref, far_ref, near_ref, out_ref):
     even = lax.rem(lax.axis_index("lon"), 2) == 0
-    lane = lane_index((LEV, COLS))
-    packed = []
-    for row in range(MID):
-        edge = jnp.where(lane < 2 * HALO, pltpu.roll(x_ref[row], HALO, 1), 0.0)
-        edge = pltpu.roll(edge, 0, 1, stride=2 * HALO, stride_axis=0)
-        packed.append(jnp.sum(edge, axis=0, keepdims=True))
-    packed = jnp.concatenate(packed, axis=0)
-    to_east = lax.rem(lane_index((MID, COLS)), 2 * HALO) < HALO
-    last = jnp.where(to_east, packed, 0.0)
-    first = jnp.where(to_east, 0.0, packed)
-    far_ref[...] = jnp.where(even, first, last)
-    near_ref[...] = jnp.where(even, last, first)
-
-
-def plain_kernel(x_ref, far_ref, near_ref, out_ref):
-    edge = far_ref[...] + near_ref[...]
-    for row in range(MID):
-        out_ref[BLOCK * row : BLOCK * row + LEV, :] = x_ref[row]
-        out_ref[BLOCK * row + LEV : BLOCK * (row + 1), :] = edge[row : row + 1]
+    far = far_ref[...]
+    peers = near_ref[MID:]
+    west = lax.rem(lane_index((MID, COLS)), 2 * HALO) < HALO
+    border = jnp.where(west, jnp.where(even, far, peers), jnp.where(even, peers, far))
+    out_ref[...] = x_ref[...]
+    out_ref[pl.ds(LEV, MID, stride=BLOCK), :] = rhs_ref[...]
+    out_ref[pl.ds(LEV + 1, MID, stride=BLOCK), :] = near_ref[0:MID]
+    out_ref[pl.ds(LEV + 2, MID, stride=BLOCK), :] = border
 
 
 def two_sum(a, b):
@@ -542,58 +561,58 @@
     return quick_sum(x, x * (((1.0 - p) - e) - a[1] * x))
 
 
-def powers_kernel(x_ref, planes_ref, temp_hbm, powers_ref, parts_ref, temp, sems):
-    moves = []
+def powers_kernel(x_ref, rows_ref, near_ref, temp_hbm, powers_ref, parts_ref, temp, sem):
     for level in range(LEV):
         temp[level] = x_ref[pl.ds(HALO * BLOCK + level, ROWS, stride=BLOCK), :]
-        moves.append(pltpu.make_async_copy(temp.at[level], temp_hbm.at[level], sems.at[level]))
-        moves[-1].start()
+    move = pltpu.make_async_copy(temp, temp_hbm, sem)
+    move.start()
+    even = lax.rem(lax.axis_index("lon"), 2) == 0
     lane = lane_index((LEV, COLS))
-    wide_lane = lane_index((MID, COLS))
-    kmt_left = planes_ref[0, :, 0:COLS]
-    kmt_right = planes_ref[0, :, COLS:]
-    kmt = pltpu.roll(jnp.where(wide_lane < HALO, kmt_right, kmt_left), COLS - HALO, 1)
-    mean = jnp.zeros((MID, COLS), jnp.float32)
-    for level in range(LEV):
-        here = x_ref[pl.ds(level, MID, stride=BLOCK), :]
-        mean = mean + jnp.where(kmt > level, here, 0.0)
-    edge = x_ref[pl.ds(LEV, MID, stride=BLOCK), :]
-    edge_kmt = jnp.where(wide_lane < HALO, kmt_left, kmt_right)
-    edge_kmt = jnp.where(wide_lane < 2 * HALO, edge_kmt, 0.0)
-    for by in (8, 16, 32, 64):
-        edge_kmt = edge_kmt + pltpu.roll(edge_kmt, by, 1)
-    edge = jnp.where(edge_kmt > (wide_lane // (2 * HALO)).astype(jnp.float32), edge, 0.0)
-    for by in (64, 32, 16, 8):
-        edge = edge + pltpu.roll(edge, by, 1)
-    moved = pltpu.roll(mean, HALO, 1)
-    mean = jnp.concatenate(
-        [
-            jnp.where(wide_lane < HALO, edge, moved),
-            jnp.where(wide_lane < HALO, moved, jnp.where(wide_lane < 2 * HALO, edge, 0.0)),
-        ],
-        axis=1,
-    )
-    sea = (planes_ref[0] > 0.0).astype(jnp.float32)
+    plane_lane = lane_index((MID, COLS))
+    border = every(x_ref, LEV + 2)
+
+    def joined(own, peer, shift):
+        first = pltpu.roll(jnp.where(even, own, peer), HALO, 1)
+        second = pltpu.roll(jnp.where(even, peer, own), HALO, 1)
+        ends = pltpu.roll(border, COLS - shift, 1) if shift else border
+        tail = jnp.where(plane_lane < 2 * HALO, ends, 0.0)
+        return jnp.concatenate(
+            [
+                jnp.where(plane_lane < HALO, ends, first),
+                jnp.where(plane_lane < HALO, first, second),
+                jnp.where(plane_lane < HALO, second, tail),
+            ],
+            axis=1,
+        )
+
+    rhs = joined(every(x_ref, LEV), every(x_ref, LEV + 1), 0)
+    kmt = joined(rows_ref[FIRST : FIRST + MID, KMT, :], near_ref[ENDS : ENDS + MID], 8)
+    helm = joined(rows_ref[FIRST : FIRST + MID, HELM, :], near_ref[ENDS + MID :], 16)
+    sea = (kmt > 0.0).astype(jnp.float32)
+    width = 3 * COLS
 
     def around(v):
         return (
             pltpu.roll(v, 1, 0)
             + pltpu.roll(v, MID - 1, 0)
             + pltpu.roll(v, 1, 1)
-            + pltpu.roll(v, 2 * COLS - 1, 1)
-        )
-
-    diagonal = planes_ref[1] + sea * around(sea)
-    powers = [sea * (mean * (1.0 / LEV) + planes_ref[2])]
+            + pltpu.roll(v, width - 1, 1)
+        )
+
+    diagonal = helm + sea * around(sea)
+    powers = [rhs]
     for _ in range(ITERS):
         v = powers[-1]
         powers.append((diagonal * v - sea * around(v)) * 0.125)
     for index, v in enumerate(powers):
-        powers_ref[index] = v
-    row = lax.broadcasted_iota(jnp.int32, (MID, 2 * COLS), 0)
-    column = lane_index((MID, 2 * COLS))
+        tiles = [pltpu.roll(v[:, COLS * k : COLS * (k + 1)], COLS - HALO, 1) for k in range(3)]
+        left = jnp.where(even, tiles[0], tiles[1])
+        right = jnp.where(even, tiles[1], tiles[2])
+        powers_ref[index] = jnp.where(plane_lane < COLS - HALO, left, right)
+    row = lax.broadcasted_iota(jnp.int32, (MID, width), 0)
+    column = lane_index((MID, width))
     own = (
-        (row >= HALO) & (row < HALO + ROWS) & (column >= HALO) & (column < HALO + COLS)
+        (row >= HALO) & (row < HALO + ROWS) & (column >= HALO) & (column < HALO + 2 * COLS)
     )
     owned = [jnp.where(own, v, 0.0) for v in powers]
     high_rows, low_rows = [], []
@@ -602,10 +621,12 @@
         tiles = [
             (p[8 * i : 8 * i + 8, 128 * j : 128 * j + 128], e[8 * i : 8 * i + 8, 128 * j : 128 * j + 128])
             for i in range(MID // 8)
-            for j in range(2)
+            for j in range(3)
         ]
         while len(tiles) > 1:
-            tiles = [pair_add(a, b) for a, b in zip(tiles[::2], tiles[1::2])]
+            tiles = [pair_add(a, b) for a, b in zip(tiles[::2], tiles[1::2])] + (
+                tiles[-1:] if len(tiles) % 2 else []
+            )
         total = tiles[0]
         for by in (4, 2, 1):
             total = pair_add(total, tuple(pltpu.roll(t, by, 0) for t in total))
@@ -623,14 +644,13 @@
     message = jnp.where(lane == spot, total[0], 0.0) + jnp.where(lane == spot + 64, total[1], 0.0)
     message = jnp.sum(message, axis=0, keepdims=True)
     parts_ref[...] = jnp.broadcast_to(message, parts_ref.shape)
-    for move in moves:
-        move.wait()
+    move.wait()
 
 
 def sum_messages(parts_ref):
     count = parts_ref.shape[0] // 8
-    tiles = [parts_ref[8 * i : 8 * i + 8, :] for i in range(count)]
-    tiles = [two_sum(a, b) for a, b in zip(tiles[::2], tiles[1::2])]
+    zero = jnp.zeros((8, COLS), jnp.float32)
+    tiles = [(parts_ref[8 * i : 8 * i + 8, :], zero) for i in range(count)]
     while len(tiles) > 1:
         tiles = [pair_add(a, b) for a, b in zip(tiles[::2], tiles[1::2])]
     total = tiles[0]
@@ -681,13 +701,12 @@
         way = [r + beta[0] * w for r, w in zip(res, way)]
     for weights, target, factor in ((sol, surface_ref, 0.125), (res, residual_ref, 1.0)):
         for i in range(MID // 8):
-            for j in range(2):
-                spot = (slice(8 * i, 8 * i + 8), slice(128 * j, 128 * j + 128))
-                value = weights[0] * powers_ref[(0,) + spot]
-                for index in range(1, len(weights)):
-                    value = value + weights[index] * powers_ref[(index,) + spot]
-                wide[spot] = value * factor
-        target[...] = wide[HALO : HALO + ROWS, HALO : HALO + COLS]
+            spot = (slice(8 * i, 8 * i + 8), slice(None))
+            value = weights[0] * powers_ref[(0,) + spot]
+            for index in range(1, len(weights)):
+                value = value + weights[index] * powers_ref[(index,) + spot]
+            wide[spot] = value * factor
+        target[...] = wide[HALO : HALO + ROWS]
 
 
 def forward(axis, periodic):
@@ -704,8 +723,8 @@
     inner, outer = {}, {}
     for i in range(lon):
         for j in range(lat):
-            inner.setdefault((i // 4, j // 4), []).append(i * lat + j)
-            outer.setdefault((i % 4, j % 4), []).append(i * lat + j)
+            inner.setdefault((i // 4, i % 2), []).append(i * lat + j)
+            outer.setdefault((i % 4, j), []).append(i * lat + j)
     return list(inner.values()), list(outer.values())
 
 
@@ -750,12 +769,16 @@
         fields + sources,
         fields,
     )
-    ends = shape((TALL // SLOTS, FIELDS, COLS), f32)
     rows, to_far, to_near, cuts = call(
-        pack_kernel, (shape((TALL, FIELDS, COLS), f32), ends, ends, shape((DEEP, COLS), f32))
+        pack_kernel,
+        (
+            shape((TALL, FIELDS, COLS), f32),
+            shape((TALL // SLOTS, FIELDS, COLS), f32),
+            shape((ENDS + 2 * MID, COLS), f32),
+            shape((DEEP, COLS), f32),
+        ),
     )(own, north, south)
     far = lax.ppermute(to_far, "lon", swap_far())
-    near = lax.ppermute(to_near, "lon", swap_near())
 
     outs = (
         shape((4 * FIELDS, 640), bf16),
@@ -774,37 +797,41 @@
         )
 
     block = shape((MID, LEV, COLS), f32)
-    inside, line, *prepared = call(
+    inside, line, to_near, *prepared = call(
         interior_kernel,
-        (block, shape((LEV, COLS), f32)) + outs,
+        (block, shape((LEV, COLS), f32), shape(to_near.shape, f32)) + outs,
         (pltpu.VMEM((TALL * FIELDS, COLS), bf16),) + closure_scratch(19),
         10**9,
-    )(rows, cuts, *raw[:7])
+    )(rows, cuts, to_near, *raw[:7])
+    near = lax.ppermute(to_near, "lon", swap_near())
     weights, tables = prepared[:4], prepared[4:] + raw[7:]
-    lines, planes = call(
+    lines = call(
         edge_kernel,
-        (block, shape((3, MID, 2 * COLS), f32)),
+        shape((BLOCK * MID, COLS), f32),
         (pltpu.VMEM((TALL, FIELDS, COLS), f32),) + closure_scratch(6),
     )(rows, far, near, inside, *weights)
 
+    def regroup(block):
+        block = block.reshape(BLOCK * blocks, 1, COLS)
+        block = lax.all_to_all(block, "lon", split_axis=0, concat_axis=0, tiled=True)
+        return block.reshape(BLOCK * blocks, COLS)
+
     def filtered_block(lines, line, tables):
-        whole = lax.all_to_all(lines, "lon", split_axis=0, concat_axis=0, tiled=True)
-        result = call(filter_kernel, shape((BLOCK * blocks, COLS), f32))(whole, line, *tables)
-        result = result.reshape(BLOCK * blocks, 1, COLS)
-        result = lax.all_to_all(result, "lon", split_axis=0, concat_axis=0, tiled=True)
-        return result.reshape(BLOCK * blocks, COLS)
+        whole = regroup(lines)
+        return regroup(
+            call(filter_kernel, shape((BLOCK * blocks, COLS), f32))(whole, line, *tables)
+        )
 
     def plain_block(lines, line, tables):
-        ends = shape((MID, COLS), f32)
-        to_far, to_near = call(ends_kernel, (ends, ends))(lines)
-        far = lax.ppermute(to_far, "lon", swap_far())
-        near = lax.ppermute(to_near, "lon", swap_near())
-        return call(plain_kernel, shape((BLOCK * MID, COLS), f32))(lines, far, near)
+        plane = shape((MID, COLS), f32)
+        rhs, ends = call(ends_kernel, (plane, plane))(lines)
+        far = lax.ppermute(ends, "lon", swap_far())
+        near = lax.ppermute(jnp.concatenate([rhs, far]), "lon", swap_near())
+        return call(plain_kernel, shape((BLOCK * MID, COLS), f32))(lines, rhs, far, near)
 
     top_row = lax.axis_index("lat") * ROWS - HALO
     polar = (top_row < BAND) | (top_row + MID > ROWS * lax.axis_size("lat") - BAND)
     back = lax.cond(polar, filtered_block, plain_block, lines, line, tables)
-    everyone = blocks * lax.axis_size("lat")
     both = ("lon", "lat")
     inner, outer = reduction_groups(blocks, lax.axis_size("lat"))
     wide = len(inner[0])
@@ -812,25 +839,25 @@
         powers_kernel,
         out_shape=(
             shape((LEV, ROWS, COLS), f32),
-            shape((ITERS + 1, MID, 2 * COLS), f32),
+            shape((ITERS + 1, MID, COLS), f32),
             shape((wide, COLS), f32),
         ),
-        in_specs=[vmem] * 2,
+        in_specs=[vmem] * 3,
         out_specs=(pl.BlockSpec(memory_space=pltpu.HBM), vmem, vmem),
-        scratch_shapes=(pltpu.VMEM((LEV, ROWS, COLS), f32), pltpu.SemaphoreType.DMA((LEV,))),
+        scratch_shapes=(pltpu.VMEM((LEV, ROWS, COLS), f32), pltpu.SemaphoreType.DMA),
         compiler_params=pltpu.CompilerParams(vmem_limit_bytes=VMEM_LIMIT),
-    )(back, planes)
+    )(back, rows, near)
     parts = lax.all_to_all(
         parts, both, split_axis=0, concat_axis=0, tiled=True, axis_index_groups=inner
     )
-    parts = call(merge_kernel, shape((everyone // wide, COLS), f32))(parts)
+    parts = call(merge_kernel, shape((len(outer[0]), COLS), f32))(parts)
     parts = lax.all_to_all(
         parts, both, split_axis=0, concat_axis=0, tiled=True, axis_index_groups=outer
     )
     surface, residual = call(
         combine_kernel,
         (shape((ROWS, COLS), f32), shape((ROWS, COLS), f32)),
-        (pltpu.VMEM((MID, 2 * COLS), f32),),
+        (pltpu.VMEM((MID, COLS), f32),),
     )(parts, powers)
     return temp_new, surface, residual
 

time: 98.6 us -> 105 us (1.065)
  blocking collectives: 61.8 us -> 68.2 us
  waiting for transfers between devices: 3.37 us -> 5.14 us
  starting transfers between devices: 19.9 us -> 18.4 us
    all_to_all x2, blocking collectives: 37.4 us -> 44.9 us  [regroup(): lax.all_to_all(block, 'lon', split_axis=0, concat_axis=0, tiled=True)]
    ppermute x1, starting transfers between devices: 10.3 us -> 7.25 us  [body(): far = lax.ppermute(to_far, 'lon', swap_far())]
    ppermute x1, waiting for transfers between devices: 0.01 us -> 1.7 us  [body(): far = lax.ppermute(to_far, 'lon', swap_far())]
    ppermute x1, starting transfers between devices: 3.42 us -> 5 us  [body(): near = lax.ppermute(to_near, 'lon', swap_near())]
    all_to_all x2, blocking collectives: 24.4 us -> 23.2 us  [body(): lax.all_to_all(parts, both, split_axis=0, concat_axis=0, tiled=True, axis...]
  transfers between devices with their start and end apart: 4 -> 4, of which waited for: 1 -> 2; matrix products, arithmetic and copies ran while one was open for 0% -> 0% of each run, Pallas kernels for 5% -> 1%
where the time goes in v9:
time: 105 us; the launch traced here: 104 us
  blocking collectives  68.2 us (65%)
  starting transfers between devices  18.4 us (18%)
  Pallas kernels  11.6 us (11%)
  waiting for transfers between devices  5.14 us (5%)
    all_to_all x2, blocking collectives, regroup(): lax.all_to_all(block, 'lon', split_axis=0, concat_axis=0, tiled=True)  44.9 us
    all_to_all x2, blocking collectives, body(): lax.all_to_all(parts, both, split_axis=0, concat_axis=0, tiled=True, axis...  23.2 us
    ppermute x1, starting transfers between devices, body(): far = lax.ppermute(to_far, 'lon', swap_far())  7.25 us
    ppermute x1, starting transfers between devices, body(): near = lax.ppermute(to_near, 'lon', swap_near())  5 us
    ppermute x1, starting transfers between devices, body(): north = lax.ppermute(bottom, 'lat', forward('lat', False))  4.83 us
    ppermute x1, waiting for transfers between devices, body(): south = lax.ppermute(top, 'lat', backward('lat', False))  3.43 us
    pallas_call x1, Pallas kernels, body(): call(interior_kernel, (block, shape((LEV, COLS), f32), shape(to_near.shap...  2.92 us
  transfers between devices with their start and end apart: 4, of which 2 were waited for; matrix products, arithmetic and copies ran while one was open for 0% of the time, Pallas kernels for 1%

profile of v9, /device:TPU:1, one launch (start us, length us, event | category | flops | bytes accessed | tf_op | source)
XLA Modules:
  0.0 104.0 jit_solution(2668008213827271587)
XLA Ops:
  0.6 1.0 shard_map.167
  1.6 4.8 %collective-permute-start.2 = (f32[13,8,128]{2,1,0:T(8,128)S(1)}, f32[13,8,128]{2,1,0:T(8,128)S(1)}, u32[]{:S(2)}, u32[]{:S(2)}) collective-permute-start(f32[13,8,128]{2,1,0:T(8,128)S(1)} %get-tuple-element.74), channel_id=1, source_target_pairs={{0,1},{1,2},{2,3},{3,4},{4,5},{5,6},{6,7},{7,8},{8,9},{9,10},{10,1... | collective-permute-start | bytes 159752 | tf_op jit(solution)/shard_map/ppermute | solution.py:761
  6.4 1.3 %collective-permute-start.3 = (f32[13,8,128]{2,1,0:T(8,128)S(1)}, f32[13,8,128]{2,1,0:T(8,128)S(1)}, u32[]{:S(2)}, u32[]{:S(2)}) collective-permute-start(f32[13,8,128]{2,1,0:T(8,128)S(1)} %get-tuple-element.75), channel_id=1, source_target_pairs={{1,0},{2,1},{3,2},{4,3},{5,4},{6,5},{7,6},{8,7},{9,8},{10,9},{11,1... | collective-permute-start | bytes 159752 | tf_op jit(solution)/shard_map/ppermute | solution.py:762
  7.7 1.5 %shard_map.166 = (f32[24,16,128]{2,1,0:T(8,128)S(1)}, bf16[9,8,64]{2,1,0:T(8,128)(2,1)S(1)}, bf16[9,64,64]{2,1,0:T(8,128)(2,1)S(1)}, bf16[9,64,64]{2,1,0:T(8,128...) custom-call(f32[8,24,128]{2,1,0:T(8,128)} %temp_hbm.1, ...), custom_call_target="tpu_custom_call" | custom-call | flops 1000000 | bytes 2000000 | tf_op jit(solution)/shard_map/pallas_call | solution.py:47
  9.3 0.0 collective-permute-done.2.north_ref
  9.3 3.4 %collective-permute-done.3.south_ref = f32[13,8,128]{2,1,0:T(8,128)S(1)} collective-permute-done((f32[13,8,128]{2,1,0:T(8,128)S(1)}, f32[13,8,128]{2,1,0:T(8,128)S(1)}, u32[]{:S(2)}, u32[]{:S(2)}) %collective-permute-start.3) | collective-permute-done | bytes 53280 | tf_op jit(solution)/shard_map/ppermute | solution.py:762
  12.7 0.3 shard_map.168
  13.0 2.9 %shard_map.169 = (f32[32,8,128]{2,1,0:T(8,128)S(1)}, f32[8,128]{1,0:T(8,128)S(1)}, f32[96,128]{1,0:T(8,128)S(1)}, bf16[64,640]{1,0:T(8,128)(2,1)S(1)}, bf16[256,...) custom-call(f32[40,16,128]{2,1,0:T(8,128)S(1)} %get-tuple-element.76, ...), custom_call_target="tpu_custom_call" | custom-call | tf_op jit(solution)/shard_map/pallas_call | solution.py:800
  15.9 5.0 %collective-permute-start.5 = (f32[96,128]{1,0:T(8,128)S(1)}, f32[96,128]{1,0:T(8,128)S(1)}, u32[]{:S(2)}, u32[]{:S(2)}) collective-permute-start(f32[96,128]{1,0:T(8,128)S(1)} %get-tuple-element.87), channel_id=1, source_target_pairs={{0,16},{16,0},{32,48},{48,32},{64,80},{80,64},{96,112},{112,96},{1... | collective-permute-start | bytes 147464 | tf_op jit(solution)/shard_map/ppermute | solution.py:806
  20.9 7.2 %collective-permute-start.4 = (f32[2,16,128]{2,1,0:T(8,128)S(1)}, f32[2,16,128]{2,1,0:T(8,128)S(1)}, u32[]{:S(2)}, u32[]{:S(2)}) collective-permute-start(f32[2,16,128]{2,1,0:T(8,128)S(1)} %get-tuple-element.77), channel_id=1, source_target_pairs={{0,496},{16,32},{32,16},{48,64},{64,48},{80,96},{96,80},{112,128},... | collective-permute-start | bytes 49160 | tf_op jit(solution)/shard_map/ppermute | solution.py:781
  28.2 1.7 %collective-permute-done.4.far_ref = f32[2,16,128]{2,1,0:T(8,128)S(1)} collective-permute-done((f32[2,16,128]{2,1,0:T(8,128)S(1)}, f32[2,16,128]{2,1,0:T(8,128)S(1)}, u32[]{:S(2)}, u32[]{:S(2)}) %collective-permute-start.4) | collective-permute-done | bytes 16416 | tf_op jit(solution)/shard_map/ppermute | solution.py:781
  29.9 0.0 collective-permute-done.5.near_ref
  29.9 1.9 %shard_map.170 = f32[352,128]{1,0:T(8,128)S(1)} custom-call(f32[40,16,128]{2,1,0:T(8,128)S(1)} %get-tuple-element.76.refs_0_.rows_ref, f32[2,16,128]{2,1,0:T(8,128)S(1)} %collective-permute-done.4.far_ref, f32[96,128]{1,0:T(8,128)S(1)} %collective-permute-done.5.near_ref, f32[32,8,128]{2,1,0:T(8,128)S(1)} %get-tuple-element.88.inside_ref, ...), custom_call_target="tpu_custom_call" | custom-call | tf_op jit(solution)/shard_map/pallas_call | solution.py:808
  31.8 46.2 %conditional.1 = (f32[352,128]{1,0:T(8,128)S(1)}) conditional(s32[]{:T(128)} %convert_element_type.3, f32[352,128]{1,0:T(8,128)S(1)} %shard_map.170, (f32[352,128]{1,0:T(8,128)S(1)}, f32[8,128]{1,0:T(8,128)S(1)}, bf16[256,256]{1,0:T(8,128)(2,1)S(1)}, bf16[256,256]{1,0:T(8,128)(2,1)S(1)}, bf16[256,256]{1,0:T(8,128)(2,1)S(1)}, ...), branch_computations={%region_0.0_spmd, %region_1.0_spmd} | conditional | flops 8192 | bytes 720904 | solution.py:834
  31.8 27.4 %all_to_all.30 = f32[352,1,128]{2,1,0:T(1,128)S(1)} all-to-all(f32[352,1,128]{2,1,0:T(1,128)S(1)} %bitcast.22), channel_id=1, replica_groups=mesh['lon'=32,'lat'=16] {'lon'}, dimensions={0} | all-to-all | bytes 360448 | tf_op jit(solution)/shard_map/cond/branch_1_fun/all_to_all | solution.py:816
  59.2 1.2 %branch_1_fun.1 = f32[352,128]{1,0:T(8,128)S(1)} custom-call(f32[352,128]{1,0:T(8,128)S(1)} %bitcast.17, f32[8,128]{1,0:T(8,128)S(1)} %get-tuple-element.27.line_ref, bf16[256,256]{1,0:T(8,128)(2,1)S(1)} %get-tuple-element.28.spread_ref, bf16[256,256]{1,0:T(8,128)(2,1)S(1)} %get-tuple-element.29.spread_low, bf16[256,256]{1,0:T(8,128)(2,1)S(1)} %get-tuple-element.30.back_ref, ...), custom_call_target="tpu_custom_call" | custom-call | tf_op jit(solution)/shard_map/cond/branch_1_fun/pallas_call | solution.py:822
  60.4 17.5 %all_to_all.31 = f32[352,1,128]{2,1,0:T(1,128)S(1)} all-to-all(f32[352,1,128]{2,1,0:T(1,128)S(1)} %bitcast.16), channel_id=1, replica_groups=mesh['lon'=32,'lat'=16] {'lon'}, dimensions={0} | all-to-all | bytes 360448 | tf_op jit(solution)/shard_map/cond/branch_1_fun/all_to_all | solution.py:816
  77.9 1.7 %shard_map.171 = (f32[8,24,128]{2,1,0:T(8,128)}, f32[5,32,128]{2,1,0:T(8,128)S(1)}, f32[32,128]{1,0:T(8,128)S(1)}) custom-call(f32[352,128]{1,0:T(8,128)S(1)} %get-tuple-element.107.x_ref, f32[40,16,128]{2,1,0:T(8,128)S(1)} %get-tuple-element.76.refs_0_.rows_ref, f32[96,128]{1,0:T(8,128)S(1)} %collective-permute-done.5.near_ref), custom_call_target="tpu_custom_call" | custom-call | tf_op jit(solution)/shard_map/pallas_call | solution.py:838
  79.6 14.4 %all_to_all.32 = f32[32,1,128]{2,1,0:T(1,128)S(1)} all-to-all(f32[32,1,128]{2,1,0:T(1,128)S(1)} %bitcast.20), channel_id=1, replica_groups={{0,1,2,3,4,5,6,7,8,9,10,11,12,13,14,15,32,33,34,35,36,37,38,39,40,41,42..., dimensions={0} | all-to-all | bytes 32768 | tf_op jit(solution)/shard_map/all_to_all | solution.py:850
  94.0 0.1 shard_map.172
  94.1 8.9 %all_to_all.33 = f32[8,1,128]{2,1,0:T(1,128)S(1)} all-to-all(f32[8,1,128]{2,1,0:T(1,128)S(1)} %bitcast.19), channel_id=1, replica_groups={{0,64,128,192,256,320,384,448},{1,65,129,193,257,321,385,449},{2,66,130..., dimensions={0} | all-to-all | bytes 8192 | tf_op jit(solution)/shard_map/all_to_all | solution.py:854
  103.0 1.1 %shard_map.173 = (f32[24,128]{1,0:T(8,128)}, f32[24,128]{1,0:T(8,128)}) custom-call(f32[8,128]{1,0:T(8,128)S(1)} %bitcast.21, f32[5,32,128]{2,1,0:T(8,128)S(1)} %get-tuple-element.104.powers_ref), custom_call_target="tpu_custom_call" | custom-call | tf_op jit(solution)/shard_map/pallas_call | solution.py:857
Async XLA Ops:
  1.6 7.7 %collective-permute-start.2 = (f32[13,8,128]{2,1,0:T(8,128)S(1)}, f32[13,8,128]{2,1,0:T(8,128)S(1)}, u32[]{:S(2)}, u32[]{:S(2)}) collective-permute-start(f32[13,8,128]{2,1,0:T(8,128)S(1)} %get-tuple-element.74), channel_id=1, source_target_pairs={{0,1},{1,2},{2,3},{3,4},{4,5},{5,6},{6,7},{7,8},{8,9},{9,10},{10,1... | collective-permute-start | bytes 159752 | tf_op jit(solution)/shard_map/ppermute | solution.py:761
  6.4 6.3 %collective-permute-start.3 = (f32[13,8,128]{2,1,0:T(8,128)S(1)}, f32[13,8,128]{2,1,0:T(8,128)S(1)}, u32[]{:S(2)}, u32[]{:S(2)}) collective-permute-start(f32[13,8,128]{2,1,0:T(8,128)S(1)} %get-tuple-element.75), channel_id=1, source_target_pairs={{1,0},{2,1},{3,2},{4,3},{5,4},{6,5},{7,6},{8,7},{9,8},{10,9},{11,1... | collective-permute-start | bytes 159752 | tf_op jit(solution)/shard_map/ppermute | solution.py:762
  15.9 14.0 %collective-permute-start.5 = (f32[96,128]{1,0:T(8,128)S(1)}, f32[96,128]{1,0:T(8,128)S(1)}, u32[]{:S(2)}, u32[]{:S(2)}) collective-permute-start(f32[96,128]{1,0:T(8,128)S(1)} %get-tuple-element.87), channel_id=1, source_target_pairs={{0,16},{16,0},{32,48},{48,32},{64,80},{80,64},{96,112},{112,96},{1... | collective-permute-start | bytes 147464 | tf_op jit(solution)/shard_map/ppermute | solution.py:806
  20.9 9.0 %collective-permute-start.4 = (f32[2,16,128]{2,1,0:T(8,128)S(1)}, f32[2,16,128]{2,1,0:T(8,128)S(1)}, u32[]{:S(2)}, u32[]{:S(2)}) collective-permute-start(f32[2,16,128]{2,1,0:T(8,128)S(1)} %get-tuple-element.77), channel_id=1, source_target_pairs={{0,496},{16,32},{32,16},{48,64},{64,48},{80,96},{96,80},{112,128},... | collective-permute-start | bytes 49160 | tf_op jit(solution)/shard_map/ppermute | solution.py:781

commit v10 on v9

--- a/solution.py
+++ b/solution.py
@@ -21,9 +21,9 @@
 TALL = ROWS + 2 * DEEP
 MID = ROWS + 2 * HALO
 BLOCK = LEV + 3
+RETURN = LEV + 4
 FIRST = DEEP - HALO
 SLOTS = 20
-ENDS = TALL // SLOTS * FIELDS
 VMEM_LIMIT = 48 * 1024 * 1024
 
 
@@ -187,9 +187,7 @@
             first = jnp.where(inside, pltpu.roll(here, HALO * slot, 1) if slot else here, first)
             last = jnp.where(inside, pltpu.roll(here, HALO * (slot + 1), 1), last)
         far_ref[part] = jnp.where(even, first, last)
-        near_ref[FIELDS * part : FIELDS * (part + 1)] = jnp.where(even, last, first)
-    for at, field in ((ENDS, KMT), (ENDS + MID, HELM)):
-        near_ref[at : at + MID] = rows_ref[FIRST : FIRST + MID, field, :]
+        near_ref[part] = jnp.where(even, last, first)
 
 
 def closure_layers(window, pairs, stride, weights, acts, masks):
@@ -279,10 +277,8 @@
 
 
 def interior_kernel(*refs):
-    rows_ref, cut_ref, slab_ref, raw, refs = refs[0], refs[1], refs[2], refs[3:10], refs[10:]
-    out_ref, line_ref, near_ref, weights, tables = refs[0], refs[1], refs[2], refs[3:7], refs[7:13]
-    refs = refs[13:]
-    near_ref[...] = slab_ref[...]
+    rows_ref, cut_ref, raw, refs = refs[0], refs[1], refs[2:9], refs[9:]
+    out_ref, line_ref, weights, tables, refs = refs[0], refs[1], refs[2:6], refs[6:12], refs[12:]
     start, mask_odd, mask_even, act_a, act_b = refs
     fill_weights(*raw[:4], *weights)
     for index, table in enumerate(raw[4:]):
@@ -322,9 +318,8 @@
     lane = lane_index((FIELDS, COLS))
     even = lax.rem(lax.axis_index("lon"), 2) == 0
     parts = range(TALL // SLOTS)
-    near = [near_ref[FIELDS * part : FIELDS * (part + 1)] for part in parts]
-    from_west = [jnp.where(even, far_ref[part], near[part]) for part in parts]
-    from_east = [jnp.where(even, near[part], far_ref[part]) for part in parts]
+    from_west = [jnp.where(even, far_ref[part], near_ref[part]) for part in parts]
+    from_east = [jnp.where(even, near_ref[part], far_ref[part]) for part in parts]
     for row in range(TALL):
         part, slot = row // SLOTS, row % SLOTS
         here = rows_ref[row]
@@ -432,19 +427,24 @@
     return dot(a[0], b[0]) + (dot(a[0], b[1]) + dot(a[1], b[0]))
 
 
-def every(ref, row):
-    return ref[pl.ds(row, ref.shape[0] // BLOCK, stride=BLOCK), :]
-
-
-def solver_rows(levels, kmt, helm, forcing):
+def every(ref, row, size):
+    return ref[pl.ds(row, ref.shape[0] // size, stride=size), :]
+
+
+def put_every(ref, row, plane):
+    ref[pl.ds(row, ref.shape[0] // RETURN, stride=RETURN), :] = plane
+
+
+def solver_rows(x_ref, levels):
+    kmt, helm, forcing = (every(x_ref, LEV + row, BLOCK) for row in range(3))
     mean = jnp.zeros(kmt.shape, jnp.float32)
     for level, plane in enumerate(levels):
         mean = mean + jnp.where(kmt > level, plane, 0.0)
     rhs = jnp.where(kmt > 0.0, mean * (1.0 / LEV) + forcing, 0.0)
+    helm = jnp.where(kmt > 0.0, helm, 0.0)
     lane = lane_index(kmt.shape)
-    ends = jnp.where(lane < 24, pltpu.roll(helm, 20, 1), 0.0)
-    ends = jnp.where(lane < 16, pltpu.roll(kmt, 12, 1), ends)
-    return rhs, jnp.where(lane < 8, pltpu.roll(rhs, 4, 1), ends)
+    ends = jnp.where(lane < 16, pltpu.roll(helm, 12, 1), 0.0)
+    return rhs, helm, jnp.where(lane < 8, pltpu.roll(rhs, 4, 1), ends)
 
 
 def filter_kernel(
@@ -458,7 +458,7 @@
     inner = (inner_ref[...], inner_low[...])
     turn_re = jnp.concatenate([twist_re_ref[...]] * (LEV // 2), axis=0)
     turn_im = jnp.concatenate([twist_im_ref[...]] * (LEV // 2), axis=0)
-    x = jnp.concatenate([every(x_ref, level) for level in range(LEV)], axis=0)
+    x = jnp.concatenate([every(x_ref, level, BLOCK) for level in range(LEV)], axis=0)
     y = split_dot((spread_ref[...], spread_low[...]), halves(x))
     re, im = y[:half], y[half:]
     re, im = re * turn_re - im * turn_im, im * turn_re + re * turn_im
@@ -474,10 +474,8 @@
     x = split_dot((back_ref[...], back_low[...]), halves(jnp.concatenate([re, im], axis=0)))
     levels = [x[blocks * level : blocks * (level + 1)] for level in range(LEV)]
     for level, plane in enumerate(levels):
-        out_ref[pl.ds(level, blocks, stride=BLOCK), :] = plane
-    rhs, ends = solver_rows(
-        levels, every(x_ref, LEV), every(x_ref, LEV + 1), every(x_ref, LEV + 2)
-    )
+        put_every(out_ref, level, plane)
+    rhs, helm, ends = solver_rows(x_ref, levels)
     shape = (blocks, COLS)
     even = lax.rem(lax.broadcasted_iota(jnp.int32, shape, 0), 2) == 0
 
@@ -489,32 +487,29 @@
         jnp.where(even, ahead(ends, -1), ahead(ends, -2)),
         jnp.where(even, ahead(ends, 2), ahead(ends, 1)),
     )
-    out_ref[pl.ds(LEV, blocks, stride=BLOCK), :] = rhs
-    out_ref[pl.ds(LEV + 1, blocks, stride=BLOCK), :] = jnp.where(
-        even, ahead(rhs, 1), ahead(rhs, -1)
-    )
-    out_ref[pl.ds(LEV + 2, blocks, stride=BLOCK), :] = border
-
-
-def ends_kernel(x_ref, rhs_ref, ends_ref):
-    rhs_ref[...], ends_ref[...] = solver_rows(
-        [every(x_ref, level) for level in range(LEV)],
-        every(x_ref, LEV),
-        every(x_ref, LEV + 1),
-        every(x_ref, LEV + 2),
-    )
+    put_every(out_ref, LEV, rhs)
+    put_every(out_ref, LEV + 1, jnp.where(even, ahead(rhs, 1), ahead(rhs, -1)))
+    put_every(out_ref, LEV + 2, jnp.where(even, ahead(helm, 1), ahead(helm, -1)))
+    put_every(out_ref, LEV + 3, border)
+
+
+def ends_kernel(x_ref, rhs_ref, helm_ref, ends_ref):
+    levels = [every(x_ref, level, BLOCK) for level in range(LEV)]
+    rhs_ref[...], helm_ref[...], ends_ref[...] = solver_rows(x_ref, levels)
 
 
 def plain_kernel(x_ref, rhs_ref, far_ref, near_ref, out_ref):
     even = lax.rem(lax.axis_index("lon"), 2) == 0
     far = far_ref[...]
-    peers = near_ref[MID:]
+    peers = near_ref[2 * MID :]
     west = lax.rem(lane_index((MID, COLS)), 2 * HALO) < HALO
     border = jnp.where(west, jnp.where(even, far, peers), jnp.where(even, peers, far))
-    out_ref[...] = x_ref[...]
-    out_ref[pl.ds(LEV, MID, stride=BLOCK), :] = rhs_ref[...]
-    out_ref[pl.ds(LEV + 1, MID, stride=BLOCK), :] = near_ref[0:MID]
-    out_ref[pl.ds(LEV + 2, MID, stride=BLOCK), :] = border
+    for level in range(LEV):
+        put_every(out_ref, level, every(x_ref, level, BLOCK))
+    put_every(out_ref, LEV, rhs_ref[...])
+    put_every(out_ref, LEV + 1, near_ref[0:MID])
+    put_every(out_ref, LEV + 2, near_ref[MID : 2 * MID])
+    put_every(out_ref, LEV + 3, border)
 
 
 def two_sum(a, b):
@@ -561,15 +556,15 @@
     return quick_sum(x, x * (((1.0 - p) - e) - a[1] * x))
 
 
-def powers_kernel(x_ref, rows_ref, near_ref, temp_hbm, powers_ref, parts_ref, temp, sem):
+def powers_kernel(x_ref, rows_ref, temp_hbm, powers_ref, parts_ref, temp, sem):
     for level in range(LEV):
-        temp[level] = x_ref[pl.ds(HALO * BLOCK + level, ROWS, stride=BLOCK), :]
+        temp[level] = x_ref[pl.ds(HALO * RETURN + level, ROWS, stride=RETURN), :]
     move = pltpu.make_async_copy(temp, temp_hbm, sem)
     move.start()
     even = lax.rem(lax.axis_index("lon"), 2) == 0
     lane = lane_index((LEV, COLS))
     plane_lane = lane_index((MID, COLS))
-    border = every(x_ref, LEV + 2)
+    border = every(x_ref, LEV + 3, RETURN)
 
     def joined(own, peer, shift):
         first = pltpu.roll(jnp.where(even, own, peer), HALO, 1)
@@ -585,10 +580,10 @@
             axis=1,
         )
 
-    rhs = joined(every(x_ref, LEV), every(x_ref, LEV + 1), 0)
-    kmt = joined(rows_ref[FIRST : FIRST + MID, KMT, :], near_ref[ENDS : ENDS + MID], 8)
-    helm = joined(rows_ref[FIRST : FIRST + MID, HELM, :], near_ref[ENDS + MID :], 16)
-    sea = (kmt > 0.0).astype(jnp.float32)
+    rhs = joined(every(x_ref, LEV, RETURN), every(x_ref, LEV + 1, RETURN), 0)
+    kmt, helm = (rows_ref[FIRST : FIRST + MID, field, :] for field in (KMT, HELM))
+    helm = joined(jnp.where(kmt > 0.0, helm, 0.0), every(x_ref, LEV + 2, RETURN), 8)
+    sea = (helm > 0.0).astype(jnp.float32)
     width = 3 * COLS
 
     def around(v):
@@ -774,11 +769,12 @@
         (
             shape((TALL, FIELDS, COLS), f32),
             shape((TALL // SLOTS, FIELDS, COLS), f32),
-            shape((ENDS + 2 * MID, COLS), f32),
+            shape((TALL // SLOTS, FIELDS, COLS), f32),
             shape((DEEP, COLS), f32),
         ),
     )(own, north, south)
     far = lax.ppermute(to_far, "lon", swap_far())
+    near = lax.ppermute(to_near, "lon", swap_near())
 
     outs = (
         shape((4 * FIELDS, 640), bf16),
@@ -797,13 +793,12 @@
         )
 
     block = shape((MID, LEV, COLS), f32)
-    inside, line, to_near, *prepared = call(
+    inside, line, *prepared = call(
         interior_kernel,
-        (block, shape((LEV, COLS), f32), shape(to_near.shape, f32)) + outs,
+        (block, shape((LEV, COLS), f32)) + outs,
         (pltpu.VMEM((TALL * FIELDS, COLS), bf16),) + closure_scratch(19),
         10**9,
-    )(rows, cuts, to_near, *raw[:7])
-    near = lax.ppermute(to_near, "lon", swap_near())
+    )(rows, cuts, *raw[:7])
     weights, tables = prepared[:4], prepared[4:] + raw[7:]
     lines = call(
         edge_kernel,
@@ -812,22 +807,22 @@
     )(rows, far, near, inside, *weights)
 
     def regroup(block):
-        block = block.reshape(BLOCK * blocks, 1, COLS)
+        block = block.reshape(-1, 1, COLS)
         block = lax.all_to_all(block, "lon", split_axis=0, concat_axis=0, tiled=True)
-        return block.reshape(BLOCK * blocks, COLS)
+        return block.reshape(-1, COLS)
 
     def filtered_block(lines, line, tables):
         whole = regroup(lines)
         return regroup(
-            call(filter_kernel, shape((BLOCK * blocks, COLS), f32))(whole, line, *tables)
+            call(filter_kernel, shape((RETURN * blocks, COLS), f32))(whole, line, *tables)
         )
 
     def plain_block(lines, line, tables):
         plane = shape((MID, COLS), f32)
-        rhs, ends = call(ends_kernel, (plane, plane))(lines)
+        rhs, helm, ends = call(ends_kernel, (plane, plane, plane))(lines)
         far = lax.ppermute(ends, "lon", swap_far())
-        near = lax.ppermute(jnp.concatenate([rhs, far]), "lon", swap_near())
-        return call(plain_kernel, shape((BLOCK * MID, COLS), f32))(lines, rhs, far, near)
+        near = lax.ppermute(jnp.concatenate([rhs, helm, far]), "lon", swap_near())
+        return call(plain_kernel, shape((RETURN * MID, COLS), f32))(lines, rhs, far, near)
 
     top_row = lax.axis_index("lat") * ROWS - HALO
     polar = (top_row < BAND) | (top_row + MID > ROWS * lax.axis_size("lat") - BAND)
@@ -842,11 +837,11 @@
             shape((ITERS + 1, MID, COLS), f32),
             shape((wide, COLS), f32),
         ),
-        in_specs=[vmem] * 3,
+        in_specs=[vmem] * 2,
         out_specs=(pl.BlockSpec(memory_space=pltpu.HBM), vmem, vmem),
         scratch_shapes=(pltpu.VMEM((LEV, ROWS, COLS), f32), pltpu.SemaphoreType.DMA),
         compiler_params=pltpu.CompilerParams(vmem_limit_bytes=VMEM_LIMIT),
-    )(back, rows, near)
+    )(back, rows)
     parts = lax.all_to_all(
         parts, both, split_axis=0, concat_axis=0, tiled=True, axis_index_groups=inner
     )

time: 105 us -> 99.9 us (0.951)
  blocking collectives: 68.2 us -> 62.8 us
  waiting for transfers between devices: 5.14 us -> 3.44 us
  starting transfers between devices: 18.4 us -> 19.9 us
    all_to_all x2, blocking collectives: 44.9 us -> 39.3 us  [regroup(): lax.all_to_all(block, 'lon', split_axis=0, concat_axis=0, tiled=True)]
    ppermute x1, starting transfers between devices: 7.25 us -> 10.3 us  [body(): far = lax.ppermute(to_far, 'lon', swap_far())]
    ppermute x1, waiting for transfers between devices: 1.7 us -> 0.01 us  [body(): far = lax.ppermute(to_far, 'lon', swap_far())]
    ppermute x1, starting transfers between devices: 5 us -> 3.42 us  [body(): near = lax.ppermute(to_near, 'lon', swap_near())]
  transfers between devices with their start and end apart: 4 -> 4, of which waited for: 2 -> 1; matrix products, arithmetic and copies ran while one was open for 0% -> 0% of each run, Pallas kernels for 1% -> 5%
where the time goes in v10:
time: 99.9 us; the launch traced here: 98.6 us
  blocking collectives  62.8 us (63%)
  starting transfers between devices  19.9 us (20%)
  Pallas kernels  11.7 us (12%)
  waiting for transfers between devices  3.44 us (3%)
    all_to_all x2, blocking collectives, regroup(): lax.all_to_all(block, 'lon', split_axis=0, concat_axis=0, tiled=True)  39.3 us
    all_to_all x2, blocking collectives, body(): lax.all_to_all(parts, both, split_axis=0, concat_axis=0, tiled=True, axis...  23.6 us
    ppermute x1, starting transfers between devices, body(): far = lax.ppermute(to_far, 'lon', swap_far())  10.3 us
    ppermute x1, starting transfers between devices, body(): north = lax.ppermute(bottom, 'lat', forward('lat', False))  4.83 us
    ppermute x1, waiting for transfers between devices, body(): south = lax.ppermute(top, 'lat', backward('lat', False))  3.43 us
    ppermute x1, starting transfers between devices, body(): near = lax.ppermute(to_near, 'lon', swap_near())  3.42 us
    pallas_call x1, Pallas kernels, body(): call(interior_kernel, (block, shape((LEV, COLS), f32)) + outs, (pltpu.VME...  2.98 us
  transfers between devices with their start and end apart: 4, of which 1 were waited for; matrix products, arithmetic and copies ran while one was open for 0% of the time, Pallas kernels for 5%

profile of v10, /device:TPU:1, one launch (start us, length us, event | category | flops | bytes accessed | tf_op | source)
XLA Modules:
  0.0 98.6 jit_solution(14556317105359650799)
XLA Ops:
  0.6 1.0 shard_map.167
  1.6 4.8 %collective-permute-start.2 = (f32[13,8,128]{2,1,0:T(8,128)S(1)}, f32[13,8,128]{2,1,0:T(8,128)S(1)}, u32[]{:S(2)}, u32[]{:S(2)}) collective-permute-start(f32[13,8,128]{2,1,0:T(8,128)S(1)} %get-tuple-element.74), channel_id=1, source_target_pairs={{0,1},{1,2},{2,3},{3,4},{4,5},{5,6},{6,7},{7,8},{8,9},{9,10},{10,1... | collective-permute-start | bytes 159752 | tf_op jit(solution)/shard_map/ppermute | solution.py:756
  6.4 1.3 %collective-permute-start.3 = (f32[13,8,128]{2,1,0:T(8,128)S(1)}, f32[13,8,128]{2,1,0:T(8,128)S(1)}, u32[]{:S(2)}, u32[]{:S(2)}) collective-permute-start(f32[13,8,128]{2,1,0:T(8,128)S(1)} %get-tuple-element.75), channel_id=1, source_target_pairs={{1,0},{2,1},{3,2},{4,3},{5,4},{6,5},{7,6},{8,7},{9,8},{10,9},{11,1... | collective-permute-start | bytes 159752 | tf_op jit(solution)/shard_map/ppermute | solution.py:757
  7.7 1.5 %shard_map.166 = (f32[24,16,128]{2,1,0:T(8,128)S(1)}, bf16[9,8,64]{2,1,0:T(8,128)(2,1)S(1)}, bf16[9,64,64]{2,1,0:T(8,128)(2,1)S(1)}, bf16[9,64,64]{2,1,0:T(8,128...) custom-call(f32[8,24,128]{2,1,0:T(8,128)} %temp_hbm.1, ...), custom_call_target="tpu_custom_call" | custom-call | flops 1000000 | bytes 2000000 | tf_op jit(solution)/shard_map/pallas_call | solution.py:47
  9.3 0.0 collective-permute-done.2.north_ref
  9.3 3.4 %collective-permute-done.3.south_ref = f32[13,8,128]{2,1,0:T(8,128)S(1)} collective-permute-done((f32[13,8,128]{2,1,0:T(8,128)S(1)}, f32[13,8,128]{2,1,0:T(8,128)S(1)}, u32[]{:S(2)}, u32[]{:S(2)}) %collective-permute-start.3) | collective-permute-done | bytes 53280 | tf_op jit(solution)/shard_map/ppermute | solution.py:757
  12.7 0.3 shard_map.168
  13.0 10.3 %collective-permute-start.4 = (f32[2,16,128]{2,1,0:T(8,128)S(1)}, f32[2,16,128]{2,1,0:T(8,128)S(1)}, u32[]{:S(2)}, u32[]{:S(2)}) collective-permute-start(f32[2,16,128]{2,1,0:T(8,128)S(1)} %get-tuple-element.77), channel_id=1, source_target_pairs={{0,496},{16,32},{32,16},{48,64},{64,48},{80,96},{96,80},{112,128},... | collective-permute-start | bytes 49160 | tf_op jit(solution)/shard_map/ppermute | solution.py:776
  23.3 3.4 %collective-permute-start.5 = (f32[2,16,128]{2,1,0:T(8,128)S(1)}, f32[2,16,128]{2,1,0:T(8,128)S(1)}, u32[]{:S(2)}, u32[]{:S(2)}) collective-permute-start(f32[2,16,128]{2,1,0:T(8,128)S(1)} %get-tuple-element.78), channel_id=1, source_target_pairs={{0,16},{16,0},{32,48},{48,32},{64,80},{80,64},{96,112},{112,96},{1... | collective-permute-start | bytes 49160 | tf_op jit(solution)/shard_map/ppermute | solution.py:777
  26.7 3.0 %shard_map.169 = (f32[32,8,128]{2,1,0:T(8,128)S(1)}, f32[8,128]{1,0:T(8,128)S(1)}, bf16[64,640]{1,0:T(8,128)(2,1)S(1)}, bf16[256,384]{1,0:T(8,128)(2,1)S(1)}, bf...) custom-call(f32[40,16,128]{2,1,0:T(8,128)S(1)} %get-tuple-element.76, ...), custom_call_target="tpu_custom_call" | custom-call | tf_op jit(solution)/shard_map/pallas_call | solution.py:796
  29.7 0.0 collective-permute-done.4.far_ref
  29.7 0.0 collective-permute-done.5.near_ref
  29.7 1.9 %shard_map.170 = f32[352,128]{1,0:T(8,128)S(1)} custom-call(f32[40,16,128]{2,1,0:T(8,128)S(1)} %get-tuple-element.76.refs_0_.rows_ref, f32[2,16,128]{2,1,0:T(8,128)S(1)} %collective-permute-done.4.far_ref, f32[2,16,128]{2,1,0:T(8,128)S(1)} %collective-permute-done.5.near_ref, f32[32,8,128]{2,1,0:T(8,128)S(1)} %get-tuple-element.87.inside_ref, ...), custom_call_target="tpu_custom_call" | custom-call | tf_op jit(solution)/shard_map/pallas_call | solution.py:803
  31.7 40.5 %conditional.1 = (f32[384,128]{1,0:T(8,128)S(1)}) conditional(s32[]{:T(128)} %convert_element_type.3, f32[352,128]{1,0:T(8,128)S(1)} %shard_map.170, (f32[352,128]{1,0:T(8,128)S(1)}, f32[8,128]{1,0:T(8,128)S(1)}, bf16[256,256]{1,0:T(8,128)(2,1)S(1)}, bf16[256,256]{1,0:T(8,128)(2,1)S(1)}, bf16[256,256]{1,0:T(8,128)(2,1)S(1)}, ...), branch_computations={%region_0.0_spmd, %region_1.0_spmd} | conditional | flops 24576 | bytes 753672 | solution.py:829
  31.7 21.5 %all_to_all.30 = f32[352,1,128]{2,1,0:T(1,128)S(1)} all-to-all(f32[352,1,128]{2,1,0:T(1,128)S(1)} %bitcast.22), channel_id=1, replica_groups=mesh['lon'=32,'lat'=16] {'lon'}, dimensions={0} | all-to-all | bytes 360448 | tf_op jit(solution)/shard_map/cond/branch_1_fun/all_to_all | solution.py:811
  53.2 1.2 %branch_1_fun.1 = f32[384,128]{1,0:T(8,128)S(1)} custom-call(f32[352,128]{1,0:T(8,128)S(1)} %bitcast.17, f32[8,128]{1,0:T(8,128)S(1)} %get-tuple-element.28.line_ref, bf16[256,256]{1,0:T(8,128)(2,1)S(1)} %get-tuple-element.29.spread_ref, bf16[256,256]{1,0:T(8,128)(2,1)S(1)} %get-tuple-element.30.spread_low, bf16[256,256]{1,0:T(8,128)(2,1)S(1)} %get-tuple-element.31.back_ref, ...), custom_call_target="tpu_custom_call" | custom-call | tf_op jit(solution)/shard_map/cond/branch_1_fun/pallas_call | solution.py:817
  54.4 17.8 %all_to_all.31 = f32[384,1,128]{2,1,0:T(1,128)S(1)} all-to-all(f32[384,1,128]{2,1,0:T(1,128)S(1)} %bitcast.16), channel_id=1, replica_groups=mesh['lon'=32,'lat'=16] {'lon'}, dimensions={0} | all-to-all | bytes 393216 | tf_op jit(solution)/shard_map/cond/branch_1_fun/all_to_all | solution.py:811
  72.2 1.7 %shard_map.171 = (f32[8,24,128]{2,1,0:T(8,128)}, f32[5,32,128]{2,1,0:T(8,128)S(1)}, f32[32,128]{1,0:T(8,128)S(1)}) custom-call(f32[384,128]{1,0:T(8,128)S(1)} %get-tuple-element.106.x_ref, f32[40,16,128]{2,1,0:T(8,128)S(1)} %get-tuple-element.76.refs_0_.rows_ref), custom_call_target="tpu_custom_call" | custom-call | tf_op jit(solution)/shard_map/pallas_call | solution.py:833
  73.9 14.5 %all_to_all.32 = f32[32,1,128]{2,1,0:T(1,128)S(1)} all-to-all(f32[32,1,128]{2,1,0:T(1,128)S(1)} %bitcast.20), channel_id=1, replica_groups={{0,1,2,3,4,5,6,7,8,9,10,11,12,13,14,15,32,33,34,35,36,37,38,39,40,41,42..., dimensions={0} | all-to-all | bytes 32768 | tf_op jit(solution)/shard_map/all_to_all | solution.py:845
  88.4 0.1 shard_map.172
  88.5 9.1 %all_to_all.33 = f32[8,1,128]{2,1,0:T(1,128)S(1)} all-to-all(f32[8,1,128]{2,1,0:T(1,128)S(1)} %bitcast.19), channel_id=1, replica_groups={{0,64,128,192,256,320,384,448},{1,65,129,193,257,321,385,449},{2,66,130..., dimensions={0} | all-to-all | bytes 8192 | tf_op jit(solution)/shard_map/all_to_all | solution.py:849
  97.6 1.1 %shard_map.173 = (f32[24,128]{1,0:T(8,128)}, f32[24,128]{1,0:T(8,128)}) custom-call(f32[8,128]{1,0:T(8,128)S(1)} %bitcast.21, f32[5,32,128]{2,1,0:T(8,128)S(1)} %get-tuple-element.103.powers_ref), custom_call_target="tpu_custom_call" | custom-call | tf_op jit(solution)/shard_map/pallas_call | solution.py:852
Async XLA Ops:
  1.6 7.7 %collective-permute-start.2 = (f32[13,8,128]{2,1,0:T(8,128)S(1)}, f32[13,8,128]{2,1,0:T(8,128)S(1)}, u32[]{:S(2)}, u32[]{:S(2)}) collective-permute-start(f32[13,8,128]{2,1,0:T(8,128)S(1)} %get-tuple-element.74), channel_id=1, source_target_pairs={{0,1},{1,2},{2,3},{3,4},{4,5},{5,6},{6,7},{7,8},{8,9},{9,10},{10,1... | collective-permute-start | bytes 159752 | tf_op jit(solution)/shard_map/ppermute | solution.py:756
  6.4 6.3 %collective-permute-start.3 = (f32[13,8,128]{2,1,0:T(8,128)S(1)}, f32[13,8,128]{2,1,0:T(8,128)S(1)}, u32[]{:S(2)}, u32[]{:S(2)}) collective-permute-start(f32[13,8,128]{2,1,0:T(8,128)S(1)} %get-tuple-element.75), channel_id=1, source_target_pairs={{1,0},{2,1},{3,2},{4,3},{5,4},{6,5},{7,6},{8,7},{9,8},{10,9},{11,1... | collective-permute-start | bytes 159752 | tf_op jit(solution)/shard_map/ppermute | solution.py:757
  13.0 16.8 %collective-permute-start.4 = (f32[2,16,128]{2,1,0:T(8,128)S(1)}, f32[2,16,128]{2,1,0:T(8,128)S(1)}, u32[]{:S(2)}, u32[]{:S(2)}) collective-permute-start(f32[2,16,128]{2,1,0:T(8,128)S(1)} %get-tuple-element.77), channel_id=1, source_target_pairs={{0,496},{16,32},{32,16},{48,64},{64,48},{80,96},{96,80},{112,128},... | collective-permute-start | bytes 49160 | tf_op jit(solution)/shard_map/ppermute | solution.py:776
  23.3 6.4 %collective-permute-start.5 = (f32[2,16,128]{2,1,0:T(8,128)S(1)}, f32[2,16,128]{2,1,0:T(8,128)S(1)}, u32[]{:S(2)}, u32[]{:S(2)}) collective-permute-start(f32[2,16,128]{2,1,0:T(8,128)S(1)} %get-tuple-element.78), channel_id=1, source_target_pairs={{0,16},{16,0},{32,48},{48,32},{64,80},{80,64},{96,112},{112,96},{1... | collective-permute-start | bytes 49160 | tf_op jit(solution)/shard_map/ppermute | solution.py:777

commit v11 on v8

--- a/solution.py
+++ b/solution.py
@@ -54,26 +54,30 @@
     )(*(pltpu.with_memory_space_constraint(source, pltpu.HBM) for source in sources))
 
 
+def even_row():
+    return lax.rem(lax.axis_index("lat"), 2) == 0
+
+
 def slab_kernel(
     temp_hbm, kmt_hbm, kappa_hbm, helm_hbm, forcing_hbm, cutoff_hbm,
-    top_ref, bottom_ref, kmt, cutoff, sems,
+    pair_ref, other_ref, kmt, cutoff, sems,
 ):
+    last = jnp.where(even_row(), ROWS - DEEP, 0)
+    slabs = [
+        (target, pl.multiple_of(start, DEEP))
+        for target, start in ((pair_ref, last), (other_ref, ROWS - DEEP - last))
+    ]
     pairs = [(kmt_hbm, kmt), (cutoff_hbm, cutoff)]
-    for target, start in ((top_ref, 0), (bottom_ref, ROWS - DEEP)):
+    for target, start in slabs:
         rows = pl.ds(start, DEEP)
         pairs.append((temp_hbm.at[:, rows], target.at[pl.ds(0, LEV)]))
         for source, field in ((kappa_hbm, KAPPA), (helm_hbm, HELM), (forcing_hbm, FORCING)):
             pairs.append((source.at[rows], target.at[field]))
-    moves = [
-        pltpu.make_async_copy(source, target, sems.at[index])
-        for index, (source, target) in enumerate(pairs)
-    ]
-    for move in moves:
-        move.start()
+    moves = fetch(*zip(*pairs), sems)
     for move in moves:
         move.wait()
-    for target, start in ((top_ref, 0), (bottom_ref, ROWS - DEEP)):
-        target[KMT] = kmt[start : start + DEEP].astype(jnp.float32)
+    for target, start in slabs:
+        target[KMT] = kmt[pl.ds(start, DEEP), :].astype(jnp.float32)
         target[CUT] = cutoff_lanes(cutoff)
 
 
@@ -162,17 +166,19 @@
     ).astype(jnp.bfloat16)
 
 
-def pack_kernel(own_ref, north_ref, south_ref, rows_ref, far_ref, near_ref, cut_ref):
+def pack_kernel(own_ref, pair_ref, other_ref, rows_ref, far_ref, near_ref, cut_ref):
+    north = [jnp.where(even_row(), other_ref[k], pair_ref[k]) for k in range(CUT + 1)]
+    south = [jnp.where(even_row(), pair_ref[k], other_ref[k]) for k in range(CUT + 1)]
     even = lax.rem(lax.axis_index("lon"), 2) == 0
     rows_ref[DEEP : DEEP + ROWS] = own_ref[...]
-    for slab_ref, start in ((north_ref, 0), (south_ref, DEEP + ROWS)):
+    for slab, start in ((north, 0), (south, DEEP + ROWS)):
         rows = slice(start, start + DEEP)
         rows_ref[rows, CUT + 1 :, :] = jnp.zeros((DEEP, FIELDS - CUT - 1, COLS), jnp.float32)
         for field in range(CUT + 1):
-            rows_ref[rows, field, :] = slab_ref[field]
+            rows_ref[rows, field, :] = slab[field]
     lane = lane_index((DEEP, COLS))
-    north = pltpu.roll(north_ref[CUT], COLS - (ROWS - DEEP), 1)
-    south = pltpu.roll(south_ref[CUT], DEEP + ROWS, 1)
+    north = pltpu.roll(north[CUT], COLS - (ROWS - DEEP), 1)
+    south = pltpu.roll(south[CUT], DEEP + ROWS, 1)
     own = pltpu.roll(jnp.broadcast_to(own_ref[0, CUT : CUT + 1, :], (DEEP, COLS)), DEEP, 1)
     cut_ref[...] = jnp.where(lane < DEEP, north, jnp.where(lane < DEEP + ROWS, own, south))
     lane = lane_index((FIELDS, COLS))
@@ -279,13 +285,18 @@
 
 def interior_kernel(*refs):
     rows_ref, cut_ref, raw, refs = refs[0], refs[1], refs[2:9], refs[9:]
-    out_ref, line_ref, weights, tables, refs = refs[0], refs[1], refs[2:6], refs[6:12], refs[12:]
+    out_ref, line_ref, strips_ref, refs = refs[0], refs[1], refs[2], refs[3:]
+    weights, tables, refs = refs[:4], refs[4:10], refs[10:]
     start, mask_odd, mask_even, act_a, act_b = refs
     fill_weights(*raw[:4], *weights)
     for index, table in enumerate(raw[4:]):
         tables[2 * index][...], tables[2 * index + 1][...] = halves(table[...])
+    lane = lane_index((FIELDS, COLS))
     for row in range(TALL):
-        start[row * FIELDS : (row + 1) * FIELDS] = first_input(rows_ref[row])
+        here = rows_ref[row]
+        start[row * FIELDS : (row + 1) * FIELDS] = first_input(here)
+        strip = jnp.where(lane < 12, pltpu.roll(here, 4, 1), pltpu.roll(here, 20, 1))
+        strips_ref[row] = jnp.where((lane >= 4) & (lane < 20), strip, 0.0)
     results = closure_layers(
         lambda chunk: start[2 * FIELDS * chunk : 2 * FIELDS * (chunk + 2)],
         TALL // 2 - 1,
@@ -313,7 +324,7 @@
 
 
 def edge_kernel(
-    rows_ref, far_ref, near_ref, inside_ref, w_in_ref, w_mid_ref, w_late_ref, w_out_ref,
+    rows_ref, far_ref, near_ref, inside_ref, own_ref, w_in_ref, w_mid_ref, w_late_ref, w_out_ref,
     out_ref, planes_ref, strips, mask_odd, mask_even, act_a, act_b,
 ):
     lane = lane_index((FIELDS, COLS))
@@ -323,11 +334,10 @@
     from_east = [jnp.where(even, near_ref[part], far_ref[part]) for part in parts]
     for row in range(TALL):
         part, slot = row // SLOTS, row % SLOTS
-        here = rows_ref[row]
-        strip = jnp.where(lane < 24, pltpu.roll(from_east[part], (20 - HALO * slot) % COLS, 1) if slot != 5 else from_east[part], 0.0)
-        strip = jnp.where(lane < 20, pltpu.roll(here, 20, 1), strip)
-        strip = jnp.where(lane < 12, pltpu.roll(here, 4, 1), strip)
-        west = pltpu.roll(from_west[part], COLS - HALO * slot, 1) if slot else from_west[part]
+        west, east = from_west[part], from_east[part]
+        west = pltpu.roll(west, COLS - HALO * slot, 1) if slot else west
+        east = pltpu.roll(east, (20 - HALO * slot) % COLS, 1) if slot != 5 else east
+        strip = jnp.where((lane >= 20) & (lane < 24), east, own_ref[row])
         strips[row] = jnp.where(lane < 4, west, strip)
 
     def side_by_side(parity, start):
@@ -542,12 +552,11 @@
     return quick_sum(x, x * (((1.0 - p) - e) - a[1] * x))
 
 
-def powers_kernel(x_ref, planes_ref, temp_hbm, powers_ref, parts_ref, temp, sems):
-    moves = []
+def powers_kernel(x_ref, planes_ref, temp_hbm, powers_ref, parts_ref, temp, sem):
     for level in range(LEV):
         temp[level] = x_ref[pl.ds(HALO * BLOCK + level, ROWS, stride=BLOCK), :]
-        moves.append(pltpu.make_async_copy(temp.at[level], temp_hbm.at[level], sems.at[level]))
-        moves[-1].start()
+    move = pltpu.make_async_copy(temp, temp_hbm, sem)
+    move.start()
     lane = lane_index((LEV, COLS))
     wide_lane = lane_index((MID, COLS))
     kmt_left = planes_ref[0, :, 0:COLS]
@@ -623,8 +632,7 @@
     message = jnp.where(lane == spot, total[0], 0.0) + jnp.where(lane == spot + 64, total[1], 0.0)
     message = jnp.sum(message, axis=0, keepdims=True)
     parts_ref[...] = jnp.broadcast_to(message, parts_ref.shape)
-    for move in moves:
-        move.wait()
+    move.wait()
 
 
 def sum_messages(parts_ref):
@@ -690,14 +698,14 @@
         target[...] = wide[HALO : HALO + ROWS, HALO : HALO + COLS]
 
 
-def forward(axis, periodic):
-    count = lax.axis_size(axis)
-    pairs = [(i, i + 1) for i in range(count - 1)]
-    return pairs + [(count - 1, 0)] if periodic else pairs
-
-
-def backward(axis, periodic):
-    return [(target, source) for source, target in forward(axis, periodic)]
+def swap_pair():
+    return [(i, i ^ 1) for i in range(lax.axis_size("lat"))]
+
+
+def swap_other():
+    count = lax.axis_size("lat")
+    pairs = [(i, i + 1) for i in range(1, count - 1, 2)]
+    return pairs + [(j, i) for i, j in pairs]
 
 
 def reduction_groups(lon, lat):
@@ -727,7 +735,7 @@
     cutoff = cutoff.reshape(1, ROWS)
     fields = (temp, kmt, kappa, helm, forcing, cutoff)
     slab = shape((CUT + 1, DEEP, COLS), f32)
-    top, bottom = pl.pallas_call(
+    to_pair, to_other = pl.pallas_call(
         slab_kernel,
         out_shape=(slab, slab),
         in_specs=[pl.BlockSpec(memory_space=pltpu.HBM)] * 6,
@@ -739,8 +747,8 @@
         ),
         compiler_params=pltpu.CompilerParams(vmem_limit_bytes=VMEM_LIMIT),
     )(*(pltpu.with_memory_space_constraint(field, pltpu.HBM) for field in fields))
-    north = lax.ppermute(bottom, "lat", forward("lat", False))
-    south = lax.ppermute(top, "lat", backward("lat", False))
+    other = lax.ppermute(to_other, "lat", swap_other())
+    pair = lax.ppermute(to_pair, "lat", swap_pair())
     tables = tuple(jnp.asarray(table) for table in filter_tables(blocks, COLS))
     sources = (jnp.transpose(conv_in, (0, 2, 1)), conv_mid, conv_late, conv_out) + tables
     own, *raw = fetching(
@@ -753,7 +761,7 @@
     ends = shape((TALL // SLOTS, FIELDS, COLS), f32)
     rows, to_far, to_near, cuts = call(
         pack_kernel, (shape((TALL, FIELDS, COLS), f32), ends, ends, shape((DEEP, COLS), f32))
-    )(own, north, south)
+    )(own, pair, other)
     far = lax.ppermute(to_far, "lon", swap_far())
     near = lax.ppermute(to_near, "lon", swap_near())
 
@@ -774,9 +782,9 @@
         )
 
     block = shape((MID, LEV, COLS), f32)
-    inside, line, *prepared = call(
+    inside, line, strips, *prepared = call(
         interior_kernel,
-        (block, shape((LEV, COLS), f32)) + outs,
+        (block, shape((LEV, COLS), f32), shape((TALL, FIELDS, COLS), f32)) + outs,
         (pltpu.VMEM((TALL * FIELDS, COLS), bf16),) + closure_scratch(19),
         10**9,
     )(rows, cuts, *raw[:7])
@@ -785,7 +793,7 @@
         edge_kernel,
         (block, shape((3, MID, 2 * COLS), f32)),
         (pltpu.VMEM((TALL, FIELDS, COLS), f32),) + closure_scratch(6),
-    )(rows, far, near, inside, *weights)
+    )(rows, far, near, inside, strips, *weights)
 
     def filtered_block(lines, line, tables):
         whole = lax.all_to_all(lines, "lon", split_axis=0, concat_axis=0, tiled=True)
@@ -817,7 +825,7 @@
         ),
         in_specs=[vmem] * 2,
         out_specs=(pl.BlockSpec(memory_space=pltpu.HBM), vmem, vmem),
-        scratch_shapes=(pltpu.VMEM((LEV, ROWS, COLS), f32), pltpu.SemaphoreType.DMA((LEV,))),
+        scratch_shapes=(pltpu.VMEM((LEV, ROWS, COLS), f32), pltpu.SemaphoreType.DMA),
         compiler_params=pltpu.CompilerParams(vmem_limit_bytes=VMEM_LIMIT),
     )(back, planes)
     parts = lax.all_to_all(

time: 98.6 us -> 98.5 us (level)
  waiting for transfers between devices: 3.37 us -> 0.01 us
  blocking collectives: 61.8 us -> 64.8 us
    all_to_all x2, blocking collectives: 24.4 us -> 28.1 us  [body(): lax.all_to_all(parts, both, split_axis=0, concat_axis=0, tiled=True, axis...]
    ppermute x2, waiting for transfers between devices: 3.36 us -> 0.01 us  [the longest x1 0.01 us: body(): pair = lax.ppermute(to_pair, 'lat', swap_pair())]
  transfers between devices with their start and end apart: 4 -> 4, of which waited for: 1 -> 0; matrix products, arithmetic and copies ran while one was open for 0% -> 0% of each run, Pallas kernels for 5% -> 5%
where the time goes in v11:
time: 98.5 us; the launch traced here: 98.1 us
  blocking collectives  64.8 us (66%)
  starting transfers between devices  20.4 us (21%)
  Pallas kernels  12.1 us (12%)
    all_to_all x2, blocking collectives, body(): lax.all_to_all(parts, both, split_axis=0, concat_axis=0, tiled=True, axis...  28.1 us
    all_to_all x1, blocking collectives, filtered_block(): lax.all_to_all(lines, 'lon', split_axis=0, concat_axis=0, tiled=True)  20 us
    all_to_all x1, blocking collectives, filtered_block(): lax.all_to_all(result, 'lon', split_axis=0, concat_axis=0, tiled=True)  16.7 us
    ppermute x1, starting transfers between devices, body(): far = lax.ppermute(to_far, 'lon', swap_far())  10.9 us
    ppermute x1, starting transfers between devices, body(): pair = lax.ppermute(to_pair, 'lat', swap_pair())  4.83 us
    ppermute x1, starting transfers between devices, body(): near = lax.ppermute(to_near, 'lon', swap_near())  4.02 us
    pallas_call x1, Pallas kernels, body(): call(interior_kernel, (block, shape((LEV, COLS), f32), shape((TALL, FIELD...  3.11 us
  transfers between devices with their start and end apart: 4, of which 0 were waited for; matrix products, arithmetic and copies ran while one was open for 0% of the time, Pallas kernels for 5%

profile of v11, /device:TPU:1, one launch (start us, length us, event | category | flops | bytes accessed | tf_op | source)
XLA Modules:
  0.0 98.1 jit_solution(6667562454991741186)
XLA Ops:
  0.6 1.0 shard_map.167
  1.6 4.8 %collective-permute-start.2 = (f32[13,8,128]{2,1,0:T(8,128)S(1)}, f32[13,8,128]{2,1,0:T(8,128)S(1)}, u32[]{:S(2)}, u32[]{:S(2)}) collective-permute-start(f32[13,8,128]{2,1,0:T(8,128)S(1)} %get-tuple-element.76), channel_id=1, source_target_pairs={{0,1},{1,0},{2,3},{3,2},{4,5},{5,4},{6,7},{7,6},{8,9},{9,8},{10,11... | collective-permute-start | bytes 159752 | tf_op jit(solution)/shard_map/ppermute | solution.py:751
  6.4 0.7 collective-permute-start.3
  7.1 1.6 %shard_map.166 = (f32[24,16,128]{2,1,0:T(8,128)S(1)}, bf16[9,8,64]{2,1,0:T(8,128)(2,1)S(1)}, bf16[9,64,64]{2,1,0:T(8,128)(2,1)S(1)}, bf16[9,64,64]{2,1,0:T(8,128...) custom-call(f32[8,24,128]{2,1,0:T(8,128)} %temp_hbm.1, ...), custom_call_target="tpu_custom_call" | custom-call | flops 1000000 | bytes 2000000 | tf_op jit(solution)/shard_map/pallas_call | solution.py:45
  8.7 0.0 collective-permute-done.2.pair_ref
  8.7 0.0 collective-permute-done.3.other_ref
  8.7 0.3 shard_map.168
  9.0 10.9 %collective-permute-start.4 = (f32[2,16,128]{2,1,0:T(8,128)S(1)}, f32[2,16,128]{2,1,0:T(8,128)S(1)}, u32[]{:S(2)}, u32[]{:S(2)}) collective-permute-start(f32[2,16,128]{2,1,0:T(8,128)S(1)} %get-tuple-element.79), channel_id=1, source_target_pairs={{0,496},{16,32},{32,16},{48,64},{64,48},{80,96},{96,80},{112,128},... | collective-permute-start | bytes 49160 | tf_op jit(solution)/shard_map/ppermute | solution.py:765
  19.9 4.0 %collective-permute-start.5 = (f32[2,16,128]{2,1,0:T(8,128)S(1)}, f32[2,16,128]{2,1,0:T(8,128)S(1)}, u32[]{:S(2)}, u32[]{:S(2)}) collective-permute-start(f32[2,16,128]{2,1,0:T(8,128)S(1)} %get-tuple-element.80), channel_id=1, source_target_pairs={{0,16},{16,0},{32,48},{48,32},{64,80},{80,64},{96,112},{112,96},{1... | collective-permute-start | bytes 49160 | tf_op jit(solution)/shard_map/ppermute | solution.py:766
  24.0 3.1 %shard_map.169 = (f32[32,8,128]{2,1,0:T(8,128)S(1)}, f32[8,128]{1,0:T(8,128)S(1)}, f32[40,16,128]{2,1,0:T(8,128)S(1)}, bf16[64,640]{1,0:T(8,128)(2,1)S(1)}, bf16...) custom-call(f32[40,16,128]{2,1,0:T(8,128)S(1)} %get-tuple-element.78, ...), custom_call_target="tpu_custom_call" | custom-call | tf_op jit(solution)/shard_map/pallas_call | solution.py:785
  27.1 0.0 collective-permute-done.4.far_ref
  27.1 0.0 collective-permute-done.5.near_ref
  27.1 1.7 %shard_map.170 = (f32[32,8,128]{2,1,0:T(8,128)S(1)}, f32[3,32,256]{2,1,0:T(8,128)S(1)}) custom-call(f32[40,16,128]{2,1,0:T(8,128)S(1)} %get-tuple-element.78.refs_0_.rows_ref, f32[2,16,128]{2,1,0:T(8,128)S(1)} %collective-permute-done.4.far_ref, f32[2,16,128]{2,1,0:T(8,128)S(1)} %collective-permute-done.5.near_ref, ...), custom_call_target="tpu_custom_call" | custom-call | tf_op jit(solution)/shard_map/pallas_call | solution.py:792
  28.9 37.9 %conditional.1 = (f32[288,128]{1,0:T(8,128)S(1)}) conditional(s32[]{:T(128)} %convert_element_type.3, f32[32,8,128]{2,1,0:T(8,128)S(1)} %get-tuple-element.95, (f32[32,8,128]{2,1,0:T(8,128)S(1)}, f32[8,128]{1,0:T(8,128)S(1)}, bf16[256,256]{1,0:T(8,128)(2,1)S(1)}, bf16[256,256]{1,0:T(8,128)(2,1)S(1)}, bf16[256,256]{1,0:T(8,128)(2,1)S(1)}, ...), branch_computations={%region_0.0_spmd, %region_1.0_spmd} | conditional | bytes 557064 | solution.py:814
  28.9 20.0 %all_to_all.30.x_ref = f32[32,8,128]{2,1,0:T(8,128)S(1)} all-to-all(f32[32,8,128]{2,1,0:T(8,128)S(1)} %get-tuple-element.26), channel_id=1, replica_groups=mesh['lon'=32,'lat'=16] {'lon'}, dimensions={0} | all-to-all | bytes 262144 | tf_op jit(solution)/shard_map/cond/branch_1_fun/all_to_all | solution.py:799
  48.9 1.2 %branch_1_fun.1 = f32[288,128]{1,0:T(8,128)S(1)} custom-call(f32[32,8,128]{2,1,0:T(8,128)S(1)} %all_to_all.30.x_ref, f32[8,128]{1,0:T(8,128)S(1)} %get-tuple-element.27.line_ref, bf16[256,256]{1,0:T(8,128)(2,1)S(1)} %get-tuple-element.28.spread_ref, bf16[256,256]{1,0:T(8,128)(2,1)S(1)} %get-tuple-element.29.spread_low, ...), custom_call_target="tpu_custom_call" | custom-call | tf_op jit(solution)/shard_map/cond/branch_1_fun/pallas_call | solution.py:800
  50.1 16.7 %all_to_all.31 = f32[288,1,128]{2,1,0:T(1,128)S(1)} all-to-all(f32[288,1,128]{2,1,0:T(1,128)S(1)} %bitcast.14), channel_id=1, replica_groups=mesh['lon'=32,'lat'=16] {'lon'}, dimensions={0} | all-to-all | bytes 294912 | tf_op jit(solution)/shard_map/cond/branch_1_fun/all_to_all | solution.py:802
  66.8 1.9 %shard_map.171 = (f32[8,24,128]{2,1,0:T(8,128)}, f32[5,32,256]{2,1,0:T(8,128)S(1)}, f32[16,128]{1,0:T(8,128)S(1)}) custom-call(f32[288,128]{1,0:T(8,128)S(1)} %get-tuple-element.111.x_ref, f32[3,32,256]{2,1,0:T(8,128)S(1)} %get-tuple-element.105.planes_ref), custom_call_target="tpu_custom_call" | custom-call | tf_op jit(solution)/shard_map/pallas_call | solution.py:819
  68.7 14.2 %all_to_all.32 = f32[16,1,128]{2,1,0:T(1,128)S(1)} all-to-all(f32[16,1,128]{2,1,0:T(1,128)S(1)} %bitcast.18), channel_id=1, replica_groups={{0,1,2,3,16,17,18,19,32,33,34,35,48,49,50,51},{4,5,6,7,20,21,22,23,36,3..., dimensions={0} | all-to-all | bytes 16384 | tf_op jit(solution)/shard_map/all_to_all | solution.py:831
  82.9 0.1 shard_map.172
  83.0 13.9 %all_to_all.33 = f32[32,1,128]{2,1,0:T(1,128)S(1)} all-to-all(f32[32,1,128]{2,1,0:T(1,128)S(1)} %bitcast.15), channel_id=1, replica_groups={{0,4,8,12,64,68,72,76,128,132,136,140,192,196,200,204,256,260,264,268,3..., dimensions={0} | all-to-all | bytes 32768 | tf_op jit(solution)/shard_map/all_to_all | solution.py:835
  96.9 1.1 %shard_map.173 = (f32[24,128]{1,0:T(8,128)}, f32[24,128]{1,0:T(8,128)}) custom-call(f32[32,128]{1,0:T(8,128)S(1)} %bitcast.16, f32[5,32,256]{2,1,0:T(8,128)S(1)} %get-tuple-element.108.powers_ref), custom_call_target="tpu_custom_call" | custom-call | tf_op jit(solution)/shard_map/pallas_call | solution.py:838
Async XLA Ops:
  1.6 7.1 %collective-permute-start.2 = (f32[13,8,128]{2,1,0:T(8,128)S(1)}, f32[13,8,128]{2,1,0:T(8,128)S(1)}, u32[]{:S(2)}, u32[]{:S(2)}) collective-permute-start(f32[13,8,128]{2,1,0:T(8,128)S(1)} %get-tuple-element.76), channel_id=1, source_target_pairs={{0,1},{1,0},{2,3},{3,2},{4,5},{5,4},{6,7},{7,6},{8,9},{9,8},{10,11... | collective-permute-start | bytes 159752 | tf_op jit(solution)/shard_map/ppermute | solution.py:751
  6.4 2.3 %collective-permute-start.3 = (f32[13,8,128]{2,1,0:T(8,128)S(1)}, f32[13,8,128]{2,1,0:T(8,128)S(1)}, u32[]{:S(2)}, u32[]{:S(2)}) collective-permute-start(f32[13,8,128]{2,1,0:T(8,128)S(1)} %get-tuple-element.77), channel_id=1, source_target_pairs={{1,2},{3,4},{5,6},{7,8},{9,10},{11,12},{13,14},{2,1},{4,3},{6,5},{... | collective-permute-start | bytes 159752 | tf_op jit(solution)/shard_map/ppermute | solution.py:750
  9.0 18.1 %collective-permute-start.4 = (f32[2,16,128]{2,1,0:T(8,128)S(1)}, f32[2,16,128]{2,1,0:T(8,128)S(1)}, u32[]{:S(2)}, u32[]{:S(2)}) collective-permute-start(f32[2,16,128]{2,1,0:T(8,128)S(1)} %get-tuple-element.79), channel_id=1, source_target_pairs={{0,496},{16,32},{32,16},{48,64},{64,48},{80,96},{96,80},{112,128},... | collective-permute-start | bytes 49160 | tf_op jit(solution)/shard_map/ppermute | solution.py:765
  19.9 7.2 %collective-permute-start.5 = (f32[2,16,128]{2,1,0:T(8,128)S(1)}, f32[2,16,128]{2,1,0:T(8,128)S(1)}, u32[]{:S(2)}, u32[]{:S(2)}) collective-permute-start(f32[2,16,128]{2,1,0:T(8,128)S(1)} %get-tuple-element.80), channel_id=1, source_target_pairs={{0,16},{16,0},{32,48},{48,32},{64,80},{80,64},{96,112},{112,96},{1... | collective-permute-start | bytes 49160 | tf_op jit(solution)/shard_map/ppermute | solution.py:766

commit v12 on v11

--- a/solution.py
+++ b/solution.py
@@ -60,7 +60,7 @@
 
 def slab_kernel(
     temp_hbm, kmt_hbm, kappa_hbm, helm_hbm, forcing_hbm, cutoff_hbm,
-    pair_ref, other_ref, kmt, cutoff, sems,
+    pair_ref, other_ref, cross_ref, kmt, cutoff, sems,
 ):
     last = jnp.where(even_row(), ROWS - DEEP, 0)
     slabs = [
@@ -79,6 +79,7 @@
     for target, start in slabs:
         target[KMT] = kmt[pl.ds(start, DEEP), :].astype(jnp.float32)
         target[CUT] = cutoff_lanes(cutoff)
+    cross_ref[...] = other_ref[...]
 
 
 def cutoff_lanes(cutoff_ref):
@@ -166,9 +167,12 @@
     ).astype(jnp.bfloat16)
 
 
-def pack_kernel(own_ref, pair_ref, other_ref, rows_ref, far_ref, near_ref, cut_ref):
-    north = [jnp.where(even_row(), other_ref[k], pair_ref[k]) for k in range(CUT + 1)]
-    south = [jnp.where(even_row(), pair_ref[k], other_ref[k]) for k in range(CUT + 1)]
+def pack_kernel(
+    own_ref, other_ref, pair_ref, cross_ref, rows_ref, far_ref, near_ref, cut_ref
+):
+    others = [other_ref[k] + cross_ref[k] for k in range(CUT + 1)]
+    north = [jnp.where(even_row(), others[k], pair_ref[k]) for k in range(CUT + 1)]
+    south = [jnp.where(even_row(), pair_ref[k], others[k]) for k in range(CUT + 1)]
     even = lax.rem(lax.axis_index("lon"), 2) == 0
     rows_ref[DEEP : DEEP + ROWS] = own_ref[...]
     for slab, start in ((north, 0), (south, DEEP + ROWS)):
@@ -702,9 +706,8 @@
     return [(i, i ^ 1) for i in range(lax.axis_size("lat"))]
 
 
-def swap_other():
-    count = lax.axis_size("lat")
-    pairs = [(i, i + 1) for i in range(1, count - 1, 2)]
+def swap_other(cross):
+    pairs = [(i, i + 1) for i in range(3 if cross else 1, lax.axis_size("lat") - 1, 4)]
     return pairs + [(j, i) for i, j in pairs]
 
 
@@ -735,11 +738,11 @@
     cutoff = cutoff.reshape(1, ROWS)
     fields = (temp, kmt, kappa, helm, forcing, cutoff)
     slab = shape((CUT + 1, DEEP, COLS), f32)
-    to_pair, to_other = pl.pallas_call(
+    to_pair, to_other, to_cross = pl.pallas_call(
         slab_kernel,
-        out_shape=(slab, slab),
+        out_shape=(slab, slab, slab),
         in_specs=[pl.BlockSpec(memory_space=pltpu.HBM)] * 6,
-        out_specs=(vmem, vmem),
+        out_specs=(vmem, vmem, vmem),
         scratch_shapes=(
             pltpu.VMEM((ROWS, COLS), jnp.int32),
             pltpu.VMEM((1, ROWS), jnp.int32),
@@ -747,8 +750,9 @@
         ),
         compiler_params=pltpu.CompilerParams(vmem_limit_bytes=VMEM_LIMIT),
     )(*(pltpu.with_memory_space_constraint(field, pltpu.HBM) for field in fields))
-    other = lax.ppermute(to_other, "lat", swap_other())
+    other = lax.ppermute(to_other, "lat", swap_other(False))
     pair = lax.ppermute(to_pair, "lat", swap_pair())
+    cross = lax.ppermute(to_cross, "lat", swap_other(True))
     tables = tuple(jnp.asarray(table) for table in filter_tables(blocks, COLS))
     sources = (jnp.transpose(conv_in, (0, 2, 1)), conv_mid, conv_late, conv_out) + tables
     own, *raw = fetching(
@@ -761,7 +765,7 @@
     ends = shape((TALL // SLOTS, FIELDS, COLS), f32)
     rows, to_far, to_near, cuts = call(
         pack_kernel, (shape((TALL, FIELDS, COLS), f32), ends, ends, shape((DEEP, COLS), f32))
-    )(own, pair, other)
+    )(own, other, pair, cross)
     far = lax.ppermute(to_far, "lon", swap_far())
     near = lax.ppermute(to_near, "lon", swap_near())
 

time: 98.5 us -> 97.5 us (0.990)
  blocking collectives: 64.8 us -> 60.6 us
  starting transfers between devices: 20.4 us -> 23.5 us
    all_to_all x2, blocking collectives: 28.1 us -> 24 us  [body(): lax.all_to_all(parts, both, split_axis=0, concat_axis=0, tiled=True, axis...]
    ppermute x1, starting transfers between devices: 4.83 us -> 8.17 us  [body(): pair = lax.ppermute(to_pair, 'lat', swap_pair())]
  transfers between devices with their start and end apart: 4 -> 5, of which waited for: 0 -> 0; matrix products, arithmetic and copies ran while one was open for 0% -> 0% of each run, Pallas kernels for 5% -> 5%
where the time goes in v12:
time: 97.5 us; the launch traced here: 97 us
  blocking collectives  60.6 us (62%)
  starting transfers between devices  23.5 us (24%)
  Pallas kernels  12.1 us (12%)
    all_to_all x2, blocking collectives, body(): lax.all_to_all(parts, both, split_axis=0, concat_axis=0, tiled=True, axis...  24 us
    all_to_all x1, blocking collectives, filtered_block(): lax.all_to_all(lines, 'lon', split_axis=0, concat_axis=0, tiled=True)  19.9 us
    all_to_all x1, blocking collectives, filtered_block(): lax.all_to_all(result, 'lon', split_axis=0, concat_axis=0, tiled=True)  16.7 us
    ppermute x1, starting transfers between devices, body(): far = lax.ppermute(to_far, 'lon', swap_far())  9.96 us
    ppermute x1, starting transfers between devices, body(): pair = lax.ppermute(to_pair, 'lat', swap_pair())  8.17 us
    ppermute x1, starting transfers between devices, body(): near = lax.ppermute(to_near, 'lon', swap_near())  4.09 us
    pallas_call x1, Pallas kernels, body(): call(interior_kernel, (block, shape((LEV, COLS), f32), shape((TALL, FIELD...  3.11 us
  transfers between devices with their start and end apart: 5, of which 0 were waited for; matrix products, arithmetic and copies ran while one was open for 0% of the time, Pallas kernels for 5%

profile of v12, /device:TPU:1, one launch (start us, length us, event | category | flops | bytes accessed | tf_op | source)
XLA Modules:
  0.0 97.0 jit_solution(11256979089978357945)
XLA Ops:
  0.6 1.0 shard_map.167
  1.6 0.7 collective-permute-start.2
  2.3 8.2 %collective-permute-start.3 = (f32[13,8,128]{2,1,0:T(8,128)S(1)}, f32[13,8,128]{2,1,0:T(8,128)S(1)}, u32[]{:S(2)}, u32[]{:S(2)}) collective-permute-start(f32[13,8,128]{2,1,0:T(8,128)S(1)} %get-tuple-element.78), channel_id=1, source_target_pairs={{0,1},{1,0},{2,3},{3,2},{4,5},{5,4},{6,7},{7,6},{8,9},{9,8},{10,11... | collective-permute-start | bytes 159752 | tf_op jit(solution)/shard_map/ppermute | solution.py:754
  10.4 0.7 collective-permute-start.4
  11.1 1.6 %shard_map.166 = (f32[24,16,128]{2,1,0:T(8,128)S(1)}, bf16[9,8,64]{2,1,0:T(8,128)(2,1)S(1)}, bf16[9,64,64]{2,1,0:T(8,128)(2,1)S(1)}, bf16[9,64,64]{2,1,0:T(8,128...) custom-call(f32[8,24,128]{2,1,0:T(8,128)} %temp_hbm.1, ...), custom_call_target="tpu_custom_call" | custom-call | flops 1000000 | bytes 2000000 | tf_op jit(solution)/shard_map/pallas_call | solution.py:45
  12.7 0.0 collective-permute-done.2.other_ref
  12.7 0.0 collective-permute-done.3.pair_ref
  12.7 0.0 collective-permute-done.4.cross_ref
  12.7 0.3 shard_map.168
  13.0 10.0 %collective-permute-start.5 = (f32[2,16,128]{2,1,0:T(8,128)S(1)}, f32[2,16,128]{2,1,0:T(8,128)S(1)}, u32[]{:S(2)}, u32[]{:S(2)}) collective-permute-start(f32[2,16,128]{2,1,0:T(8,128)S(1)} %get-tuple-element.81), channel_id=1, source_target_pairs={{0,496},{16,32},{32,16},{48,64},{64,48},{80,96},{96,80},{112,128},... | collective-permute-start | bytes 49160 | tf_op jit(solution)/shard_map/ppermute | solution.py:769
  23.0 4.1 %collective-permute-start.6 = (f32[2,16,128]{2,1,0:T(8,128)S(1)}, f32[2,16,128]{2,1,0:T(8,128)S(1)}, u32[]{:S(2)}, u32[]{:S(2)}) collective-permute-start(f32[2,16,128]{2,1,0:T(8,128)S(1)} %get-tuple-element.82), channel_id=1, source_target_pairs={{0,16},{16,0},{32,48},{48,32},{64,80},{80,64},{96,112},{112,96},{1... | collective-permute-start | bytes 49160 | tf_op jit(solution)/shard_map/ppermute | solution.py:770
  27.1 3.1 %shard_map.169 = (f32[32,8,128]{2,1,0:T(8,128)S(1)}, f32[8,128]{1,0:T(8,128)S(1)}, f32[40,16,128]{2,1,0:T(8,128)S(1)}, bf16[64,640]{1,0:T(8,128)(2,1)S(1)}, bf16...) custom-call(f32[40,16,128]{2,1,0:T(8,128)S(1)} %get-tuple-element.80, ...), custom_call_target="tpu_custom_call" | custom-call | tf_op jit(solution)/shard_map/pallas_call | solution.py:789
  30.2 0.0 collective-permute-done.5.far_ref
  30.2 0.0 collective-permute-done.6.near_ref
  30.2 1.7 %shard_map.170 = (f32[32,8,128]{2,1,0:T(8,128)S(1)}, f32[3,32,256]{2,1,0:T(8,128)S(1)}) custom-call(f32[40,16,128]{2,1,0:T(8,128)S(1)} %get-tuple-element.80.refs_0_.rows_ref, f32[2,16,128]{2,1,0:T(8,128)S(1)} %collective-permute-done.5.far_ref, f32[2,16,128]{2,1,0:T(8,128)S(1)} %collective-permute-done.6.near_ref, ...), custom_call_target="tpu_custom_call" | custom-call | tf_op jit(solution)/shard_map/pallas_call | solution.py:796
  32.0 37.8 %conditional.1 = (f32[288,128]{1,0:T(8,128)S(1)}) conditional(s32[]{:T(128)} %convert_element_type.3, f32[32,8,128]{2,1,0:T(8,128)S(1)} %get-tuple-element.97, (f32[32,8,128]{2,1,0:T(8,128)S(1)}, f32[8,128]{1,0:T(8,128)S(1)}, bf16[256,256]{1,0:T(8,128)(2,1)S(1)}, bf16[256,256]{1,0:T(8,128)(2,1)S(1)}, bf16[256,256]{1,0:T(8,128)(2,1)S(1)}, ...), branch_computations={%region_0.0_spmd, %region_1.0_spmd} | conditional | bytes 557064 | solution.py:818
  32.0 19.9 %all_to_all.30.x_ref = f32[32,8,128]{2,1,0:T(8,128)S(1)} all-to-all(f32[32,8,128]{2,1,0:T(8,128)S(1)} %get-tuple-element.26), channel_id=1, replica_groups=mesh['lon'=32,'lat'=16] {'lon'}, dimensions={0} | all-to-all | bytes 262144 | tf_op jit(solution)/shard_map/cond/branch_1_fun/all_to_all | solution.py:803
  51.9 1.2 %branch_1_fun.1 = f32[288,128]{1,0:T(8,128)S(1)} custom-call(f32[32,8,128]{2,1,0:T(8,128)S(1)} %all_to_all.30.x_ref, f32[8,128]{1,0:T(8,128)S(1)} %get-tuple-element.27.line_ref, bf16[256,256]{1,0:T(8,128)(2,1)S(1)} %get-tuple-element.28.spread_ref, bf16[256,256]{1,0:T(8,128)(2,1)S(1)} %get-tuple-element.29.spread_low, ...), custom_call_target="tpu_custom_call" | custom-call | tf_op jit(solution)/shard_map/cond/branch_1_fun/pallas_call | solution.py:804
  53.1 16.7 %all_to_all.31 = f32[288,1,128]{2,1,0:T(1,128)S(1)} all-to-all(f32[288,1,128]{2,1,0:T(1,128)S(1)} %bitcast.14), channel_id=1, replica_groups=mesh['lon'=32,'lat'=16] {'lon'}, dimensions={0} | all-to-all | bytes 294912 | tf_op jit(solution)/shard_map/cond/branch_1_fun/all_to_all | solution.py:806
  69.8 1.9 %shard_map.171 = (f32[8,24,128]{2,1,0:T(8,128)}, f32[5,32,256]{2,1,0:T(8,128)S(1)}, f32[16,128]{1,0:T(8,128)S(1)}) custom-call(f32[288,128]{1,0:T(8,128)S(1)} %get-tuple-element.113.x_ref, f32[3,32,256]{2,1,0:T(8,128)S(1)} %get-tuple-element.107.planes_ref), custom_call_target="tpu_custom_call" | custom-call | tf_op jit(solution)/shard_map/pallas_call | solution.py:823
  71.8 10.5 %all_to_all.32 = f32[16,1,128]{2,1,0:T(1,128)S(1)} all-to-all(f32[16,1,128]{2,1,0:T(1,128)S(1)} %bitcast.18), channel_id=1, replica_groups={{0,1,2,3,16,17,18,19,32,33,34,35,48,49,50,51},{4,5,6,7,20,21,22,23,36,3..., dimensions={0} | all-to-all | bytes 16384 | tf_op jit(solution)/shard_map/all_to_all | solution.py:835
  82.3 0.1 shard_map.172
  82.4 13.5 %all_to_all.33 = f32[32,1,128]{2,1,0:T(1,128)S(1)} all-to-all(f32[32,1,128]{2,1,0:T(1,128)S(1)} %bitcast.15), channel_id=1, replica_groups={{0,4,8,12,64,68,72,76,128,132,136,140,192,196,200,204,256,260,264,268,3..., dimensions={0} | all-to-all | bytes 32768 | tf_op jit(solution)/shard_map/all_to_all | solution.py:839
  95.9 1.1 %shard_map.173 = (f32[24,128]{1,0:T(8,128)}, f32[24,128]{1,0:T(8,128)}) custom-call(f32[32,128]{1,0:T(8,128)S(1)} %bitcast.16, f32[5,32,256]{2,1,0:T(8,128)S(1)} %get-tuple-element.110.powers_ref), custom_call_target="tpu_custom_call" | custom-call | tf_op jit(solution)/shard_map/pallas_call | solution.py:842
Async XLA Ops:
  1.6 11.1 %collective-permute-start.2 = (f32[13,8,128]{2,1,0:T(8,128)S(1)}, f32[13,8,128]{2,1,0:T(8,128)S(1)}, u32[]{:S(2)}, u32[]{:S(2)}) collective-permute-start(f32[13,8,128]{2,1,0:T(8,128)S(1)} %get-tuple-element.77), channel_id=1, source_target_pairs={{1,2},{5,6},{9,10},{13,14},{2,1},{6,5},{10,9},{14,13},{17,18},{21,... | collective-permute-start | bytes 159752 | tf_op jit(solution)/shard_map/ppermute | solution.py:753
  2.3 10.5 %collective-permute-start.3 = (f32[13,8,128]{2,1,0:T(8,128)S(1)}, f32[13,8,128]{2,1,0:T(8,128)S(1)}, u32[]{:S(2)}, u32[]{:S(2)}) collective-permute-start(f32[13,8,128]{2,1,0:T(8,128)S(1)} %get-tuple-element.78), channel_id=1, source_target_pairs={{0,1},{1,0},{2,3},{3,2},{4,5},{5,4},{6,7},{7,6},{8,9},{9,8},{10,11... | collective-permute-start | bytes 159752 | tf_op jit(solution)/shard_map/ppermute | solution.py:754
  10.4 2.3 %collective-permute-start.4 = (f32[13,8,128]{2,1,0:T(8,128)S(1)}, f32[13,8,128]{2,1,0:T(8,128)S(1)}, u32[]{:S(2)}, u32[]{:S(2)}) collective-permute-start(f32[13,8,128]{2,1,0:T(8,128)S(1)} %get-tuple-element.79), channel_id=1, source_target_pairs={{3,4},{7,8},{11,12},{4,3},{8,7},{12,11},{19,20},{23,24},{27,28},{2... | collective-permute-start | bytes 159752 | tf_op jit(solution)/shard_map/ppermute | solution.py:755
  13.0 17.2 %collective-permute-start.5 = (f32[2,16,128]{2,1,0:T(8,128)S(1)}, f32[2,16,128]{2,1,0:T(8,128)S(1)}, u32[]{:S(2)}, u32[]{:S(2)}) collective-permute-start(f32[2,16,128]{2,1,0:T(8,128)S(1)} %get-tuple-element.81), channel_id=1, source_target_pairs={{0,496},{16,32},{32,16},{48,64},{64,48},{80,96},{96,80},{112,128},... | collective-permute-start | bytes 49160 | tf_op jit(solution)/shard_map/ppermute | solution.py:769
  23.0 7.2 %collective-permute-start.6 = (f32[2,16,128]{2,1,0:T(8,128)S(1)}, f32[2,16,128]{2,1,0:T(8,128)S(1)}, u32[]{:S(2)}, u32[]{:S(2)}) collective-permute-start(f32[2,16,128]{2,1,0:T(8,128)S(1)} %get-tuple-element.82), channel_id=1, source_target_pairs={{0,16},{16,0},{32,48},{48,32},{64,80},{80,64},{96,112},{112,96},{1... | collective-permute-start | bytes 49160 | tf_op jit(solution)/shard_map/ppermute | solution.py:770

commit v13 on v12

--- a/solution.py
+++ b/solution.py
@@ -601,22 +601,18 @@
     for _ in range(ITERS):
         v = powers[-1]
         powers.append((diagonal * v - sea * around(v)) * 0.125)
+    row = lax.broadcasted_iota(jnp.int32, (MID, COLS), 0)
+    inside = (row >= HALO) & (row < HALO + ROWS)
+    owned = []
     for index, v in enumerate(powers):
-        powers_ref[index] = v
-    row = lax.broadcasted_iota(jnp.int32, (MID, 2 * COLS), 0)
-    column = lane_index((MID, 2 * COLS))
-    own = (
-        (row >= HALO) & (row < HALO + ROWS) & (column >= HALO) & (column < HALO + COLS)
-    )
-    owned = [jnp.where(own, v, 0.0) for v in powers]
+        left, right = (pltpu.roll(v[:, k : k + COLS], COLS - HALO, 1) for k in (0, COLS))
+        cut = jnp.where(wide_lane < COLS - HALO, left, right)
+        powers_ref[index] = cut
+        owned.append(jnp.where(inside, cut, 0.0))
     high_rows, low_rows = [], []
     for order in range(2 * ITERS):
         p, e = two_product(owned[order // 2], owned[order - order // 2])
-        tiles = [
-            (p[8 * i : 8 * i + 8, 128 * j : 128 * j + 128], e[8 * i : 8 * i + 8, 128 * j : 128 * j + 128])
-            for i in range(MID // 8)
-            for j in range(2)
-        ]
+        tiles = [(p[8 * i : 8 * i + 8], e[8 * i : 8 * i + 8]) for i in range(MID // 8)]
         while len(tiles) > 1:
             tiles = [pair_add(a, b) for a, b in zip(tiles[::2], tiles[1::2])]
         total = tiles[0]
@@ -693,13 +689,12 @@
         way = [r + beta[0] * w for r, w in zip(res, way)]
     for weights, target, factor in ((sol, surface_ref, 0.125), (res, residual_ref, 1.0)):
         for i in range(MID // 8):
-            for j in range(2):
-                spot = (slice(8 * i, 8 * i + 8), slice(128 * j, 128 * j + 128))
-                value = weights[0] * powers_ref[(0,) + spot]
-                for index in range(1, len(weights)):
-                    value = value + weights[index] * powers_ref[(index,) + spot]
-                wide[spot] = value * factor
-        target[...] = wide[HALO : HALO + ROWS, HALO : HALO + COLS]
+            spot = slice(8 * i, 8 * i + 8)
+            value = weights[0] * powers_ref[0, spot]
+            for index in range(1, len(weights)):
+                value = value + weights[index] * powers_ref[index, spot]
+            wide[spot] = value * factor
+        target[...] = wide[HALO : HALO + ROWS]
 
 
 def swap_pair():
@@ -824,7 +819,7 @@
         powers_kernel,
         out_shape=(
             shape((LEV, ROWS, COLS), f32),
-            shape((ITERS + 1, MID, 2 * COLS), f32),
+            shape((ITERS + 1, MID, COLS), f32),
             shape((wide, COLS), f32),
         ),
         in_specs=[vmem] * 2,
@@ -842,7 +837,7 @@
     surface, residual = call(
         combine_kernel,
         (shape((ROWS, COLS), f32), shape((ROWS, COLS), f32)),
-        (pltpu.VMEM((MID, 2 * COLS), f32),),
+        (pltpu.VMEM((MID, COLS), f32),),
     )(parts, powers)
     return temp_new, surface, residual
 

time: 97.5 us -> 97.5 us (level)
  no operation moved by 1% of the time
where the time goes in v13:
time: 97.5 us; the launch traced here: 97 us
  blocking collectives  60.6 us (62%)
  starting transfers between devices  23.5 us (24%)
  Pallas kernels  12.1 us (12%)
    all_to_all x2, blocking collectives, body(): lax.all_to_all(parts, both, split_axis=0, concat_axis=0, tiled=True, axis...  24 us
    all_to_all x1, blocking collectives, filtered_block(): lax.all_to_all(lines, 'lon', split_axis=0, concat_axis=0, tiled=True)  19.9 us
    all_to_all x1, blocking collectives, filtered_block(): lax.all_to_all(result, 'lon', split_axis=0, concat_axis=0, tiled=True)  16.7 us
    ppermute x1, starting transfers between devices, body(): far = lax.ppermute(to_far, 'lon', swap_far())  9.96 us
    ppermute x1, starting transfers between devices, body(): pair = lax.ppermute(to_pair, 'lat', swap_pair())  8.17 us
    ppermute x1, starting transfers between devices, body(): near = lax.ppermute(to_near, 'lon', swap_near())  4.09 us
    pallas_call x1, Pallas kernels, body(): call(interior_kernel, (block, shape((LEV, COLS), f32), shape((TALL, FIELD...  3.11 us
    pallas_call x1, Pallas kernels, body(): pl.pallas_call(powers_kernel, out_shape=(shape((LEV, ROWS, COLS), f32), s...  1.97 us
  transfers between devices with their start and end apart: 5, of which 0 were waited for; matrix products, arithmetic and copies ran while one was open for 0% of the time, Pallas kernels for 5%

profile of v13, /device:TPU:1, one launch (start us, length us, event | category | flops | bytes accessed | tf_op | source)
XLA Modules:
  0.0 97.0 jit_solution(8374539329214327294)
XLA Ops:
  0.6 1.0 shard_map.167
  1.6 0.7 collective-permute-start.2
  2.3 8.2 %collective-permute-start.3 = (f32[13,8,128]{2,1,0:T(8,128)S(1)}, f32[13,8,128]{2,1,0:T(8,128)S(1)}, u32[]{:S(2)}, u32[]{:S(2)}) collective-permute-start(f32[13,8,128]{2,1,0:T(8,128)S(1)} %get-tuple-element.78), channel_id=1, source_target_pairs={{0,1},{1,0},{2,3},{3,2},{4,5},{5,4},{6,7},{7,6},{8,9},{9,8},{10,11... | collective-permute-start | bytes 159752 | tf_op jit(solution)/shard_map/ppermute | solution.py:749
  10.4 0.7 collective-permute-start.4
  11.1 1.6 %shard_map.166 = (f32[24,16,128]{2,1,0:T(8,128)S(1)}, bf16[9,8,64]{2,1,0:T(8,128)(2,1)S(1)}, bf16[9,64,64]{2,1,0:T(8,128)(2,1)S(1)}, bf16[9,64,64]{2,1,0:T(8,128...) custom-call(f32[8,24,128]{2,1,0:T(8,128)} %temp_hbm.1, ...), custom_call_target="tpu_custom_call" | custom-call | flops 1000000 | bytes 2000000 | tf_op jit(solution)/shard_map/pallas_call | solution.py:45
  12.7 0.0 collective-permute-done.2.other_ref
  12.7 0.0 collective-permute-done.3.pair_ref
  12.7 0.0 collective-permute-done.4.cross_ref
  12.7 0.3 shard_map.168
  13.0 10.0 %collective-permute-start.5 = (f32[2,16,128]{2,1,0:T(8,128)S(1)}, f32[2,16,128]{2,1,0:T(8,128)S(1)}, u32[]{:S(2)}, u32[]{:S(2)}) collective-permute-start(f32[2,16,128]{2,1,0:T(8,128)S(1)} %get-tuple-element.81), channel_id=1, source_target_pairs={{0,496},{16,32},{32,16},{48,64},{64,48},{80,96},{96,80},{112,128},... | collective-permute-start | bytes 49160 | tf_op jit(solution)/shard_map/ppermute | solution.py:764
  23.0 4.1 %collective-permute-start.6 = (f32[2,16,128]{2,1,0:T(8,128)S(1)}, f32[2,16,128]{2,1,0:T(8,128)S(1)}, u32[]{:S(2)}, u32[]{:S(2)}) collective-permute-start(f32[2,16,128]{2,1,0:T(8,128)S(1)} %get-tuple-element.82), channel_id=1, source_target_pairs={{0,16},{16,0},{32,48},{48,32},{64,80},{80,64},{96,112},{112,96},{1... | collective-permute-start | bytes 49160 | tf_op jit(solution)/shard_map/ppermute | solution.py:765
  27.1 3.1 %shard_map.169 = (f32[32,8,128]{2,1,0:T(8,128)S(1)}, f32[8,128]{1,0:T(8,128)S(1)}, f32[40,16,128]{2,1,0:T(8,128)S(1)}, bf16[64,640]{1,0:T(8,128)(2,1)S(1)}, bf16...) custom-call(f32[40,16,128]{2,1,0:T(8,128)S(1)} %get-tuple-element.80, ...), custom_call_target="tpu_custom_call" | custom-call | tf_op jit(solution)/shard_map/pallas_call | solution.py:784
  30.2 0.0 collective-permute-done.5.far_ref
  30.2 0.0 collective-permute-done.6.near_ref
  30.2 1.7 %shard_map.170 = (f32[32,8,128]{2,1,0:T(8,128)S(1)}, f32[3,32,256]{2,1,0:T(8,128)S(1)}) custom-call(f32[40,16,128]{2,1,0:T(8,128)S(1)} %get-tuple-element.80.refs_0_.rows_ref, f32[2,16,128]{2,1,0:T(8,128)S(1)} %collective-permute-done.5.far_ref, f32[2,16,128]{2,1,0:T(8,128)S(1)} %collective-permute-done.6.near_ref, ...), custom_call_target="tpu_custom_call" | custom-call | tf_op jit(solution)/shard_map/pallas_call | solution.py:791
  32.0 37.8 %conditional.1 = (f32[288,128]{1,0:T(8,128)S(1)}) conditional(s32[]{:T(128)} %convert_element_type.3, f32[32,8,128]{2,1,0:T(8,128)S(1)} %get-tuple-element.97, (f32[32,8,128]{2,1,0:T(8,128)S(1)}, f32[8,128]{1,0:T(8,128)S(1)}, bf16[256,256]{1,0:T(8,128)(2,1)S(1)}, bf16[256,256]{1,0:T(8,128)(2,1)S(1)}, bf16[256,256]{1,0:T(8,128)(2,1)S(1)}, ...), branch_computations={%region_0.0_spmd, %region_1.0_spmd} | conditional | bytes 557064 | solution.py:813
  32.0 19.9 %all_to_all.30.x_ref = f32[32,8,128]{2,1,0:T(8,128)S(1)} all-to-all(f32[32,8,128]{2,1,0:T(8,128)S(1)} %get-tuple-element.26), channel_id=1, replica_groups=mesh['lon'=32,'lat'=16] {'lon'}, dimensions={0} | all-to-all | bytes 262144 | tf_op jit(solution)/shard_map/cond/branch_1_fun/all_to_all | solution.py:798
  51.9 1.2 %branch_1_fun.1 = f32[288,128]{1,0:T(8,128)S(1)} custom-call(f32[32,8,128]{2,1,0:T(8,128)S(1)} %all_to_all.30.x_ref, f32[8,128]{1,0:T(8,128)S(1)} %get-tuple-element.27.line_ref, bf16[256,256]{1,0:T(8,128)(2,1)S(1)} %get-tuple-element.28.spread_ref, bf16[256,256]{1,0:T(8,128)(2,1)S(1)} %get-tuple-element.29.spread_low, ...), custom_call_target="tpu_custom_call" | custom-call | tf_op jit(solution)/shard_map/cond/branch_1_fun/pallas_call | solution.py:799
  53.1 16.7 %all_to_all.31 = f32[288,1,128]{2,1,0:T(1,128)S(1)} all-to-all(f32[288,1,128]{2,1,0:T(1,128)S(1)} %bitcast.14), channel_id=1, replica_groups=mesh['lon'=32,'lat'=16] {'lon'}, dimensions={0} | all-to-all | bytes 294912 | tf_op jit(solution)/shard_map/cond/branch_1_fun/all_to_all | solution.py:801
  69.8 2.0 %shard_map.171 = (f32[8,24,128]{2,1,0:T(8,128)}, f32[5,32,128]{2,1,0:T(8,128)S(1)}, f32[16,128]{1,0:T(8,128)S(1)}) custom-call(f32[288,128]{1,0:T(8,128)S(1)} %get-tuple-element.113.x_ref, f32[3,32,256]{2,1,0:T(8,128)S(1)} %get-tuple-element.107.planes_ref), custom_call_target="tpu_custom_call" | custom-call | tf_op jit(solution)/shard_map/pallas_call | solution.py:818
  71.8 10.5 %all_to_all.32 = f32[16,1,128]{2,1,0:T(1,128)S(1)} all-to-all(f32[16,1,128]{2,1,0:T(1,128)S(1)} %bitcast.18), channel_id=1, replica_groups={{0,1,2,3,16,17,18,19,32,33,34,35,48,49,50,51},{4,5,6,7,20,21,22,23,36,3..., dimensions={0} | all-to-all | bytes 16384 | tf_op jit(solution)/shard_map/all_to_all | solution.py:830
  82.4 0.1 shard_map.172
  82.5 13.5 %all_to_all.33 = f32[32,1,128]{2,1,0:T(1,128)S(1)} all-to-all(f32[32,1,128]{2,1,0:T(1,128)S(1)} %bitcast.15), channel_id=1, replica_groups={{0,4,8,12,64,68,72,76,128,132,136,140,192,196,200,204,256,260,264,268,3..., dimensions={0} | all-to-all | bytes 32768 | tf_op jit(solution)/shard_map/all_to_all | solution.py:834
  96.0 1.1 %shard_map.173 = (f32[24,128]{1,0:T(8,128)}, f32[24,128]{1,0:T(8,128)}) custom-call(f32[32,128]{1,0:T(8,128)S(1)} %bitcast.16, f32[5,32,128]{2,1,0:T(8,128)S(1)} %get-tuple-element.110.powers_ref), custom_call_target="tpu_custom_call" | custom-call | tf_op jit(solution)/shard_map/pallas_call | solution.py:837
Async XLA Ops:
  1.6 11.1 %collective-permute-start.2 = (f32[13,8,128]{2,1,0:T(8,128)S(1)}, f32[13,8,128]{2,1,0:T(8,128)S(1)}, u32[]{:S(2)}, u32[]{:S(2)}) collective-permute-start(f32[13,8,128]{2,1,0:T(8,128)S(1)} %get-tuple-element.77), channel_id=1, source_target_pairs={{1,2},{5,6},{9,10},{13,14},{2,1},{6,5},{10,9},{14,13},{17,18},{21,... | collective-permute-start | bytes 159752 | tf_op jit(solution)/shard_map/ppermute | solution.py:748
  2.3 10.5 %collective-permute-start.3 = (f32[13,8,128]{2,1,0:T(8,128)S(1)}, f32[13,8,128]{2,1,0:T(8,128)S(1)}, u32[]{:S(2)}, u32[]{:S(2)}) collective-permute-start(f32[13,8,128]{2,1,0:T(8,128)S(1)} %get-tuple-element.78), channel_id=1, source_target_pairs={{0,1},{1,0},{2,3},{3,2},{4,5},{5,4},{6,7},{7,6},{8,9},{9,8},{10,11... | collective-permute-start | bytes 159752 | tf_op jit(solution)/shard_map/ppermute | solution.py:749
  10.4 2.3 %collective-permute-start.4 = (f32[13,8,128]{2,1,0:T(8,128)S(1)}, f32[13,8,128]{2,1,0:T(8,128)S(1)}, u32[]{:S(2)}, u32[]{:S(2)}) collective-permute-start(f32[13,8,128]{2,1,0:T(8,128)S(1)} %get-tuple-element.79), channel_id=1, source_target_pairs={{3,4},{7,8},{11,12},{4,3},{8,7},{12,11},{19,20},{23,24},{27,28},{2... | collective-permute-start | bytes 159752 | tf_op jit(solution)/shard_map/ppermute | solution.py:750
  13.0 17.2 %collective-permute-start.5 = (f32[2,16,128]{2,1,0:T(8,128)S(1)}, f32[2,16,128]{2,1,0:T(8,128)S(1)}, u32[]{:S(2)}, u32[]{:S(2)}) collective-permute-start(f32[2,16,128]{2,1,0:T(8,128)S(1)} %get-tuple-element.81), channel_id=1, source_target_pairs={{0,496},{16,32},{32,16},{48,64},{64,48},{80,96},{96,80},{112,128},... | collective-permute-start | bytes 49160 | tf_op jit(solution)/shard_map/ppermute | solution.py:764
  23.0 7.2 %collective-permute-start.6 = (f32[2,16,128]{2,1,0:T(8,128)S(1)}, f32[2,16,128]{2,1,0:T(8,128)S(1)}, u32[]{:S(2)}, u32[]{:S(2)}) collective-permute-start(f32[2,16,128]{2,1,0:T(8,128)S(1)} %get-tuple-element.82), channel_id=1, source_target_pairs={{0,16},{16,0},{32,48},{48,32},{64,80},{80,64},{96,112},{112,96},{1... | collective-permute-start | bytes 49160 | tf_op jit(solution)/shard_map/ppermute | solution.py:765

commit v14 on v13

--- a/solution.py
+++ b/solution.py
@@ -625,12 +625,15 @@
     for order in range(1, 2 * ITERS):
         high = jnp.where(where == order, high_rows[order], high)
         low = jnp.where(where == order, low_rows[order], low)
-    total = (high, low)
-    for by in (64, 32, 16, 8, 4, 2, 1):
-        total = pair_add(total, tuple(pltpu.roll(t, by, 1) for t in total))
-    spot = lax.broadcasted_iota(jnp.int32, (8, COLS), 0)
-    message = jnp.where(lane == spot, total[0], 0.0) + jnp.where(lane == spot + 64, total[1], 0.0)
-    message = jnp.sum(message, axis=0, keepdims=True)
+    high, low = high.T, low.T
+    tiles = [(high[8 * i : 8 * i + 8], low[8 * i : 8 * i + 8]) for i in range(COLS // 8)]
+    while len(tiles) > 1:
+        tiles = [pair_add(a, b) for a, b in zip(tiles[::2], tiles[1::2])]
+    total = tiles[0]
+    for by in (4, 2, 1):
+        total = pair_add(total, tuple(pltpu.roll(t, by, 0) for t in total))
+    gap = jnp.zeros((1, COLS // 2 - 2 * ITERS), jnp.float32)
+    message = jnp.concatenate([total[0][:1], gap, total[1][:1], gap], axis=1)
     parts_ref[...] = jnp.broadcast_to(message, parts_ref.shape)
     move.wait()
 

time: 97.5 us -> 97.3 us (level)
  no operation moved by 1% of the time
where the time goes in v14:
time: 97.3 us; the launch traced here: 96.8 us
  blocking collectives  60.6 us (62%)
  starting transfers between devices  23.5 us (24%)
  Pallas kernels  11.9 us (12%)
    all_to_all x2, blocking collectives, body(): lax.all_to_all(parts, both, split_axis=0, concat_axis=0, tiled=True, axis...  24 us
    all_to_all x1, blocking collectives, filtered_block(): lax.all_to_all(lines, 'lon', split_axis=0, concat_axis=0, tiled=True)  19.9 us
    all_to_all x1, blocking collectives, filtered_block(): lax.all_to_all(result, 'lon', split_axis=0, concat_axis=0, tiled=True)  16.7 us
    ppermute x1, starting transfers between devices, body(): far = lax.ppermute(to_far, 'lon', swap_far())  9.96 us
    ppermute x1, starting transfers between devices, body(): pair = lax.ppermute(to_pair, 'lat', swap_pair())  8.17 us
    ppermute x1, starting transfers between devices, body(): near = lax.ppermute(to_near, 'lon', swap_near())  4.09 us
    pallas_call x1, Pallas kernels, body(): call(interior_kernel, (block, shape((LEV, COLS), f32), shape((TALL, FIELD...  3.11 us
  transfers between devices with their start and end apart: 5, of which 0 were waited for; matrix products, arithmetic and copies ran while one was open for 0% of the time, Pallas kernels for 5%

profile of v14, /device:TPU:1, one launch (start us, length us, event | category | flops | bytes accessed | tf_op | source)
XLA Modules:
  0.0 96.8 jit_solution(12637041118518761961)
XLA Ops:
  0.6 1.0 shard_map.167
  1.6 0.7 collective-permute-start.2
  2.3 8.2 %collective-permute-start.3 = (f32[13,8,128]{2,1,0:T(8,128)S(1)}, f32[13,8,128]{2,1,0:T(8,128)S(1)}, u32[]{:S(2)}, u32[]{:S(2)}) collective-permute-start(f32[13,8,128]{2,1,0:T(8,128)S(1)} %get-tuple-element.78), channel_id=1, source_target_pairs={{0,1},{1,0},{2,3},{3,2},{4,5},{5,4},{6,7},{7,6},{8,9},{9,8},{10,11... | collective-permute-start | bytes 159752 | tf_op jit(solution)/shard_map/ppermute | solution.py:752
  10.4 0.7 collective-permute-start.4
  11.1 1.6 %shard_map.166 = (f32[24,16,128]{2,1,0:T(8,128)S(1)}, bf16[9,8,64]{2,1,0:T(8,128)(2,1)S(1)}, bf16[9,64,64]{2,1,0:T(8,128)(2,1)S(1)}, bf16[9,64,64]{2,1,0:T(8,128...) custom-call(f32[8,24,128]{2,1,0:T(8,128)} %temp_hbm.1, ...), custom_call_target="tpu_custom_call" | custom-call | flops 1000000 | bytes 2000000 | tf_op jit(solution)/shard_map/pallas_call | solution.py:45
  12.7 0.0 collective-permute-done.2.other_ref
  12.7 0.0 collective-permute-done.3.pair_ref
  12.7 0.0 collective-permute-done.4.cross_ref
  12.7 0.3 shard_map.168
  13.0 10.0 %collective-permute-start.5 = (f32[2,16,128]{2,1,0:T(8,128)S(1)}, f32[2,16,128]{2,1,0:T(8,128)S(1)}, u32[]{:S(2)}, u32[]{:S(2)}) collective-permute-start(f32[2,16,128]{2,1,0:T(8,128)S(1)} %get-tuple-element.81), channel_id=1, source_target_pairs={{0,496},{16,32},{32,16},{48,64},{64,48},{80,96},{96,80},{112,128},... | collective-permute-start | bytes 49160 | tf_op jit(solution)/shard_map/ppermute | solution.py:767
  23.0 4.1 %collective-permute-start.6 = (f32[2,16,128]{2,1,0:T(8,128)S(1)}, f32[2,16,128]{2,1,0:T(8,128)S(1)}, u32[]{:S(2)}, u32[]{:S(2)}) collective-permute-start(f32[2,16,128]{2,1,0:T(8,128)S(1)} %get-tuple-element.82), channel_id=1, source_target_pairs={{0,16},{16,0},{32,48},{48,32},{64,80},{80,64},{96,112},{112,96},{1... | collective-permute-start | bytes 49160 | tf_op jit(solution)/shard_map/ppermute | solution.py:768
  27.1 3.1 %shard_map.169 = (f32[32,8,128]{2,1,0:T(8,128)S(1)}, f32[8,128]{1,0:T(8,128)S(1)}, f32[40,16,128]{2,1,0:T(8,128)S(1)}, bf16[64,640]{1,0:T(8,128)(2,1)S(1)}, bf16...) custom-call(f32[40,16,128]{2,1,0:T(8,128)S(1)} %get-tuple-element.80, ...), custom_call_target="tpu_custom_call" | custom-call | tf_op jit(solution)/shard_map/pallas_call | solution.py:787
  30.2 0.0 collective-permute-done.5.far_ref
  30.2 0.0 collective-permute-done.6.near_ref
  30.2 1.7 %shard_map.170 = (f32[32,8,128]{2,1,0:T(8,128)S(1)}, f32[3,32,256]{2,1,0:T(8,128)S(1)}) custom-call(f32[40,16,128]{2,1,0:T(8,128)S(1)} %get-tuple-element.80.refs_0_.rows_ref, f32[2,16,128]{2,1,0:T(8,128)S(1)} %collective-permute-done.5.far_ref, f32[2,16,128]{2,1,0:T(8,128)S(1)} %collective-permute-done.6.near_ref, ...), custom_call_target="tpu_custom_call" | custom-call | tf_op jit(solution)/shard_map/pallas_call | solution.py:794
  32.0 37.8 %conditional.1 = (f32[288,128]{1,0:T(8,128)S(1)}) conditional(s32[]{:T(128)} %convert_element_type.3, f32[32,8,128]{2,1,0:T(8,128)S(1)} %get-tuple-element.97, (f32[32,8,128]{2,1,0:T(8,128)S(1)}, f32[8,128]{1,0:T(8,128)S(1)}, bf16[256,256]{1,0:T(8,128)(2,1)S(1)}, bf16[256,256]{1,0:T(8,128)(2,1)S(1)}, bf16[256,256]{1,0:T(8,128)(2,1)S(1)}, ...), branch_computations={%region_0.0_spmd, %region_1.0_spmd} | conditional | bytes 557064 | solution.py:816
  32.0 19.9 %all_to_all.30.x_ref = f32[32,8,128]{2,1,0:T(8,128)S(1)} all-to-all(f32[32,8,128]{2,1,0:T(8,128)S(1)} %get-tuple-element.26), channel_id=1, replica_groups=mesh['lon'=32,'lat'=16] {'lon'}, dimensions={0} | all-to-all | bytes 262144 | tf_op jit(solution)/shard_map/cond/branch_1_fun/all_to_all | solution.py:801
  51.9 1.2 %branch_1_fun.1 = f32[288,128]{1,0:T(8,128)S(1)} custom-call(f32[32,8,128]{2,1,0:T(8,128)S(1)} %all_to_all.30.x_ref, f32[8,128]{1,0:T(8,128)S(1)} %get-tuple-element.27.line_ref, bf16[256,256]{1,0:T(8,128)(2,1)S(1)} %get-tuple-element.28.spread_ref, bf16[256,256]{1,0:T(8,128)(2,1)S(1)} %get-tuple-element.29.spread_low, ...), custom_call_target="tpu_custom_call" | custom-call | tf_op jit(solution)/shard_map/cond/branch_1_fun/pallas_call | solution.py:802
  53.1 16.7 %all_to_all.31 = f32[288,1,128]{2,1,0:T(1,128)S(1)} all-to-all(f32[288,1,128]{2,1,0:T(1,128)S(1)} %bitcast.14), channel_id=1, replica_groups=mesh['lon'=32,'lat'=16] {'lon'}, dimensions={0} | all-to-all | bytes 294912 | tf_op jit(solution)/shard_map/cond/branch_1_fun/all_to_all | solution.py:804
  69.8 1.8 %shard_map.171 = (f32[8,24,128]{2,1,0:T(8,128)}, f32[5,32,128]{2,1,0:T(8,128)S(1)}, f32[16,128]{1,0:T(8,128)S(1)}) custom-call(f32[288,128]{1,0:T(8,128)S(1)} %get-tuple-element.113.x_ref, f32[3,32,256]{2,1,0:T(8,128)S(1)} %get-tuple-element.107.planes_ref), custom_call_target="tpu_custom_call" | custom-call | tf_op jit(solution)/shard_map/pallas_call | solution.py:821
  71.6 10.5 %all_to_all.32 = f32[16,1,128]{2,1,0:T(1,128)S(1)} all-to-all(f32[16,1,128]{2,1,0:T(1,128)S(1)} %bitcast.18), channel_id=1, replica_groups={{0,1,2,3,16,17,18,19,32,33,34,35,48,49,50,51},{4,5,6,7,20,21,22,23,36,3..., dimensions={0} | all-to-all | bytes 16384 | tf_op jit(solution)/shard_map/all_to_all | solution.py:833
  82.2 0.1 shard_map.172
  82.3 13.5 %all_to_all.33 = f32[32,1,128]{2,1,0:T(1,128)S(1)} all-to-all(f32[32,1,128]{2,1,0:T(1,128)S(1)} %bitcast.15), channel_id=1, replica_groups={{0,4,8,12,64,68,72,76,128,132,136,140,192,196,200,204,256,260,264,268,3..., dimensions={0} | all-to-all | bytes 32768 | tf_op jit(solution)/shard_map/all_to_all | solution.py:837
  95.8 1.1 %shard_map.173 = (f32[24,128]{1,0:T(8,128)}, f32[24,128]{1,0:T(8,128)}) custom-call(f32[32,128]{1,0:T(8,128)S(1)} %bitcast.16, f32[5,32,128]{2,1,0:T(8,128)S(1)} %get-tuple-element.110.powers_ref), custom_call_target="tpu_custom_call" | custom-call | tf_op jit(solution)/shard_map/pallas_call | solution.py:840
Async XLA Ops:
  1.6 11.1 %collective-permute-start.2 = (f32[13,8,128]{2,1,0:T(8,128)S(1)}, f32[13,8,128]{2,1,0:T(8,128)S(1)}, u32[]{:S(2)}, u32[]{:S(2)}) collective-permute-start(f32[13,8,128]{2,1,0:T(8,128)S(1)} %get-tuple-element.77), channel_id=1, source_target_pairs={{1,2},{5,6},{9,10},{13,14},{2,1},{6,5},{10,9},{14,13},{17,18},{21,... | collective-permute-start | bytes 159752 | tf_op jit(solution)/shard_map/ppermute | solution.py:751
  2.3 10.5 %collective-permute-start.3 = (f32[13,8,128]{2,1,0:T(8,128)S(1)}, f32[13,8,128]{2,1,0:T(8,128)S(1)}, u32[]{:S(2)}, u32[]{:S(2)}) collective-permute-start(f32[13,8,128]{2,1,0:T(8,128)S(1)} %get-tuple-element.78), channel_id=1, source_target_pairs={{0,1},{1,0},{2,3},{3,2},{4,5},{5,4},{6,7},{7,6},{8,9},{9,8},{10,11... | collective-permute-start | bytes 159752 | tf_op jit(solution)/shard_map/ppermute | solution.py:752
  10.4 2.3 %collective-permute-start.4 = (f32[13,8,128]{2,1,0:T(8,128)S(1)}, f32[13,8,128]{2,1,0:T(8,128)S(1)}, u32[]{:S(2)}, u32[]{:S(2)}) collective-permute-start(f32[13,8,128]{2,1,0:T(8,128)S(1)} %get-tuple-element.79), channel_id=1, source_target_pairs={{3,4},{7,8},{11,12},{4,3},{8,7},{12,11},{19,20},{23,24},{27,28},{2... | collective-permute-start | bytes 159752 | tf_op jit(solution)/shard_map/ppermute | solution.py:753
  13.0 17.2 %collective-permute-start.5 = (f32[2,16,128]{2,1,0:T(8,128)S(1)}, f32[2,16,128]{2,1,0:T(8,128)S(1)}, u32[]{:S(2)}, u32[]{:S(2)}) collective-permute-start(f32[2,16,128]{2,1,0:T(8,128)S(1)} %get-tuple-element.81), channel_id=1, source_target_pairs={{0,496},{16,32},{32,16},{48,64},{64,48},{80,96},{96,80},{112,128},... | collective-permute-start | bytes 49160 | tf_op jit(solution)/shard_map/ppermute | solution.py:767
  23.0 7.2 %collective-permute-start.6 = (f32[2,16,128]{2,1,0:T(8,128)S(1)}, f32[2,16,128]{2,1,0:T(8,128)S(1)}, u32[]{:S(2)}, u32[]{:S(2)}) collective-permute-start(f32[2,16,128]{2,1,0:T(8,128)S(1)} %get-tuple-element.82), channel_id=1, source_target_pairs={{0,16},{16,0},{32,48},{48,32},{64,80},{80,64},{96,112},{112,96},{1... | collective-permute-start | bytes 49160 | tf_op jit(solution)/shard_map/ppermute | solution.py:768

commit v15 on v12

--- a/solution.py
+++ b/solution.py
@@ -629,12 +629,15 @@
     for order in range(1, 2 * ITERS):
         high = jnp.where(where == order, high_rows[order], high)
         low = jnp.where(where == order, low_rows[order], low)
-    total = (high, low)
-    for by in (64, 32, 16, 8, 4, 2, 1):
-        total = pair_add(total, tuple(pltpu.roll(t, by, 1) for t in total))
-    spot = lax.broadcasted_iota(jnp.int32, (8, COLS), 0)
-    message = jnp.where(lane == spot, total[0], 0.0) + jnp.where(lane == spot + 64, total[1], 0.0)
-    message = jnp.sum(message, axis=0, keepdims=True)
+    high, low = high.T, low.T
+    tiles = [(high[8 * i : 8 * i + 8], low[8 * i : 8 * i + 8]) for i in range(COLS // 8)]
+    while len(tiles) > 1:
+        tiles = [pair_add(a, b) for a, b in zip(tiles[::2], tiles[1::2])]
+    total = tiles[0]
+    for by in (4, 2, 1):
+        total = pair_add(total, tuple(pltpu.roll(t, by, 0) for t in total))
+    gap = jnp.zeros((1, COLS // 2 - 2 * ITERS), jnp.float32)
+    message = jnp.concatenate([total[0][:1], gap, total[1][:1], gap], axis=1)
     parts_ref[...] = jnp.broadcast_to(message, parts_ref.shape)
     move.wait()
 

time: 97.5 us -> 97.3 us (level)
  no operation moved by 1% of the time
where the time goes in v15:
time: 97.3 us; the launch traced here: 96.9 us
  blocking collectives  60.6 us (62%)
  starting transfers between devices  23.5 us (24%)
  Pallas kernels  11.9 us (12%)
    all_to_all x2, blocking collectives, body(): lax.all_to_all(parts, both, split_axis=0, concat_axis=0, tiled=True, axis...  24 us
    all_to_all x1, blocking collectives, filtered_block(): lax.all_to_all(lines, 'lon', split_axis=0, concat_axis=0, tiled=True)  19.9 us
    all_to_all x1, blocking collectives, filtered_block(): lax.all_to_all(result, 'lon', split_axis=0, concat_axis=0, tiled=True)  16.7 us
    ppermute x1, starting transfers between devices, body(): far = lax.ppermute(to_far, 'lon', swap_far())  9.96 us
    ppermute x1, starting transfers between devices, body(): pair = lax.ppermute(to_pair, 'lat', swap_pair())  8.17 us
    ppermute x1, starting transfers between devices, body(): near = lax.ppermute(to_near, 'lon', swap_near())  4.09 us
    pallas_call x1, Pallas kernels, body(): call(interior_kernel, (block, shape((LEV, COLS), f32), shape((TALL, FIELD...  3.11 us
  transfers between devices with their start and end apart: 5, of which 0 were waited for; matrix products, arithmetic and copies ran while one was open for 0% of the time, Pallas kernels for 5%

profile of v15, /device:TPU:1, one launch (start us, length us, event | category | flops | bytes accessed | tf_op | source)
XLA Modules:
  0.0 96.9 jit_solution(9073300172912013044)
XLA Ops:
  0.6 1.0 shard_map.167
  1.6 0.7 collective-permute-start.2
  2.3 8.2 %collective-permute-start.3 = (f32[13,8,128]{2,1,0:T(8,128)S(1)}, f32[13,8,128]{2,1,0:T(8,128)S(1)}, u32[]{:S(2)}, u32[]{:S(2)}) collective-permute-start(f32[13,8,128]{2,1,0:T(8,128)S(1)} %get-tuple-element.78), channel_id=1, source_target_pairs={{0,1},{1,0},{2,3},{3,2},{4,5},{5,4},{6,7},{7,6},{8,9},{9,8},{10,11... | collective-permute-start | bytes 159752 | tf_op jit(solution)/shard_map/ppermute | solution.py:757
  10.4 0.7 collective-permute-start.4
  11.1 1.6 %shard_map.166 = (f32[24,16,128]{2,1,0:T(8,128)S(1)}, bf16[9,8,64]{2,1,0:T(8,128)(2,1)S(1)}, bf16[9,64,64]{2,1,0:T(8,128)(2,1)S(1)}, bf16[9,64,64]{2,1,0:T(8,128...) custom-call(f32[8,24,128]{2,1,0:T(8,128)} %temp_hbm.1, ...), custom_call_target="tpu_custom_call" | custom-call | flops 1000000 | bytes 2000000 | tf_op jit(solution)/shard_map/pallas_call | solution.py:45
  12.7 0.0 collective-permute-done.2.other_ref
  12.7 0.0 collective-permute-done.3.pair_ref
  12.7 0.0 collective-permute-done.4.cross_ref
  12.7 0.3 shard_map.168
  13.0 10.0 %collective-permute-start.5 = (f32[2,16,128]{2,1,0:T(8,128)S(1)}, f32[2,16,128]{2,1,0:T(8,128)S(1)}, u32[]{:S(2)}, u32[]{:S(2)}) collective-permute-start(f32[2,16,128]{2,1,0:T(8,128)S(1)} %get-tuple-element.81), channel_id=1, source_target_pairs={{0,496},{16,32},{32,16},{48,64},{64,48},{80,96},{96,80},{112,128},... | collective-permute-start | bytes 49160 | tf_op jit(solution)/shard_map/ppermute | solution.py:772
  23.0 4.1 %collective-permute-start.6 = (f32[2,16,128]{2,1,0:T(8,128)S(1)}, f32[2,16,128]{2,1,0:T(8,128)S(1)}, u32[]{:S(2)}, u32[]{:S(2)}) collective-permute-start(f32[2,16,128]{2,1,0:T(8,128)S(1)} %get-tuple-element.82), channel_id=1, source_target_pairs={{0,16},{16,0},{32,48},{48,32},{64,80},{80,64},{96,112},{112,96},{1... | collective-permute-start | bytes 49160 | tf_op jit(solution)/shard_map/ppermute | solution.py:773
  27.1 3.1 %shard_map.169 = (f32[32,8,128]{2,1,0:T(8,128)S(1)}, f32[8,128]{1,0:T(8,128)S(1)}, f32[40,16,128]{2,1,0:T(8,128)S(1)}, bf16[64,640]{1,0:T(8,128)(2,1)S(1)}, bf16...) custom-call(f32[40,16,128]{2,1,0:T(8,128)S(1)} %get-tuple-element.80, ...), custom_call_target="tpu_custom_call" | custom-call | tf_op jit(solution)/shard_map/pallas_call | solution.py:792
  30.2 0.0 collective-permute-done.5.far_ref
  30.2 0.0 collective-permute-done.6.near_ref
  30.2 1.7 %shard_map.170 = (f32[32,8,128]{2,1,0:T(8,128)S(1)}, f32[3,32,256]{2,1,0:T(8,128)S(1)}) custom-call(f32[40,16,128]{2,1,0:T(8,128)S(1)} %get-tuple-element.80.refs_0_.rows_ref, f32[2,16,128]{2,1,0:T(8,128)S(1)} %collective-permute-done.5.far_ref, f32[2,16,128]{2,1,0:T(8,128)S(1)} %collective-permute-done.6.near_ref, ...), custom_call_target="tpu_custom_call" | custom-call | tf_op jit(solution)/shard_map/pallas_call | solution.py:799
  32.0 37.8 %conditional.1 = (f32[288,128]{1,0:T(8,128)S(1)}) conditional(s32[]{:T(128)} %convert_element_type.3, f32[32,8,128]{2,1,0:T(8,128)S(1)} %get-tuple-element.97, (f32[32,8,128]{2,1,0:T(8,128)S(1)}, f32[8,128]{1,0:T(8,128)S(1)}, bf16[256,256]{1,0:T(8,128)(2,1)S(1)}, bf16[256,256]{1,0:T(8,128)(2,1)S(1)}, bf16[256,256]{1,0:T(8,128)(2,1)S(1)}, ...), branch_computations={%region_0.0_spmd, %region_1.0_spmd} | conditional | bytes 557064 | solution.py:821
  32.0 19.9 %all_to_all.30.x_ref = f32[32,8,128]{2,1,0:T(8,128)S(1)} all-to-all(f32[32,8,128]{2,1,0:T(8,128)S(1)} %get-tuple-element.26), channel_id=1, replica_groups=mesh['lon'=32,'lat'=16] {'lon'}, dimensions={0} | all-to-all | bytes 262144 | tf_op jit(solution)/shard_map/cond/branch_1_fun/all_to_all | solution.py:806
  51.9 1.2 %branch_1_fun.1 = f32[288,128]{1,0:T(8,128)S(1)} custom-call(f32[32,8,128]{2,1,0:T(8,128)S(1)} %all_to_all.30.x_ref, f32[8,128]{1,0:T(8,128)S(1)} %get-tuple-element.27.line_ref, bf16[256,256]{1,0:T(8,128)(2,1)S(1)} %get-tuple-element.28.spread_ref, bf16[256,256]{1,0:T(8,128)(2,1)S(1)} %get-tuple-element.29.spread_low, ...), custom_call_target="tpu_custom_call" | custom-call | tf_op jit(solution)/shard_map/cond/branch_1_fun/pallas_call | solution.py:807
  53.1 16.7 %all_to_all.31 = f32[288,1,128]{2,1,0:T(1,128)S(1)} all-to-all(f32[288,1,128]{2,1,0:T(1,128)S(1)} %bitcast.14), channel_id=1, replica_groups=mesh['lon'=32,'lat'=16] {'lon'}, dimensions={0} | all-to-all | bytes 294912 | tf_op jit(solution)/shard_map/cond/branch_1_fun/all_to_all | solution.py:809
  69.8 1.8 %shard_map.171 = (f32[8,24,128]{2,1,0:T(8,128)}, f32[5,32,256]{2,1,0:T(8,128)S(1)}, f32[16,128]{1,0:T(8,128)S(1)}) custom-call(f32[288,128]{1,0:T(8,128)S(1)} %get-tuple-element.113.x_ref, f32[3,32,256]{2,1,0:T(8,128)S(1)} %get-tuple-element.107.planes_ref), custom_call_target="tpu_custom_call" | custom-call | tf_op jit(solution)/shard_map/pallas_call | solution.py:826
  71.6 10.5 %all_to_all.32 = f32[16,1,128]{2,1,0:T(1,128)S(1)} all-to-all(f32[16,1,128]{2,1,0:T(1,128)S(1)} %bitcast.18), channel_id=1, replica_groups={{0,1,2,3,16,17,18,19,32,33,34,35,48,49,50,51},{4,5,6,7,20,21,22,23,36,3..., dimensions={0} | all-to-all | bytes 16384 | tf_op jit(solution)/shard_map/all_to_all | solution.py:838
  82.1 0.1 shard_map.172
  82.2 13.5 %all_to_all.33 = f32[32,1,128]{2,1,0:T(1,128)S(1)} all-to-all(f32[32,1,128]{2,1,0:T(1,128)S(1)} %bitcast.15), channel_id=1, replica_groups={{0,4,8,12,64,68,72,76,128,132,136,140,192,196,200,204,256,260,264,268,3..., dimensions={0} | all-to-all | bytes 32768 | tf_op jit(solution)/shard_map/all_to_all | solution.py:842
  95.7 1.1 %shard_map.173 = (f32[24,128]{1,0:T(8,128)}, f32[24,128]{1,0:T(8,128)}) custom-call(f32[32,128]{1,0:T(8,128)S(1)} %bitcast.16, f32[5,32,256]{2,1,0:T(8,128)S(1)} %get-tuple-element.110.powers_ref), custom_call_target="tpu_custom_call" | custom-call | tf_op jit(solution)/shard_map/pallas_call | solution.py:845
Async XLA Ops:
  1.6 11.1 %collective-permute-start.2 = (f32[13,8,128]{2,1,0:T(8,128)S(1)}, f32[13,8,128]{2,1,0:T(8,128)S(1)}, u32[]{:S(2)}, u32[]{:S(2)}) collective-permute-start(f32[13,8,128]{2,1,0:T(8,128)S(1)} %get-tuple-element.77), channel_id=1, source_target_pairs={{1,2},{5,6},{9,10},{13,14},{2,1},{6,5},{10,9},{14,13},{17,18},{21,... | collective-permute-start | bytes 159752 | tf_op jit(solution)/shard_map/ppermute | solution.py:756
  2.3 10.5 %collective-permute-start.3 = (f32[13,8,128]{2,1,0:T(8,128)S(1)}, f32[13,8,128]{2,1,0:T(8,128)S(1)}, u32[]{:S(2)}, u32[]{:S(2)}) collective-permute-start(f32[13,8,128]{2,1,0:T(8,128)S(1)} %get-tuple-element.78), channel_id=1, source_target_pairs={{0,1},{1,0},{2,3},{3,2},{4,5},{5,4},{6,7},{7,6},{8,9},{9,8},{10,11... | collective-permute-start | bytes 159752 | tf_op jit(solution)/shard_map/ppermute | solution.py:757
  10.4 2.3 %collective-permute-start.4 = (f32[13,8,128]{2,1,0:T(8,128)S(1)}, f32[13,8,128]{2,1,0:T(8,128)S(1)}, u32[]{:S(2)}, u32[]{:S(2)}) collective-permute-start(f32[13,8,128]{2,1,0:T(8,128)S(1)} %get-tuple-element.79), channel_id=1, source_target_pairs={{3,4},{7,8},{11,12},{4,3},{8,7},{12,11},{19,20},{23,24},{27,28},{2... | collective-permute-start | bytes 159752 | tf_op jit(solution)/shard_map/ppermute | solution.py:758
  13.0 17.2 %collective-permute-start.5 = (f32[2,16,128]{2,1,0:T(8,128)S(1)}, f32[2,16,128]{2,1,0:T(8,128)S(1)}, u32[]{:S(2)}, u32[]{:S(2)}) collective-permute-start(f32[2,16,128]{2,1,0:T(8,128)S(1)} %get-tuple-element.81), channel_id=1, source_target_pairs={{0,496},{16,32},{32,16},{48,64},{64,48},{80,96},{96,80},{112,128},... | collective-permute-start | bytes 49160 | tf_op jit(solution)/shard_map/ppermute | solution.py:772
  23.0 7.2 %collective-permute-start.6 = (f32[2,16,128]{2,1,0:T(8,128)S(1)}, f32[2,16,128]{2,1,0:T(8,128)S(1)}, u32[]{:S(2)}, u32[]{:S(2)}) collective-permute-start(f32[2,16,128]{2,1,0:T(8,128)S(1)} %get-tuple-element.82), channel_id=1, source_target_pairs={{0,16},{16,0},{32,48},{48,32},{64,80},{80,64},{96,112},{112,96},{1... | collective-permute-start | bytes 49160 | tf_op jit(solution)/shard_map/ppermute | solution.py:773
